TPU v7x, 32 devices: a whole 2x2x4 slice. The times are simulated.
32 devices in a mesh: comp: 4 (over x, core), dom: 8 (over z, y).
Axes of the slice: x: 2, y: 2, z: 4, core: 2. Of those that a mesh axis runs over, the one named last changes fastest.
Arguments:
- air_warmth: float32 [16, 64, 4096], P(None, None, ('comp', 'dom')), may hold values from -6 to 6
- eastern_breeze: bfloat16 [16, 64, 4096], P(None, None, ('comp', 'dom')), may hold values from -6 to 6
- northern_breeze: bfloat16 [16, 64, 4096], P(None, None, ('comp', 'dom')), may hold values from -6 to 6
- reciprocal_breadth: float32 [4096], P(('comp', 'dom')), may hold values from 0.5 to 2
- panel_neighbours: int32 [4, 4096], P(None, ('comp', 'dom')), may hold values from 0 to 4095, as said below
- transfer_coefficients: bfloat16 [1024, 128, 128], P(('comp', 'dom')), may hold values from -0.375 to 0.375
- transfer_across_tile: int32 [1024], P(('comp', 'dom')), may hold values from 0 to 15, as said below
- transfer_holder: int32 [1024, 1], P(('comp', 'dom')), may hold values from 0 to 31; in each aligned block of 32 rows (0 to 31, 32 to 63, ...) at most 2 rows name the same one
- transfer_down_tile: int32 [1024], P(('comp', 'dom')), may hold values from 0 to 31
- water_elevation: float32 [131072], P(('comp', 'dom')), may hold values from -6 to 6
- depth_mean_current: float32 [2, 131072], P(None, ('comp', 'dom')), may hold values from -6 to 6
- marine_skin_warmth: float32 [131072], P(('comp', 'dom')), may hold values from -6 to 6
- patch_neighbours: int32 [6, 131072], P(None, ('comp', 'dom')), may hold values from -1 to 4607, as said below
- interface_span: float32 [6, 131072], P(None, ('comp', 'dom')), may hold values from 0.5 to 2
Outputs:
- closing_air_warmth: float32 [16, 64, 4096], P(None, None, ('comp', 'dom'))
- level_out: float32 [131072], P(('comp', 'dom'))
- velocity_out: float32 [2, 131072], P(None, ('comp', 'dom'))
- updated_sea_warmth: float32 [131072], P(('comp', 'dom'))
Inputs may be any that keep to these rules, and one draw needn't show every extreme that they name: `panel_neighbours`: entry [k, e] is the element across side k (south, east, north, west) of e, whose side (k + 2) mod 4 faces e with the points in the same order; the relation is symmetric. It lies in e's aligned block of 128 elements, or for k = 1 in the next block and for k = 3 in the previous one, cyclically. In each block exactly 32 elements have their east partner in the next block and exactly 32 their west partner in the previous one. `transfer_across_tile`: in each aligned block of 32 entries every value 0 .. 15 appears exactly 2 times. `transfer_holder`: in each aligned block of 32 rows no owner is named more than 2 times, a bound that some block reaches. `patch_neighbours`: with cells in aligned blocks of 4096, a cell's extended positions are the last 256 cells of the previous block (0 .. 255), its own block (256 .. 4351) and the first 256 cells of the next block, cyclically. Entry [k, i] is -1 or the position of a cell j whose slot (k + 3) mod 6 names i; only cells among the first 256 of a block have neighbours in the previous block, and only cells among the last 256 in the next one.
All inputs are finite; a program needn't handle non-finite values.
Results may differ from a plain program's by a relative error of at most 0.0026.
Values may be sent and summed in bfloat16 or wider, within the bound.
No kernel may reach another device: no remote copies, remote signals or barrier semaphores. Data moves between devices by JAX's collectives and lax.ppermute only.
A program may use at most 64 MiB of HBM per device.

v0:
```python
import math

import jax
import jax.numpy as jnp
import numpy as np
from jax import lax
from jax.sharding import PartitionSpec as P

OY = 256
NSUB = 4


STEP_SIZE = 0.05
JUMP_WEIGHT = 4.0
NUDGING_SPEED = 0.5
DAMPING = 0.9
GRAVITY = 0.3
WIND_GAIN = 0.3
DEPTH_RATE = 0.3
WARMING_COEFF = 0.3
SPREADING_COEFF = 0.5


def shifted(value, axis, steps):
    count = lax.axis_size(axis)
    pairs = [(source, (source + steps) % count) for source in range(count)]
    return lax.ppermute(value, axis, pairs)


def with_halo(value, sides, width):
    for axis, dim in sides:
        size, length = (lax.axis_size(axis), value.shape[dim])
        up = [(i, (i + 1) % size) for i in range(size)]
        down = [(j, i) for i, j in up]
        last = lax.slice_in_dim(value, length - width, length, axis=dim)
        first = lax.slice_in_dim(value, 0, width, axis=dim)
        before = lax.ppermute(last, axis, up)
        after = lax.ppermute(first, axis, down)
        value = jnp.concatenate([before, value, after], axis=dim)
    return value


def derivative_tables():
    points = np.array([-1.0, -1.0 / np.sqrt(5.0), 1.0 / np.sqrt(5.0), 1.0])
    barycentric = np.array(
        [
            1.0 / np.prod([points[source] - points[other] for other in range(4) if other != source])
            for source in range(4)
        ]
    )
    lagrange = np.zeros((4, 4))
    for target in range(4):
        for source in range(4):
            if target != source:
                lagrange[target, source] = (
                    barycentric[source] / barycentric[target] / (points[target] - points[source])
                )
        lagrange[target, target] = -np.sum(lagrange[target])
    identity = np.eye(4)
    return (
        jnp.asarray(np.kron(identity, lagrange), jnp.float32),
        jnp.asarray(np.kron(lagrange, identity), jnp.float32),
    )


def edge_trace(state_now, side_index):
    if side_index == 0:
        return state_now[0:4]
    if side_index == 1:
        return state_now[3::4]
    if side_index == 2:
        return state_now[12:16]
    return state_now[0::4]


def add_side(penalty, side_index, values):
    if side_index == 0:
        return penalty.at[0:4].add(values)
    if side_index == 1:
        return penalty.at[3::4].add(values)
    if side_index == 2:
        return penalty.at[12:16].add(values)
    return penalty.at[0::4].add(values)


def atmos_step(state_now, eastern_breeze, northern_breeze, reciprocal_breadth, edge_plan):
    local_ids, remote_ids, near_flags, send_east, send_west = edge_plan
    diff_x, diff_y = derivative_tables()
    east_side = edge_trace(state_now, 1)
    west_side = edge_trace(state_now, 3)
    from_next = shifted(west_side, ("comp", "dom"), -1)
    from_prev = shifted(east_side, ("comp", "dom"), 1)
    grad_x = jnp.einsum("pq,qle->ple", diff_x, state_now, precision=lax.Precision.HIGHEST)
    grad_y = jnp.einsum("pq,qle->ple", diff_y, state_now, precision=lax.Precision.HIGHEST)
    advect = -(
        eastern_breeze.astype(jnp.float32) * grad_x + northern_breeze.astype(jnp.float32) * grad_y
    )
    penalty = jnp.zeros_like(state_now)
    for side_index in range(4):
        facing = jnp.take(
            edge_trace(state_now, (side_index + 2) % 4), local_ids[side_index], axis=2
        )
        if side_index == 1:
            facing = jnp.where(near_flags[1], facing, jnp.take(from_next, remote_ids[1], axis=2))
        if side_index == 3:
            facing = jnp.where(near_flags[3], facing, jnp.take(from_prev, remote_ids[3], axis=2))
        penalty = add_side(penalty, side_index, facing - edge_trace(state_now, side_index))
    return state_now + STEP_SIZE * reciprocal_breadth * (advect + JUMP_WEIGHT * penalty)


def surface_fluxes(state_now, eastern_breeze, northern_breeze):
    lower_u = eastern_breeze[:, 0, :].astype(jnp.float32)
    lower_v = northern_breeze[:, 0, :].astype(jnp.float32)
    wind_speed = jnp.sqrt(lower_u * lower_u + lower_v * lower_v + 1.0)
    return jnp.stack(
        [wind_speed * state_now[:, 0, :], wind_speed * lower_u, wind_speed * lower_v]
    ).astype(jnp.bfloat16)


def cell_weights(patch_neighbours, interface_span):
    present = patch_neighbours >= 0
    angles = jnp.arange(6, dtype=jnp.float32)[:, None] * (math.pi / 3.0)
    weight_x = jnp.where(present, jnp.cos(angles) * interface_span / 3.0, 0.0)
    weight_y = jnp.where(present, jnp.sin(angles) * interface_span / 3.0, 0.0)
    central_coefficient = jnp.where(present, interface_span / 6.0, 0.0)
    return (weight_x, weight_y, central_coefficient)


def slot_layout(owners, devices, capacity):
    owner_table = (owners[:, None] == jnp.arange(devices, dtype=jnp.int32)[None, :]).astype(
        jnp.int32
    )
    slot_rank = jnp.sum(jnp.cumsum(owner_table, axis=0) * owner_table, axis=1) - 1
    return owners * capacity + slot_rank


def shards(
    air_warmth,
    eastern_breeze,
    northern_breeze,
    reciprocal_breadth,
    panel_neighbours,
    transfer_coefficients,
    transfer_across_tile,
    transfer_holder,
    transfer_down_tile,
    water_elevation,
    depth_mean_current,
    marine_skin_warmth,
    patch_neighbours,
    interface_span,
):
    devices = lax.axis_size(("comp", "dom"))
    shard_index = lax.axis_index(("comp", "dom"))
    elem_count = air_warmth.shape[2]
    local_ids = panel_neighbours % elem_count
    offsets = (panel_neighbours // elem_count - shard_index) % devices
    near_flags = offsets == 0
    edge_plan = (local_ids, local_ids, near_flags, None, None)
    after_first = atmos_step(
        air_warmth, eastern_breeze, northern_breeze, reciprocal_breadth, edge_plan
    )
    fluxes = surface_fluxes(after_first, eastern_breeze, northern_breeze)
    block_width = transfer_coefficients.shape[1]
    tile_lines = transfer_coefficients.shape[2]
    sources = fluxes.reshape(fluxes.shape[0], -1, block_width)
    picked_data = jnp.take(sources, transfer_across_tile, axis=1)
    partial_sums = jnp.einsum(
        "fbc,bcr->bfr", picked_data, transfer_coefficients, preferred_element_type=jnp.float32
    )
    block_count = transfer_across_tile.shape[0]
    capacity = max(2, 2 * block_count // devices)
    slot_index = slot_layout(transfer_holder[:, 0], devices, capacity)
    cell_count = water_elevation.shape[0]
    tiled_groups = cell_count // tile_lines
    outgoing = (
        jnp.zeros((devices * capacity, partial_sums.shape[1] * tile_lines), jnp.float32)
        .at[slot_index]
        .set(partial_sums.reshape(block_count, -1))
    )
    wanted = (
        jnp.full((devices * capacity,), tiled_groups, jnp.int32)
        .at[slot_index]
        .set(transfer_down_tile)
    )
    arrived, wanted_row_list = (
        lax.all_to_all(outgoing, ("comp", "dom"), split_axis=0, concat_axis=0, tiled=True),
        lax.all_to_all(wanted, ("comp", "dom"), split_axis=0, concat_axis=0, tiled=True),
    )
    chosen = (
        wanted_row_list[:, None] == jnp.arange(tiled_groups, dtype=jnp.int32)[None, :]
    ).astype(jnp.float32)
    thermal_driver = jnp.einsum("sr,sk->rk", chosen, arrived, precision=lax.Precision.HIGHEST)
    thermal_driver = (
        thermal_driver.reshape(tiled_groups, -1, tile_lines)
        .transpose(1, 0, 2)
        .reshape(-1, cell_count)
    )
    matrix_lines = OY
    tally_across = cell_count // matrix_lines
    present = patch_neighbours >= 0
    spread = jnp.where(present, patch_neighbours, 0)
    weight_x, weight_y, central_coefficient = cell_weights(patch_neighbours, interface_span)

    def neighbours(extended):
        return extended.reshape(extended.shape[0], -1)[:, spread]

    ocean_rims = with_halo(
        jnp.stack([water_elevation, marine_skin_warmth]).reshape(2, tally_across, matrix_lines),
        ((("comp", "dom"), 1),),
        1,
    )
    near_start = neighbours(ocean_rims)
    near_level = near_start[0]
    adjacent_warmth = near_start[1]
    updated_sea_warmth = (
        marine_skin_warmth
        + WARMING_COEFF * thermal_driver[0]
        + SPREADING_COEFF
        * jnp.sum(central_coefficient * (adjacent_warmth - marine_skin_warmth), axis=0)
    )
    halfway_sea_warmth = updated_sea_warmth.astype(jnp.bfloat16)
    answer_blocks = jnp.take(
        halfway_sea_warmth.reshape(tiled_groups, tile_lines),
        jnp.minimum(wanted_row_list, tiled_groups - 1),
        axis=0,
    )
    incoming_data = lax.all_to_all(
        answer_blocks, ("comp", "dom"), split_axis=0, concat_axis=0, tiled=True
    )
    water_rise = water_elevation
    eastern_current = depth_mean_current[0]
    northern_current = depth_mean_current[1]
    for substep in range(NSUB):
        slope_x = jnp.sum(weight_x * (near_level - water_rise), axis=0)
        slope_y = jnp.sum(weight_y * (near_level - water_rise), axis=0)
        eastern_current = (
            DAMPING * eastern_current - GRAVITY * slope_x + WIND_GAIN * thermal_driver[1]
        )
        northern_current = (
            DAMPING * northern_current - GRAVITY * slope_y + WIND_GAIN * thermal_driver[2]
        )
        flow_rims = with_halo(
            jnp.stack([eastern_current, northern_current]).reshape(2, tally_across, matrix_lines),
            ((("comp", "dom"), 1),),
            1,
        )
        near_flow = neighbours(flow_rims)
        spread_sum = jnp.sum(
            weight_x * (near_flow[0] - eastern_current)
            + weight_y * (near_flow[1] - northern_current),
            axis=0,
        )
        water_rise = water_rise - DEPTH_RATE * spread_sum
        if substep + 1 < NSUB:
            near_level = neighbours(
                with_halo(
                    water_rise.reshape(1, tally_across, matrix_lines), ((("comp", "dom"), 1),), 1
                )
            )[0]
    own_blocks = jnp.take(incoming_data, slot_index, axis=0)
    contribution = jnp.einsum(
        "bcr,br->bc", transfer_coefficients, own_blocks, preferred_element_type=jnp.float32
    )
    column_blocks = sources.shape[1]
    collected_columns = (
        jnp.arange(column_blocks, dtype=jnp.int32)[:, None] == transfer_across_tile[None, :]
    ).astype(jnp.float32)
    joined_sea_warmth = jnp.dot(
        collected_columns, contribution, precision=lax.Precision.HIGHEST
    ).reshape(air_warmth.shape[0], elem_count)
    later_advance = atmos_step(
        after_first, eastern_breeze, northern_breeze, reciprocal_breadth, edge_plan
    )
    lowest_layer = later_advance[:, 0, :]
    closing_air_warmth = later_advance.at[:, 0, :].set(
        lowest_layer + NUDGING_SPEED * (joined_sea_warmth - lowest_layer)
    )
    return (
        closing_air_warmth,
        water_rise,
        jnp.stack([eastern_current, northern_current]),
        updated_sea_warmth,
    )


def solution(mesh):
    return jax.shard_map(
        shards,
        mesh=mesh,
        in_specs=(
            P(None, None, ("comp", "dom")),
            P(None, None, ("comp", "dom")),
            P(None, None, ("comp", "dom")),
            P(("comp", "dom")),
            P(None, ("comp", "dom")),
            P(("comp", "dom"), None, None),
            P(("comp", "dom")),
            P(("comp", "dom"), None),
            P(("comp", "dom")),
            P(("comp", "dom")),
            P(None, ("comp", "dom")),
            P(("comp", "dom")),
            P(None, ("comp", "dom")),
            P(None, ("comp", "dom")),
        ),
        out_specs=(
            P(None, None, ("comp", "dom")),
            P(("comp", "dom")),
            P(None, ("comp", "dom")),
            P(("comp", "dom")),
        ),
        check_vma=False,
    )
```

profile of v0, /device:TPU:0, one launch (start us, length us, event | category | flops | bytes accessed | tf_op | source)
XLA Modules:
  0.0 1057.2 jit_solution(6056507654365284764)
XLA Ops:
  5.1 7.3 all-to-all-start
  13.9 1.8 collective-permute-start.4
  15.7 3.6 collective-permute-start.5
  19.2 1.8 fusion.91
  32.0 1.8 copy.183
  33.8 2.8 convolution_multiply_fusion.3
  39.6 1.8 copy.185
  41.4 1.4 gather_fusion.14
  49.4 1.5 copy.231
  50.9 81.9 %gather_fusion.1 = f32[24576,2]{1,0:T(8,128)} fusion(f32[2,4608]{0,1:T(8,128)S(1)} %bitcast.300, s32[24576]{0:T(1024)S(1)} %broadcast_clamp_fusion), kind=kCustom, calls=%fused_computation.13 | custom fusion | bytes 491520 | tf_op jit(solution)/shard_map/gather | solution.py:206
  132.9 9.1 copy.232
  142.1 1.8 multiply_reduce_fusion.6
  143.9 1.7 copy.201
  145.6 2.5 gather_fusion.16
  148.2 1.7 copy.202
  149.9 1.8 fusion.45
  151.7 5.3 collective-permute-start
  157.7 1.7 copy.190
  159.4 1.6 copy.203
  161.0 2.5 gather_fusion.12
  164.6 1.7 copy.192
  166.3 2.5 gather_fusion.13
  168.9 1.7 copy.193
  174.1 1.9 fusion.14
  177.0 1.6 scatter_fusion.1
  178.6 2.6 fusion.9
  181.2 1.4 slice.302
  182.6 1.4 slice.301
  185.9 1.3 collective-permute-start.3
  191.8 4.9 all-to-all-start.1
  197.9 1.4 fusion.90
  207.1 1.6 gather_fusion.19
  208.7 1.7 copy.211
  211.5 1.6 gather_fusion.22
  216.1 1.7 copy_add_fusion
  220.2 1.7 collective-permute-start.6
  221.8 3.7 collective-permute-start.7
  225.6 1.7 fusion.43
  227.3 2.1 copy.233
  229.4 83.5 %gather_fusion.4 = f32[24576,2]{1,0:T(8,128)} fusion(f32[2,4608]{0,1:T(8,128)} %bitcast.301, s32[24576]{0:T(1024)S(1)} %broadcast_clamp_fusion), kind=kCustom, calls=%fused_computation.16 | custom fusion | bytes 491520 | tf_op jit(solution)/shard_map/gather | solution.py:206
  312.9 8.3 copy.234
  322.7 4.8 collective-permute-start.9
  330.2 135.5 %gather_fusion.5 = f32[24576]{0:T(1024)S(1)} fusion(f32[4608]{0:T(1024)S(1)} %reshape.654, s32[24576]{0:T(1024)S(1)} %broadcast_clamp_fusion), kind=kCustom, calls=%fused_computation.17 | custom fusion | bytes 294912 | tf_op jit(solution)/shard_map/gather | solution.py:206
  466.3 5.3 collective-permute-start.11
  471.6 1.8 fusion.4
  474.1 1.5 copy.235
  475.6 81.9 %gather_fusion.6 = f32[24576,2]{1,0:T(8,128)} fusion(f32[2,4608]{0,1:T(8,128)S(1)} %bitcast.302, s32[24576]{0:T(1024)S(1)} %broadcast_clamp_fusion), kind=kCustom, calls=%fused_computation.18 | custom fusion | bytes 491520 | tf_op jit(solution)/shard_map/gather | solution.py:206
  557.5 8.4 copy.236
  566.2 5.3 collective-permute-start.13
  572.9 135.5 %gather_fusion.7 = f32[24576]{0:T(1024)S(1)} fusion(f32[4608]{0:T(1024)S(1)} %reshape.672, s32[24576]{0:T(1024)S(1)} %broadcast_clamp_fusion), kind=kCustom, calls=%fused_computation.19 | custom fusion | bytes 294912 | tf_op jit(solution)/shard_map/gather | solution.py:206
  708.9 5.3 collective-permute-start.15
  714.3 1.3 convert_bitcast_fusion
  715.6 1.4 gather_fusion.2
  717.6 1.5 copy.237
  719.1 81.9 %gather_fusion.8 = f32[24576,2]{1,0:T(8,128)} fusion(f32[2,4608]{0,1:T(8,128)S(1)} %bitcast.303, s32[24576]{0:T(1024)S(1)} %broadcast_clamp_fusion), kind=kCustom, calls=%fused_computation.20 | custom fusion | bytes 491520 | tf_op jit(solution)/shard_map/gather | solution.py:206
  801.0 8.4 copy.238
  809.7 5.3 collective-permute-start.17
  815.8 2.8 all-to-all-start.2
  818.6 135.5 %gather_fusion.9 = f32[24576]{0:T(1024)S(1)} fusion(f32[4608]{0:T(1024)S(1)} %reshape.690, s32[24576]{0:T(1024)S(1)} %broadcast_clamp_fusion), kind=kCustom, calls=%fused_computation.21 | custom fusion | bytes 294912 | tf_op jit(solution)/shard_map/gather | solution.py:206
  954.6 1.5 collective-permute-start.18
  956.1 3.9 collective-permute-start.19
  961.9 1.5 copy.239
  963.4 81.9 %gather_fusion.10 = f32[24576,2]{1,0:T(8,128)} fusion(f32[2,4608]{0,1:T(8,128)S(1)} %bitcast.299, s32[24576]{0:T(1024)S(1)} %broadcast_clamp_fusion), kind=kCustom, calls=%fused_computation.22 | custom fusion | bytes 491520 | tf_op jit(solution)/shard_map/gather | solution.py:206
  1045.4 8.4 copy.240
  (351 shorter events, 68.5 us)
Async XLA Ops:
  0.6 189.1 %copy-start = (bf16[32,128,128]{2,1,0:T(8,128)(2,1)S(1)}, bf16[32,128,128]{2,1,0:T(8,128)(2,1)}, u32[]{:S(2)}) copy-start(bf16[32,128,128]{2,1,0:T(8,128)(2,1)} %param.35) | copy-start | bytes 3145732
  3.6 27.4 %copy-start.77 = (s32[32,1]{0,1:T(1,128)}, s32[32,1]{0,1:T(1,128)S(1)}, u32[]{:S(2)}) copy-start(s32[32,1]{0,1:T(1,128)S(1)} %get-tuple-element.93) | copy-start | bytes 388
  5.1 40.3 %all-to-all-start = ((s32[32,2,1]{1,2,0:T(1,128)}), s32[32,2,1]{1,2,0:T(1,128)S(1)}, u32[]{:S(2)}, u32[]{:S(2)}) async-start(s32[32,2,1]{1,2,0:T(1,128)} %bitcast.27), calls=%async_computation | async-start | bytes 32768 | tf_op jit(solution)/shard_map/all_to_all | solution.py:188
  13.9 34.9 %collective-permute-start.4 = (f32[2,1,256]{2,1,0:T(1,128)S(1)}, f32[2,1,256]{2,1,0:T(1,128)S(1)}, u32[]{:S(2)}, u32[]{:S(2)}) collective-permute-start(f32[2,1,256]{2,1,0:T(1,128)S(1)} %get-tuple-element.129), channel_id=1, source_target_pairs={{0,1},{1,2},{2,3},{3,4},{4,5},{5,6},{6,7},{7,8},{8,9},{9,10},{10,1... | collective-permute-start | bytes 6152 | tf_op jit(solution)/shard_map/ppermute | solution.py:37
  15.7 33.0 %collective-permute-start.5 = (f32[2,1,256]{2,1,0:T(1,128)S(1)}, f32[2,1,256]{2,1,0:T(1,128)S(1)}, u32[]{:S(2)}, u32[]{:S(2)}) collective-permute-start(f32[2,1,256]{2,1,0:T(1,128)S(1)} %get-tuple-element.130), channel_id=1, source_target_pairs={{1,0},{2,1},{3,2},{4,3},{5,4},{6,5},{7,6},{8,7},{9,8},{10,9},{11,1... | collective-permute-start | bytes 6152 | tf_op jit(solution)/shard_map/ppermute | solution.py:38
  22.4 121.5 %collective-permute-start.1 = (f32[4,64,128]{2,0,1:T(4,128)}, f32[4,64,128]{2,0,1:T(4,128)}, u32[]{:S(2)}, u32[]{:S(2)}) collective-permute-start(f32[4,64,128]{2,0,1:T(4,128)} %copy.286), channel_id=1, source_target_pairs={{0,1},{1,2},{2,3},{3,4},{4,5},{5,6},{6,7},{7,8},{8,9},{9,10},{10,1... | collective-permute-start | bytes 393224 | tf_op jit(solution)/shard_map/ppermute | solution.py:27
  30.9 17.8 %copy-start.64 = (s32[1024]{0:T(1024)}, s32[1024]{0:T(1024)S(1)}, u32[]{:S(2)}) copy-start(s32[1024]{0:T(1024)S(1)} %pad_clamp_fusion.3) | copy-start | bytes 12292
  31.0 111.1 %copy-start.44 = (f32[4096]{0:T(1024)S(1)}, f32[4096]{0:T(1024)}, u32[]{:S(2)}) copy-start(f32[4096]{0:T(1024)} %param.39) | copy-start | bytes 49156
  132.8 17.1 %copy-start.14 = (f32[128,4,64]{0,1,2:T(4,128)S(1)}, f32[128,4,64]{0,1,2:T(4,128)}, u32[]{:S(2)}) copy-start(f32[128,4,64]{0,1,2:T(4,128)} %copy.200) | copy-start | bytes 393220
  132.8 37.8 %copy-start.13 = (f32[4,64,128]{2,1,0:T(8,128)S(1)}, f32[4,64,128]{2,1,0:T(8,128)}, u32[]{:S(2)}) copy-start(f32[4,64,128]{2,1,0:T(8,128)} %copy-done.12) | copy-start | bytes 393220
  132.8 37.8 %copy-start.71 = (pred[128]{0:T(512)(128)(4,1)S(1)}, pred[128]{0:T(512)(128)(4,1)}, u32[]{:S(2)}) copy-start(pred[128]{0:T(512)(128)(4,1)} %get-tuple-element.140) | copy-start | bytes 388
  132.8 37.8 %copy-start.72 = (pred[128]{0:T(512)(128)(4,1)S(1)}, pred[128]{0:T(512)(128)(4,1)}, u32[]{:S(2)}) copy-start(pred[128]{0:T(512)(128)(4,1)} %get-tuple-element.144) | copy-start | bytes 388
  132.8 38.8 %copy-start.6 = (f32[16,64,128]{2,1,0:T(8,128)S(1)}, f32[16,64,128]{2,1,0:T(8,128)}, u32[]{:S(2)}) copy-start(f32[16,64,128]{2,1,0:T(8,128)} %scatter-add.48.clone) | copy-start | bytes 1572868
  132.8 38.8 %copy-start.75 = (s32[4]{0:T(128)S(1)}, s32[4]{0:T(128)}, u32[]{:S(2)}) copy-start(s32[4]{0:T(128)} %add_bitcast_fusion) | copy-start | bytes 52
  132.8 41.2 %copy-start.11 = (f32[4,64,128]{1,0,2:T(4,128)S(1)}, f32[4,64,128]{1,0,2:T(4,128)}, u32[]{:S(2)}) copy-start(f32[4,64,128]{1,0,2:T(4,128)} %copy-done.10) | copy-start | bytes 393220
  132.9 41.2 %copy-start.67 = (pred[128]{0:T(512)(128)(4,1)S(1)}, pred[128]{0:T(512)(128)(4,1)}, u32[]{:S(2)}) copy-start(pred[128]{0:T(512)(128)(4,1)} %get-tuple-element.102) | copy-start | bytes 388
  132.9 44.2 %copy-start.73 = (s32[4]{0:T(128)S(1)}, s32[4]{0:T(128)}, u32[]{:S(2)}) copy-start(s32[4]{0:T(128)} %fusion.82) | copy-start | bytes 52
  132.9 45.7 %copy-start.5 = (f32[16,64,128]{2,1,0:T(8,128)S(1)}, f32[16,64,128]{2,1,0:T(8,128)}, u32[]{:S(2)}) copy-start(f32[16,64,128]{2,1,0:T(8,128)} %param.30) | copy-start | bytes 1572868
  132.9 45.7 %copy-start.8 = (bf16[16,64,128]{2,1,0:T(8,128)(2,1)S(1)}, bf16[16,64,128]{2,1,0:T(8,128)(2,1)}, u32[]{:S(2)}) copy-start(bf16[16,64,128]{2,1,0:T(8,128)(2,1)} %param.32) | copy-start | bytes 786436
  132.9 45.7 %copy-start.51 = (f32[16,16,1]{1,0,2:T(8,128)S(1)}, f32[16,16,1]{1,0,2:T(8,128)}, u32[]{:S(2)}) copy-start(f32[16,16,1]{1,0,2:T(8,128)} %constant.275) | copy-start | bytes 3076
  132.9 45.7 %copy-start.78 = (f32[128]{0:T(128)S(1)}, f32[128]{0:T(128)}, u32[]{:S(2)}) copy-start(f32[128]{0:T(128)} %broadcast_multiply_fusion.8) | copy-start | bytes 1540
  132.9 56.8 %copy-start.81 = (pred[32]{0:T(512)(128)(4,1)S(1)}, pred[32]{0:T(512)(128)(4,1)}, u32[]{:S(2)}) copy-start(pred[32]{0:T(512)(128)(4,1)} %compare_and_fusion.4) | copy-start | bytes 100
  142.0 63.4 %copy-start.7 = (bf16[16,64,128]{2,1,0:T(8,128)(2,1)S(1)}, bf16[16,64,128]{2,1,0:T(8,128)(2,1)}, u32[]{:S(2)}) copy-start(bf16[16,64,128]{2,1,0:T(8,128)(2,1)} %param.31) | copy-start | bytes 786436
  142.0 63.4 %copy-start.49 = (f32[16,16,1]{1,0,2:T(8,128)S(1)}, f32[16,16,1]{1,0,2:T(8,128)}, u32[]{:S(2)}) copy-start(f32[16,16,1]{1,0,2:T(8,128)} %constant.274) | copy-start | bytes 3076
  151.7 12.9 %collective-permute-start = (f32[4,64,128]{2,0,1:T(4,128)}, f32[4,64,128]{2,0,1:T(4,128)}, u32[]{:S(2)}, u32[]{:S(2)}) collective-permute-start(f32[4,64,128]{2,0,1:T(4,128)} %get-tuple-element.99), channel_id=1, source_target_pairs={{0,31},{1,0},{2,1},{3,2},{4,3},{5,4},{6,5},{7,6},{8,7},{9,8},{10,9... | collective-permute-start | bytes 393224 | tf_op jit(solution)/shard_map/ppermute | solution.py:27
  184.0 22.1 %collective-permute-start.2 = (f32[4,64,128]{2,0,1:T(4,128)}, f32[4,64,128]{2,0,1:T(4,128)}, u32[]{:S(2)}, u32[]{:S(2)}) collective-permute-start(f32[4,64,128]{2,0,1:T(4,128)} %slice.301), channel_id=1, source_target_pairs={{0,31},{1,0},{2,1},{3,2},{4,3},{5,4},{6,5},{7,6},{8,7},{9,8},{10,9... | collective-permute-start | bytes 393224 | tf_op jit(solution)/shard_map/ppermute | solution.py:27
  185.9 24.5 %collective-permute-start.3 = (f32[4,64,128]{2,0,1:T(4,128)}, f32[4,64,128]{2,0,1:T(4,128)}, u32[]{:S(2)}, u32[]{:S(2)}) collective-permute-start(f32[4,64,128]{2,0,1:T(4,128)} %slice.302), channel_id=1, source_target_pairs={{0,1},{1,2},{2,3},{3,4},{4,5},{5,6},{6,7},{7,8},{8,9},{9,10},{10,1... | collective-permute-start | bytes 393224 | tf_op jit(solution)/shard_map/ppermute | solution.py:27
  191.8 26.0 %all-to-all-start.1 = ((f32[32,2,384]{2,1,0:T(2,128)}), f32[32,2,384]{2,1,0:T(2,128)S(1)}, u32[]{:S(2)}, u32[]{:S(2)}) async-start(f32[32,2,384]{2,1,0:T(2,128)} %all_to_all.25), calls=%async_computation.1 | async-start | bytes 196608 | tf_op jit(solution)/shard_map/all_to_all | solution.py:187
  205.3 115.9 %copy-start.58 = (f32[6]{0:T(128)S(1)}, f32[6]{0:T(128)}, u32[]{:S(2)}) copy-start(f32[6]{0:T(128)} %fusion.80) | copy-start | bytes 76
  206.1 123.3 %copy-start.74 = (s32[4]{0:T(128)S(1)}, s32[4]{0:T(128)}, u32[]{:S(2)}) copy-start(s32[4]{0:T(128)} %fusion.82) | copy-start | bytes 52
  218.6 111.5 %copy-start.17 = (f32[1,32,128]{2,1,0:T(8,128)}, f32[1,32,128]{2,1,0:T(8,128)S(1)}, u32[]{:S(2)}) copy-start(f32[1,32,128]{2,1,0:T(8,128)S(1)} %get-tuple-element.117) | copy-start | bytes 49156
  218.6 490.1 %copy-start.15 = (f32[1,32,128]{2,1,0:T(8,128)}, f32[1,32,128]{2,1,0:T(8,128)S(1)}, u32[]{:S(2)}) copy-start(f32[1,32,128]{2,1,0:T(8,128)S(1)} %get-tuple-element.118) | copy-start | bytes 49156
  220.1 110.0 %copy-start.39 = (f32[1,4096]{1,0:T(1,128)}, f32[1,4096]{1,0:T(1,128)S(1)}, u32[]{:S(2)}) copy-start(f32[1,4096]{1,0:T(1,128)S(1)} %get-tuple-element.128) | copy-start | bytes 49156
  220.1 110.0 %copy-start.41 = (f32[1,4096]{1,0:T(1,128)}, f32[1,4096]{1,0:T(1,128)S(1)}, u32[]{:S(2)}) copy-start(f32[1,4096]{1,0:T(1,128)S(1)} %get-tuple-element.127) | copy-start | bytes 49156
  220.2 7.1 collective-permute-start.6
  221.8 5.4 collective-permute-start.7
  322.1 143.7 %copy-start.23 = (f32[4096]{0:T(1024)}, f32[4096]{0:T(1024)S(1)}, u32[]{:S(2)}) copy-start(f32[4096]{0:T(1024)S(1)} %multiply_subtract_fusion.3) | copy-start | bytes 49156
  322.2 7.9 collective-permute-start.8
  322.7 7.4 collective-permute-start.9
  330.2 135.6 %copy-start.59 = (f32[6]{0:T(128)S(1)}, f32[6]{0:T(128)}, u32[]{:S(2)}) copy-start(f32[6]{0:T(128)} %fusion.80) | copy-start | bytes 76
  330.2 135.8 %copy-start.18 = (f32[1,32,128]{2,1,0:T(8,128)S(1)}, f32[1,32,128]{2,1,0:T(8,128)}, u32[]{:S(2)}) copy-start(f32[1,32,128]{2,1,0:T(8,128)} %copy-done.17) | copy-start | bytes 49156
  330.2 135.8 %copy-start.42 = (f32[1,4096]{1,0:T(1,128)S(1)}, f32[1,4096]{1,0:T(1,128)}, u32[]{:S(2)}) copy-start(f32[1,4096]{1,0:T(1,128)} %copy-done.41) | copy-start | bytes 49156
  330.2 135.9 %copy-start.40 = (f32[1,4096]{1,0:T(1,128)S(1)}, f32[1,4096]{1,0:T(1,128)}, u32[]{:S(2)}) copy-start(f32[1,4096]{1,0:T(1,128)} %copy-done.39) | copy-start | bytes 49156
  330.2 141.4 %copy-start.52 = (f32[16,16,1]{1,0,2:T(8,128)S(1)}, f32[16,16,1]{1,0,2:T(8,128)}, u32[]{:S(2)}) copy-start(f32[16,16,1]{1,0,2:T(8,128)} %constant.275) | copy-start | bytes 3076
  330.2 141.4 %copy-start.79 = (f32[128]{0:T(128)S(1)}, f32[128]{0:T(128)}, u32[]{:S(2)}) copy-start(f32[128]{0:T(128)} %broadcast_multiply_fusion.8) | copy-start | bytes 1540
  466.2 7.2 collective-permute-start.10
  466.3 7.1 collective-permute-start.11
  566.1 142.4 %copy-start.25 = (f32[4096]{0:T(1024)}, f32[4096]{0:T(1024)S(1)}, u32[]{:S(2)}) copy-start(f32[4096]{0:T(1024)S(1)} %multiply_subtract_fusion.2) | copy-start | bytes 49156
  566.1 6.7 collective-permute-start.12
  566.2 6.6 collective-permute-start.13
  572.9 135.8 %copy-start.19 = (f32[1,32,128]{2,1,0:T(8,128)S(1)}, f32[1,32,128]{2,1,0:T(8,128)}, u32[]{:S(2)}) copy-start(f32[1,32,128]{2,1,0:T(8,128)} %copy-done.17) | copy-start | bytes 49156
  572.9 141.4 %copy-start.46 = (f32[4096]{0:T(1024)S(1)}, f32[4096]{0:T(1024)}, u32[]{:S(2)}) copy-start(f32[4096]{0:T(1024)} %param.41) | copy-start | bytes 49156
  572.9 141.4 %copy-start.48 = (f32[4096]{0:T(1024)S(1)}, f32[4096]{0:T(1024)}, u32[]{:S(2)}) copy-start(f32[4096]{0:T(1024)} %get-tuple-element.83) | copy-start | bytes 49156
  708.8 100.8 %copy-start.26 = (f32[4096]{0:T(1024)S(1)}, f32[4096]{0:T(1024)}, u32[]{:S(2)}) copy-start(f32[4096]{0:T(1024)} %copy-done.25) | copy-start | bytes 49156
  708.9 8.1 collective-permute-start.14
  708.9 8.0 collective-permute-start.15
  809.6 144.6 %copy-start.21 = (f32[4096]{0:T(1024)}, f32[4096]{0:T(1024)S(1)}, u32[]{:S(2)}) copy-start(f32[4096]{0:T(1024)S(1)} %multiply_subtract_fusion.1) | copy-start | bytes 49156
  809.7 8.9 collective-permute-start.16
  809.7 8.8 collective-permute-start.17
  815.8 238.8 %all-to-all-start.2 = ((bf16[32,2,128]{2,1,0:T(2,128)(2,1)}), bf16[32,2,128]{2,1,0:T(2,128)(2,1)S(1)}, u32[]{:S(2)}, u32[]{:S(2)}) async-start(bf16[32,2,128]{2,1,0:T(2,128)(2,1)} %broadcast_select_fusion), calls=%async_computation.2 | async-start | bytes 32768 | tf_op jit(solution)/shard_map/all_to_all | solution.py:228
  818.6 135.8 %copy-start.20 = (f32[1,32,128]{2,1,0:T(8,128)S(1)}, f32[1,32,128]{2,1,0:T(8,128)}, u32[]{:S(2)}) copy-start(f32[1,32,128]{2,1,0:T(8,128)} %copy-done.17) | copy-start | bytes 49156
  818.6 135.9 %copy-start.16 = (f32[1,32,128]{2,1,0:T(8,128)S(1)}, f32[1,32,128]{2,1,0:T(8,128)}, u32[]{:S(2)}) copy-start(f32[1,32,128]{2,1,0:T(8,128)} %copy-done.15) | copy-start | bytes 49156
  954.6 6.7 collective-permute-start.18
  956.1 5.2 collective-permute-start.19
  (41 other events, 362.6 us)
where the time goes:
time: 1060 us
  local copies, waits for them, and re-layouts  938 us (88%)
  starting transfers between devices  65.7 us (6%)
  other arithmetic  40.3 us (4%)
    gather x13, local copies, waits for them, and re-layouts, neighbours(): return extended.reshape(extended.shape[0], -1)[:, spread]  860 us
    ppermute x8, starting transfers between devices, with_halo(): after = lax.ppermute(first, axis, down)  37.4 us
  transfers between devices with their start and end apart: 23, of which 1 were waited for; matrix products, arithmetic and copies ran while one was open for 38% of the time, Pallas kernels for 0%

commit v1 on v0

v1 whole, which is shorter than its diff:
```python
import math

import jax
import jax.numpy as jnp
import numpy as np
from jax import lax
from jax.experimental import pallas as pl
from jax.experimental.pallas import tpu as pltpu
from jax.sharding import PartitionSpec as P

OY = 256
NSUB = 4
CAP = 2

STEP_SIZE = 0.05
JUMP_WEIGHT = 4.0
NUDGING_SPEED = 0.5
DAMPING = 0.9
GRAVITY = 0.3
WIND_GAIN = 0.3
DEPTH_RATE = 0.3
WARMING_COEFF = 0.3
SPREADING_COEFF = 0.5

RING = ("comp", "dom")
LANES = 128
HALO = OY // LANES
COS = [math.cos(k * math.pi / 3.0) for k in range(6)]
SIN = [0.0 if k % 3 == 0 else math.sin(k * math.pi / 3.0) for k in range(6)]

ROW_EDGE, ROW_BREADTH, ROW_ETA, ROW_U, ROW_V, ROW_SST = 0, 4, 8, 10, 12, 14
ROW_PX, ROW_PY, ROW_IDX, ROW_W, ROWS_FIRST = 16, 18, 24, 40, 56
PER_DEST, ROW_IDS = 16, 14


def shifted(value, steps):
    count = lax.axis_size(RING)
    return lax.ppermute(value, RING, [(i, (i + steps) % count) for i in range(count)])


def exchange(value):
    return lax.all_to_all(value, RING, split_axis=0, concat_axis=0, tiled=True)


def gll_matrix():
    points = np.array([-1.0, -1.0 / np.sqrt(5.0), 1.0 / np.sqrt(5.0), 1.0])
    barycentric = [
        1.0 / np.prod([points[s] - points[o] for o in range(4) if o != s]) for s in range(4)
    ]
    table = np.zeros((4, 4))
    for t in range(4):
        for s in range(4):
            if t != s:
                table[t, s] = barycentric[s] / barycentric[t] / (points[t] - points[s])
    for t in (0, 3):
        table[t, t] = -np.sum(table[t])
    return [[float(np.float32(value)) for value in line] for line in table]


GLL = gll_matrix()


def vmem(count):
    return [pl.BlockSpec(memory_space=pltpu.VMEM)] * count


def smem(count):
    return [pl.BlockSpec(memory_space=pltpu.SMEM)] * count


def shape_of(*dims, dtype=jnp.float32):
    return jax.ShapeDtypeStruct(dims, dtype)


PARAMS = pltpu.CompilerParams(vmem_limit_bytes=24 * 1024 * 1024)


def lane_take(rows, ids):
    return jnp.take_along_axis(rows, ids, axis=1, mode="promise_in_bounds")


def wide(row, lines):
    return jnp.broadcast_to(row, (lines, row.shape[1]))


def side_ids(pn):
    count = pn.shape[1]
    bits = count.bit_length() - 1
    table = pn[...]
    ids = [table[k : k + 1] & (count - 1) for k in range(4)]
    home = lax.shift_right_logical(table[0:1], bits)
    near = [lax.shift_right_logical(table[k : k + 1], bits) == home for k in range(4)]
    return ids, near


def element_step(state, east_wind, north_wind, scale, facing):
    jumps = [None] * 16
    sides = (
        (0, 1, 2, 3),
        (3, 7, 11, 15),
        (12, 13, 14, 15),
        (0, 4, 8, 12),
    )
    for k in range(4):
        for n, p in enumerate(sides[k]):
            term = facing[k][n] - state[p]
            jumps[p] = term if jumps[p] is None else jumps[p] + term
    result = []
    for p in range(16):
        i, j = p % 4, p // 4
        grad_x = grad_y = None
        for m in range(4):
            if GLL[i][m] != 0.0:
                term = GLL[i][m] * state[m + 4 * j]
                grad_x = term if grad_x is None else grad_x + term
            if GLL[j][m] != 0.0:
                term = GLL[j][m] * state[i + 4 * m]
                grad_y = term if grad_y is None else grad_y + term
        change = -(east_wind(p) * grad_x + north_wind(p) * grad_y)
        if jumps[p] is not None:
            change = change + JUMP_WEIGHT * jumps[p]
        result.append(state[p] + scale * change)
    return result


def local_step_kernel(air, eastern, northern, breadth, pn, loc, east, west):
    ids, near = side_ids(pn)
    lines = air.shape[1]
    state = [air[p] for p in range(16)]
    scale = STEP_SIZE * breadth[...]
    ids = [wide(line, lines) for line in ids]
    facing = [
        [lane_take(state[12 + n], ids[0]) for n in range(4)],
        [jnp.where(near[1], lane_take(state[4 * n], ids[1]), 0.0) for n in range(4)],
        [lane_take(state[n], ids[2]) for n in range(4)],
        [jnp.where(near[3], lane_take(state[3 + 4 * n], ids[3]), 0.0) for n in range(4)],
    ]
    result = element_step(
        state,
        lambda p: eastern[p].astype(jnp.float32),
        lambda p: northern[p].astype(jnp.float32),
        scale,
        facing,
    )
    for p in range(16):
        loc[p] = result[p]
    for n in range(4):
        east[0, n] = state[3 + 4 * n].astype(jnp.bfloat16)
        east[1, n] = result[3 + 4 * n].astype(jnp.bfloat16)
        west[0, n] = state[4 * n].astype(jnp.bfloat16)
        west[1, n] = result[4 * n].astype(jnp.bfloat16)


def second_step_kernel(
    loc, eastern, northern, breadth, pn, east, west, next_west, prev_east, first_prev, first_next, out
):
    ids, near = side_ids(pn)
    lines = loc.shape[1]
    scale = STEP_SIZE * breadth[...]
    jump = JUMP_WEIGHT * scale
    ids = [wide(line, lines) for line in ids]
    state = [loc[p] for p in range(16)]

    def across(table, side, breadth_row):
        own = [table[0, n].astype(jnp.float32) for n in range(4)]
        there = next_west if side == 1 else prev_east
        factor = JUMP_WEIGHT * STEP_SIZE * lane_take(wide(breadth_row, lines), ids[side])
        values, beyond = [], []
        for n in range(4):
            values.append(
                jnp.where(near[side], 0.0, lane_take(there[0, n].astype(jnp.float32), ids[side]))
            )
            beyond.append(
                lane_take(there[1, n].astype(jnp.float32), ids[side]) + factor * own[n]
            )
        return values, beyond

    east_now, east_beyond = across(east, 1, first_next[ROW_BREADTH : ROW_BREADTH + 1])
    west_now, west_beyond = across(west, 3, first_prev[ROW_BREADTH : ROW_BREADTH + 1])
    for n in range(4):
        state[3 + 4 * n] = state[3 + 4 * n] + jump * east_now[n]
        state[4 * n] = state[4 * n] + jump * west_now[n]
    facing = [
        [lane_take(state[12 + n], ids[0]) for n in range(4)],
        [jnp.where(near[1], lane_take(state[4 * n], ids[1]), east_beyond[n]) for n in range(4)],
        [lane_take(state[n], ids[2]) for n in range(4)],
        [jnp.where(near[3], lane_take(state[3 + 4 * n], ids[3]), west_beyond[n]) for n in range(4)],
    ]
    result = element_step(
        state,
        lambda p: eastern[p].astype(jnp.float32),
        lambda p: northern[p].astype(jnp.float32),
        scale,
        facing,
    )
    for p in range(16):
        out[p] = result[p]


def forward_kernel(
    holder, down, across, loc, eastern, northern, breadth, pn, from_prev, from_next, weights,
    out, taken, flux, parts, *, devices, tiles
):
    ids, near = side_ids(pn)
    jump = (JUMP_WEIGHT * STEP_SIZE) * breadth[...]
    from_east = lane_take(from_next[0:8], wide(ids[1], 8))
    from_west = lane_take(from_prev[0:8], wide(ids[3], 8))
    from_east = jnp.where(near[1], 0.0, jump * from_east)
    from_west = jnp.where(near[3], 0.0, jump * from_west)
    flux[...] = jnp.zeros_like(flux)
    for p in range(16):
        value = loc[p, 0:1]
        if p % 4 == 3:
            value = value + from_east[p // 4 : p // 4 + 1]
        if p % 4 == 0:
            value = value + from_west[p // 4 : p // 4 + 1]
        u = eastern[p].astype(jnp.float32)[0:1]
        v = northern[p].astype(jnp.float32)[0:1]
        speed = jnp.sqrt(u * u + v * v + 1.0)
        flux[p, 0:1] = speed * value
        flux[p, 1:2] = speed * u
        flux[p, 2:3] = speed * v
    parts[...] = jnp.zeros_like(parts)
    parts[:, ROW_IDS : ROW_IDS + 1, :] = jnp.full((devices, 1, LANES), -1.0, jnp.float32)
    for owner in range(devices):
        taken[owner] = 0
    lane = lax.broadcasted_iota(jnp.int32, (1, LANES), 1)

    def mark(owner, slot, number):
        ids_row = parts[owner, ROW_IDS : ROW_IDS + 1, :]
        parts[owner, ROW_IDS : ROW_IDS + 1, :] = jnp.where(
            lane == slot, jnp.full((1, LANES), number, jnp.int32).astype(jnp.float32), ids_row
        )

    for b in range(weights.shape[0]):
        owner = holder[b, 0]
        rank = jnp.minimum(taken[owner], CAP - 1)
        taken[owner] = taken[owner] + 1
        tile = down[b]
        sums = jnp.dot(
            flux[across[b]].astype(jnp.bfloat16), weights[b], preferred_element_type=jnp.float32
        )
        for f in range(3):
            parts[owner, pl.ds(3 * rank + f, 1), :] = sums[f : f + 1]
        mark(owner, rank, tile)
        after = jnp.where(owner + 1 == devices, 0, owner + 1)
        before = jnp.where(owner == 0, devices - 1, owner - 1)
        for f in range(2):
            parts[after, pl.ds(6 + 2 * rank + f, 1), :] = sums[1 + f : 2 + f]
            parts[before, pl.ds(10 + 2 * rank + f, 1), :] = sums[1 + f : 2 + f]
        last = tile - (tiles - HALO)
        mark(after, 2 + rank, jnp.where(last >= 0, tiles + last, -1))
        mark(before, 4 + rank, jnp.where(tile < HALO, tiles + HALO + tile, -1))
    out[...] = parts[...].astype(jnp.bfloat16)


def back_kernel(holder, across, arrived, weights, second, out, taken, surface, *, devices):
    for owner in range(devices):
        taken[owner] = 0
    surface[...] = jnp.zeros_like(surface)
    for b in range(weights.shape[0]):
        owner = holder[b, 0]
        rank = jnp.minimum(taken[owner], CAP - 1)
        taken[owner] = taken[owner] + 1
        line = arrived[owner, pl.ds(rank, 1), :]
        share = lax.dot_general(
            wide(line, 8).astype(jnp.bfloat16),
            weights[b],
            (((1,), (1,)), ((), ())),
            preferred_element_type=jnp.float32,
        )
        column = across[b]
        surface[column, 0:1] = surface[column, 0:1] + share[0:1]
    out[...] = second[...]
    for p in range(16):
        lowest = second[p, 0:1]
        out[p, 0:1] = lowest + NUDGING_SPEED * (surface[p, 0:1] - lowest)


def split_index(idx):
    return lax.shift_right_arithmetic(idx, 7), idx & (LANES - 1)


def pick(idx, sources):
    high, low = split_index(idx)
    result = jnp.zeros(idx.shape, jnp.float32)
    for number, line in sources:
        result = jnp.where(high == number, lane_take(wide(line, idx.shape[0]), low), result)
    return result


def own_sources(ref):
    return [(HALO + r, ref[r : r + 1]) for r in range(ref.shape[0])]


def combine(terms, factors):
    total = None
    for term, factor in zip(terms, factors):
        if factor != 0.0:
            total = factor * term if total is None else total + factor * term
    return total


def pair_sums(table):
    terms = [table[HALO * k : HALO * (k + 1)] for k in range(6)]
    return combine(terms, COS), combine(terms, SIN)


def rim_partial(rim_idx, rim_w, eta, first):
    rows = rim_idx.shape[0]
    found = pick(rim_idx, own_sources(eta))
    centre = eta[first : first + HALO]
    centre = jnp.concatenate([centre] * (rows // HALO), axis=0)
    return pair_sums(rim_w * (found - centre))


def prepare_kernel(
    air, breadth, eta, sst, flow, nb, span, idx, w, rim_idx, rim_w, u, v, up, dn
):
    tiles = eta.shape[0]
    for r in range(tiles):
        cut = slice(r * LANES, (r + 1) * LANES)
        links = nb[:, cut]
        factors = jnp.where(links >= 0, span[:, cut] * (1.0 / 3.0), 0.0)
        for k in range(6):
            idx[k * tiles + r : k * tiles + r + 1] = links[k : k + 1]
            w[k * tiles + r : k * tiles + r + 1] = factors[k : k + 1]
        u[r : r + 1] = flow[0:1, cut]
        v[r : r + 1] = flow[1:2, cut]
    for side, first in ((0, 0), (1, tiles - HALO)):
        rim_idx[side, 12:16] = jnp.full((4, LANES), -1, jnp.int32)
        rim_w[side, 12:16] = jnp.zeros((4, LANES), jnp.float32)
        for k in range(6):
            cut = slice(k * tiles + first, k * tiles + first + HALO)
            rim_idx[side, HALO * k : HALO * (k + 1)] = idx[cut]
            rim_w[side, HALO * k : HALO * (k + 1)] = w[cut]
    for side, first, target in ((0, 0, dn), (1, tiles - HALO, up)):
        target[...] = jnp.zeros_like(target)
        for n in range(4):
            p = 4 * n if side == 0 else 3 + 4 * n
            target[ROW_EDGE + n : ROW_EDGE + n + 1] = air[p, 0:1]
        target[ROW_BREADTH : ROW_BREADTH + 1] = breadth[...]
        part_x, part_y = rim_partial(rim_idx[side], rim_w[side], eta, first)
        cut = slice(first, first + HALO)
        target[ROW_ETA : ROW_ETA + HALO] = eta[cut]
        target[ROW_U : ROW_U + HALO] = u[cut]
        target[ROW_V : ROW_V + HALO] = v[cut]
        target[ROW_SST : ROW_SST + HALO] = sst[cut]
        target[ROW_PX : ROW_PX + HALO] = part_x
        target[ROW_PY : ROW_PY + HALO] = part_y
        target[ROW_IDX : ROW_IDX + 16] = rim_idx[side].astype(jnp.float32)
        target[ROW_W : ROW_W + 16] = rim_w[side]


def own_gradient(idx, w, eta, gx, gy):
    tiles = eta.shape[0]

    def chunk(c, carry):
        at = pl.multiple_of(c * 8, 8)
        centre = eta[pl.ds(at, 8)]
        terms = []
        for k in range(6):
            found = pick(idx[pl.ds(k * tiles + at, 8)], own_sources(eta))
            terms.append(w[pl.ds(k * tiles + at, 8)] * (found - centre))
        gx[pl.ds(at, 8)] = combine(terms, COS)
        gy[pl.ds(at, 8)] = combine(terms, SIN)
        return carry

    lax.fori_loop(0, tiles // 8, chunk, 0)


def gradient_kernel(idx, w, eta, gx, gy):
    own_gradient(idx, w, eta, gx, gy)


def first_gradient_kernel(idx, w, eta, sst, gx, gy, spread):
    own_gradient(idx, w, eta, gx, gy)
    tiles = eta.shape[0]

    def chunk(c, carry):
        at = pl.multiple_of(c * 8, 8)
        centre = sst[pl.ds(at, 8)]
        total = jnp.zeros_like(centre)
        for k in range(6):
            found = pick(idx[pl.ds(k * tiles + at, 8)], own_sources(sst))
            total = total + w[pl.ds(k * tiles + at, 8)] * (found - centre)
        spread[pl.ds(at, 8)] = total
        return carry

    lax.fori_loop(0, tiles // 8, chunk, 0)


def outer_terms(idx, w, outer, tiles):
    result = []
    for at, offset, base in ((0, 0, 0), (tiles - 8, tiles + HALO, HALO)):
        sources = [(offset + q, outer[base + q : base + q + 1]) for q in range(HALO)]
        terms = []
        for k in range(6):
            rows = slice(k * tiles + at, k * tiles + at + 8)
            terms.append(w[rows] * pick(idx[rows], sources))
        result.append((at, terms))
    return result


def subcycle(
    gx, gy, eta, u, v, sides, fu, fv, fside, before, after, idx, w, side_idx, side_w,
    rim_idx, rim_w, flow, flow_outer, eta_new, u_new, v_new, sides_new, up, dn
):
    tiles = eta.shape[0]
    outer = jnp.concatenate([before[0], after[0]], axis=0)
    u_new[...] = DAMPING * u[...] - GRAVITY * gx[...] + WIND_GAIN * fu[...]
    v_new[...] = DAMPING * v[...] - GRAVITY * gy[...] + WIND_GAIN * fv[...]
    for at, terms in outer_terms(idx, w, outer, tiles):
        u_new[at : at + 8] = u_new[at : at + 8] - GRAVITY * combine(terms, COS)
        v_new[at : at + 8] = v_new[at : at + 8] - GRAVITY * combine(terms, SIN)
    slopes = []
    for side, offset, first, part in (
        (0, tiles + HALO, 0, before),
        (1, 0, tiles - HALO, after),
    ):
        sources = [(offset + q, eta[first + q : first + q + 1]) for q in range(HALO)]
        add_x, add_y = pair_sums(side_w[side] * pick(side_idx[side], sources))
        slopes.append((part[1] + add_x, part[2] + add_y))
    slope = jnp.concatenate([slopes[0][0], slopes[1][0], slopes[0][1], slopes[1][1]], axis=0)
    sides_next = DAMPING * sides[...] - GRAVITY * slope + WIND_GAIN * fside[...]
    u_all, v_all = u_new[...], v_new[...]
    u_side, v_side = sides_next[0 : 2 * HALO], sides_next[2 * HALO : 4 * HALO]
    for kk in range(3):
        if kk == 0:
            flow[kk] = u_all
            flow_outer[kk, 0 : 2 * HALO] = u_side
        else:
            flow[kk] = COS[kk] * u_all + SIN[kk] * v_all
            flow_outer[kk, 0 : 2 * HALO] = COS[kk] * u_side + SIN[kk] * v_side

    def chunk(c, carry):
        at = pl.multiple_of(c * 8, 8)
        total = jnp.zeros((8, LANES), jnp.float32)
        for kk in range(3):
            sources = [(HALO + r, flow[kk, r : r + 1]) for r in range(tiles)]
            sources += [(q, flow_outer[kk, q : q + 1]) for q in range(HALO)]
            sources += [
                (tiles + HALO + q, flow_outer[kk, HALO + q : HALO + q + 1]) for q in range(HALO)
            ]
            centre = flow[kk, pl.ds(at, 8)]
            one = pick(idx[pl.ds(kk * tiles + at, 8)], sources) - centre
            two = pick(idx[pl.ds((kk + 3) * tiles + at, 8)], sources) - centre
            total = (
                total
                + w[pl.ds(kk * tiles + at, 8)] * one
                - w[pl.ds((kk + 3) * tiles + at, 8)] * two
            )
        eta_new[pl.ds(at, 8)] = eta[pl.ds(at, 8)] - DEPTH_RATE * total
        return carry

    lax.fori_loop(0, tiles // 8, chunk, 0)
    if up is None:
        return
    sides_new[...] = sides_next
    for side, first, target in ((0, 0, dn), (1, tiles - HALO, up)):
        part_x, part_y = rim_partial(rim_idx[side], rim_w[side], eta_new, first)
        target[0:HALO] = eta_new[first : first + HALO]
        target[HALO : 2 * HALO] = part_x
        target[2 * HALO : 3 * HALO] = part_y
        target[3 * HALO : 4 * HALO] = jnp.zeros((HALO, LANES), jnp.float32)


def rim_of(ref, rows):
    return tuple(ref[row : row + HALO] for row in rows)


def first_ocean_kernel(
    arrived, first_prev, first_next, gx, gy, eta, u, v, sst, spread, idx, w, rim_idx, rim_w,
    eta_new, u_new, v_new, sides_new, up, dn, fu, fv, fside, side_idx, side_w, warm, answers,
    flow, flow_outer, sides
):
    tiles = eta.shape[0]
    devices = arrived.shape[0]
    parts = arrived[...].astype(jnp.float32)
    ids = parts[:, ROW_IDS, :]
    number = lax.broadcasted_iota(jnp.int32, (devices, LANES), 1).astype(jnp.float32)
    chosen = [
        jnp.where(ids[:, j : j + 1] == number, 1.0, 0.0).astype(jnp.bfloat16) for j in range(6)
    ]
    nothing = jnp.zeros((devices, LANES), jnp.float32)
    lines = []
    for j in range(6):
        rows = [3 * j, 3 * j + 1, 3 * j + 2] if j < 2 else [None, 2 * j + 2, 2 * j + 3]
        lines.append(
            jnp.concatenate([nothing if r is None else parts[:, r, :] for r in rows], axis=1)
        )
    forcing = lax.dot_general(
        jnp.concatenate(chosen, axis=0),
        jnp.concatenate(lines, axis=0).astype(jnp.bfloat16),
        (((0,), (0,)), ((), ())),
        preferred_element_type=jnp.float32,
    )
    fu[...] = forcing[0:tiles, LANES : 2 * LANES]
    fv[...] = forcing[0:tiles, 2 * LANES : 3 * LANES]
    fside[0 : 2 * HALO] = forcing[tiles : tiles + 2 * HALO, LANES : 2 * LANES]
    fside[2 * HALO : 4 * HALO] = forcing[tiles : tiles + 2 * HALO, 2 * LANES : 3 * LANES]

    outer = jnp.concatenate(
        [first_prev[ROW_SST : ROW_SST + HALO], first_next[ROW_SST : ROW_SST + HALO]], axis=0
    )
    warm[...] = (
        sst[...]
        + WARMING_COEFF * forcing[0:tiles, 0:LANES]
        + (0.5 * SPREADING_COEFF) * spread[...]
    )
    for at, terms in outer_terms(idx, w, outer, tiles):
        warm[at : at + 8] = warm[at : at + 8] + (0.5 * SPREADING_COEFF) * combine(
            terms, [1.0] * 6
        )
    half = warm[...].astype(jnp.bfloat16)
    for j in range(CAP):
        answers[:, j, :] = jnp.dot(
            chosen[j][:, 0:tiles], half, preferred_element_type=jnp.float32
        )
    answers[:, CAP:8, :] = jnp.zeros((devices, 8 - CAP, LANES), jnp.float32)

    for side, ref in ((0, first_prev), (1, first_next)):
        side_idx[side] = ref[ROW_IDX : ROW_IDX + 16].astype(jnp.int32)
        side_w[side] = ref[ROW_W : ROW_W + 16]
        for n, row in ((0, ROW_U), (1, ROW_V)):
            at = HALO * (2 * n + side)
            sides[at : at + HALO] = ref[row : row + HALO]
    rows = (ROW_ETA, ROW_PX, ROW_PY)
    subcycle(
        gx, gy, eta, u, v, sides, fu, fv, fside, rim_of(first_prev, rows), rim_of(first_next, rows),
        idx, w, side_idx, side_w, rim_idx, rim_w, flow, flow_outer,
        eta_new, u_new, v_new, sides_new, up, dn
    )


def ocean_kernel(
    from_prev, from_next, gx, gy, eta, u, v, sides, fu, fv, fside, idx, w, side_idx, side_w,
    rim_idx, rim_w, eta_new, u_new, v_new, sides_new, up, dn, flow, flow_outer
):
    rows = (0, HALO, 2 * HALO)
    subcycle(
        gx, gy, eta, u, v, sides, fu, fv, fside, rim_of(from_prev, rows), rim_of(from_next, rows),
        idx, w, side_idx, side_w, rim_idx, rim_w, flow, flow_outer,
        eta_new, u_new, v_new, sides_new, up, dn
    )


def last_ocean_kernel(
    from_prev, from_next, gx, gy, eta, u, v, sides, fu, fv, fside, idx, w, side_idx, side_w,
    rim_idx, rim_w, eta_new, velocity, u_new, v_new, flow, flow_outer
):
    rows = (0, HALO, 2 * HALO)
    subcycle(
        gx, gy, eta, u, v, sides, fu, fv, fside, rim_of(from_prev, rows), rim_of(from_next, rows),
        idx, w, side_idx, side_w, rim_idx, rim_w, flow, flow_outer,
        eta_new, u_new, v_new, None, None, None
    )
    for r in range(eta.shape[0]):
        cut = slice(r * LANES, (r + 1) * LANES)
        velocity[0:1, cut] = u_new[r : r + 1]
        velocity[1:2, cut] = v_new[r : r + 1]


def shards(
    air_warmth,
    eastern_breeze,
    northern_breeze,
    reciprocal_breadth,
    panel_neighbours,
    transfer_coefficients,
    transfer_across_tile,
    transfer_holder,
    transfer_down_tile,
    water_elevation,
    depth_mean_current,
    marine_skin_warmth,
    patch_neighbours,
    interface_span,
):
    devices = lax.axis_size(RING)
    points, levels, elements = air_warmth.shape
    cells = water_elevation.shape[0]
    tiles = cells // LANES
    breadth = reciprocal_breadth.reshape(1, elements)
    eta = water_elevation.reshape(tiles, LANES)
    sst = marine_skin_warmth.reshape(tiles, LANES)
    cell_rows = shape_of(tiles, LANES)
    rim_rows = shape_of(4 * HALO, LANES)

    lowest = pl.BlockSpec((points, 8, elements), lambda i: (0, 0, 0))
    lowest_wind = pl.BlockSpec((points, 16, elements), lambda i: (0, 0, 0))

    idx, w, rim_idx, rim_w, u, v, up, dn = pl.pallas_call(
        prepare_kernel,
        grid=(1,),
        in_specs=[lowest] + vmem(6),
        out_specs=vmem(8),
        out_shape=(
            shape_of(6 * tiles, LANES, dtype=jnp.int32),
            shape_of(6 * tiles, LANES),
            shape_of(2, 16, LANES, dtype=jnp.int32),
            shape_of(2, 16, LANES),
            cell_rows,
            cell_rows,
            shape_of(ROWS_FIRST, LANES),
            shape_of(ROWS_FIRST, LANES),
        ),
        compiler_params=PARAMS,
        name="prepare",
    )(air_warmth, breadth, eta, sst, depth_mean_current, patch_neighbours, interface_span)
    first_prev, first_next = shifted(up, 1), shifted(dn, -1)

    block = pl.BlockSpec((points, 16, elements), lambda i: (0, i, 0))
    edge_block = pl.BlockSpec((2, 4, 16, elements), lambda i: (0, 0, i, 0))
    whole = [
        pl.BlockSpec((1, elements), lambda i: (0, 0)),
        pl.BlockSpec((4, elements), lambda i: (0, 0)),
    ]
    edge_shape = shape_of(2, 4, levels, elements, dtype=jnp.bfloat16)
    loc, east, west = pl.pallas_call(
        local_step_kernel,
        grid=(levels // 16,),
        in_specs=[block, block, block] + whole,
        out_specs=[block, edge_block, edge_block],
        out_shape=(shape_of(points, levels, elements), edge_shape, edge_shape),
        compiler_params=PARAMS,
        name="local_step",
    )(air_warmth, eastern_breeze, northern_breeze, breadth, panel_neighbours)
    prev_east, next_west = shifted(east, 1), shifted(west, -1)

    gx, gy, spread = pl.pallas_call(
        first_gradient_kernel,
        in_specs=vmem(4),
        out_specs=vmem(3),
        out_shape=(cell_rows,) * 3,
        compiler_params=PARAMS,
        name="first_gradient",
    )(idx, w, eta, sst)

    outgoing = pl.pallas_call(
        lambda *refs: forward_kernel(*refs, devices=devices, tiles=tiles),
        grid=(1,),
        in_specs=smem(3) + [lowest, lowest_wind, lowest_wind] + vmem(5),
        out_specs=pl.BlockSpec(memory_space=pltpu.VMEM),
        out_shape=shape_of(devices, PER_DEST, LANES, dtype=jnp.bfloat16),
        scratch_shapes=[
            pltpu.SMEM((devices,), jnp.int32),
            pltpu.VMEM((points, 8, elements), jnp.float32),
            pltpu.VMEM((devices, PER_DEST, LANES), jnp.float32),
        ],
        compiler_params=PARAMS,
        name="forward_remap",
    )(
        transfer_holder, transfer_down_tile, transfer_across_tile, loc, eastern_breeze,
        northern_breeze, breadth, panel_neighbours, first_prev, first_next, transfer_coefficients
    )
    arrived = exchange(outgoing)

    flow_scratch = [
        pltpu.VMEM((3, tiles, LANES), jnp.float32),
        pltpu.VMEM((3, 8, LANES), jnp.float32),
    ]
    tables = (idx, w)
    (
        eta, u, v, sides, up, dn, fu, fv, fside, side_idx, side_w, warm, answers
    ) = pl.pallas_call(
        first_ocean_kernel,
        in_specs=vmem(14),
        out_specs=vmem(13),
        out_shape=(
            cell_rows, cell_rows, cell_rows, rim_rows, rim_rows, rim_rows,
            cell_rows, cell_rows, rim_rows,
            shape_of(2, 16, LANES, dtype=jnp.int32), shape_of(2, 16, LANES),
            cell_rows, shape_of(devices, 8, LANES),
        ),
        scratch_shapes=flow_scratch + [pltpu.VMEM((4 * HALO, LANES), jnp.float32)],
        compiler_params=PARAMS,
        name="first_ocean",
    )(
        arrived, first_prev, first_next, gx, gy, eta, u, v, sst, spread, idx, w, rim_idx, rim_w
    )
    from_prev, from_next = shifted(up, 1), shifted(dn, -1)
    answered = exchange(answers)

    for substep in range(1, NSUB):
        gx, gy = pl.pallas_call(
            gradient_kernel,
            in_specs=vmem(3),
            out_specs=vmem(2),
            out_shape=(cell_rows,) * 2,
            compiler_params=PARAMS,
            name="gradient",
        )(idx, w, eta)
        operands = (
            from_prev, from_next, gx, gy, eta, u, v, sides, fu, fv, fside, idx, w,
            side_idx, side_w, rim_idx, rim_w
        )
        if substep + 1 < NSUB:
            eta, u, v, sides, up, dn = pl.pallas_call(
                ocean_kernel,
                in_specs=vmem(17),
                out_specs=vmem(6),
                out_shape=(cell_rows,) * 3 + (rim_rows,) * 3,
                scratch_shapes=flow_scratch,
                compiler_params=PARAMS,
                name="ocean",
            )(*operands)
            from_prev, from_next = shifted(up, 1), shifted(dn, -1)
        else:
            eta, velocity = pl.pallas_call(
                last_ocean_kernel,
                in_specs=vmem(17),
                out_specs=vmem(2),
                out_shape=(cell_rows, shape_of(2, cells)),
                scratch_shapes=[pltpu.VMEM((tiles, LANES), jnp.float32)] * 2 + flow_scratch,
                compiler_params=PARAMS,
                name="last_ocean",
            )(*operands)

    second = pl.pallas_call(
        second_step_kernel,
        grid=(levels // 16,),
        in_specs=[block, block, block] + whole + [edge_block] * 4 + [
            pl.BlockSpec((ROWS_FIRST, LANES), lambda i: (0, 0))
        ] * 2,
        out_specs=block,
        out_shape=shape_of(points, levels, elements),
        compiler_params=PARAMS,
        name="second_step",
    )(
        loc, eastern_breeze, northern_breeze, breadth, panel_neighbours, east, west,
        next_west, prev_east, first_prev, first_next
    )

    closing = pl.pallas_call(
        lambda *refs: back_kernel(*refs, devices=devices),
        grid=(1,),
        in_specs=smem(2) + vmem(2) + [lowest],
        out_specs=lowest,
        out_shape=shape_of(points, levels, elements),
        scratch_shapes=[
            pltpu.SMEM((devices,), jnp.int32),
            pltpu.VMEM((points, 8, elements), jnp.float32),
        ],
        input_output_aliases={4: 0},
        compiler_params=PARAMS,
        name="back_remap",
    )(transfer_holder, transfer_across_tile, answered, transfer_coefficients, second)
    return closing, eta.reshape(cells), velocity, warm.reshape(cells)


def solution(mesh):
    split = P(RING)
    last = P(None, RING)
    field = P(None, None, RING)
    return jax.shard_map(
        shards,
        mesh=mesh,
        in_specs=(
            field,
            field,
            field,
            split,
            last,
            P(RING, None, None),
            split,
            P(RING, None),
            split,
            split,
            last,
            split,
            last,
            last,
        ),
        out_specs=(field, split, last, split),
        check_vma=False,
    )
```

time: 1060 us -> 73.8 us (0.07)
  local copies, waits for them, and re-layouts: 938 us -> 11.5 us
  other arithmetic: 40.3 us -> 0 us
  starting transfers between devices: 65.7 us -> 33.5 us
  Pallas kernels: 0 us -> 21.6 us
    gather x38 -> x0, local copies, waits for them, and re-layouts: 891 us -> none  [the longest x13 860 us: neighbours(): return extended.reshape(extended.shape[0], -1)[:, spread]]
    ppermute x20 -> x10, starting transfers between devices: 50.6 us -> 28.1 us  [shifted(): lax.ppermute(value, RING, [(i, (i + steps) % count) for i in range(count)])]
    pallas_call x0 -> x13, Pallas kernels: none -> 21.6 us  [the longest x3 3.52 us: shards(): pl.pallas_call(gradient_kernel, in_specs=vmem(3), out_specs=vmem(2), out_...]
  transfers between devices with their start and end apart: 23 -> 12, of which waited for: 1 -> 4; matrix products, arithmetic and copies ran while one was open for 38% -> 1% of each run, Pallas kernels for 0% -> 20%
where the time goes in v1:
time: 73.8 us; the launch traced here: 73.1 us
  starting transfers between devices  33.5 us (45%)
  Pallas kernels  21.6 us (29%)
  local copies, waits for them, and re-layouts  11.5 us (16%)
  waiting for transfers between devices  5.67 us (8%)
  between operations  0.84 us (1%)
    ppermute x10, starting transfers between devices, shifted(): lax.ppermute(value, RING, [(i, (i + steps) % count) for i in range(count)])  28.1 us
    unnamed x43, local copies, waits for them, and re-layouts  11.5 us
    all_to_all x2, starting transfers between devices, exchange(): return lax.all_to_all(value, RING, split_axis=0, concat_axis=0, tiled=True)  5.45 us
    all_to_all x2, waiting for transfers between devices, exchange(): return lax.all_to_all(value, RING, split_axis=0, concat_axis=0, tiled=True)  5.36 us
    pallas_call x3, Pallas kernels, shards(): pl.pallas_call(gradient_kernel, in_specs=vmem(3), out_specs=vmem(2), out_...  3.52 us
    pallas_call x2, Pallas kernels, shards(): pl.pallas_call(ocean_kernel, in_specs=vmem(17), out_specs=vmem(6), out_sh...  3.42 us
    pallas_call x1, Pallas kernels, shards(): pl.pallas_call(first_ocean_kernel, in_specs=vmem(14), out_specs=vmem(13),...  2.62 us
    pallas_call x1, Pallas kernels, shards(): pl.pallas_call(first_gradient_kernel, in_specs=vmem(4), out_specs=vmem(3)...  2.35 us
  transfers between devices with their start and end apart: 12, of which 4 were waited for; matrix products, arithmetic and copies ran while one was open for 1% of the time, Pallas kernels for 20%

profile of v1, /device:TPU:0, one launch (start us, length us, event | category | flops | bytes accessed | tf_op | source)
XLA Modules:
  0.0 73.1 jit_solution(2606833443425723673)
XLA Ops:
  0.6 0.0 copy-start
  0.6 0.0 copy-start.5
  0.7 1.1 %copy-done.5 = f32[16,64,128]{2,1,0:T(8,128)S(1)} copy-done((f32[16,64,128]{2,1,0:T(8,128)S(1)}, f32[16,64,128]{2,1,0:T(8,128)}, u32[]{:S(2)}) %copy-start.5) | copy-done | bytes 524312
  1.8 0.7 copy-done.7
  2.5 0.7 copy-done.9
  3.2 0.9 %copy-done.11 = s32[6,4096]{1,0:T(8,128)S(1)} copy-done((s32[6,4096]{1,0:T(8,128)S(1)}, s32[6,4096]{1,0:T(8,128)}, u32[]{:S(2)}) %copy-start.11) | copy-done | bytes 98328
  4.1 0.9 %copy-done.12 = f32[6,4096]{1,0:T(8,128)S(1)} copy-done((f32[6,4096]{1,0:T(8,128)S(1)}, f32[6,4096]{1,0:T(8,128)}, u32[]{:S(2)}) %copy-start.12) | copy-done | bytes 98328
  5.0 0.8 %copy-done.13 = f32[2,4096]{1,0:T(2,128)S(1)} copy-done((f32[2,4096]{1,0:T(2,128)S(1)}, f32[2,4096]{1,0:T(2,128)}, u32[]{:S(2)}) %copy-start.13) | copy-done | bytes 32792
  5.8 0.7 copy-done.16
  6.4 0.3 prepare.1
  6.7 3.0 %collective-permute-start = (f32[56,128]{1,0:T(8,128)S(1)}, f32[56,128]{1,0:T(8,128)S(1)}, u32[]{:S(2)}, u32[]{:S(2)}) collective-permute-start(f32[56,128]{1,0:T(8,128)S(1)} %get-tuple-element.52), channel_id=1, source_target_pairs={{0,1},{1,2},{2,3},{3,4},{4,5},{5,6},{6,7},{7,8},{8,9},{9,10},{10,1... | collective-permute-start | bytes 86024 | tf_op jit(solution)/shard_map/ppermute | solution.py:38
  9.8 3.5 %collective-permute-start.1 = (f32[56,128]{1,0:T(8,128)S(1)}, f32[56,128]{1,0:T(8,128)S(1)}, u32[]{:S(2)}, u32[]{:S(2)}) collective-permute-start(f32[56,128]{1,0:T(8,128)S(1)} %get-tuple-element.53), channel_id=1, source_target_pairs={{0,31},{1,0},{2,1},{3,2},{4,3},{5,4},{6,5},{7,6},{8,7},{9,8},{10,9... | collective-permute-start | bytes 86024 | tf_op jit(solution)/shard_map/ppermute | solution.py:38
  13.2 0.7 %copy.20.refs_0_ = s32[32,1]{1,0:T(8,128)S(1)} copy(s32[32,1]{0,1:T(1,128)} %param.21) | data formatting | bytes 256 | tf_op args[7]
  14.0 0.9 %copy-done.1 = bf16[16,64,128]{2,1,0:T(8,128)(2,1)S(1)} copy-done((bf16[16,64,128]{2,1,0:T(8,128)(2,1)S(1)}, bf16[16,64,128]{2,1,0:T(8,128)(2,1)}, u32[]{:S(2)}) %copy-start.1) | copy-done | bytes 262168
  14.9 0.9 %copy-done.3 = bf16[16,64,128]{2,1,0:T(8,128)(2,1)S(1)} copy-done((bf16[16,64,128]{2,1,0:T(8,128)(2,1)S(1)}, bf16[16,64,128]{2,1,0:T(8,128)(2,1)}, u32[]{:S(2)}) %copy-start.3) | copy-done | bytes 262168
  15.9 1.0 %copy-done.6 = f32[16,64,128]{2,1,0:T(8,128)S(1)} copy-done((f32[16,64,128]{2,1,0:T(8,128)S(1)}, f32[16,64,128]{2,1,0:T(8,128)}, u32[]{:S(2)}) %copy-start.6) | copy-done | bytes 524312
  16.9 0.7 copy-done.14
  17.6 0.7 copy-done.17
  18.3 0.8 %local_step.1 = (f32[16,64,128]{2,1,0:T(8,128)S(1)}, bf16[2,4,64,128]{3,2,1,0:T(8,128)(2,1)S(1)}, bf16[2,4,64,128]{3,2,1,0:T(8,128)(2,1)S(1)}) custom-call(f32[16,64,128]{2,1,0:T(8,128)S(1)} %copy-done.6, bf16[16,64,128]{2,1,0:T(8,128)(2,1)S(1)} %copy-done.1, bf16[16,64,128]{2,1,0:T(8,128)(2,1)S(1)} %copy-done.3, f32[1,128]{1,0:T(1,128)S(1)} %bitcast.12, ...), custom_call_target="tpu_custom_call" | custom-call | tf_op jit(solution)/shard_map/local_step/pallas_call | solution.py:620
  19.0 0.0 copy-start.19
  19.0 0.0 copy-start.20
  19.1 0.0 collective-permute-done.refs_8_.first_prev
  19.1 0.0 collective-permute-done.1.refs_9_.first_next
  19.1 0.0 copy-done
  19.1 0.1 copy-done.2
  19.2 0.1 copy-done.4
  19.3 0.4 copy-done.19
  19.7 0.0 copy-done.20
  19.7 2.2 %forward_remap.1 = bf16[32,16,128]{2,1,0:T(8,128)(2,1)} custom-call(s32[32,1]{1,0:T(8,128)S(1)} %copy.20.refs_0_, s32[32]{0:T(128)S(1)} %copy-done.20, s32[32]{0:T(128)S(1)} %copy-done.19, f32[16,64,128]{2,1,0:T(8,128)S(1)} %get-tuple-element.51.refs_3_.loc, bf16[16,64,128]{2,1,0:T(8,128)(2,1)S(1)} %copy-done.2, bf16[16,64,128]{2,1,0:T(8,128)(2,1)S(1)} %copy-done.4, ...), custom_call_target="tpu_custom_call" | custom-call | tf_op jit(solution)/shard_map/forward_remap/pallas_call | solution.py:640
  21.9 2.9 %all-to-all-start = ((bf16[32,16,128]{2,1,0:T(8,128)(2,1)}), bf16[32,16,128]{2,1,0:T(8,128)(2,1)S(1)}, u32[]{:S(2)}, u32[]{:S(2)}) async-start(bf16[32,16,128]{2,1,0:T(8,128)(2,1)} %forward_remap.1), calls=%async_computation | async-start | bytes 262144 | tf_op jit(solution)/shard_map/all_to_all | solution.py:42
  24.8 0.0 copy-done.8
  24.8 0.0 copy-done.10
  24.9 2.4 %first_gradient.1 = (f32[32,128]{1,0:T(8,128)S(1)}, f32[32,128]{1,0:T(8,128)S(1)}, f32[32,128]{1,0:T(8,128)S(1)}) custom-call(s32[192,128]{1,0:T(8,128)S(1)} %get-tuple-element.54.idx, f32[192,128]{1,0:T(8,128)S(1)} %get-tuple-element.55.w, f32[32,128]{1,0:T(8,128)S(1)} %bitcast.6, f32[32,128]{1,0:T(8,128)S(1)} %bitcast.9), custom_call_target="tpu_custom_call" | custom-call | tf_op jit(solution)/shard_map/first_gradient/pallas_call | solution.py:631
  27.2 5.4 %all-to-all-done.arrived = bf16[32,16,128]{2,1,0:T(8,128)(2,1)S(1)} async-done(((bf16[32,16,128]{2,1,0:T(8,128)(2,1)}), bf16[32,16,128]{2,1,0:T(8,128)(2,1)S(1)}, u32[]{:S(2)}, u32[]{:S(2)}) %all-to-all-start) | async-done | bytes 131104 | tf_op jit(solution)/shard_map/all_to_all | solution.py:42
  32.6 2.6 %first_ocean.1 = (f32[32,128]{1,0:T(8,128)S(1)}, f32[32,128]{1,0:T(8,128)S(1)}, f32[32,128]{1,0:T(8,128)S(1)}, f32[8,128]{1,0:T(8,128)S(1)}, f32[8,128]{1,0:T(8,...) custom-call(bf16[32,16,128]{2,1,0:T(8,128)(2,1)S(1)} %all-to-all-don, ...), custom_call_target="tpu_custom_call" | custom-call | tf_op jit(solution)/shard_map/first_ocean/pallas_call | solution.py:666
  35.2 2.6 %all-to-all-start.1 = ((f32[32,8,128]{2,1,0:T(8,128)}), f32[32,8,128]{2,1,0:T(8,128)S(1)}, u32[]{:S(2)}, u32[]{:S(2)}) async-start(f32[32,8,128]{2,1,0:T(8,128)} %get-tuple-element.63), calls=%async_computation.1 | async-start | bytes 262144 | tf_op jit(solution)/shard_map/all_to_all | solution.py:42
  37.8 1.7 %collective-permute-start.3 = (bf16[2,4,64,128]{3,2,1,0:T(8,128)(2,1)S(1)}, bf16[2,4,64,128]{3,2,1,0:T(8,128)(2,1)S(1)}, u32[]{:S(2)}, u32[]{:S(2)}) collective-permute-start(bf16[2,4,64,128]{3,2,1,0:T(8,128)(2,1)S(1)} %get-tuple-element.64.east), channel_id=1, source_target_pairs={{0,1},{1,2},{2,3},{3,4},{4,5},{5,6},{6,7},{7,8},{8,9},{9,10},{10,1... | collective-permute-start | bytes 393224 | tf_op jit(solution)/shard_map/ppermute | solution.py:38
  39.5 3.7 %collective-permute-start.2 = (bf16[2,4,64,128]{3,2,1,0:T(8,128)(2,1)S(1)}, bf16[2,4,64,128]{3,2,1,0:T(8,128)(2,1)S(1)}, u32[]{:S(2)}, u32[]{:S(2)}) collective-permute-start(bf16[2,4,64,128]{3,2,1,0:T(8,128)(2,1)S(1)} %get-tuple-element.65.west), channel_id=1, source_target_pairs={{0,31},{1,0},{2,1},{3,2},{4,3},{5,4},{6,5},{7,6},{8,7},{9,8},{10,9... | collective-permute-start | bytes 393224 | tf_op jit(solution)/shard_map/ppermute | solution.py:38
  43.2 0.0 collective-permute-start.4
  43.2 5.3 %collective-permute-start.5 = (f32[8,128]{1,0:T(8,128)S(1)}, f32[8,128]{1,0:T(8,128)S(1)}, u32[]{:S(2)}, u32[]{:S(2)}) collective-permute-start(f32[8,128]{1,0:T(8,128)S(1)} %get-tuple-element.67), channel_id=1, source_target_pairs={{0,31},{1,0},{2,1},{3,2},{4,3},{5,4},{6,5},{7,6},{8,7},{9,8},{10,9... | collective-permute-start | bytes 12296 | tf_op jit(solution)/shard_map/ppermute | solution.py:38
  48.5 1.2 %gradient.3 = (f32[32,128]{1,0:T(8,128)S(1)}, f32[32,128]{1,0:T(8,128)S(1)}) custom-call(s32[192,128]{1,0:T(8,128)S(1)} %get-tuple-element.54.idx, f32[192,128]{1,0:T(8,128)S(1)} %get-tuple-element.55.w, f32[32,128]{1,0:T(8,128)S(1)} %get-tuple-element.68.eta), custom_call_target="tpu_custom_call" | custom-call | tf_op jit(solution)/shard_map/gradient/pallas_call | solution.py:686
  49.7 0.1 collective-permute-done.4.from_prev
  49.8 0.0 collective-permute-done.5.from_next
  49.8 1.7 %ocean.2 = (f32[32,128]{1,0:T(8,128)S(1)}, f32[32,128]{1,0:T(8,128)S(1)}, f32[32,128]{1,0:T(8,128)S(1)}, f32[8,128]{1,0:T(8,128)S(1)}, f32[8,128]{1,0:T(8,128)S(1)}, /*index=5*/f32[8,128]{1,0:T(8,128)S(1)}) custom-call(f32[8,128]{1,0:T(8,128)S(1)} %collective-permute-done.4.from_prev, f32[8,128]{1,0:T(8,128)S(1)} %collective-permute-done.5.from_next, ...), custom_call_target="tpu_custom_call" | custom-call | tf_op jit(solution)/shard_map/ocean/pallas_call | solution.py:699
  51.6 0.1 collective-permute-start.6
  51.6 5.4 %collective-permute-start.7 = (f32[8,128]{1,0:T(8,128)S(1)}, f32[8,128]{1,0:T(8,128)S(1)}, u32[]{:S(2)}, u32[]{:S(2)}) collective-permute-start(f32[8,128]{1,0:T(8,128)S(1)} %get-tuple-element.80), channel_id=1, source_target_pairs={{0,31},{1,0},{2,1},{3,2},{4,3},{5,4},{6,5},{7,6},{8,7},{9,8},{10,9... | collective-permute-start | bytes 12296 | tf_op jit(solution)/shard_map/ppermute | solution.py:38
  57.0 1.2 %gradient.4 = (f32[32,128]{1,0:T(8,128)S(1)}, f32[32,128]{1,0:T(8,128)S(1)}) custom-call(s32[192,128]{1,0:T(8,128)S(1)} %get-tuple-element.54.idx, f32[192,128]{1,0:T(8,128)S(1)} %get-tuple-element.55.w, f32[32,128]{1,0:T(8,128)S(1)} %get-tuple-element.81.eta), custom_call_target="tpu_custom_call" | custom-call | tf_op jit(solution)/shard_map/gradient/pallas_call | solution.py:686
  58.2 0.1 collective-permute-done.6.from_prev
  58.2 0.1 collective-permute-done.7.from_next
  58.3 1.7 %ocean.3 = (f32[32,128]{1,0:T(8,128)S(1)}, f32[32,128]{1,0:T(8,128)S(1)}, f32[32,128]{1,0:T(8,128)S(1)}, f32[8,128]{1,0:T(8,128)S(1)}, f32[8,128]{1,0:T(8,128)S(1)}, /*index=5*/f32[8,128]{1,0:T(8,128)S(1)}) custom-call(f32[8,128]{1,0:T(8,128)S(1)} %collective-permute-done.6.from_prev, f32[8,128]{1,0:T(8,128)S(1)} %collective-permute-done.7.from_next, ...), custom_call_target="tpu_custom_call" | custom-call | tf_op jit(solution)/shard_map/ocean/pallas_call | solution.py:699
  60.0 0.0 copy-start.15
  60.0 0.0 copy-start.18
  60.0 0.1 collective-permute-start.8
  60.1 5.4 %collective-permute-start.9 = (f32[8,128]{1,0:T(8,128)S(1)}, f32[8,128]{1,0:T(8,128)S(1)}, u32[]{:S(2)}, u32[]{:S(2)}) collective-permute-start(f32[8,128]{1,0:T(8,128)S(1)} %get-tuple-element.88), channel_id=1, source_target_pairs={{0,31},{1,0},{2,1},{3,2},{4,3},{5,4},{6,5},{7,6},{8,7},{9,8},{10,9... | collective-permute-start | bytes 12296 | tf_op jit(solution)/shard_map/ppermute | solution.py:38
  65.5 0.0 collective-permute-done.3.prev_east
  65.5 0.0 collective-permute-done.2.next_west
  65.5 0.0 copy-done.15
  65.5 2.2 %second_step.1.refs_4_ = f32[16,64,128]{2,1,0:T(8,128)} custom-call(f32[16,64,128]{2,1,0:T(8,128)S(1)} %get-tuple-element.51.refs_3_.loc, bf16[16,64,128]{2,1,0:T(8,128)(2,1)S(1)} %copy-done.2, bf16[16,64,128]{2,1,0:T(8,128)(2,1)S(1)} %copy-done.4, f32[1,128]{1,0:T(1,128)S(1)} %bitcast.14, s32[4,128]{1,0:T(4,128)S(1)} %copy-done.15, ...), custom_call_target="tpu_custom_call" | custom-call | tf_op jit(solution)/shard_map/second_step/pallas_call | solution.py:720
  67.7 1.2 %gradient.5 = (f32[32,128]{1,0:T(8,128)S(1)}, f32[32,128]{1,0:T(8,128)S(1)}) custom-call(s32[192,128]{1,0:T(8,128)S(1)} %get-tuple-element.54.idx, f32[192,128]{1,0:T(8,128)S(1)} %get-tuple-element.55.w, f32[32,128]{1,0:T(8,128)S(1)} %get-tuple-element.89.eta), custom_call_target="tpu_custom_call" | custom-call | tf_op jit(solution)/shard_map/gradient/pallas_call | solution.py:686
  68.8 0.0 collective-permute-done.8.from_prev
  68.9 0.0 collective-permute-done.9.from_next
  68.9 2.1 %last_ocean.1 = (f32[32,128]{1,0:T(8,128)}, f32[2,4096]{1,0:T(2,128)}) custom-call(f32[8,128]{1,0:T(8,128)S(1)} %collective-permute-done.8.from_prev, f32[8,128]{1,0:T(8,128)S(1)} %collective-permute-done.9.from_next, f32[32,128]{1,0:T(8,128)S(1)} %get-tuple-element.90.gx, f32[32,128]{1,0:T(8,128)S(1)} %get-tuple-element.91.gy, ...), custom_call_target="tpu_custom_call" | custom-call | tf_op jit(solution)/shard_map/last_ocean/pallas_call | solution.py:710
  70.9 0.0 all-to-all-done.1.refs_2_
  70.9 2.2 %back_remap.1 = f32[16,64,128]{2,1,0:T(8,128)} custom-call(s32[32,1]{1,0:T(8,128)S(1)} %copy.20.refs_0_, s32[32]{0:T(128)S(1)} %copy-done.19, f32[32,8,128]{2,1,0:T(8,128)S(1)} %all-to-all-done.1.refs_2_, bf16[32,128,128]{2,1,0:T(8,128)(2,1)S(1)} %copy-done, f32[16,64,128]{2,1,0:T(8,128)} %second_step.1.refs_4_), custom_call_target="tpu_custom_call", output_to_operand_aliasing={{}: (4, {})} | custom-call | tf_op jit(solution)/shard_map/back_remap/pallas_call | solution.py:735
  (16 shorter events, 0.0 us)
Async XLA Ops:
  0.6 18.4 %copy-start = (bf16[32,128,128]{2,1,0:T(8,128)(2,1)S(1)}, bf16[32,128,128]{2,1,0:T(8,128)(2,1)}, u32[]{:S(2)}) copy-start(bf16[32,128,128]{2,1,0:T(8,128)(2,1)} %refs_3_.1) | copy-start | bytes 3145732
  0.6 1.1 %copy-start.5 = (f32[16,64,128]{2,1,0:T(8,128)S(1)}, f32[16,64,128]{2,1,0:T(8,128)}, u32[]{:S(2)}) copy-start(f32[16,64,128]{2,1,0:T(8,128)} %air.3) | copy-start | bytes 1572868
  1.8 0.7 copy-start.7
  2.5 0.7 copy-start.9
  3.2 0.9 %copy-start.11 = (s32[6,4096]{1,0:T(8,128)S(1)}, s32[6,4096]{1,0:T(8,128)}, u32[]{:S(2)}) copy-start(s32[6,4096]{1,0:T(8,128)} %nb.1) | copy-start | bytes 294916
  4.1 0.9 %copy-start.12 = (f32[6,4096]{1,0:T(8,128)S(1)}, f32[6,4096]{1,0:T(8,128)}, u32[]{:S(2)}) copy-start(f32[6,4096]{1,0:T(8,128)} %span.1) | copy-start | bytes 294916
  5.0 0.8 %copy-start.13 = (f32[2,4096]{1,0:T(2,128)S(1)}, f32[2,4096]{1,0:T(2,128)}, u32[]{:S(2)}) copy-start(f32[2,4096]{1,0:T(2,128)} %flow.1) | copy-start | bytes 98308
  5.8 0.7 copy-start.16
  6.7 12.3 %collective-permute-start = (f32[56,128]{1,0:T(8,128)S(1)}, f32[56,128]{1,0:T(8,128)S(1)}, u32[]{:S(2)}, u32[]{:S(2)}) collective-permute-start(f32[56,128]{1,0:T(8,128)S(1)} %get-tuple-element.52), channel_id=1, source_target_pairs={{0,1},{1,2},{2,3},{3,4},{4,5},{5,6},{6,7},{7,8},{8,9},{9,10},{10,1... | collective-permute-start | bytes 86024 | tf_op jit(solution)/shard_map/ppermute | solution.py:38
  9.8 9.3 %collective-permute-start.1 = (f32[56,128]{1,0:T(8,128)S(1)}, f32[56,128]{1,0:T(8,128)S(1)}, u32[]{:S(2)}, u32[]{:S(2)}) collective-permute-start(f32[56,128]{1,0:T(8,128)S(1)} %get-tuple-element.53), channel_id=1, source_target_pairs={{0,31},{1,0},{2,1},{3,2},{4,3},{5,4},{6,5},{7,6},{8,7},{9,8},{10,9... | collective-permute-start | bytes 86024 | tf_op jit(solution)/shard_map/ppermute | solution.py:38
  14.0 0.9 %copy-start.1 = (bf16[16,64,128]{2,1,0:T(8,128)(2,1)S(1)}, bf16[16,64,128]{2,1,0:T(8,128)(2,1)}, u32[]{:S(2)}) copy-start(bf16[16,64,128]{2,1,0:T(8,128)(2,1)} %eastern.3) | copy-start | bytes 786436
  14.9 0.9 %copy-start.3 = (bf16[16,64,128]{2,1,0:T(8,128)(2,1)S(1)}, bf16[16,64,128]{2,1,0:T(8,128)(2,1)}, u32[]{:S(2)}) copy-start(bf16[16,64,128]{2,1,0:T(8,128)(2,1)} %northern.3) | copy-start | bytes 786436
  15.9 1.0 %copy-start.6 = (f32[16,64,128]{2,1,0:T(8,128)S(1)}, f32[16,64,128]{2,1,0:T(8,128)}, u32[]{:S(2)}) copy-start(f32[16,64,128]{2,1,0:T(8,128)} %air.3) | copy-start | bytes 1572868
  16.9 0.7 copy-start.14
  17.6 0.7 copy-start.17
  18.3 0.9 %copy-start.2 = (bf16[16,64,128]{2,1,0:T(8,128)(2,1)S(1)}, bf16[16,64,128]{2,1,0:T(8,128)(2,1)}, u32[]{:S(2)}) copy-start(bf16[16,64,128]{2,1,0:T(8,128)(2,1)} %eastern.3) | copy-start | bytes 786436
  18.3 1.0 %copy-start.4 = (bf16[16,64,128]{2,1,0:T(8,128)(2,1)S(1)}, bf16[16,64,128]{2,1,0:T(8,128)(2,1)}, u32[]{:S(2)}) copy-start(bf16[16,64,128]{2,1,0:T(8,128)(2,1)} %northern.3) | copy-start | bytes 786436
  19.0 0.7 copy-start.19
  19.0 0.7 copy-start.20
  21.9 2.9 %copy-start.8 = (f32[4096]{0:T(1024)S(1)}, f32[4096]{0:T(1024)}, u32[]{:S(2)}) copy-start(f32[4096]{0:T(1024)} %param.23) | copy-start | bytes 49156
  21.9 2.9 %copy-start.10 = (f32[4096]{0:T(1024)S(1)}, f32[4096]{0:T(1024)}, u32[]{:S(2)}) copy-start(f32[4096]{0:T(1024)} %param.25) | copy-start | bytes 49156
  21.9 10.6 %all-to-all-start = ((bf16[32,16,128]{2,1,0:T(8,128)(2,1)}), bf16[32,16,128]{2,1,0:T(8,128)(2,1)S(1)}, u32[]{:S(2)}, u32[]{:S(2)}) async-start(bf16[32,16,128]{2,1,0:T(8,128)(2,1)} %forward_remap.1), calls=%async_computation | async-start | bytes 262144 | tf_op jit(solution)/shard_map/all_to_all | solution.py:42
  35.2 35.7 %all-to-all-start.1 = ((f32[32,8,128]{2,1,0:T(8,128)}), f32[32,8,128]{2,1,0:T(8,128)S(1)}, u32[]{:S(2)}, u32[]{:S(2)}) async-start(f32[32,8,128]{2,1,0:T(8,128)} %get-tuple-element.63), calls=%async_computation.1 | async-start | bytes 262144 | tf_op jit(solution)/shard_map/all_to_all | solution.py:42
  37.8 27.7 %collective-permute-start.3 = (bf16[2,4,64,128]{3,2,1,0:T(8,128)(2,1)S(1)}, bf16[2,4,64,128]{3,2,1,0:T(8,128)(2,1)S(1)}, u32[]{:S(2)}, u32[]{:S(2)}) collective-permute-start(bf16[2,4,64,128]{3,2,1,0:T(8,128)(2,1)S(1)} %get-tuple-element.64.east), channel_id=1, source_target_pairs={{0,1},{1,2},{2,3},{3,4},{4,5},{5,6},{6,7},{7,8},{8,9},{9,10},{10,1... | collective-permute-start | bytes 393224 | tf_op jit(solution)/shard_map/ppermute | solution.py:38
  39.5 26.0 %collective-permute-start.2 = (bf16[2,4,64,128]{3,2,1,0:T(8,128)(2,1)S(1)}, bf16[2,4,64,128]{3,2,1,0:T(8,128)(2,1)S(1)}, u32[]{:S(2)}, u32[]{:S(2)}) collective-permute-start(bf16[2,4,64,128]{3,2,1,0:T(8,128)(2,1)S(1)} %get-tuple-element.65.west), channel_id=1, source_target_pairs={{0,31},{1,0},{2,1},{3,2},{4,3},{5,4},{6,5},{7,6},{8,7},{9,8},{10,9... | collective-permute-start | bytes 393224 | tf_op jit(solution)/shard_map/ppermute | solution.py:38
  43.2 6.6 %collective-permute-start.4 = (f32[8,128]{1,0:T(8,128)S(1)}, f32[8,128]{1,0:T(8,128)S(1)}, u32[]{:S(2)}, u32[]{:S(2)}) collective-permute-start(f32[8,128]{1,0:T(8,128)S(1)} %get-tuple-element.66), channel_id=1, source_target_pairs={{0,1},{1,2},{2,3},{3,4},{4,5},{5,6},{6,7},{7,8},{8,9},{9,10},{10,1... | collective-permute-start | bytes 12296 | tf_op jit(solution)/shard_map/ppermute | solution.py:38
  43.2 6.7 %collective-permute-start.5 = (f32[8,128]{1,0:T(8,128)S(1)}, f32[8,128]{1,0:T(8,128)S(1)}, u32[]{:S(2)}, u32[]{:S(2)}) collective-permute-start(f32[8,128]{1,0:T(8,128)S(1)} %get-tuple-element.67), channel_id=1, source_target_pairs={{0,31},{1,0},{2,1},{3,2},{4,3},{5,4},{6,5},{7,6},{8,7},{9,8},{10,9... | collective-permute-start | bytes 12296 | tf_op jit(solution)/shard_map/ppermute | solution.py:38
  51.6 6.7 %collective-permute-start.6 = (f32[8,128]{1,0:T(8,128)S(1)}, f32[8,128]{1,0:T(8,128)S(1)}, u32[]{:S(2)}, u32[]{:S(2)}) collective-permute-start(f32[8,128]{1,0:T(8,128)S(1)} %get-tuple-element.79), channel_id=1, source_target_pairs={{0,1},{1,2},{2,3},{3,4},{4,5},{5,6},{6,7},{7,8},{8,9},{9,10},{10,1... | collective-permute-start | bytes 12296 | tf_op jit(solution)/shard_map/ppermute | solution.py:38
  51.6 6.7 %collective-permute-start.7 = (f32[8,128]{1,0:T(8,128)S(1)}, f32[8,128]{1,0:T(8,128)S(1)}, u32[]{:S(2)}, u32[]{:S(2)}) collective-permute-start(f32[8,128]{1,0:T(8,128)S(1)} %get-tuple-element.80), channel_id=1, source_target_pairs={{0,31},{1,0},{2,1},{3,2},{4,3},{5,4},{6,5},{7,6},{8,7},{9,8},{10,9... | collective-permute-start | bytes 12296 | tf_op jit(solution)/shard_map/ppermute | solution.py:38
  60.0 5.5 %copy-start.15 = (s32[4,128]{1,0:T(4,128)S(1)}, s32[4,128]{1,0:T(4,128)}, u32[]{:S(2)}) copy-start(s32[4,128]{1,0:T(4,128)} %pn.3) | copy-start | bytes 6148
  60.0 5.4 %copy-start.18 = (f32[128]{0:T(128)S(1)}, f32[128]{0:T(128)}, u32[]{:S(2)}) copy-start(f32[128]{0:T(128)} %param.17) | copy-start | bytes 1540
  60.0 8.8 %collective-permute-start.8 = (f32[8,128]{1,0:T(8,128)S(1)}, f32[8,128]{1,0:T(8,128)S(1)}, u32[]{:S(2)}, u32[]{:S(2)}) collective-permute-start(f32[8,128]{1,0:T(8,128)S(1)} %get-tuple-element.87), channel_id=1, source_target_pairs={{0,1},{1,2},{2,3},{3,4},{4,5},{5,6},{6,7},{7,8},{8,9},{9,10},{10,1... | collective-permute-start | bytes 12296 | tf_op jit(solution)/shard_map/ppermute | solution.py:38
  60.1 8.7 %collective-permute-start.9 = (f32[8,128]{1,0:T(8,128)S(1)}, f32[8,128]{1,0:T(8,128)S(1)}, u32[]{:S(2)}, u32[]{:S(2)}) collective-permute-start(f32[8,128]{1,0:T(8,128)S(1)} %get-tuple-element.88), channel_id=1, source_target_pairs={{0,31},{1,0},{2,1},{3,2},{4,3},{5,4},{6,5},{7,6},{8,7},{9,8},{10,9... | collective-permute-start | bytes 12296 | tf_op jit(solution)/shard_map/ppermute | solution.py:38

commit v2 on v1

v2 whole, which is shorter than its diff:
```python
import math

import jax
import jax.numpy as jnp
import numpy as np
from jax import lax
from jax.experimental import pallas as pl
from jax.experimental.pallas import tpu as pltpu
from jax.sharding import PartitionSpec as P

OY = 256
NSUB = 4
CAP = 2

STEP_SIZE = 0.05
JUMP_WEIGHT = 4.0
NUDGING_SPEED = 0.5
DAMPING = 0.9
GRAVITY = 0.3
WIND_GAIN = 0.3
DEPTH_RATE = 0.3
WARMING_COEFF = 0.3
SPREADING_COEFF = 0.5

RING = ("comp", "dom")
LANES = 128
HALO = OY // LANES
COS = [math.cos(k * math.pi / 3.0) for k in range(6)]
SIN = [0.0 if k % 3 == 0 else math.sin(k * math.pi / 3.0) for k in range(6)]

ROW_EDGE, ROW_BREADTH, ROW_ETA, ROW_U, ROW_V, ROW_SST = 0, 4, 8, 10, 12, 14
ROW_PX, ROW_PY, ROW_IDX, ROW_W, ROWS_FIRST = 16, 18, 24, 40, 56
PER_DEST, ROW_HEAT, ROW_IDS = 16, 12, 14


def swapped(value, first):
    count = lax.axis_size(RING)
    pairs = []
    for i in range(first, count + first, 2):
        pairs += [(i % count, (i + 1) % count), ((i + 1) % count, i % count)]
    return lax.ppermute(value, RING, pairs)


def swap_both(far, near):
    got_far = swapped(far, 1)
    return got_far, swapped(near, 0)


class Received:
    def __init__(self, far, near, odd):
        self.far, self.near, self.odd = far, near, odd

    def flag(self, rows):
        return jnp.broadcast_to(self.odd[0:1], rows.shape) > 0

    def prev(self, *cut):
        far, near = self.far[cut], self.near[cut]
        return jnp.where(self.flag(far), near, far)

    def next(self, *cut):
        far, near = self.far[cut], self.near[cut]
        return jnp.where(self.flag(far), far, near)

    def rim(self, side, row):
        cut = slice(row, row + HALO)
        return self.prev(cut) if side == 0 else self.next(cut)

    def rims(self, side, rows):
        return tuple(self.rim(side, row) for row in rows)


def arrange(up, dn, odd, far, near):
    flag = jnp.broadcast_to(odd[0:1], up.shape) > 0
    far[...] = jnp.where(flag, up[...], dn[...])
    near[...] = jnp.where(flag, dn[...], up[...])


def exchange(value):
    return lax.all_to_all(value, RING, split_axis=0, concat_axis=0, tiled=True)


def gll_matrix():
    points = np.array([-1.0, -1.0 / np.sqrt(5.0), 1.0 / np.sqrt(5.0), 1.0])
    barycentric = [
        1.0 / np.prod([points[s] - points[o] for o in range(4) if o != s]) for s in range(4)
    ]
    table = np.zeros((4, 4))
    for t in range(4):
        for s in range(4):
            if t != s:
                table[t, s] = barycentric[s] / barycentric[t] / (points[t] - points[s])
    for t in (0, 3):
        table[t, t] = -np.sum(table[t])
    return [[float(np.float32(value)) for value in line] for line in table]


GLL = gll_matrix()


def vmem(count):
    return [pl.BlockSpec(memory_space=pltpu.VMEM)] * count


def hbm(count):
    return [pl.BlockSpec(memory_space=pltpu.HBM)] * count


def in_hbm(*arrays):
    return [pltpu.with_memory_space_constraint(array, pltpu.HBM) for array in arrays]


def smem(count):
    return [pl.BlockSpec(memory_space=pltpu.SMEM)] * count


def shape_of(*dims, dtype=jnp.float32):
    return jax.ShapeDtypeStruct(dims, dtype)


PARAMS = pltpu.CompilerParams(vmem_limit_bytes=24 * 1024 * 1024)


def lane_take(rows, ids):
    return jnp.take_along_axis(rows, ids, axis=1, mode="promise_in_bounds")


def wide(row, lines):
    return jnp.broadcast_to(row, (lines, row.shape[1]))


def side_ids(pn):
    count = pn.shape[1]
    bits = count.bit_length() - 1
    table = pn[...]
    ids = [table[k : k + 1] & (count - 1) for k in range(4)]
    home = lax.shift_right_logical(table[0:1], bits)
    near = [lax.shift_right_logical(table[k : k + 1], bits) == home for k in range(4)]
    return ids, near


def element_step(state, east_wind, north_wind, scale, facing):
    jumps = [None] * 16
    sides = (
        (0, 1, 2, 3),
        (3, 7, 11, 15),
        (12, 13, 14, 15),
        (0, 4, 8, 12),
    )
    for k in range(4):
        for n, p in enumerate(sides[k]):
            term = facing[k][n] - state[p]
            jumps[p] = term if jumps[p] is None else jumps[p] + term
    result = []
    for p in range(16):
        i, j = p % 4, p // 4
        grad_x = grad_y = None
        for m in range(4):
            if GLL[i][m] != 0.0:
                term = GLL[i][m] * state[m + 4 * j]
                grad_x = term if grad_x is None else grad_x + term
            if GLL[j][m] != 0.0:
                term = GLL[j][m] * state[i + 4 * m]
                grad_y = term if grad_y is None else grad_y + term
        change = -(east_wind(p) * grad_x + north_wind(p) * grad_y)
        if jumps[p] is not None:
            change = change + JUMP_WEIGHT * jumps[p]
        result.append(state[p] + scale * change)
    return result


def load(pairs, sems):
    copies = [
        pltpu.make_async_copy(source, target, sems.at[n])
        for n, (source, target) in enumerate(pairs)
    ]
    for copy in copies:
        copy.start()
    return copies


def as_column(row):
    count = row.shape[1]
    return jnp.transpose(jnp.broadcast_to(row, (count, count)))


def edge_tables(partner, remote):
    count = partner.shape[1]
    pack = count // 4
    lane = lax.broadcasted_iota(jnp.int32, (count, count), 1)
    line = lax.broadcasted_iota(jnp.int32, (count, count), 0)
    flag = jnp.where(remote, 1.0, 0.0)
    rank = jnp.sum(jnp.where(line < lane, as_column(flag), 0.0), axis=0, keepdims=True)
    rank = as_column(jnp.where(remote, rank, -1.0))
    slot = (lane & (pack - 1)).astype(jnp.float32)
    chosen = jnp.sum(
        jnp.where(rank == slot, line.astype(jnp.float32), 0.0), axis=0, keepdims=True
    ).astype(jnp.int32)
    key = jnp.where(remote, partner, 2 * count).astype(jnp.float32)
    before = jnp.where(as_column(key) < key, 1.0, 0.0)
    place = jnp.sum(before, axis=0, keepdims=True).astype(jnp.int32)
    return chosen, jnp.minimum(place, pack - 1)


def slot_rows(holder_row, down_row, devices, tiles):
    blocks = holder_row.shape[1]
    earlier = lax.broadcasted_iota(jnp.int32, (blocks, blocks), 0) < lax.broadcasted_iota(
        jnp.int32, (blocks, blocks), 1
    )
    number = holder_row.astype(jnp.float32)
    same = as_column(number) == number
    rank = jnp.sum(jnp.where(same & earlier, 1, 0), axis=0, keepdims=True)
    rank = jnp.minimum(rank, CAP - 1)
    target = lax.broadcasted_iota(jnp.int32, (devices, blocks), 0)
    after = jnp.where(holder_row + 1 == devices, 0, holder_row + 1)
    before = jnp.where(holder_row == 0, devices - 1, holder_row - 1)
    last = down_row - (tiles - HALO)
    lane = lax.broadcasted_iota(jnp.int32, (devices, LANES), 1)
    result = jnp.full((devices, LANES), -1.0, jnp.float32)
    for n, (owner, number) in enumerate(
        (
            (holder_row, down_row),
            (after, jnp.where(last >= 0, tiles + last, -1)),
            (before, jnp.where(down_row < HALO, tiles + HALO + down_row, -1)),
        )
    ):
        for slot in range(CAP):
            named = (target == owner) & (rank == slot)
            value = jnp.sum(
                jnp.where(named, (number + 1).astype(jnp.float32), 0.0), axis=1, keepdims=True
            )
            result = jnp.where(lane == CAP * n + slot, value - 1.0, result)
    return result


def home_facing(state, ids, near):
    return [
        [lane_take(state[12 + n], ids[0]) for n in range(4)],
        [jnp.where(near[1], lane_take(state[4 * n], ids[1]), 0.0) for n in range(4)],
        [lane_take(state[n], ids[2]) for n in range(4)],
        [jnp.where(near[3], lane_take(state[3 + 4 * n], ids[3]), 0.0) for n in range(4)],
    ]


def plan_kernel(
    air_hbm, eastern_hbm, northern_hbm, breadth_hbm, pn_hbm, holder_hbm, across_hbm, down_hbm,
    flux, slots, breadth, pn, holder, across, air, eastern, northern, down, sems,
    *, devices, tiles
):
    copies = load(
        (
            (air_hbm.at[:, pl.ds(0, 8), :], air),
            (eastern_hbm.at[:, pl.ds(0, 16), :], eastern),
            (northern_hbm.at[:, pl.ds(0, 16), :], northern),
            (breadth_hbm, breadth),
            (pn_hbm, pn),
            (holder_hbm, holder),
            (across_hbm, across),
            (down_hbm, down),
        ),
        sems,
    )
    for copy in copies:
        copy.wait()
    lines, count = air.shape[1], air.shape[2]
    ids, near = side_ids(pn)
    ids = [wide(line, lines) for line in ids]
    state = [air[p] for p in range(16)]
    u = [eastern[p].astype(jnp.float32)[0:lines] for p in range(16)]
    v = [northern[p].astype(jnp.float32)[0:lines] for p in range(16)]
    result = element_step(
        state, lambda p: u[p], lambda p: v[p], STEP_SIZE * breadth[...],
        home_facing(state, ids, near)
    )
    for p in range(16):
        speed = jnp.sqrt(u[p] * u[p] + v[p] * v[p] + 1.0)
        flux[p, 0:1] = result[p][0:1]
        flux[p, 1:2] = (speed * u[p])[0:1]
        flux[p, 2:3] = (speed * v[p])[0:1]
        flux[p, 3:4] = speed[0:1]
        flux[p, 4:8] = jnp.zeros((4, count), jnp.float32)
    slots[...] = slot_rows(holder[...], down[...], devices, tiles)


def local_step_kernel(
    air_hbm, eastern_hbm, northern_hbm, breadth, pn, loc, eastern, northern, east, west,
    east_pack, west_pack, places, air, sems
):
    copies = load(((air_hbm, air), (eastern_hbm, eastern), (northern_hbm, northern)), sems)
    count = breadth.shape[1]
    lines = 16
    ids, near = side_ids(pn)
    chosen_east, place_east = edge_tables(ids[1], jnp.logical_not(near[1]))
    chosen_west, place_west = edge_tables(ids[3], jnp.logical_not(near[3]))
    places[...] = jnp.zeros_like(places)
    places[0:1] = place_east
    places[1:2] = place_west
    chosen_east, chosen_west = wide(chosen_east, lines), wide(chosen_west, lines)
    group = lax.broadcasted_iota(jnp.int32, (lines, count), 1) // (count // 4)
    scale = STEP_SIZE * breadth[...]
    ids = [wide(line, lines) for line in ids]

    def packed(values, chosen):
        result = jnp.zeros((lines, count), jnp.float32)
        for n in range(4):
            result = jnp.where(group == n, lane_take(values[n], chosen), result)
        return result

    for copy in copies:
        copy.wait()
    levels = air.shape[1]

    def chunk(c, carry):
        at = pl.multiple_of(c * lines, lines)
        rows = pl.ds(at, lines)
        state = [air[p, rows] for p in range(16)]
        result = element_step(
            state,
            lambda p: eastern[p, rows].astype(jnp.float32),
            lambda p: northern[p, rows].astype(jnp.float32),
            scale,
            home_facing(state, ids, near),
        )
        for p in range(16):
            loc[p, rows] = result[p]
        beyond = pl.ds(pl.multiple_of(levels + at, lines), lines)
        for own, pack, chosen, first in (
            (east, east_pack, chosen_east, 3),
            (west, west_pack, chosen_west, 0),
        ):
            for n in range(4):
                own[n, rows] = state[first + 4 * n].astype(jnp.bfloat16)
            pack[rows] = packed([state[first + 4 * n] for n in range(4)], chosen)
            pack[beyond] = packed([result[first + 4 * n] for n in range(4)], chosen)
        return carry

    lax.fori_loop(0, levels // lines, chunk, 0)


def second_step_kernel(
    loc, eastern, northern, breadth, pn, east, west, far, near_swap, places, first_far,
    first_near, odd, surface, out_hbm, out, sems
):
    ids, near = side_ids(pn)
    levels, count = loc.shape[1], loc.shape[2]
    lines = 16
    pack = count // 4
    scale = STEP_SIZE * breadth[...]
    jump = JUMP_WEIGHT * scale
    ids = [wide(line, lines) for line in ids]
    got = Received(far, near_swap, odd)
    first = Received(first_far, first_near, odd)
    row = slice(ROW_BREADTH, ROW_BREADTH + 1)
    factors = [
        JUMP_WEIGHT * STEP_SIZE * lane_take(wide(line, lines), ids[side])
        for side, line in ((1, first.next(row)), (3, first.prev(row)))
    ]
    spots = [
        [wide(places[n : n + 1] + m * pack, lines) for m in range(4)] for n in (0, 1)
    ]

    def copy_out(c):
        rows = pl.ds(pl.multiple_of(c * lines, lines), lines)
        return pltpu.make_async_copy(out.at[:, rows, :], out_hbm.at[:, rows, :], sems.at[c])

    def chunk(c, carry):
        at = pl.multiple_of(c * lines, lines)
        rows = pl.ds(at, lines)
        now = pl.ds(pl.multiple_of(4 * HALO + at, 8), lines)
        later = pl.ds(pl.multiple_of(4 * HALO + levels + at, 8), lines)
        state = [loc[p, rows] for p in range(16)]

        def across(own, there_now, there_next, side, factor, spot):
            values, beyond = [], []
            for n in range(4):
                values.append(jnp.where(near[side], 0.0, lane_take(there_now, spot[n])))
                beyond.append(
                    lane_take(there_next, spot[n]) + factor * own[n, rows].astype(jnp.float32)
                )
            return values, beyond

        east_now, east_beyond = across(
            east, got.next(now), got.next(later), 1, factors[0], spots[0]
        )
        west_now, west_beyond = across(
            west, got.prev(now), got.prev(later), 3, factors[1], spots[1]
        )
        for n in range(4):
            state[3 + 4 * n] = state[3 + 4 * n] + jump * east_now[n]
            state[4 * n] = state[4 * n] + jump * west_now[n]
        facing = home_facing(state, ids, near)
        facing[1] = [jnp.where(near[1], facing[1][n], east_beyond[n]) for n in range(4)]
        facing[3] = [jnp.where(near[3], facing[3][n], west_beyond[n]) for n in range(4)]
        result = element_step(
            state,
            lambda p: eastern[p, rows].astype(jnp.float32),
            lambda p: northern[p, rows].astype(jnp.float32),
            scale,
            facing,
        )
        for p in range(16):
            out[p, rows] = result[p]

        @pl.when(c == 0)
        def _():
            for p in range(16):
                lowest = out[p, 0:1]
                out[p, 0:1] = lowest + NUDGING_SPEED * (surface[p : p + 1] - lowest)

        copy_out(c).start()
        return carry

    lax.fori_loop(0, levels // lines, chunk, 0)

    def finish(c, carry):
        copy_out(c).wait()
        return carry

    lax.fori_loop(0, levels // lines, finish, 0)


def forward_kernel(
    holder, across, flux, slots, breadth, pn, first_far, first_near, odd, weights,
    out, taken, source, own, *, devices
):
    ids, near = side_ids(pn)
    jump = (JUMP_WEIGHT * STEP_SIZE) * breadth[...]
    first = Received(first_far, first_near, odd)
    from_east = lane_take(first.next(slice(0, 8)), wide(ids[1], 8))
    from_west = lane_take(first.prev(slice(0, 8)), wide(ids[3], 8))
    from_east = jnp.where(near[1], 0.0, jump * from_east)
    from_west = jnp.where(near[3], 0.0, jump * from_west)
    for p in range(16):
        value = flux[p, 0:1]
        if p % 4 == 3:
            value = value + from_east[p // 4 : p // 4 + 1]
        if p % 4 == 0:
            value = value + from_west[p // 4 : p // 4 + 1]
        source[p] = flux[p]
        source[p, 0:1] = flux[p, 3:4] * value
    own[...] = jnp.zeros_like(own)
    for owner in range(devices):
        taken[owner] = 0
    for b in range(weights.shape[0]):
        owner = holder[0, b]
        rank = jnp.minimum(taken[owner], CAP - 1)
        taken[owner] = taken[owner] + 1
        sums = jnp.dot(
            source[across[0, b]].astype(jnp.bfloat16), weights[b], preferred_element_type=jnp.float32
        )
        own[owner, pl.ds(2 * rank, 1), :] = sums[1:2]
        own[owner, pl.ds(2 * rank + 1, 1), :] = sums[2:3]
        own[owner, pl.ds(4 + rank, 1), :] = sums[0:1]
    line = lax.broadcasted_iota(jnp.int32, (8, LANES), 0)
    for d in range(devices):
        mine = own[d]
        prev = own[(d - 1) % devices]
        following = own[(d + 1) % devices]
        top = jnp.concatenate([mine[0:4], prev[0:4]], axis=0)
        bottom = jnp.where(line < 4, following, mine)
        bottom = jnp.where(line == ROW_IDS - 8, wide(slots[d : d + 1], 8), bottom)
        out[d] = jnp.concatenate([top, bottom], axis=0).astype(jnp.bfloat16)


def back_kernel(holder, across, arrived, weights, surface, taken, places, share, *, devices):
    for owner in range(devices):
        taken[owner] = 0
    blocks = weights.shape[0]
    points = surface.shape[0]
    for column in range(points):
        taken[devices + column] = 0
    for b in range(blocks):
        owner = holder[0, b]
        rank = jnp.minimum(taken[owner], CAP - 1)
        taken[owner] = taken[owner] + 1
        column = across[0, b]
        seen = jnp.minimum(taken[devices + column], 1)
        taken[devices + column] = taken[devices + column] + 1
        places[2 * column + seen] = b
        line = arrived[owner, pl.ds(rank, 1), :]
        share[b] = lax.dot_general(
            wide(line, 8).astype(jnp.bfloat16),
            weights[b],
            (((1,), (1,)), ((), ())),
            preferred_element_type=jnp.float32,
        )
    for p in range(points):
        surface[p : p + 1] = share[places[2 * p], 0:1] + share[places[2 * p + 1], 0:1]


def split_index(idx):
    return lax.shift_right_arithmetic(idx, 7), idx & (LANES - 1)


def pick(idx, sources):
    high, low = split_index(idx)
    result = jnp.zeros(idx.shape, jnp.float32)
    for number, line in sources:
        result = jnp.where(high == number, lane_take(wide(line, idx.shape[0]), low), result)
    return result


def own_sources(ref):
    return [(HALO + r, ref[r : r + 1]) for r in range(ref.shape[0])]


def combine(terms, factors):
    total = None
    for term, factor in zip(terms, factors):
        if factor != 0.0:
            total = factor * term if total is None else total + factor * term
    return total


def pair_sums(table):
    terms = [table[HALO * k : HALO * (k + 1)] for k in range(6)]
    return combine(terms, COS), combine(terms, SIN)


def rim_partial(rim_idx, rim_w, eta, first):
    rows = rim_idx.shape[0]
    found = pick(rim_idx, own_sources(eta))
    centre = eta[first : first + HALO]
    centre = jnp.concatenate([centre] * (rows // HALO), axis=0)
    return pair_sums(rim_w * (found - centre))


def prepare_kernel(
    air_hbm, breadth_hbm, pn_hbm, eta_hbm, sst_hbm, flow_hbm, nb_hbm, span_hbm,
    idx, w, rim_idx, rim_w, u, v, eta, sst, far, near, odd, up, dn, air, breadth, pn, flow, nb,
    span, sems
):
    copies = load(
        (
            (nb_hbm, nb),
            (span_hbm, span),
            (flow_hbm, flow),
            (eta_hbm, eta),
            (sst_hbm, sst),
            (breadth_hbm, breadth),
            (pn_hbm, pn),
            (air_hbm.at[:, pl.ds(0, 8), :], air),
        ),
        sems,
    )
    for copy in copies:
        copy.wait()
    shard = lax.shift_right_logical(pn[0:1], pn.shape[1].bit_length() - 1)
    odd[...] = wide(shard & 1, 8)
    tiles = eta.shape[0]
    for r in range(tiles):
        cut = slice(r * LANES, (r + 1) * LANES)
        links = nb[:, cut]
        factors = jnp.where(links >= 0, span[:, cut] * (1.0 / 3.0), 0.0)
        for k in range(6):
            idx[k * tiles + r : k * tiles + r + 1] = links[k : k + 1]
            w[k * tiles + r : k * tiles + r + 1] = factors[k : k + 1]
        u[r : r + 1] = flow[0:1, cut]
        v[r : r + 1] = flow[1:2, cut]
    for side, first in ((0, 0), (1, tiles - HALO)):
        rim_idx[side, 12:16] = jnp.full((4, LANES), -1, jnp.int32)
        rim_w[side, 12:16] = jnp.zeros((4, LANES), jnp.float32)
        for k in range(6):
            cut = slice(k * tiles + first, k * tiles + first + HALO)
            rim_idx[side, HALO * k : HALO * (k + 1)] = idx[cut]
            rim_w[side, HALO * k : HALO * (k + 1)] = w[cut]
    for side, first, target in ((0, 0, dn), (1, tiles - HALO, up)):
        target[...] = jnp.zeros_like(target)
        for n in range(4):
            p = 4 * n if side == 0 else 3 + 4 * n
            target[ROW_EDGE + n : ROW_EDGE + n + 1] = air[p, 0:1]
        target[ROW_BREADTH : ROW_BREADTH + 1] = breadth[...]
        part_x, part_y = rim_partial(rim_idx[side], rim_w[side], eta, first)
        cut = slice(first, first + HALO)
        target[ROW_ETA : ROW_ETA + HALO] = eta[cut]
        target[ROW_U : ROW_U + HALO] = u[cut]
        target[ROW_V : ROW_V + HALO] = v[cut]
        target[ROW_SST : ROW_SST + HALO] = sst[cut]
        target[ROW_PX : ROW_PX + HALO] = part_x
        target[ROW_PY : ROW_PY + HALO] = part_y
        target[ROW_IDX : ROW_IDX + 16] = rim_idx[side].astype(jnp.float32)
        target[ROW_W : ROW_W + 16] = rim_w[side]
    arrange(up, dn, odd, far, near)


def own_gradient(idx, w, eta, gx, gy):
    tiles = eta.shape[0]

    def chunk(c, carry):
        at = pl.multiple_of(c * 8, 8)
        centre = eta[pl.ds(at, 8)]
        terms = []
        for k in range(6):
            found = pick(idx[pl.ds(k * tiles + at, 8)], own_sources(eta))
            terms.append(w[pl.ds(k * tiles + at, 8)] * (found - centre))
        gx[pl.ds(at, 8)] = combine(terms, COS)
        gy[pl.ds(at, 8)] = combine(terms, SIN)
        return carry

    lax.fori_loop(0, tiles // 8, chunk, 0)


def inner_kernel(idx, w, eta, u, v, fu, fv, eta_part, u_part, v_part, flow):
    own_gradient(idx, w, eta, u_part, v_part)
    tiles = eta.shape[0]
    u_part[...] = DAMPING * u[...] - GRAVITY * u_part[...] + WIND_GAIN * fu[...]
    v_part[...] = DAMPING * v[...] - GRAVITY * v_part[...] + WIND_GAIN * fv[...]
    fill_flow(flow, u_part[...], v_part[...])

    def chunk(c, carry):
        at = pl.multiple_of(c * 8, 8)
        total = jnp.zeros((8, LANES), jnp.float32)
        for kk in range(3):
            sources = [(HALO + r, flow[kk, r : r + 1]) for r in range(tiles)]
            centre = flow[kk, pl.ds(at, 8)]
            one = pick(idx[pl.ds(kk * tiles + at, 8)], sources) - centre
            two = pick(idx[pl.ds((kk + 3) * tiles + at, 8)], sources) - centre
            total = (
                total
                + w[pl.ds(kk * tiles + at, 8)] * one
                - w[pl.ds((kk + 3) * tiles + at, 8)] * two
            )
        eta_part[pl.ds(at, 8)] = eta[pl.ds(at, 8)] - DEPTH_RATE * total
        return carry

    lax.fori_loop(0, tiles // 8, chunk, 0)


def first_gradient_kernel(idx, w, eta, sst, gx, gy, spread):
    own_gradient(idx, w, eta, gx, gy)
    tiles = eta.shape[0]

    def chunk(c, carry):
        at = pl.multiple_of(c * 8, 8)
        centre = sst[pl.ds(at, 8)]
        total = jnp.zeros_like(centre)
        for k in range(6):
            found = pick(idx[pl.ds(k * tiles + at, 8)], own_sources(sst))
            total = total + w[pl.ds(k * tiles + at, 8)] * (found - centre)
        spread[pl.ds(at, 8)] = total
        return carry

    lax.fori_loop(0, tiles // 8, chunk, 0)


def fill_flow(flow, u, v):
    flow[0] = u
    for kk in (1, 2):
        flow[kk] = COS[kk] * u + SIN[kk] * v


def side_currents(eta, sides, fside, before, after, side_idx, side_w):
    tiles = eta.shape[0]
    slopes = []
    for side, offset, first, part in (
        (0, tiles + HALO, 0, before),
        (1, 0, tiles - HALO, after),
    ):
        sources = [(offset + q, eta[first + q : first + q + 1]) for q in range(HALO)]
        add_x, add_y = pair_sums(side_w[side] * pick(side_idx[side], sources))
        slopes.append((part[1] + add_x, part[2] + add_y))
    slope = jnp.concatenate([slopes[0][0], slopes[1][0], slopes[0][1], slopes[1][1]], axis=0)
    return DAMPING * sides[...] - GRAVITY * slope + WIND_GAIN * fside[...]


def rim_slopes(rim_idx, rim_w, before, after, tiles):
    result = []
    for side, offset, part in ((0, 0, before), (1, tiles + HALO, after)):
        sources = [(offset + q, part[0][q : q + 1]) for q in range(HALO)]
        result.append(pair_sums(rim_w[side] * pick(rim_idx[side], sources)))
    return result


def send_rims(eta, rim_idx, rim_w, odd, far, near, up, dn):
    tiles = eta.shape[0]
    for side, first, target in ((0, 0, dn), (1, tiles - HALO, up)):
        part_x, part_y = rim_partial(rim_idx[side], rim_w[side], eta, first)
        target[0:HALO] = eta[first : first + HALO]
        target[HALO : 2 * HALO] = part_x
        target[2 * HALO : 3 * HALO] = part_y
        target[3 * HALO : 4 * HALO] = jnp.zeros((HALO, LANES), jnp.float32)
    rows = pl.ds(0, 4 * HALO)
    arrange(up, dn, odd, far.at[rows], near.at[rows])


def first_subcycle(
    gx, gy, eta, u, v, sides, fu, fv, fside, before, after, idx, w, side_idx, side_w,
    rim_idx, rim_w, flow, flow_outer, eta_new, u_new, v_new, sides_new
):
    tiles = eta.shape[0]
    u_new[...] = DAMPING * u[...] - GRAVITY * gx[...] + WIND_GAIN * fu[...]
    v_new[...] = DAMPING * v[...] - GRAVITY * gy[...] + WIND_GAIN * fv[...]
    slopes = rim_slopes(rim_idx, rim_w, before, after, tiles)
    for first, (add_x, add_y) in zip((0, tiles - HALO), slopes):
        rows = slice(first, first + HALO)
        u_new[rows] = u_new[rows] - GRAVITY * add_x
        v_new[rows] = v_new[rows] - GRAVITY * add_y
    sides_next = side_currents(eta, sides, fside, before, after, side_idx, side_w)
    sides_new[...] = sides_next
    fill_flow(flow, u_new[...], v_new[...])
    fill_flow(flow_outer, sides_next[0 : 2 * HALO], sides_next[2 * HALO : 4 * HALO])

    def chunk(c, carry):
        at = pl.multiple_of(c * 8, 8)
        total = jnp.zeros((8, LANES), jnp.float32)
        for kk in range(3):
            sources = [(HALO + r, flow[kk, r : r + 1]) for r in range(tiles)]
            sources += [(q, flow_outer[kk, q : q + 1]) for q in range(HALO)]
            sources += [
                (tiles + HALO + q, flow_outer[kk, HALO + q : HALO + q + 1]) for q in range(HALO)
            ]
            centre = flow[kk, pl.ds(at, 8)]
            one = pick(idx[pl.ds(kk * tiles + at, 8)], sources) - centre
            two = pick(idx[pl.ds((kk + 3) * tiles + at, 8)], sources) - centre
            total = (
                total
                + w[pl.ds(kk * tiles + at, 8)] * one
                - w[pl.ds((kk + 3) * tiles + at, 8)] * two
            )
        eta_new[pl.ds(at, 8)] = eta[pl.ds(at, 8)] - DEPTH_RATE * total
        return carry

    lax.fori_loop(0, tiles // 8, chunk, 0)


def outer_subcycle(
    eta, eta_part, u_part, v_part, sides, fside, before, after, idx, w, side_idx, side_w,
    rim_idx, rim_w, flow_outer, eta_new, u_new, v_new
):
    tiles = eta.shape[0]
    slopes = rim_slopes(rim_idx, rim_w, before, after, tiles)
    sides_next = side_currents(eta, sides, fside, before, after, side_idx, side_w)
    u_new[...] = u_part[...]
    v_new[...] = v_part[...]
    changes_u = [-GRAVITY * slopes[side][0] for side in (0, 1)]
    changes_v = [-GRAVITY * slopes[side][1] for side in (0, 1)]
    for side, first in ((0, 0), (1, tiles - HALO)):
        rows = slice(first, first + HALO)
        u_new[rows] = u_new[rows] + changes_u[side]
        v_new[rows] = v_new[rows] + changes_v[side]
    fill_flow(
        flow_outer,
        jnp.concatenate([sides_next[0 : 2 * HALO]] + changes_u, axis=0),
        jnp.concatenate([sides_next[2 * HALO : 4 * HALO]] + changes_v, axis=0),
    )
    for c in range(tiles // 8):
        at = c * 8
        total = jnp.zeros((8, LANES), jnp.float32)
        for kk in range(3):
            line = lambda n: flow_outer[kk, n : n + 1]
            sources = [(HALO + q, line(2 * HALO + q)) for q in range(HALO)]
            sources += [(tiles + q, line(3 * HALO + q)) for q in range(HALO)]
            if at == 0:
                sources += [(q, line(q)) for q in range(HALO)]
            if at + 8 == tiles:
                sources += [(tiles + HALO + q, line(HALO + q)) for q in range(HALO)]
            total = (
                total
                + w[kk * tiles + at : kk * tiles + at + 8]
                * pick(idx[kk * tiles + at : kk * tiles + at + 8], sources)
                - w[(kk + 3) * tiles + at : (kk + 3) * tiles + at + 8]
                * pick(idx[(kk + 3) * tiles + at : (kk + 3) * tiles + at + 8], sources)
            )
        eta_new[at : at + 8] = eta_part[at : at + 8] - DEPTH_RATE * total
    for side, first in ((0, 0), (1, tiles - HALO)):
        centre = jnp.zeros((HALO, LANES), jnp.float32)
        for kk in range(3):
            factor = (
                rim_w[side, HALO * kk : HALO * (kk + 1)]
                - rim_w[side, HALO * (kk + 3) : HALO * (kk + 4)]
            )
            start = (2 + side) * HALO
            centre = centre + factor * flow_outer[kk, start : start + HALO]
        rows = slice(first, first + HALO)
        eta_new[rows] = eta_new[rows] + DEPTH_RATE * centre
    return sides_next


def first_ocean_kernel(
    arrived, first_far, first_near, odd, gx, gy, eta, u, v, idx, w, rim_idx, rim_w,
    east_pack, west_pack, eta_new, u_new, v_new, sides_new, far, near, fu, fv, fside, side_idx,
    side_w, heat, ids, flow, flow_outer, sides, up, dn
):
    tiles = eta.shape[0]
    devices = arrived.shape[0]
    parts = arrived[...].astype(jnp.float32)
    ids[...] = parts[:, ROW_IDS, :]
    number = lax.broadcasted_iota(jnp.int32, (devices, LANES), 1).astype(jnp.float32)
    nothing = jnp.zeros((devices, LANES), jnp.float32)
    chosen, lines = [], []
    for j in range(3 * CAP):
        chosen.append(jnp.where(ids[:, j : j + 1] == number, 1.0, 0.0))
        first = parts[:, ROW_HEAT + j, :] if j < CAP else nothing
        lines.append(
            jnp.concatenate([first, parts[:, 2 * j, :], parts[:, 2 * j + 1, :]], axis=1)
        )
    forcing = lax.dot_general(
        jnp.concatenate(chosen, axis=0).astype(jnp.bfloat16),
        jnp.concatenate(lines, axis=0).astype(jnp.bfloat16),
        (((0,), (0,)), ((), ())),
        preferred_element_type=jnp.float32,
    )
    heat[...] = forcing[0:tiles, 0:LANES]
    fu[...] = forcing[0:tiles, LANES : 2 * LANES]
    fv[...] = forcing[0:tiles, 2 * LANES : 3 * LANES]
    fside[0 : 2 * HALO] = forcing[tiles : tiles + 2 * HALO, LANES : 2 * LANES]
    fside[2 * HALO : 4 * HALO] = forcing[tiles : tiles + 2 * HALO, 2 * LANES : 3 * LANES]
    first = Received(first_far, first_near, odd)
    for side, part in ((0, first.prev), (1, first.next)):
        side_idx[side] = part(slice(ROW_IDX, ROW_IDX + 16)).astype(jnp.int32)
        side_w[side] = part(slice(ROW_W, ROW_W + 16))
        for n, row in ((0, ROW_U), (1, ROW_V)):
            at = HALO * (2 * n + side)
            sides[at : at + HALO] = first.rim(side, row)
    rows = (ROW_ETA, ROW_PX, ROW_PY)
    first_subcycle(
        gx, gy, eta, u, v, sides, fu, fv, fside, first.rims(0, rows), first.rims(1, rows), idx, w, side_idx, side_w, rim_idx, rim_w, flow, flow_outer,
        eta_new, u_new, v_new, sides_new
    )
    send_rims(eta_new, rim_idx, rim_w, odd, far, near, up, dn)
    flag = jnp.broadcast_to(odd[0:1], east_pack.shape) > 0
    far[4 * HALO :] = jnp.where(flag, east_pack[...], west_pack[...])
    near[4 * HALO :] = jnp.where(flag, west_pack[...], east_pack[...])


def sea_kernel(
    first_far, first_near, odd, sst, heat, spread, ids, rim_idx, rim_w, warm, answers
):
    first = Received(first_far, first_near, odd)
    tiles = sst.shape[0]
    devices = ids.shape[0]
    warm[...] = (
        sst[...] + WARMING_COEFF * heat[...] + (0.5 * SPREADING_COEFF) * spread[...]
    )
    for side, start, offset in ((0, 0, 0), (1, tiles - HALO, tiles + HALO)):
        rim = first.rim(side, ROW_SST)
        sources = [(offset + q, rim[q : q + 1]) for q in range(HALO)]
        found = rim_w[side] * pick(rim_idx[side], sources)
        total = combine([found[HALO * k : HALO * (k + 1)] for k in range(6)], [1.0] * 6)
        rows = slice(start, start + HALO)
        warm[rows] = warm[rows] + (0.5 * SPREADING_COEFF) * total
    half = warm[...].astype(jnp.bfloat16)
    number = lax.broadcasted_iota(jnp.int32, (devices, tiles), 1).astype(jnp.float32)
    for j in range(CAP):
        chosen = jnp.where(ids[:, j : j + 1] == number, 1.0, 0.0).astype(jnp.bfloat16)
        answers[:, j, :] = jnp.dot(chosen, half, preferred_element_type=jnp.float32)


def ocean_kernel(
    far, near, odd, eta, eta_part, u_part, v_part, sides, fside, idx, w, side_idx, side_w,
    rim_idx, rim_w, eta_new, u_new, v_new, sides_new, far_new, near_new, flow_outer, up, dn
):
    rows = (0, HALO, 2 * HALO)
    got = Received(far, near, odd)
    sides_new[...] = outer_subcycle(
        eta, eta_part, u_part, v_part, sides, fside, got.rims(0, rows), got.rims(1, rows), idx, w, side_idx, side_w, rim_idx, rim_w, flow_outer,
        eta_new, u_new, v_new
    )
    send_rims(eta_new, rim_idx, rim_w, odd, far_new, near_new, up, dn)


def last_ocean_kernel(
    far, near, odd, eta, eta_part, u_part, v_part, sides, fside, idx, w, side_idx, side_w,
    rim_idx, rim_w, eta_new, velocity, u_new, v_new, flow_outer
):
    rows = (0, HALO, 2 * HALO)
    got = Received(far, near, odd)
    outer_subcycle(
        eta, eta_part, u_part, v_part, sides, fside, got.rims(0, rows), got.rims(1, rows), idx, w, side_idx, side_w, rim_idx, rim_w, flow_outer,
        eta_new, u_new, v_new
    )
    for r in range(eta.shape[0]):
        cut = slice(r * LANES, (r + 1) * LANES)
        velocity[0:1, cut] = u_new[r : r + 1]
        velocity[1:2, cut] = v_new[r : r + 1]


def shards(
    air_warmth,
    eastern_breeze,
    northern_breeze,
    reciprocal_breadth,
    panel_neighbours,
    transfer_coefficients,
    transfer_across_tile,
    transfer_holder,
    transfer_down_tile,
    water_elevation,
    depth_mean_current,
    marine_skin_warmth,
    patch_neighbours,
    interface_span,
):
    devices = lax.axis_size(RING)
    points, levels, elements = air_warmth.shape
    cells = water_elevation.shape[0]
    tiles = cells // LANES
    blocks = transfer_holder.shape[0]
    cell_rows = shape_of(tiles, LANES)
    rim_rows = shape_of(4 * HALO, LANES)
    dma = pltpu.SemaphoreType.DMA
    air, eastern, northern, breadth_hbm, pn_hbm = in_hbm(
        air_warmth, eastern_breeze, northern_breeze, reciprocal_breadth.reshape(1, elements),
        panel_neighbours
    )

    idx, w, rim_idx, rim_w, u, v, eta, sst, far, near, odd = pl.pallas_call(
        prepare_kernel,
        in_specs=hbm(8),
        out_specs=vmem(11),
        out_shape=(
            shape_of(6 * tiles, LANES, dtype=jnp.int32),
            shape_of(6 * tiles, LANES),
            shape_of(2, 16, LANES, dtype=jnp.int32),
            shape_of(2, 16, LANES),
            cell_rows,
            cell_rows,
            cell_rows,
            cell_rows,
            shape_of(ROWS_FIRST, LANES),
            shape_of(ROWS_FIRST, LANES),
            shape_of(8, elements, dtype=jnp.int32),
        ),
        scratch_shapes=[
            pltpu.VMEM((ROWS_FIRST, LANES), jnp.float32),
            pltpu.VMEM((ROWS_FIRST, LANES), jnp.float32),
            pltpu.VMEM((points, 8, elements), jnp.float32),
            pltpu.VMEM((1, elements), jnp.float32),
            pltpu.VMEM((4, elements), jnp.int32),
            pltpu.VMEM((2, cells), jnp.float32),
            pltpu.VMEM((6, cells), jnp.int32),
            pltpu.VMEM((6, cells), jnp.float32),
            dma((8,)),
        ],
        compiler_params=PARAMS,
        name="prepare",
    )(
        air,
        breadth_hbm,
        pn_hbm,
        *in_hbm(
            water_elevation.reshape(tiles, LANES),
            marine_skin_warmth.reshape(tiles, LANES),
            depth_mean_current,
            patch_neighbours,
            interface_span,
        ),
    )
    first_far, first_near = swap_both(far, near)

    one_row = shape_of(1, blocks, dtype=jnp.int32)
    low_wind = pltpu.VMEM((points, 16, elements), jnp.bfloat16)
    flux, slots, breadth, pn, holder, across = pl.pallas_call(
        lambda *refs: plan_kernel(*refs, devices=devices, tiles=tiles),
        in_specs=hbm(8),
        out_specs=vmem(6),
        out_shape=(
            shape_of(points, 8, elements), shape_of(devices, LANES), shape_of(1, elements),
            shape_of(4, elements, dtype=jnp.int32), one_row, one_row
        ),
        scratch_shapes=[
            pltpu.VMEM((points, 8, elements), jnp.float32), low_wind, low_wind,
            pltpu.VMEM((1, blocks), jnp.int32), dma((8,))
        ],
        compiler_params=PARAMS,
        name="plan",
    )(
        air,
        eastern,
        northern,
        breadth_hbm,
        pn_hbm,
        *in_hbm(
            transfer_holder.reshape(1, blocks),
            transfer_across_tile.reshape(1, blocks),
            transfer_down_tile.reshape(1, blocks),
        ),
    )

    outgoing = pl.pallas_call(
        lambda *refs: forward_kernel(*refs, devices=devices),
        in_specs=smem(2) + vmem(8),
        out_specs=pl.BlockSpec(memory_space=pltpu.VMEM),
        out_shape=shape_of(devices, PER_DEST, LANES, dtype=jnp.bfloat16),
        scratch_shapes=[
            pltpu.SMEM((devices,), jnp.int32),
            pltpu.VMEM((points, 8, elements), jnp.float32),
            pltpu.VMEM((devices, 8, LANES), jnp.float32),
        ],
        compiler_params=PARAMS,
        name="forward_remap",
    )(
        holder, across, flux, slots, breadth, pn, first_far, first_near, odd,
        transfer_coefficients
    )
    outgoing, pn, gradient_eta = lax.optimization_barrier((outgoing, pn, eta))
    arrived = exchange(outgoing)
    gx, gy, spread = pl.pallas_call(
        first_gradient_kernel,
        in_specs=vmem(4),
        out_specs=vmem(3),
        out_shape=(cell_rows,) * 3,
        compiler_params=PARAMS,
        name="first_gradient",
    )(idx, w, gradient_eta, sst)

    field = shape_of(points, levels, elements)
    edge = shape_of(4, levels, elements, dtype=jnp.bfloat16)
    pack = shape_of(2 * levels, elements)
    wind = shape_of(points, levels, elements, dtype=jnp.bfloat16)
    loc, eastern, northern, east, west, east_pack, west_pack, places = pl.pallas_call(
        local_step_kernel,
        in_specs=hbm(3) + vmem(2),
        out_specs=vmem(8),
        out_shape=(
            field, wind, wind, edge, edge, pack, pack, shape_of(8, elements, dtype=jnp.int32)
        ),
        scratch_shapes=[pltpu.VMEM((points, levels, elements), jnp.float32), dma((3,))],
        compiler_params=PARAMS,
        name="local_step",
    )(air, eastern, northern, breadth, pn)

    rim_scratch = pltpu.VMEM((4 * HALO, LANES), jnp.float32)
    second_rows = shape_of(4 * HALO + 2 * levels, elements)
    flow_scratch = [
        pltpu.VMEM((3, tiles, LANES), jnp.float32),
        pltpu.VMEM((3, 2 * HALO, LANES), jnp.float32),
    ]
    (
        eta, u, v, sides, far, near, fu, fv, fside, side_idx, side_w, heat, ids
    ) = pl.pallas_call(
        first_ocean_kernel,
        in_specs=vmem(15),
        out_specs=vmem(13),
        out_shape=(
            cell_rows, cell_rows, cell_rows, rim_rows, second_rows, second_rows,
            cell_rows, cell_rows, rim_rows,
            shape_of(2, 16, LANES, dtype=jnp.int32), shape_of(2, 16, LANES),
            cell_rows, shape_of(devices, LANES),
        ),
        scratch_shapes=flow_scratch + [rim_scratch] * 3,
        compiler_params=PARAMS,
        name="first_ocean",
    )(
        arrived, first_far, first_near, odd, gx, gy, eta, u, v, idx, w, rim_idx, rim_w,
        east_pack, west_pack
    )
    far, near = swap_both(far, near)
    edges_far, edges_near = far, near

    for substep in range(1, NSUB):
        eta_part, u_part, v_part = pl.pallas_call(
            inner_kernel,
            in_specs=vmem(7),
            out_specs=vmem(3),
            out_shape=(cell_rows,) * 3,
            scratch_shapes=flow_scratch[:1],
            compiler_params=PARAMS,
            name="inner",
        )(idx, w, eta, u, v, fu, fv)
        if substep == 1:
            eta_part, heat = lax.optimization_barrier((eta_part, heat))
            warm, answers = pl.pallas_call(
                sea_kernel,
                in_specs=vmem(9),
                out_specs=vmem(2),
                out_shape=(cell_rows, shape_of(devices, CAP, LANES)),
                compiler_params=PARAMS,
                name="sea",
            )(first_far, first_near, odd, sst, heat, spread, ids, rim_idx, rim_w)
            answered = exchange(answers)
        operands = (
            far, near, odd, eta, eta_part, u_part, v_part, sides, fside, idx, w, side_idx, side_w, rim_idx, rim_w
        )
        outer_scratch = [pltpu.VMEM((3, 4 * HALO, LANES), jnp.float32)]
        if substep + 1 < NSUB:
            eta, u, v, sides, far, near = pl.pallas_call(
                ocean_kernel,
                in_specs=vmem(15),
                out_specs=vmem(6),
                out_shape=(cell_rows,) * 3 + (rim_rows,) * 3,
                scratch_shapes=outer_scratch + [rim_scratch] * 2,
                compiler_params=PARAMS,
                name="ocean",
            )(*operands)
            far, near = swap_both(far, near)
        else:
            eta, velocity = pl.pallas_call(
                last_ocean_kernel,
                in_specs=vmem(15),
                out_specs=vmem(2),
                out_shape=(cell_rows, shape_of(2, cells)),
                scratch_shapes=[pltpu.VMEM((tiles, LANES), jnp.float32)] * 2 + outer_scratch,
                compiler_params=PARAMS,
                name="last_ocean",
            )(*operands)

    surface = pl.pallas_call(
        lambda *refs: back_kernel(*refs, devices=devices),
        in_specs=smem(2) + vmem(2),
        out_specs=pl.BlockSpec(memory_space=pltpu.VMEM),
        out_shape=shape_of(points, LANES),
        scratch_shapes=[
            pltpu.SMEM((devices + points,), jnp.int32),
            pltpu.SMEM((2 * points,), jnp.int32),
            pltpu.VMEM((blocks, 8, LANES), jnp.float32),
        ],
        compiler_params=PARAMS,
        name="back_remap",
    )(holder, across, answered, transfer_coefficients)

    closing = pl.pallas_call(
        second_step_kernel,
        in_specs=vmem(14),
        out_specs=pl.BlockSpec(memory_space=pltpu.HBM),
        out_shape=pltpu.HBM((points, levels, elements), jnp.float32),
        scratch_shapes=[
            pltpu.VMEM((points, levels, elements), jnp.float32), dma((levels // 16,))
        ],
        compiler_params=PARAMS,
        name="second_step",
    )(
        loc, eastern, northern, breadth, pn, east, west, edges_far, edges_near, places,
        first_far, first_near, odd, surface
    )
    return closing, eta.reshape(cells), velocity, warm.reshape(cells)


def solution(mesh):
    split = P(RING)
    last = P(None, RING)
    field = P(None, None, RING)
    return jax.shard_map(
        shards,
        mesh=mesh,
        in_specs=(
            field,
            field,
            field,
            split,
            last,
            P(RING, None, None),
            split,
            P(RING, None),
            split,
            split,
            last,
            split,
            last,
            last,
        ),
        out_specs=(field, split, last, split),
        check_vma=False,
    )
```

time: 73.8 us -> 56.7 us (0.77)
  local copies, waits for them, and re-layouts: 11.5 us -> 0.01 us
  starting transfers between devices: 33.5 us -> 24.3 us
  Pallas kernels: 21.6 us -> 24.2 us
  waiting for transfers between devices: 5.67 us -> 7.21 us
    unnamed x43 -> x2, local copies, waits for them, and re-layouts: 11.5 us -> 0.01 us
    ppermute x10 -> x8, starting transfers between devices: 28.1 us -> 17.4 us  [swapped(): return lax.ppermute(value, RING, pairs)]
    ppermute x10 -> x8, waiting for transfers between devices: 0.31 us -> 3.85 us  [swapped(): return lax.ppermute(value, RING, pairs)]
    pallas_call x12 -> x14, Pallas kernels: 19.2 us -> 21.8 us  [the longest x3 7.12 us: shards(): pl.pallas_call(inner_kernel, in_specs=vmem(7), out_specs=vmem(3), out_sha...]
    all_to_all x2, waiting for transfers between devices: 5.36 us -> 3.36 us  [exchange(): return lax.all_to_all(value, RING, split_axis=0, concat_axis=0, tiled=True)]
    all_to_all x2, starting transfers between devices: 5.45 us -> 6.91 us  [exchange(): return lax.all_to_all(value, RING, split_axis=0, concat_axis=0, tiled=True)]
  transfers between devices with their start and end apart: 12 -> 10, of which waited for: 4 -> 4; matrix products, arithmetic and copies ran while one was open for 1% -> 0% of each run, Pallas kernels for 20% -> 32%
where the time goes in v2:
time: 56.7 us; the launch traced here: 56.4 us
  starting transfers between devices  24.3 us (43%)
  Pallas kernels  24.2 us (43%)
  waiting for transfers between devices  7.21 us (13%)
  between operations  0.77 us (1%)
    ppermute x8, starting transfers between devices, swapped(): return lax.ppermute(value, RING, pairs)  17.4 us
    pallas_call x3, Pallas kernels, shards(): pl.pallas_call(inner_kernel, in_specs=vmem(7), out_specs=vmem(3), out_sha...  7.12 us
    all_to_all x2, starting transfers between devices, exchange(): return lax.all_to_all(value, RING, split_axis=0, concat_axis=0, tiled=True)  6.91 us
    ppermute x8, waiting for transfers between devices, swapped(): return lax.ppermute(value, RING, pairs)  3.85 us
    all_to_all x2, waiting for transfers between devices, exchange(): return lax.all_to_all(value, RING, split_axis=0, concat_axis=0, tiled=True)  3.36 us
    pallas_call x1, Pallas kernels, shards(): pl.pallas_call(first_gradient_kernel, in_specs=vmem(4), out_specs=vmem(3)...  2.35 us
    pallas_call x1, Pallas kernels, shards(): pl.pallas_call(local_step_kernel, in_specs=hbm(3) + vmem(2), out_specs=vm...  2.02 us
    pallas_call x1, Pallas kernels, shards(): pl.pallas_call(first_ocean_kernel, in_specs=vmem(15), out_specs=vmem(13),...  1.88 us
  transfers between devices with their start and end apart: 10, of which 4 were waited for; matrix products, arithmetic and copies ran while one was open for 0% of the time, Pallas kernels for 32%

profile of v2, /device:TPU:0, one launch (start us, length us, event | category | flops | bytes accessed | tf_op | source)
XLA Modules:
  0.0 56.4 jit_solution(864209168634306810)
XLA Ops:
  0.6 0.0 copy-start
  0.6 1.6 %prepare.1 = (s32[192,128]{1,0:T(8,128)S(1)}, f32[192,128]{1,0:T(8,128)S(1)}, s32[2,16,128]{2,1,0:T(8,128)S(1)}, f32[2,16,128]{2,1,0:T(8,128)S(1)}, f32[32,128]{...) custom-call(f32[16,64,128]{2,1,0:T(8,128)} %air_hbm.3, ...), custom_call_target="tpu_custom_call" | custom-call | tf_op jit(solution)/shard_map/prepare/pallas_call | solution.py:906
  2.3 6.4 %collective-permute-start = (f32[56,128]{1,0:T(8,128)S(1)}, f32[56,128]{1,0:T(8,128)S(1)}, u32[]{:S(2)}, u32[]{:S(2)}) collective-permute-start(f32[56,128]{1,0:T(8,128)S(1)} %get-tuple-element.81), channel_id=1, source_target_pairs={{1,2},{2,1},{3,4},{4,3},{5,6},{6,5},{7,8},{8,7},{9,10},{10,9},{11,... | collective-permute-start | bytes 86024 | tf_op jit(solution)/shard_map/ppermute | solution.py:41
  8.7 0.0 collective-permute-start.1
  8.7 1.2 %plan.1 = (f32[16,8,128]{2,1,0:T(8,128)S(1)}, f32[32,128]{1,0:T(8,128)S(1)}, f32[1,128]{1,0:T(1,128)S(1)}, s32[4,128]{1,0:T(4,128)S(1)}, s32[1,32]{1,0:T(1,128)S(1)}, /*index=5*/s32[1,32]{1,0:T(1,128)S(1)}) custom-call(f32[16,64,128]{2,1,0:T(8,128)} %air_hbm.3, bf16[16,64,128]{2,1,0:T(8,128)(2,1)} %eastern_hbm.1, bf16[16,64,128]{2,1,0:T(8,128)(2,1)} %northern_hbm.1, ...), custom_call_target="tpu_custom_call" | custom-call | tf_op jit(solution)/shard_map/plan/pallas_call | solution.py:952
  9.9 0.5 collective-permute-done.refs_6_.first_far
  10.5 2.1 %collective-permute-done.1.refs_7_.first_near = f32[56,128]{1,0:T(8,128)S(1)} collective-permute-done((f32[56,128]{1,0:T(8,128)S(1)}, f32[56,128]{1,0:T(8,128)S(1)}, u32[]{:S(2)}, u32[]{:S(2)}) %collective-permute-start.1) | collective-permute-done | bytes 28704 | tf_op jit(solution)/shard_map/ppermute | solution.py:41
  12.6 0.0 copy-done
  12.6 1.7 %forward_remap.1 = bf16[32,16,128]{2,1,0:T(8,128)(2,1)} custom-call(s32[1,32]{1,0:T(1,128)S(1)} %get-tuple-element.76.refs_0_, s32[1,32]{1,0:T(1,128)S(1)} %get-tuple-element.77.refs_1_, f32[16,8,128]{2,1,0:T(8,128)S(1)} %get-tuple-element.78.refs_2_, f32[32,128]{1,0:T(8,128)S(1)} %get-tuple-element.79.refs_3_, ...), custom_call_target="tpu_custom_call" | custom-call | tf_op jit(solution)/shard_map/forward_remap/pallas_call | solution.py:979
  14.3 3.4 %all-to-all-start = ((bf16[32,16,128]{2,1,0:T(8,128)(2,1)}), bf16[32,16,128]{2,1,0:T(8,128)(2,1)S(1)}, u32[]{:S(2)}, u32[]{:S(2)}) async-start(bf16[32,16,128]{2,1,0:T(8,128)(2,1)} %forward_remap.1), calls=%async_computation | async-start | bytes 262144 | tf_op jit(solution)/shard_map/all_to_all | solution.py:79
  17.7 2.0 %local_step.1 = (f32[16,64,128]{2,1,0:T(8,128)S(1)}, bf16[16,64,128]{2,1,0:T(8,128)(2,1)S(1)}, bf16[16,64,128]{2,1,0:T(8,128)(2,1)S(1)}, bf16[4,64,128]{2,1,0:T(...) custom-call(f32[16,64,128]{2,1,0:T(8,128)} %air_hbm.3, ...), custom_call_target="tpu_custom_call" | custom-call | tf_op jit(solution)/shard_map/local_step/pallas_call | solution.py:1010
  19.7 2.4 %first_gradient.1 = (f32[32,128]{1,0:T(8,128)S(1)}, f32[32,128]{1,0:T(8,128)S(1)}, f32[32,128]{1,0:T(8,128)S(1)}) custom-call(s32[192,128]{1,0:T(8,128)S(1)} %get-tuple-element.92.idx, f32[192,128]{1,0:T(8,128)S(1)} %get-tuple-element.93.w, f32[32,128]{1,0:T(8,128)S(1)} %get-tuple-element.94.eta, f32[32,128]{1,0:T(8,128)S(1)} %get-tuple-element.95.sst), custom_call_target="tpu_custom_call" | custom-call | tf_op jit(solution)/shard_map/first_gradient/pallas_call | solution.py:997
  22.0 3.4 %all-to-all-done.arrived = bf16[32,16,128]{2,1,0:T(8,128)(2,1)S(1)} async-done(((bf16[32,16,128]{2,1,0:T(8,128)(2,1)}), bf16[32,16,128]{2,1,0:T(8,128)(2,1)S(1)}, u32[]{:S(2)}, u32[]{:S(2)}) %all-to-all-start) | async-done | bytes 131104 | tf_op jit(solution)/shard_map/all_to_all | solution.py:79
  25.4 1.9 %first_ocean.1 = (f32[32,128]{1,0:T(8,128)S(1)}, f32[32,128]{1,0:T(8,128)S(1)}, f32[32,128]{1,0:T(8,128)S(1)}, f32[8,128]{1,0:T(8,128)S(1)}, f32[136,128]{1,0:T(...) custom-call(bf16[32,16,128]{2,1,0:T(8,128)(2,1)S(1)} %all-to-all-don, ...), custom_call_target="tpu_custom_call" | custom-call | tf_op jit(solution)/shard_map/first_ocean/pallas_call | solution.py:1030
  27.3 2.0 %collective-permute-start.2 = (f32[136,128]{1,0:T(8,128)S(1)}, f32[136,128]{1,0:T(8,128)S(1)}, u32[]{:S(2)}, u32[]{:S(2)}) collective-permute-start(f32[136,128]{1,0:T(8,128)S(1)} %get-tuple-element.104), channel_id=1, source_target_pairs={{1,2},{2,1},{3,4},{4,3},{5,6},{6,5},{7,8},{8,7},{9,10},{10,9},{11,... | collective-permute-start | bytes 208904 | tf_op jit(solution)/shard_map/ppermute | solution.py:41
  29.2 0.6 %collective-permute-start.3 = (f32[136,128]{1,0:T(8,128)S(1)}, f32[136,128]{1,0:T(8,128)S(1)}, u32[]{:S(2)}, u32[]{:S(2)}) collective-permute-start(f32[136,128]{1,0:T(8,128)S(1)} %get-tuple-element.105), channel_id=1, source_target_pairs={{0,1},{1,0},{2,3},{3,2},{4,5},{5,4},{6,7},{7,6},{8,9},{9,8},{10,11... | collective-permute-start | bytes 208904 | tf_op jit(solution)/shard_map/ppermute | solution.py:41
  29.8 2.4 %inner.3 = (f32[32,128]{1,0:T(8,128)S(1)}, f32[32,128]{1,0:T(8,128)S(1)}, f32[32,128]{1,0:T(8,128)S(1)}) custom-call(s32[192,128]{1,0:T(8,128)S(1)} %get-tuple-element.92.idx, f32[192,128]{1,0:T(8,128)S(1)} %get-tuple-element.93.w, f32[32,128]{1,0:T(8,128)S(1)} %get-tuple-element.107.eta, f32[32,128]{1,0:T(8,128)S(1)} %get-tuple-element.108.u, ...), custom_call_target="tpu_custom_call" | custom-call | tf_op jit(solution)/shard_map/inner/pallas_call | solution.py:1051
  32.2 0.9 %sea.1 = (f32[32,128]{1,0:T(8,128)}, f32[32,2,128]{2,1,0:T(2,128)}) custom-call(f32[56,128]{1,0:T(8,128)S(1)} %collective-permute-done.refs_6_.first_far, f32[56,128]{1,0:T(8,128)S(1)} %collective-permute-done.1.refs_7_.first_near, s32[8,128]{1,0:T(8,128)S(1)} %get-tuple-element.83.refs_8_.odd, f32[32,128]{1,0:T(8,128)S(1)} %get-tuple-element.95.sst, ...), custom_call_target="tpu_custom_call" | custom-call | tf_op jit(solution)/shard_map/sea/pallas_call | solution.py:1062
  33.0 3.5 %all-to-all-start.1 = ((f32[32,2,128]{2,1,0:T(2,128)}), f32[32,2,128]{2,1,0:T(2,128)S(1)}, u32[]{:S(2)}, u32[]{:S(2)}) async-start(f32[32,2,128]{2,1,0:T(2,128)} %get-tuple-element.117), calls=%async_computation.1 | async-start | bytes 65536 | tf_op jit(solution)/shard_map/all_to_all | solution.py:79
  36.6 0.0 collective-permute-done.2.far
  36.6 0.0 collective-permute-done.3.near_swap.near
  36.6 0.7 %ocean.2 = (f32[32,128]{1,0:T(8,128)S(1)}, f32[32,128]{1,0:T(8,128)S(1)}, f32[32,128]{1,0:T(8,128)S(1)}, f32[8,128]{1,0:T(8,128)S(1)}, f32[8,128]{1,0:T(8,128)S(1)}, /*index=5*/f32[8,128]{1,0:T(8,128)S(1)}) custom-call(f32[136,128]{1,0:T(8,128)S(1)} %collective-permute-done.2.far, f32[136,128]{1,0:T(8,128)S(1)} %collective-permute-done.3.near_swap.near, ...), custom_call_target="tpu_custom_call" | custom-call | tf_op jit(solution)/shard_map/ocean/pallas_call | solution.py:1076
  37.3 5.3 %collective-permute-start.4 = (f32[8,128]{1,0:T(8,128)S(1)}, f32[8,128]{1,0:T(8,128)S(1)}, u32[]{:S(2)}, u32[]{:S(2)}) collective-permute-start(f32[8,128]{1,0:T(8,128)S(1)} %get-tuple-element.125), channel_id=1, source_target_pairs={{1,2},{2,1},{3,4},{4,3},{5,6},{6,5},{7,8},{8,7},{9,10},{10,9},{11,... | collective-permute-start | bytes 12296 | tf_op jit(solution)/shard_map/ppermute | solution.py:41
  42.5 0.0 collective-permute-start.5
  42.6 2.4 %inner.4 = (f32[32,128]{1,0:T(8,128)S(1)}, f32[32,128]{1,0:T(8,128)S(1)}, f32[32,128]{1,0:T(8,128)S(1)}) custom-call(s32[192,128]{1,0:T(8,128)S(1)} %get-tuple-element.92.idx, f32[192,128]{1,0:T(8,128)S(1)} %get-tuple-element.93.w, f32[32,128]{1,0:T(8,128)S(1)} %get-tuple-element.127.eta, f32[32,128]{1,0:T(8,128)S(1)} %get-tuple-element.128.u, ...), custom_call_target="tpu_custom_call" | custom-call | tf_op jit(solution)/shard_map/inner/pallas_call | solution.py:1051
  44.9 0.0 collective-permute-done.4.far
  44.9 1.2 %collective-permute-done.5.near = f32[8,128]{1,0:T(8,128)S(1)} collective-permute-done((f32[8,128]{1,0:T(8,128)S(1)}, f32[8,128]{1,0:T(8,128)S(1)}, u32[]{:S(2)}, u32[]{:S(2)}) %collective-permute-start.5) | collective-permute-done | bytes 4128 | tf_op jit(solution)/shard_map/ppermute | solution.py:41
  46.2 0.7 %ocean.3 = (f32[32,128]{1,0:T(8,128)S(1)}, f32[32,128]{1,0:T(8,128)S(1)}, f32[32,128]{1,0:T(8,128)S(1)}, f32[8,128]{1,0:T(8,128)S(1)}, f32[8,128]{1,0:T(8,128)S(1)}, /*index=5*/f32[8,128]{1,0:T(8,128)S(1)}) custom-call(f32[8,128]{1,0:T(8,128)S(1)} %collective-permute-done.4.far, f32[8,128]{1,0:T(8,128)S(1)} %collective-permute-done.5.near, ...), custom_call_target="tpu_custom_call" | custom-call | tf_op jit(solution)/shard_map/ocean/pallas_call | solution.py:1076
  46.8 3.1 %collective-permute-start.6 = (f32[8,128]{1,0:T(8,128)S(1)}, f32[8,128]{1,0:T(8,128)S(1)}, u32[]{:S(2)}, u32[]{:S(2)}) collective-permute-start(f32[8,128]{1,0:T(8,128)S(1)} %get-tuple-element.134), channel_id=1, source_target_pairs={{1,2},{2,1},{3,4},{4,3},{5,6},{6,5},{7,8},{8,7},{9,10},{10,9},{11,... | collective-permute-start | bytes 12296 | tf_op jit(solution)/shard_map/ppermute | solution.py:41
  49.9 0.0 collective-permute-start.7
  49.9 0.0 all-to-all-done.1.refs_2_
  49.9 1.2 %back_remap.1.surface = f32[16,128]{1,0:T(8,128)S(1)} custom-call(s32[1,32]{1,0:T(1,128)S(1)} %get-tuple-element.76.refs_0_, s32[1,32]{1,0:T(1,128)S(1)} %get-tuple-element.77.refs_1_, f32[32,2,128]{2,1,0:T(2,128)S(1)} %all-to-all-done.1.refs_2_, bf16[32,128,128]{2,1,0:T(8,128)(2,1)S(1)} %copy-done), custom_call_target="tpu_custom_call" | custom-call | tf_op jit(solution)/shard_map/back_remap/pallas_call | solution.py:1097
  51.1 1.8 %second_step.1 = f32[16,64,128]{2,1,0:T(8,128)} custom-call(f32[16,64,128]{2,1,0:T(8,128)S(1)} %get-tuple-element.86.loc, bf16[16,64,128]{2,1,0:T(8,128)(2,1)S(1)} %get-tuple-element.87.eastern, bf16[16,64,128]{2,1,0:T(8,128)(2,1)S(1)} %get-tuple-element.88.northern, f32[1,128]{1,0:T(1,128)S(1)} %get-tuple-element.75.refs_4_.breadth, ...), custom_call_target="tpu_custom_call" | custom-call | tf_op jit(solution)/shard_map/second_step/pallas_call | solution.py:1111
  53.0 2.4 %inner.5 = (f32[32,128]{1,0:T(8,128)S(1)}, f32[32,128]{1,0:T(8,128)S(1)}, f32[32,128]{1,0:T(8,128)S(1)}) custom-call(s32[192,128]{1,0:T(8,128)S(1)} %get-tuple-element.92.idx, f32[192,128]{1,0:T(8,128)S(1)} %get-tuple-element.93.w, f32[32,128]{1,0:T(8,128)S(1)} %get-tuple-element.136.eta, f32[32,128]{1,0:T(8,128)S(1)} %get-tuple-element.137.u, ...), custom_call_target="tpu_custom_call" | custom-call | tf_op jit(solution)/shard_map/inner/pallas_call | solution.py:1051
  55.3 0.0 collective-permute-done.6.far
  55.4 0.0 collective-permute-done.7.near
  55.4 1.0 %last_ocean.1 = (f32[32,128]{1,0:T(8,128)}, f32[2,4096]{1,0:T(2,128)}) custom-call(f32[8,128]{1,0:T(8,128)S(1)} %collective-permute-done.6.far, f32[8,128]{1,0:T(8,128)S(1)} %collective-permute-done.7.near, s32[8,128]{1,0:T(8,128)S(1)} %get-tuple-element.83.refs_8_.odd, f32[32,128]{1,0:T(8,128)S(1)} %get-tuple-element.136.eta, ...), custom_call_target="tpu_custom_call" | custom-call | tf_op jit(solution)/shard_map/last_ocean/pallas_call | solution.py:1087
Async XLA Ops:
  0.6 11.9 %copy-start = (bf16[32,128,128]{2,1,0:T(8,128)(2,1)S(1)}, bf16[32,128,128]{2,1,0:T(8,128)(2,1)}, u32[]{:S(2)}) copy-start(bf16[32,128,128]{2,1,0:T(8,128)(2,1)} %refs_3_.1) | copy-start | bytes 3145732
  2.3 8.2 %collective-permute-start = (f32[56,128]{1,0:T(8,128)S(1)}, f32[56,128]{1,0:T(8,128)S(1)}, u32[]{:S(2)}, u32[]{:S(2)}) collective-permute-start(f32[56,128]{1,0:T(8,128)S(1)} %get-tuple-element.81), channel_id=1, source_target_pairs={{1,2},{2,1},{3,4},{4,3},{5,6},{6,5},{7,8},{8,7},{9,10},{10,9},{11,... | collective-permute-start | bytes 86024 | tf_op jit(solution)/shard_map/ppermute | solution.py:41
  8.7 3.9 %collective-permute-start.1 = (f32[56,128]{1,0:T(8,128)S(1)}, f32[56,128]{1,0:T(8,128)S(1)}, u32[]{:S(2)}, u32[]{:S(2)}) collective-permute-start(f32[56,128]{1,0:T(8,128)S(1)} %get-tuple-element.82), channel_id=1, source_target_pairs={{0,1},{1,0},{2,3},{3,2},{4,5},{5,4},{6,7},{7,6},{8,9},{9,8},{10,11... | collective-permute-start | bytes 86024 | tf_op jit(solution)/shard_map/ppermute | solution.py:41
  14.3 11.1 %all-to-all-start = ((bf16[32,16,128]{2,1,0:T(8,128)(2,1)}), bf16[32,16,128]{2,1,0:T(8,128)(2,1)S(1)}, u32[]{:S(2)}, u32[]{:S(2)}) async-start(bf16[32,16,128]{2,1,0:T(8,128)(2,1)} %forward_remap.1), calls=%async_computation | async-start | bytes 262144 | tf_op jit(solution)/shard_map/all_to_all | solution.py:79
  27.3 9.3 %collective-permute-start.2 = (f32[136,128]{1,0:T(8,128)S(1)}, f32[136,128]{1,0:T(8,128)S(1)}, u32[]{:S(2)}, u32[]{:S(2)}) collective-permute-start(f32[136,128]{1,0:T(8,128)S(1)} %get-tuple-element.104), channel_id=1, source_target_pairs={{1,2},{2,1},{3,4},{4,3},{5,6},{6,5},{7,8},{8,7},{9,10},{10,9},{11,... | collective-permute-start | bytes 208904 | tf_op jit(solution)/shard_map/ppermute | solution.py:41
  29.2 7.4 %collective-permute-start.3 = (f32[136,128]{1,0:T(8,128)S(1)}, f32[136,128]{1,0:T(8,128)S(1)}, u32[]{:S(2)}, u32[]{:S(2)}) collective-permute-start(f32[136,128]{1,0:T(8,128)S(1)} %get-tuple-element.105), channel_id=1, source_target_pairs={{0,1},{1,0},{2,3},{3,2},{4,5},{5,4},{6,7},{7,6},{8,9},{9,8},{10,11... | collective-permute-start | bytes 208904 | tf_op jit(solution)/shard_map/ppermute | solution.py:41
  33.0 16.9 %all-to-all-start.1 = ((f32[32,2,128]{2,1,0:T(2,128)}), f32[32,2,128]{2,1,0:T(2,128)S(1)}, u32[]{:S(2)}, u32[]{:S(2)}) async-start(f32[32,2,128]{2,1,0:T(2,128)} %get-tuple-element.117), calls=%async_computation.1 | async-start | bytes 65536 | tf_op jit(solution)/shard_map/all_to_all | solution.py:79
  37.3 7.7 %collective-permute-start.4 = (f32[8,128]{1,0:T(8,128)S(1)}, f32[8,128]{1,0:T(8,128)S(1)}, u32[]{:S(2)}, u32[]{:S(2)}) collective-permute-start(f32[8,128]{1,0:T(8,128)S(1)} %get-tuple-element.125), channel_id=1, source_target_pairs={{1,2},{2,1},{3,4},{4,3},{5,6},{6,5},{7,8},{8,7},{9,10},{10,9},{11,... | collective-permute-start | bytes 12296 | tf_op jit(solution)/shard_map/ppermute | solution.py:41
  42.5 3.6 %collective-permute-start.5 = (f32[8,128]{1,0:T(8,128)S(1)}, f32[8,128]{1,0:T(8,128)S(1)}, u32[]{:S(2)}, u32[]{:S(2)}) collective-permute-start(f32[8,128]{1,0:T(8,128)S(1)} %get-tuple-element.126), channel_id=1, source_target_pairs={{0,1},{1,0},{2,3},{3,2},{4,5},{5,4},{6,7},{7,6},{8,9},{9,8},{10,11... | collective-permute-start | bytes 12296 | tf_op jit(solution)/shard_map/ppermute | solution.py:41
  46.8 8.5 %collective-permute-start.6 = (f32[8,128]{1,0:T(8,128)S(1)}, f32[8,128]{1,0:T(8,128)S(1)}, u32[]{:S(2)}, u32[]{:S(2)}) collective-permute-start(f32[8,128]{1,0:T(8,128)S(1)} %get-tuple-element.134), channel_id=1, source_target_pairs={{1,2},{2,1},{3,4},{4,3},{5,6},{6,5},{7,8},{8,7},{9,10},{10,9},{11,... | collective-permute-start | bytes 12296 | tf_op jit(solution)/shard_map/ppermute | solution.py:41
  49.9 5.4 %collective-permute-start.7 = (f32[8,128]{1,0:T(8,128)S(1)}, f32[8,128]{1,0:T(8,128)S(1)}, u32[]{:S(2)}, u32[]{:S(2)}) collective-permute-start(f32[8,128]{1,0:T(8,128)S(1)} %get-tuple-element.135), channel_id=1, source_target_pairs={{0,1},{1,0},{2,3},{3,2},{4,5},{5,4},{6,7},{7,6},{8,9},{9,8},{10,11... | collective-permute-start | bytes 12296 | tf_op jit(solution)/shard_map/ppermute | solution.py:41

commit v3 on v2

--- a/solution.py
+++ b/solution.py
@@ -201,15 +201,18 @@
     return chosen, jnp.minimum(place, pack - 1)
 
 
-def slot_rows(holder_row, down_row, devices, tiles):
+def rank_among_equals(row, most):
+    count = row.shape[1]
+    earlier = lax.broadcasted_iota(jnp.int32, (count, count), 0) < lax.broadcasted_iota(
+        jnp.int32, (count, count), 1
+    )
+    number = row.astype(jnp.float32)
+    same = as_column(number) == number
+    return jnp.minimum(jnp.sum(jnp.where(same & earlier, 1, 0), axis=0, keepdims=True), most)
+
+
+def slot_rows(holder_row, rank, down_row, devices, tiles):
     blocks = holder_row.shape[1]
-    earlier = lax.broadcasted_iota(jnp.int32, (blocks, blocks), 0) < lax.broadcasted_iota(
-        jnp.int32, (blocks, blocks), 1
-    )
-    number = holder_row.astype(jnp.float32)
-    same = as_column(number) == number
-    rank = jnp.sum(jnp.where(same & earlier, 1, 0), axis=0, keepdims=True)
-    rank = jnp.minimum(rank, CAP - 1)
     target = lax.broadcasted_iota(jnp.int32, (devices, blocks), 0)
     after = jnp.where(holder_row + 1 == devices, 0, holder_row + 1)
     before = jnp.where(holder_row == 0, devices - 1, holder_row - 1)
@@ -243,8 +246,8 @@
 
 def plan_kernel(
     air_hbm, eastern_hbm, northern_hbm, breadth_hbm, pn_hbm, holder_hbm, across_hbm, down_hbm,
-    flux, slots, breadth, pn, holder, across, air, eastern, northern, down, sems,
-    *, devices, tiles
+    nb, span, flow, flux, slots, breadth, pn, across, own_rows, heat_rows, answer_rows, places,
+    idx, w, u, v, air, eastern, northern, holder, down, sems, *, devices, tiles
 ):
     copies = load(
         (
@@ -259,6 +262,7 @@
         ),
         sems,
     )
+    fill_tables(nb, span, flow, idx, w, u, v)
     for copy in copies:
         copy.wait()
     lines, count = air.shape[1], air.shape[2]
@@ -278,7 +282,12 @@
         flux[p, 2:3] = (speed * v[p])[0:1]
         flux[p, 3:4] = speed[0:1]
         flux[p, 4:8] = jnp.zeros((4, count), jnp.float32)
-    slots[...] = slot_rows(holder[...], down[...], devices, tiles)
+    rank = rank_among_equals(holder[...], CAP - 1)
+    slots[...] = slot_rows(holder[...], rank, down[...], devices, tiles)
+    own_rows[...] = holder[...] * 8 + 2 * rank
+    heat_rows[...] = holder[...] * 8 + 4 + rank
+    answer_rows[...] = holder[...] * CAP + rank
+    places[...] = across[...] * 2 + rank_among_equals(across[...], 1)
 
 
 def local_step_kernel(
@@ -419,8 +428,8 @@
 
 
 def forward_kernel(
-    holder, across, flux, slots, breadth, pn, first_far, first_near, odd, weights,
-    out, taken, source, own, *, devices
+    across, own_rows, heat_rows, flux, slots, breadth, pn, first_far, first_near, odd, weights,
+    out, source, own, *, devices
 ):
     ids, near = side_ids(pn)
     jump = (JUMP_WEIGHT * STEP_SIZE) * breadth[...]
@@ -438,53 +447,37 @@
         source[p] = flux[p]
         source[p, 0:1] = flux[p, 3:4] * value
     own[...] = jnp.zeros_like(own)
-    for owner in range(devices):
-        taken[owner] = 0
     for b in range(weights.shape[0]):
-        owner = holder[0, b]
-        rank = jnp.minimum(taken[owner], CAP - 1)
-        taken[owner] = taken[owner] + 1
         sums = jnp.dot(
             source[across[0, b]].astype(jnp.bfloat16), weights[b], preferred_element_type=jnp.float32
         )
-        own[owner, pl.ds(2 * rank, 1), :] = sums[1:2]
-        own[owner, pl.ds(2 * rank + 1, 1), :] = sums[2:3]
-        own[owner, pl.ds(4 + rank, 1), :] = sums[0:1]
+        row = own_rows[0, b]
+        own[pl.ds(row, 1), :] = sums[1:2]
+        own[pl.ds(row + 1, 1), :] = sums[2:3]
+        own[pl.ds(heat_rows[0, b], 1), :] = sums[0:1]
     line = lax.broadcasted_iota(jnp.int32, (8, LANES), 0)
     for d in range(devices):
-        mine = own[d]
-        prev = own[(d - 1) % devices]
-        following = own[(d + 1) % devices]
+        mine, prev, following = (
+            own[8 * (n % devices) : 8 * (n % devices) + 8] for n in (d, d - 1, d + 1)
+        )
         top = jnp.concatenate([mine[0:4], prev[0:4]], axis=0)
         bottom = jnp.where(line < 4, following, mine)
         bottom = jnp.where(line == ROW_IDS - 8, wide(slots[d : d + 1], 8), bottom)
         out[d] = jnp.concatenate([top, bottom], axis=0).astype(jnp.bfloat16)
 
 
-def back_kernel(holder, across, arrived, weights, surface, taken, places, share, *, devices):
-    for owner in range(devices):
-        taken[owner] = 0
-    blocks = weights.shape[0]
-    points = surface.shape[0]
-    for column in range(points):
-        taken[devices + column] = 0
-    for b in range(blocks):
-        owner = holder[0, b]
-        rank = jnp.minimum(taken[owner], CAP - 1)
-        taken[owner] = taken[owner] + 1
-        column = across[0, b]
-        seen = jnp.minimum(taken[devices + column], 1)
-        taken[devices + column] = taken[devices + column] + 1
-        places[2 * column + seen] = b
-        line = arrived[owner, pl.ds(rank, 1), :]
-        share[b] = lax.dot_general(
+def back_kernel(answer_rows, places, arrived, weights, surface, lines, share):
+    lines[...] = arrived[...].reshape(lines.shape)
+    for b in range(weights.shape[0]):
+        line = lines[pl.ds(answer_rows[0, b], 1), :]
+        share[places[0, b]] = lax.dot_general(
             wide(line, 8).astype(jnp.bfloat16),
             weights[b],
             (((1,), (1,)), ((), ())),
             preferred_element_type=jnp.float32,
         )
-    for p in range(points):
-        surface[p : p + 1] = share[places[2 * p], 0:1] + share[places[2 * p + 1], 0:1]
+    for p in range(surface.shape[0]):
+        surface[p : p + 1] = share[2 * p, 0:1] + share[2 * p + 1, 0:1]
 
 
 def split_index(idx):
@@ -499,8 +492,29 @@
     return result
 
 
-def own_sources(ref):
-    return [(HALO + r, ref[r : r + 1]) for r in range(ref.shape[0])]
+def fill_pack(values, packed, scales):
+    tiles = values.shape[0]
+    half = tiles // 2
+    largest = jnp.maximum(jnp.max(jnp.abs(values), axis=1, keepdims=True), 1e-30)
+    number = jnp.floor(values * (32767.0 / largest) + 0.5).astype(jnp.int32)
+    packed[...] = (number[half:] << 16) | (number[:half] & 0xFFFF)
+    lane = lax.broadcasted_iota(jnp.int32, (tiles, LANES), 1)
+    line = lax.broadcasted_iota(jnp.int32, (tiles, LANES), 0)
+    row = jnp.sum(jnp.where(lane == line, largest * (1.0 / 32767.0), 0.0), axis=0, keepdims=True)
+    scales[...] = wide(row, 8)
+
+
+def pick_own(idx, packed, scales):
+    lines = idx.shape[0]
+    half = packed.shape[0]
+    high, low = split_index(idx)
+    own = high - HALO
+    row = jnp.where(own >= half, own - half, own)
+    words = jnp.zeros(idx.shape, jnp.int32)
+    for r in range(half):
+        words = jnp.where(row == r, lane_take(wide(packed[r : r + 1], lines), low), words)
+    number = jnp.where(own >= half, words >> 16, (words << 16) >> 16)
+    return number.astype(jnp.float32) * lane_take(wide(scales[0:1], lines), own & (LANES - 1))
 
 
 def combine(terms, factors):
@@ -516,9 +530,9 @@
     return combine(terms, COS), combine(terms, SIN)
 
 
-def rim_partial(rim_idx, rim_w, eta, first):
+def rim_partial(rim_idx, rim_w, eta, packed, scales, first):
     rows = rim_idx.shape[0]
-    found = pick(rim_idx, own_sources(eta))
+    found = pick_own(rim_idx, packed, scales)
     centre = eta[first : first + HALO]
     centre = jnp.concatenate([centre] * (rows // HALO), axis=0)
     return pair_sums(rim_w * (found - centre))
@@ -526,8 +540,8 @@
 
 def prepare_kernel(
     air_hbm, breadth_hbm, pn_hbm, eta_hbm, sst_hbm, flow_hbm, nb_hbm, span_hbm,
-    idx, w, rim_idx, rim_w, u, v, eta, sst, far, near, odd, up, dn, air, breadth, pn, flow, nb,
-    span, sems
+    nb, span, flow, rim_idx, rim_w, eta, eta_pack, eta_scale, sst, far, near, odd,
+    up, dn, air, breadth, pn, sems
 ):
     copies = load(
         (
@@ -547,33 +561,33 @@
     shard = lax.shift_right_logical(pn[0:1], pn.shape[1].bit_length() - 1)
     odd[...] = wide(shard & 1, 8)
     tiles = eta.shape[0]
-    for r in range(tiles):
-        cut = slice(r * LANES, (r + 1) * LANES)
-        links = nb[:, cut]
-        factors = jnp.where(links >= 0, span[:, cut] * (1.0 / 3.0), 0.0)
-        for k in range(6):
-            idx[k * tiles + r : k * tiles + r + 1] = links[k : k + 1]
-            w[k * tiles + r : k * tiles + r + 1] = factors[k : k + 1]
-        u[r : r + 1] = flow[0:1, cut]
-        v[r : r + 1] = flow[1:2, cut]
+    fill_pack(eta[...], eta_pack, eta_scale)
     for side, first in ((0, 0), (1, tiles - HALO)):
         rim_idx[side, 12:16] = jnp.full((4, LANES), -1, jnp.int32)
         rim_w[side, 12:16] = jnp.zeros((4, LANES), jnp.float32)
-        for k in range(6):
-            cut = slice(k * tiles + first, k * tiles + first + HALO)
-            rim_idx[side, HALO * k : HALO * (k + 1)] = idx[cut]
-            rim_w[side, HALO * k : HALO * (k + 1)] = w[cut]
+        for j in range(HALO):
+            cut = slice((first + j) * LANES, (first + j + 1) * LANES)
+            links = nb[:, cut]
+            factors = slot_factors(links, span[:, cut])
+            for k in range(6):
+                at = HALO * k + j
+                rim_idx[side, at : at + 1] = links[k : k + 1]
+                rim_w[side, at : at + 1] = factors[k : k + 1]
     for side, first, target in ((0, 0, dn), (1, tiles - HALO, up)):
         target[...] = jnp.zeros_like(target)
         for n in range(4):
             p = 4 * n if side == 0 else 3 + 4 * n
             target[ROW_EDGE + n : ROW_EDGE + n + 1] = air[p, 0:1]
         target[ROW_BREADTH : ROW_BREADTH + 1] = breadth[...]
-        part_x, part_y = rim_partial(rim_idx[side], rim_w[side], eta, first)
+        part_x, part_y = rim_partial(
+            rim_idx[side], rim_w[side], eta, eta_pack, eta_scale, first
+        )
         cut = slice(first, first + HALO)
         target[ROW_ETA : ROW_ETA + HALO] = eta[cut]
-        target[ROW_U : ROW_U + HALO] = u[cut]
-        target[ROW_V : ROW_V + HALO] = v[cut]
+        for j in range(HALO):
+            here = slice((first + j) * LANES, (first + j + 1) * LANES)
+            target[ROW_U + j : ROW_U + j + 1] = flow[0:1, here]
+            target[ROW_V + j : ROW_V + j + 1] = flow[1:2, here]
         target[ROW_SST : ROW_SST + HALO] = sst[cut]
         target[ROW_PX : ROW_PX + HALO] = part_x
         target[ROW_PY : ROW_PY + HALO] = part_y
@@ -582,64 +596,97 @@
     arrange(up, dn, odd, far, near)
 
 
-def own_gradient(idx, w, eta, gx, gy):
+def slot_factors(links, span):
+    return jnp.where(links >= 0, span * (1.0 / 3.0), 0.0)
+
+
+def fill_tables(nb, span, flow, idx, w, u, v):
+    tiles = u.shape[0]
+    for r in range(tiles):
+        cut = slice(r * LANES, (r + 1) * LANES)
+        links = nb[:, cut]
+        factors = slot_factors(links, span[:, cut])
+        for k in range(6):
+            idx[k * tiles + r : k * tiles + r + 1] = links[k : k + 1]
+            w[k * tiles + r : k * tiles + r + 1] = factors[k : k + 1]
+        u[r : r + 1] = flow[0:1, cut]
+        v[r : r + 1] = flow[1:2, cut]
+
+
+def own_gradient(idx, w, eta, packed, scales, gx, gy):
     tiles = eta.shape[0]
 
-    def chunk(c, carry):
-        at = pl.multiple_of(c * 8, 8)
+    def chunk(at):
         centre = eta[pl.ds(at, 8)]
         terms = []
         for k in range(6):
-            found = pick(idx[pl.ds(k * tiles + at, 8)], own_sources(eta))
+            found = pick_own(idx[pl.ds(k * tiles + at, 8)], packed, scales)
             terms.append(w[pl.ds(k * tiles + at, 8)] * (found - centre))
         gx[pl.ds(at, 8)] = combine(terms, COS)
         gy[pl.ds(at, 8)] = combine(terms, SIN)
-        return carry
-
-    lax.fori_loop(0, tiles // 8, chunk, 0)
-
-
-def inner_kernel(idx, w, eta, u, v, fu, fv, eta_part, u_part, v_part, flow):
-    own_gradient(idx, w, eta, u_part, v_part)
+
+    for c in range(tiles // 8):
+        chunk(c * 8)
+
+
+def own_spread(at, idx, w, flow, packed, scales):
+    tiles = flow.shape[1]
+    total = jnp.zeros((8, LANES), jnp.float32)
+    for kk in range(3):
+        centre = flow[kk, pl.ds(at, 8)]
+        for k, sign in ((kk, 1.0), (kk + 3, -1.0)):
+            rows = pl.ds(k * tiles + at, 8)
+            found = pick_own(idx[rows], packed.at[kk], scales.at[kk])
+            total = total + sign * w[rows] * (found - centre)
+    return total
+
+
+def inner_kernel(
+    idx, w, eta, eta_pack, eta_scale, u, v, fu, fv, eta_part, u_part, v_part,
+    flow, flow_pack, flow_scale
+):
+    own_gradient(idx, w, eta, eta_pack, eta_scale, u_part, v_part)
     tiles = eta.shape[0]
     u_part[...] = DAMPING * u[...] - GRAVITY * u_part[...] + WIND_GAIN * fu[...]
     v_part[...] = DAMPING * v[...] - GRAVITY * v_part[...] + WIND_GAIN * fv[...]
     fill_flow(flow, u_part[...], v_part[...])
-
-    def chunk(c, carry):
-        at = pl.multiple_of(c * 8, 8)
-        total = jnp.zeros((8, LANES), jnp.float32)
-        for kk in range(3):
-            sources = [(HALO + r, flow[kk, r : r + 1]) for r in range(tiles)]
-            centre = flow[kk, pl.ds(at, 8)]
-            one = pick(idx[pl.ds(kk * tiles + at, 8)], sources) - centre
-            two = pick(idx[pl.ds((kk + 3) * tiles + at, 8)], sources) - centre
-            total = (
-                total
-                + w[pl.ds(kk * tiles + at, 8)] * one
-                - w[pl.ds((kk + 3) * tiles + at, 8)] * two
-            )
+    for kk in range(3):
+        fill_pack(flow[kk], flow_pack.at[kk], flow_scale.at[kk])
+
+    def chunk(at):
+        total = own_spread(at, idx, w, flow, flow_pack, flow_scale)
         eta_part[pl.ds(at, 8)] = eta[pl.ds(at, 8)] - DEPTH_RATE * total
-        return carry
-
-    lax.fori_loop(0, tiles // 8, chunk, 0)
-
-
-def first_gradient_kernel(idx, w, eta, sst, gx, gy, spread):
-    own_gradient(idx, w, eta, gx, gy)
+
+    for c in range(tiles // 8):
+        chunk(c * 8)
+
+
+def first_gradient_kernel(
+    idx, w, eta, eta_pack, eta_scale, sst, first_far, first_near, odd, rim_idx, rim_w,
+    gx, gy, base, sst_pack, sst_scale
+):
+    own_gradient(idx, w, eta, eta_pack, eta_scale, gx, gy)
     tiles = eta.shape[0]
-
-    def chunk(c, carry):
-        at = pl.multiple_of(c * 8, 8)
+    fill_pack(sst[...], sst_pack, sst_scale)
+
+    def chunk(at):
         centre = sst[pl.ds(at, 8)]
         total = jnp.zeros_like(centre)
         for k in range(6):
-            found = pick(idx[pl.ds(k * tiles + at, 8)], own_sources(sst))
+            found = pick_own(idx[pl.ds(k * tiles + at, 8)], sst_pack, sst_scale)
             total = total + w[pl.ds(k * tiles + at, 8)] * (found - centre)
-        spread[pl.ds(at, 8)] = total
-        return carry
-
-    lax.fori_loop(0, tiles // 8, chunk, 0)
+        base[pl.ds(at, 8)] = centre + (0.5 * SPREADING_COEFF) * total
+
+    for c in range(tiles // 8):
+        chunk(c * 8)
+    first = Received(first_far, first_near, odd)
+    for side, start, offset in ((0, 0, 0), (1, tiles - HALO, tiles + HALO)):
+        rim = first.rim(side, ROW_SST)
+        sources = [(offset + q, rim[q : q + 1]) for q in range(HALO)]
+        found = rim_w[side] * pick(rim_idx[side], sources)
+        total = combine([found[HALO * k : HALO * (k + 1)] for k in range(6)], [1.0] * 6)
+        rows = slice(start, start + HALO)
+        base[rows] = base[rows] + (0.5 * SPREADING_COEFF) * total
 
 
 def fill_flow(flow, u, v):
@@ -670,10 +717,13 @@
     return result
 
 
-def send_rims(eta, rim_idx, rim_w, odd, far, near, up, dn):
+def send_rims(eta, eta_pack, eta_scale, rim_idx, rim_w, odd, far, near, up, dn):
     tiles = eta.shape[0]
+    fill_pack(eta[...], eta_pack, eta_scale)
     for side, first, target in ((0, 0, dn), (1, tiles - HALO, up)):
-        part_x, part_y = rim_partial(rim_idx[side], rim_w[side], eta, first)
+        part_x, part_y = rim_partial(
+            rim_idx[side], rim_w[side], eta, eta_pack, eta_scale, first
+        )
         target[0:HALO] = eta[first : first + HALO]
         target[HALO : 2 * HALO] = part_x
         target[2 * HALO : 3 * HALO] = part_y
@@ -684,7 +734,7 @@
 
 def first_subcycle(
     gx, gy, eta, u, v, sides, fu, fv, fside, before, after, idx, w, side_idx, side_w,
-    rim_idx, rim_w, flow, flow_outer, eta_new, u_new, v_new, sides_new
+    rim_idx, rim_w, flow, flow_pack, flow_scale, flow_outer, eta_new, u_new, v_new, sides_new
 ):
     tiles = eta.shape[0]
     u_new[...] = DAMPING * u[...] - GRAVITY * gx[...] + WIND_GAIN * fu[...]
@@ -698,28 +748,28 @@
     sides_new[...] = sides_next
     fill_flow(flow, u_new[...], v_new[...])
     fill_flow(flow_outer, sides_next[0 : 2 * HALO], sides_next[2 * HALO : 4 * HALO])
-
-    def chunk(c, carry):
-        at = pl.multiple_of(c * 8, 8)
-        total = jnp.zeros((8, LANES), jnp.float32)
+    for kk in range(3):
+        fill_pack(flow[kk], flow_pack.at[kk], flow_scale.at[kk])
+
+    def chunk(at):
+        total = own_spread(at, idx, w, flow, flow_pack, flow_scale)
+        eta_new[pl.ds(at, 8)] = eta[pl.ds(at, 8)] - DEPTH_RATE * total
+
+    for c in range(tiles // 8):
+        chunk(c * 8)
+    for side, first, offset in ((0, 0, 0), (1, tiles - HALO, tiles + HALO)):
+        total = jnp.zeros((HALO, LANES), jnp.float32)
         for kk in range(3):
-            sources = [(HALO + r, flow[kk, r : r + 1]) for r in range(tiles)]
-            sources += [(q, flow_outer[kk, q : q + 1]) for q in range(HALO)]
-            sources += [
-                (tiles + HALO + q, flow_outer[kk, HALO + q : HALO + q + 1]) for q in range(HALO)
-            ]
-            centre = flow[kk, pl.ds(at, 8)]
-            one = pick(idx[pl.ds(kk * tiles + at, 8)], sources) - centre
-            two = pick(idx[pl.ds((kk + 3) * tiles + at, 8)], sources) - centre
+            at = side * HALO
+            sources = [(offset + q, flow_outer[kk, at + q : at + q + 1]) for q in range(HALO)]
+            found = rim_w[side] * pick(rim_idx[side], sources)
             total = (
                 total
-                + w[pl.ds(kk * tiles + at, 8)] * one
-                - w[pl.ds((kk + 3) * tiles + at, 8)] * two
+                + found[HALO * kk : HALO * (kk + 1)]
+                - found[HALO * (kk + 3) : HALO * (kk + 4)]
             )
-        eta_new[pl.ds(at, 8)] = eta[pl.ds(at, 8)] - DEPTH_RATE * total
-        return carry
-
-    lax.fori_loop(0, tiles // 8, chunk, 0)
+        rows = slice(first, first + HALO)
+        eta_new[rows] = eta_new[rows] - DEPTH_RATE * total
 
 
 def outer_subcycle(
@@ -777,8 +827,9 @@
 
 def first_ocean_kernel(
     arrived, first_far, first_near, odd, gx, gy, eta, u, v, idx, w, rim_idx, rim_w,
-    east_pack, west_pack, eta_new, u_new, v_new, sides_new, far, near, fu, fv, fside, side_idx,
-    side_w, heat, ids, flow, flow_outer, sides, up, dn
+    east_pack, west_pack, eta_new, eta_pack, eta_scale, u_new, v_new, sides_new, far, near,
+    fu, fv, fside, side_idx, side_w, heat, ids,
+    flow, flow_pack, flow_scale, flow_outer, sides, up, dn
 ):
     tiles = eta.shape[0]
     devices = arrived.shape[0]
@@ -813,31 +864,19 @@
             sides[at : at + HALO] = first.rim(side, row)
     rows = (ROW_ETA, ROW_PX, ROW_PY)
     first_subcycle(
-        gx, gy, eta, u, v, sides, fu, fv, fside, first.rims(0, rows), first.rims(1, rows), idx, w, side_idx, side_w, rim_idx, rim_w, flow, flow_outer,
+        gx, gy, eta, u, v, sides, fu, fv, fside, first.rims(0, rows), first.rims(1, rows), idx, w, side_idx, side_w, rim_idx, rim_w, flow, flow_pack, flow_scale, flow_outer,
         eta_new, u_new, v_new, sides_new
     )
-    send_rims(eta_new, rim_idx, rim_w, odd, far, near, up, dn)
+    send_rims(eta_new, eta_pack, eta_scale, rim_idx, rim_w, odd, far, near, up, dn)
     flag = jnp.broadcast_to(odd[0:1], east_pack.shape) > 0
     far[4 * HALO :] = jnp.where(flag, east_pack[...], west_pack[...])
     near[4 * HALO :] = jnp.where(flag, west_pack[...], east_pack[...])
 
 
-def sea_kernel(
-    first_far, first_near, odd, sst, heat, spread, ids, rim_idx, rim_w, warm, answers
-):
-    first = Received(first_far, first_near, odd)
-    tiles = sst.shape[0]
+def sea_kernel(base, heat, ids, warm, answers):
+    tiles = base.shape[0]
     devices = ids.shape[0]
-    warm[...] = (
-        sst[...] + WARMING_COEFF * heat[...] + (0.5 * SPREADING_COEFF) * spread[...]
-    )
-    for side, start, offset in ((0, 0, 0), (1, tiles - HALO, tiles + HALO)):
-        rim = first.rim(side, ROW_SST)
-        sources = [(offset + q, rim[q : q + 1]) for q in range(HALO)]
-        found = rim_w[side] * pick(rim_idx[side], sources)
-        total = combine([found[HALO * k : HALO * (k + 1)] for k in range(6)], [1.0] * 6)
-        rows = slice(start, start + HALO)
-        warm[rows] = warm[rows] + (0.5 * SPREADING_COEFF) * total
+    warm[...] = base[...] + WARMING_COEFF * heat[...]
     half = warm[...].astype(jnp.bfloat16)
     number = lax.broadcasted_iota(jnp.int32, (devices, tiles), 1).astype(jnp.float32)
     for j in range(CAP):
@@ -847,7 +886,8 @@
 
 def ocean_kernel(
     far, near, odd, eta, eta_part, u_part, v_part, sides, fside, idx, w, side_idx, side_w,
-    rim_idx, rim_w, eta_new, u_new, v_new, sides_new, far_new, near_new, flow_outer, up, dn
+    rim_idx, rim_w, eta_new, eta_pack, eta_scale, u_new, v_new, sides_new, far_new, near_new,
+    flow_outer, up, dn
 ):
     rows = (0, HALO, 2 * HALO)
     got = Received(far, near, odd)
@@ -855,7 +895,9 @@
         eta, eta_part, u_part, v_part, sides, fside, got.rims(0, rows), got.rims(1, rows), idx, w, side_idx, side_w, rim_idx, rim_w, flow_outer,
         eta_new, u_new, v_new
     )
-    send_rims(eta_new, rim_idx, rim_w, odd, far_new, near_new, up, dn)
+    send_rims(
+        eta_new, eta_pack, eta_scale, rim_idx, rim_w, odd, far_new, near_new, up, dn
+    )
 
 
 def last_ocean_kernel(
@@ -903,18 +945,21 @@
         panel_neighbours
     )
 
-    idx, w, rim_idx, rim_w, u, v, eta, sst, far, near, odd = pl.pallas_call(
+    pack_rows = shape_of(tiles // 2, LANES, dtype=jnp.int32)
+    scale_rows = shape_of(8, LANES)
+    nb, span, flow, rim_idx, rim_w, eta, eta_pack, eta_scale, sst, far, near, odd = pl.pallas_call(
         prepare_kernel,
         in_specs=hbm(8),
-        out_specs=vmem(11),
+        out_specs=vmem(12),
         out_shape=(
-            shape_of(6 * tiles, LANES, dtype=jnp.int32),
-            shape_of(6 * tiles, LANES),
+            shape_of(6, cells, dtype=jnp.int32),
+            shape_of(6, cells),
+            shape_of(2, cells),
             shape_of(2, 16, LANES, dtype=jnp.int32),
             shape_of(2, 16, LANES),
             cell_rows,
-            cell_rows,
-            cell_rows,
+            pack_rows,
+            scale_rows,
             cell_rows,
             shape_of(ROWS_FIRST, LANES),
             shape_of(ROWS_FIRST, LANES),
@@ -926,9 +971,6 @@
             pltpu.VMEM((points, 8, elements), jnp.float32),
             pltpu.VMEM((1, elements), jnp.float32),
             pltpu.VMEM((4, elements), jnp.int32),
-            pltpu.VMEM((2, cells), jnp.float32),
-            pltpu.VMEM((6, cells), jnp.int32),
-            pltpu.VMEM((6, cells), jnp.float32),
             dma((8,)),
         ],
         compiler_params=PARAMS,
@@ -949,17 +991,21 @@
 
     one_row = shape_of(1, blocks, dtype=jnp.int32)
     low_wind = pltpu.VMEM((points, 16, elements), jnp.bfloat16)
-    flux, slots, breadth, pn, holder, across = pl.pallas_call(
+    (
+        flux, slots, breadth, pn, across, own_rows, heat_rows, answer_rows, places, idx, w, u, v
+    ) = pl.pallas_call(
         lambda *refs: plan_kernel(*refs, devices=devices, tiles=tiles),
-        in_specs=hbm(8),
-        out_specs=vmem(6),
+        in_specs=hbm(8) + vmem(3),
+        out_specs=vmem(13),
         out_shape=(
             shape_of(points, 8, elements), shape_of(devices, LANES), shape_of(1, elements),
-            shape_of(4, elements, dtype=jnp.int32), one_row, one_row
+            shape_of(4, elements, dtype=jnp.int32), one_row, one_row, one_row, one_row, one_row,
+            shape_of(6 * tiles, LANES, dtype=jnp.int32), shape_of(6 * tiles, LANES),
+            cell_rows, cell_rows
         ),
         scratch_shapes=[
             pltpu.VMEM((points, 8, elements), jnp.float32), low_wind, low_wind,
-            pltpu.VMEM((1, blocks), jnp.int32), dma((8,))
+            pltpu.VMEM((1, blocks), jnp.int32), pltpu.VMEM((1, blocks), jnp.int32), dma((8,))
         ],
         compiler_params=PARAMS,
         name="plan",
@@ -974,40 +1020,47 @@
             transfer_across_tile.reshape(1, blocks),
             transfer_down_tile.reshape(1, blocks),
         ),
+        nb,
+        span,
+        flow,
     )
 
     outgoing = pl.pallas_call(
         lambda *refs: forward_kernel(*refs, devices=devices),
-        in_specs=smem(2) + vmem(8),
+        in_specs=smem(3) + vmem(8),
         out_specs=pl.BlockSpec(memory_space=pltpu.VMEM),
         out_shape=shape_of(devices, PER_DEST, LANES, dtype=jnp.bfloat16),
         scratch_shapes=[
-            pltpu.SMEM((devices,), jnp.int32),
             pltpu.VMEM((points, 8, elements), jnp.float32),
-            pltpu.VMEM((devices, 8, LANES), jnp.float32),
+            pltpu.VMEM((devices * 8, LANES), jnp.float32),
         ],
         compiler_params=PARAMS,
         name="forward_remap",
     )(
-        holder, across, flux, slots, breadth, pn, first_far, first_near, odd,
+        across, own_rows, heat_rows, flux, slots, breadth, pn, first_far, first_near, odd,
         transfer_coefficients
     )
     outgoing, pn, gradient_eta = lax.optimization_barrier((outgoing, pn, eta))
     arrived = exchange(outgoing)
-    gx, gy, spread = pl.pallas_call(
+    gx, gy, base = pl.pallas_call(
         first_gradient_kernel,
-        in_specs=vmem(4),
+        in_specs=vmem(11),
         out_specs=vmem(3),
         out_shape=(cell_rows,) * 3,
+        scratch_shapes=[
+            pltpu.VMEM((tiles // 2, LANES), jnp.int32), pltpu.VMEM((8, LANES), jnp.float32)
+        ],
         compiler_params=PARAMS,
         name="first_gradient",
-    )(idx, w, gradient_eta, sst)
+    )(
+        idx, w, gradient_eta, eta_pack, eta_scale, sst, first_far, first_near, odd, rim_idx, rim_w
+    )
 
     field = shape_of(points, levels, elements)
     edge = shape_of(4, levels, elements, dtype=jnp.bfloat16)
     pack = shape_of(2 * levels, elements)
     wind = shape_of(points, levels, elements, dtype=jnp.bfloat16)
-    loc, eastern, northern, east, west, east_pack, west_pack, places = pl.pallas_call(
+    loc, eastern, northern, east, west, east_pack, west_pack, edge_places = pl.pallas_call(
         local_step_kernel,
         in_specs=hbm(3) + vmem(2),
         out_specs=vmem(8),
@@ -1023,16 +1076,19 @@
     second_rows = shape_of(4 * HALO + 2 * levels, elements)
     flow_scratch = [
         pltpu.VMEM((3, tiles, LANES), jnp.float32),
+        pltpu.VMEM((3, tiles // 2, LANES), jnp.int32),
+        pltpu.VMEM((3, 8, LANES), jnp.float32),
         pltpu.VMEM((3, 2 * HALO, LANES), jnp.float32),
     ]
     (
-        eta, u, v, sides, far, near, fu, fv, fside, side_idx, side_w, heat, ids
+        eta, eta_pack, eta_scale, u, v, sides, far, near, fu, fv, fside, side_idx, side_w,
+        heat, ids
     ) = pl.pallas_call(
         first_ocean_kernel,
         in_specs=vmem(15),
-        out_specs=vmem(13),
+        out_specs=vmem(15),
         out_shape=(
-            cell_rows, cell_rows, cell_rows, rim_rows, second_rows, second_rows,
+            cell_rows, pack_rows, scale_rows, cell_rows, cell_rows, rim_rows, second_rows, second_rows,
             cell_rows, cell_rows, rim_rows,
             shape_of(2, 16, LANES, dtype=jnp.int32), shape_of(2, 16, LANES),
             cell_rows, shape_of(devices, LANES),
@@ -1050,34 +1106,49 @@
     for substep in range(1, NSUB):
         eta_part, u_part, v_part = pl.pallas_call(
             inner_kernel,
-            in_specs=vmem(7),
+            in_specs=vmem(9),
             out_specs=vmem(3),
             out_shape=(cell_rows,) * 3,
-            scratch_shapes=flow_scratch[:1],
+            scratch_shapes=flow_scratch[:3],
             compiler_params=PARAMS,
             name="inner",
-        )(idx, w, eta, u, v, fu, fv)
+        )(idx, w, eta, eta_pack, eta_scale, u, v, fu, fv)
         if substep == 1:
             eta_part, heat = lax.optimization_barrier((eta_part, heat))
             warm, answers = pl.pallas_call(
                 sea_kernel,
-                in_specs=vmem(9),
+                in_specs=vmem(3),
                 out_specs=vmem(2),
                 out_shape=(cell_rows, shape_of(devices, CAP, LANES)),
                 compiler_params=PARAMS,
                 name="sea",
-            )(first_far, first_near, odd, sst, heat, spread, ids, rim_idx, rim_w)
+            )(base, heat, ids)
             answered = exchange(answers)
+        if substep == 2:
+            eta_part, answered = lax.optimization_barrier((eta_part, answered))
+            surface = pl.pallas_call(
+                back_kernel,
+                in_specs=smem(2) + vmem(2),
+                out_specs=pl.BlockSpec(memory_space=pltpu.VMEM),
+                out_shape=shape_of(points, LANES),
+                scratch_shapes=[
+                    pltpu.VMEM((devices * CAP, LANES), jnp.float32),
+                    pltpu.VMEM((blocks, 8, LANES), jnp.float32),
+                ],
+                compiler_params=PARAMS,
+                name="back_remap",
+            )(answer_rows, places, answered, transfer_coefficients)
+            eta_part, surface = lax.optimization_barrier((eta_part, surface))
         operands = (
             far, near, odd, eta, eta_part, u_part, v_part, sides, fside, idx, w, side_idx, side_w, rim_idx, rim_w
         )
         outer_scratch = [pltpu.VMEM((3, 4 * HALO, LANES), jnp.float32)]
         if substep + 1 < NSUB:
-            eta, u, v, sides, far, near = pl.pallas_call(
+            eta, eta_pack, eta_scale, u, v, sides, far, near = pl.pallas_call(
                 ocean_kernel,
                 in_specs=vmem(15),
-                out_specs=vmem(6),
-                out_shape=(cell_rows,) * 3 + (rim_rows,) * 3,
+                out_specs=vmem(8),
+                out_shape=(cell_rows, pack_rows, scale_rows) + (cell_rows,) * 2 + (rim_rows,) * 3,
                 scratch_shapes=outer_scratch + [rim_scratch] * 2,
                 compiler_params=PARAMS,
                 name="ocean",
@@ -1094,20 +1165,6 @@
                 name="last_ocean",
             )(*operands)
 
-    surface = pl.pallas_call(
-        lambda *refs: back_kernel(*refs, devices=devices),
-        in_specs=smem(2) + vmem(2),
-        out_specs=pl.BlockSpec(memory_space=pltpu.VMEM),
-        out_shape=shape_of(points, LANES),
-        scratch_shapes=[
-            pltpu.SMEM((devices + points,), jnp.int32),
-            pltpu.SMEM((2 * points,), jnp.int32),
-            pltpu.VMEM((blocks, 8, LANES), jnp.float32),
-        ],
-        compiler_params=PARAMS,
-        name="back_remap",
-    )(holder, across, answered, transfer_coefficients)
-
     closing = pl.pallas_call(
         second_step_kernel,
         in_specs=vmem(14),
@@ -1119,7 +1176,7 @@
         compiler_params=PARAMS,
         name="second_step",
     )(
-        loc, eastern, northern, breadth, pn, east, west, edges_far, edges_near, places,
+        loc, eastern, northern, breadth, pn, east, west, edges_far, edges_near, edge_places,
         first_far, first_near, odd, surface
     )
     return closing, eta.reshape(cells), velocity, warm.reshape(cells)

time: 56.7 us -> 53.5 us (0.944)
  Pallas kernels: 24.2 us -> 19.7 us
  waiting for transfers between devices: 7.21 us -> 8.52 us
    pallas_call x10, Pallas kernels: 16.4 us -> 11.9 us  [the longest x3 4.09 us: shards(): pl.pallas_call(inner_kernel, in_specs=vmem(9), out_specs=vmem(3), out_sha...]
    all_to_all x2, waiting for transfers between devices: 3.36 us -> 4.4 us  [exchange(): return lax.all_to_all(value, RING, split_axis=0, concat_axis=0, tiled=True)]
  transfers between devices with their start and end apart: 10 -> 10, of which waited for: 4 -> 5; matrix products, arithmetic and copies ran while one was open for 0% -> 0% of each run, Pallas kernels for 32% -> 25%
where the time goes in v3:
time: 53.5 us; the launch traced here: 53.2 us
  starting transfers between devices  24.3 us (45%)
  Pallas kernels  19.7 us (37%)
  waiting for transfers between devices  8.52 us (16%)
  between operations  0.75 us (1%)
    ppermute x8, starting transfers between devices, swapped(): return lax.ppermute(value, RING, pairs)  17.4 us
    all_to_all x2, starting transfers between devices, exchange(): return lax.all_to_all(value, RING, split_axis=0, concat_axis=0, tiled=True)  6.9 us
    all_to_all x2, waiting for transfers between devices, exchange(): return lax.all_to_all(value, RING, split_axis=0, concat_axis=0, tiled=True)  4.4 us
    ppermute x8, waiting for transfers between devices, swapped(): return lax.ppermute(value, RING, pairs)  4.12 us
    pallas_call x3, Pallas kernels, shards(): pl.pallas_call(inner_kernel, in_specs=vmem(9), out_specs=vmem(3), out_sha...  4.09 us
    pallas_call x1, Pallas kernels, shards(): pl.pallas_call(local_step_kernel, in_specs=hbm(3) + vmem(2), out_specs=vm...  2.02 us
    pallas_call x1, Pallas kernels, shards(): pl.pallas_call(second_step_kernel, in_specs=vmem(14), out_specs=pl.BlockS...  1.8 us
    pallas_call x1, Pallas kernels, shards(): pl.pallas_call(lambda *refs: forward_kernel(*refs, devices=devices), in_s...  1.69 us
  transfers between devices with their start and end apart: 10, of which 5 were waited for; matrix products, arithmetic and copies ran while one was open for 0% of the time, Pallas kernels for 25%

profile of v3, /device:TPU:0, one launch (start us, length us, event | category | flops | bytes accessed | tf_op | source)
XLA Modules:
  0.0 53.2 jit_solution(7863702912695733858)
XLA Ops:
  0.6 0.0 copy-start
  0.6 1.5 %prepare.1 = (s32[6,4096]{1,0:T(8,128)S(1)}, f32[6,4096]{1,0:T(8,128)S(1)}, f32[2,4096]{1,0:T(2,128)S(1)}, s32[2,16,128]{2,1,0:T(8,128)S(1)}, f32[2,16,128]{2,1,...) custom-call(f32[16,64,128]{2,1,0:T(8,128)} %air_hbm.3, ...), custom_call_target="tpu_custom_call" | custom-call | tf_op jit(solution)/shard_map/prepare/pallas_call | solution.py:950
  2.2 6.4 %collective-permute-start = (f32[56,128]{1,0:T(8,128)S(1)}, f32[56,128]{1,0:T(8,128)S(1)}, u32[]{:S(2)}, u32[]{:S(2)}) collective-permute-start(f32[56,128]{1,0:T(8,128)S(1)} %get-tuple-element.103), channel_id=1, source_target_pairs={{1,2},{2,1},{3,4},{4,3},{5,6},{6,5},{7,8},{8,7},{9,10},{10,9},{11,... | collective-permute-start | bytes 86024 | tf_op jit(solution)/shard_map/ppermute | solution.py:41
  8.6 0.0 collective-permute-start.1
  8.6 1.2 %plan.1 = (f32[16,8,128]{2,1,0:T(8,128)S(1)}, f32[32,128]{1,0:T(8,128)S(1)}, f32[1,128]{1,0:T(1,128)S(1)}, s32[4,128]{1,0:T(4,128)S(1)}, s32[1,32]{1,0:T(1,128)S...) custom-call(f32[16,64,128]{2,1,0:T(8,128)} %air_hbm.3, ...), custom_call_target="tpu_custom_call" | custom-call | tf_op jit(solution)/shard_map/plan/pallas_call | solution.py:996
  9.8 0.6 %collective-permute-done.refs_7_.first_far = f32[56,128]{1,0:T(8,128)S(1)} collective-permute-done((f32[56,128]{1,0:T(8,128)S(1)}, f32[56,128]{1,0:T(8,128)S(1)}, u32[]{:S(2)}, u32[]{:S(2)}) %collective-permute-start) | collective-permute-done | bytes 28704 | tf_op jit(solution)/shard_map/ppermute | solution.py:41
  10.4 2.1 %collective-permute-done.1.refs_8_.first_near = f32[56,128]{1,0:T(8,128)S(1)} collective-permute-done((f32[56,128]{1,0:T(8,128)S(1)}, f32[56,128]{1,0:T(8,128)S(1)}, u32[]{:S(2)}, u32[]{:S(2)}) %collective-permute-start.1) | collective-permute-done | bytes 28704 | tf_op jit(solution)/shard_map/ppermute | solution.py:41
  12.5 0.0 copy-done
  12.5 1.7 %forward_remap.1 = bf16[32,16,128]{2,1,0:T(8,128)(2,1)} custom-call(s32[1,32]{1,0:T(1,128)S(1)} %get-tuple-element.97.refs_0_, s32[1,32]{1,0:T(1,128)S(1)} %get-tuple-element.98.refs_1_, s32[1,32]{1,0:T(1,128)S(1)} %get-tuple-element.99.refs_2_, f32[16,8,128]{2,1,0:T(8,128)S(1)} %get-tuple-element.100.refs_3_, f32[32,128]{1,0:T(8,128)S(1)} %get-tuple-element.101.refs_4_, ...), custom_call_target="tpu_custom_call" | custom-call | tf_op jit(solution)/shard_map/forward_remap/pallas_call | solution.py:1028
  14.2 3.4 %all-to-all-start = ((bf16[32,16,128]{2,1,0:T(8,128)(2,1)}), bf16[32,16,128]{2,1,0:T(8,128)(2,1)S(1)}, u32[]{:S(2)}, u32[]{:S(2)}) async-start(bf16[32,16,128]{2,1,0:T(8,128)(2,1)} %forward_remap.1), calls=%async_computation | async-start | bytes 262144 | tf_op jit(solution)/shard_map/all_to_all | solution.py:79
  17.6 2.0 %local_step.1 = (f32[16,64,128]{2,1,0:T(8,128)S(1)}, bf16[16,64,128]{2,1,0:T(8,128)(2,1)S(1)}, bf16[16,64,128]{2,1,0:T(8,128)(2,1)S(1)}, bf16[4,64,128]{2,1,0:T(...) custom-call(f32[16,64,128]{2,1,0:T(8,128)} %air_hbm.3, ...), custom_call_target="tpu_custom_call" | custom-call | tf_op jit(solution)/shard_map/local_step/pallas_call | solution.py:1063
  19.6 1.3 %first_gradient.1 = (f32[32,128]{1,0:T(8,128)S(1)}, f32[32,128]{1,0:T(8,128)S(1)}, f32[32,128]{1,0:T(8,128)S(1)}) custom-call(s32[192,128]{1,0:T(8,128)S(1)} %get-tuple-element.114.idx, f32[192,128]{1,0:T(8,128)S(1)} %get-tuple-element.115.w, f32[32,128]{1,0:T(8,128)S(1)} %get-tuple-element.116.eta, s32[16,128]{1,0:T(8,128)S(1)} %get-tuple-element.117.eta_pack, ...), custom_call_target="tpu_custom_call" | custom-call | tf_op jit(solution)/shard_map/first_gradient/pallas_call | solution.py:1045
  20.9 4.4 %all-to-all-done.arrived = bf16[32,16,128]{2,1,0:T(8,128)(2,1)S(1)} async-done(((bf16[32,16,128]{2,1,0:T(8,128)(2,1)}), bf16[32,16,128]{2,1,0:T(8,128)(2,1)S(1)}, u32[]{:S(2)}, u32[]{:S(2)}) %all-to-all-start) | async-done | bytes 131104 | tf_op jit(solution)/shard_map/all_to_all | solution.py:79
  25.3 1.5 %first_ocean.1 = (f32[32,128]{1,0:T(8,128)S(1)}, s32[16,128]{1,0:T(8,128)S(1)}, f32[8,128]{1,0:T(8,128)S(1)}, f32[32,128]{1,0:T(8,128)S(1)}, f32[32,128]{1,0:T(8...) custom-call(bf16[32,16,128]{2,1,0:T(8,128)(2,1)S(1)} %all-to-all-don, ...), custom_call_target="tpu_custom_call" | custom-call | tf_op jit(solution)/shard_map/first_ocean/pallas_call | solution.py:1086
  26.8 1.7 %collective-permute-start.2 = (f32[136,128]{1,0:T(8,128)S(1)}, f32[136,128]{1,0:T(8,128)S(1)}, u32[]{:S(2)}, u32[]{:S(2)}) collective-permute-start(f32[136,128]{1,0:T(8,128)S(1)} %get-tuple-element.128), channel_id=1, source_target_pairs={{1,2},{2,1},{3,4},{4,3},{5,6},{6,5},{7,8},{8,7},{9,10},{10,9},{11,... | collective-permute-start | bytes 208904 | tf_op jit(solution)/shard_map/ppermute | solution.py:41
  28.5 0.8 %collective-permute-start.3 = (f32[136,128]{1,0:T(8,128)S(1)}, f32[136,128]{1,0:T(8,128)S(1)}, u32[]{:S(2)}, u32[]{:S(2)}) collective-permute-start(f32[136,128]{1,0:T(8,128)S(1)} %get-tuple-element.129), channel_id=1, source_target_pairs={{0,1},{1,0},{2,3},{3,2},{4,5},{5,4},{6,7},{7,6},{8,9},{9,8},{10,11... | collective-permute-start | bytes 208904 | tf_op jit(solution)/shard_map/ppermute | solution.py:41
  29.3 1.4 %inner.3 = (f32[32,128]{1,0:T(8,128)S(1)}, f32[32,128]{1,0:T(8,128)S(1)}, f32[32,128]{1,0:T(8,128)S(1)}) custom-call(s32[192,128]{1,0:T(8,128)S(1)} %get-tuple-element.114.idx, f32[192,128]{1,0:T(8,128)S(1)} %get-tuple-element.115.w, f32[32,128]{1,0:T(8,128)S(1)} %get-tuple-element.131.eta, s32[16,128]{1,0:T(8,128)S(1)} %get-tuple-element.132.eta_pack, ...), custom_call_target="tpu_custom_call" | custom-call | tf_op jit(solution)/shard_map/inner/pallas_call | solution.py:1107
  30.7 0.8 %sea.1 = (f32[32,128]{1,0:T(8,128)}, f32[32,2,128]{2,1,0:T(2,128)}) custom-call(f32[32,128]{1,0:T(8,128)S(1)} %get-tuple-element.153.base, f32[32,128]{1,0:T(8,128)S(1)} %get-tuple-element.154.heat, f32[32,128]{1,0:T(8,128)S(1)} %get-tuple-element.155.ids), custom_call_target="tpu_custom_call" | custom-call | tf_op jit(solution)/shard_map/sea/pallas_call | solution.py:1118
  31.5 3.5 %all-to-all-start.1 = ((f32[32,2,128]{2,1,0:T(2,128)}), f32[32,2,128]{2,1,0:T(2,128)S(1)}, u32[]{:S(2)}, u32[]{:S(2)}) async-start(f32[32,2,128]{2,1,0:T(2,128)} %get-tuple-element.156), calls=%async_computation.1 | async-start | bytes 65536 | tf_op jit(solution)/shard_map/all_to_all | solution.py:79
  35.0 0.0 collective-permute-done.2.far
  35.0 0.0 collective-permute-done.3.near.near_swap
  35.0 0.7 %ocean.2 = (f32[32,128]{1,0:T(8,128)S(1)}, s32[16,128]{1,0:T(8,128)S(1)}, f32[8,128]{1,0:T(8,128)S(1)}, f32[32,128]{1,0:T(8,128)S(1)}, f32[32,128]{1,0:T(8,128)S...) custom-call(f32[136,128]{1,0:T(8,128)S(1)} %collective-permute-done.2.far, ...), custom_call_target="tpu_custom_call" | custom-call | tf_op jit(solution)/shard_map/ocean/pallas_call | solution.py:1147
  35.8 5.3 %collective-permute-start.4 = (f32[8,128]{1,0:T(8,128)S(1)}, f32[8,128]{1,0:T(8,128)S(1)}, u32[]{:S(2)}, u32[]{:S(2)}) collective-permute-start(f32[8,128]{1,0:T(8,128)S(1)} %get-tuple-element.162), channel_id=1, source_target_pairs={{1,2},{2,1},{3,4},{4,3},{5,6},{6,5},{7,8},{8,7},{9,10},{10,9},{11,... | collective-permute-start | bytes 12296 | tf_op jit(solution)/shard_map/ppermute | solution.py:41
  41.1 0.0 collective-permute-start.5
  41.1 1.4 %inner.4 = (f32[32,128]{1,0:T(8,128)S(1)}, f32[32,128]{1,0:T(8,128)S(1)}, f32[32,128]{1,0:T(8,128)S(1)}) custom-call(s32[192,128]{1,0:T(8,128)S(1)} %get-tuple-element.114.idx, f32[192,128]{1,0:T(8,128)S(1)} %get-tuple-element.115.w, f32[32,128]{1,0:T(8,128)S(1)} %get-tuple-element.147.eta, s32[16,128]{1,0:T(8,128)S(1)} %get-tuple-element.148.eta_pack, ...), custom_call_target="tpu_custom_call" | custom-call | tf_op jit(solution)/shard_map/inner/pallas_call | solution.py:1107
  42.4 0.0 all-to-all-done.1.arrived
  42.4 1.2 %back_remap.1.surface = f32[16,128]{1,0:T(8,128)S(1)} custom-call(s32[1,32]{1,0:T(1,128)S(1)} %get-tuple-element.158.answer_rows, s32[1,32]{1,0:T(1,128)S(1)} %get-tuple-element.159.places, f32[32,2,128]{2,1,0:T(2,128)S(1)} %all-to-all-done.1.arrived, bf16[32,128,128]{2,1,0:T(8,128)(2,1)S(1)} %copy-done), custom_call_target="tpu_custom_call" | custom-call | tf_op jit(solution)/shard_map/back_remap/pallas_call | solution.py:1129
  43.7 0.0 collective-permute-done.4.far
  43.7 1.0 %collective-permute-done.5.near = f32[8,128]{1,0:T(8,128)S(1)} collective-permute-done((f32[8,128]{1,0:T(8,128)S(1)}, f32[8,128]{1,0:T(8,128)S(1)}, u32[]{:S(2)}, u32[]{:S(2)}) %collective-permute-start.5) | collective-permute-done | bytes 4128 | tf_op jit(solution)/shard_map/ppermute | solution.py:41
  44.7 0.7 %ocean.3 = (f32[32,128]{1,0:T(8,128)S(1)}, s32[16,128]{1,0:T(8,128)S(1)}, f32[8,128]{1,0:T(8,128)S(1)}, f32[32,128]{1,0:T(8,128)S(1)}, f32[32,128]{1,0:T(8,128)S...) custom-call(f32[8,128]{1,0:T(8,128)S(1)} %collective-permute-done.4.far, ...), custom_call_target="tpu_custom_call" | custom-call | tf_op jit(solution)/shard_map/ocean/pallas_call | solution.py:1147
  45.4 3.1 %collective-permute-start.6 = (f32[8,128]{1,0:T(8,128)S(1)}, f32[8,128]{1,0:T(8,128)S(1)}, u32[]{:S(2)}, u32[]{:S(2)}) collective-permute-start(f32[8,128]{1,0:T(8,128)S(1)} %get-tuple-element.168), channel_id=1, source_target_pairs={{1,2},{2,1},{3,4},{4,3},{5,6},{6,5},{7,8},{8,7},{9,10},{10,9},{11,... | collective-permute-start | bytes 12296 | tf_op jit(solution)/shard_map/ppermute | solution.py:41
  48.5 0.0 collective-permute-start.7
  48.5 1.8 %second_step.1 = f32[16,64,128]{2,1,0:T(8,128)} custom-call(f32[16,64,128]{2,1,0:T(8,128)S(1)} %get-tuple-element.108.loc, bf16[16,64,128]{2,1,0:T(8,128)(2,1)S(1)} %get-tuple-element.109.eastern, bf16[16,64,128]{2,1,0:T(8,128)(2,1)S(1)} %get-tuple-element.110.northern, f32[1,128]{1,0:T(1,128)S(1)} %get-tuple-element.96.refs_5_.breadth, ...), custom_call_target="tpu_custom_call" | custom-call | tf_op jit(solution)/shard_map/second_step/pallas_call | solution.py:1168
  50.3 1.4 %inner.5 = (f32[32,128]{1,0:T(8,128)S(1)}, f32[32,128]{1,0:T(8,128)S(1)}, f32[32,128]{1,0:T(8,128)S(1)}) custom-call(s32[192,128]{1,0:T(8,128)S(1)} %get-tuple-element.114.idx, f32[192,128]{1,0:T(8,128)S(1)} %get-tuple-element.115.w, f32[32,128]{1,0:T(8,128)S(1)} %get-tuple-element.170.eta, s32[16,128]{1,0:T(8,128)S(1)} %get-tuple-element.171.eta_pack, ...), custom_call_target="tpu_custom_call" | custom-call | tf_op jit(solution)/shard_map/inner/pallas_call | solution.py:1107
  51.7 0.4 collective-permute-done.6.far
  52.1 0.0 collective-permute-done.7.near
  52.1 1.0 %last_ocean.1 = (f32[32,128]{1,0:T(8,128)}, f32[2,4096]{1,0:T(2,128)}) custom-call(f32[8,128]{1,0:T(8,128)S(1)} %collective-permute-done.6.far, f32[8,128]{1,0:T(8,128)S(1)} %collective-permute-done.7.near, s32[8,128]{1,0:T(8,128)S(1)} %get-tuple-element.105.refs_9_.odd, f32[32,128]{1,0:T(8,128)S(1)} %get-tuple-element.170.eta, ...), custom_call_target="tpu_custom_call" | custom-call | tf_op jit(solution)/shard_map/last_ocean/pallas_call | solution.py:1158
Async XLA Ops:
  0.6 11.9 %copy-start = (bf16[32,128,128]{2,1,0:T(8,128)(2,1)S(1)}, bf16[32,128,128]{2,1,0:T(8,128)(2,1)}, u32[]{:S(2)}) copy-start(bf16[32,128,128]{2,1,0:T(8,128)(2,1)} %weights.1) | copy-start | bytes 3145732
  2.2 8.2 %collective-permute-start = (f32[56,128]{1,0:T(8,128)S(1)}, f32[56,128]{1,0:T(8,128)S(1)}, u32[]{:S(2)}, u32[]{:S(2)}) collective-permute-start(f32[56,128]{1,0:T(8,128)S(1)} %get-tuple-element.103), channel_id=1, source_target_pairs={{1,2},{2,1},{3,4},{4,3},{5,6},{6,5},{7,8},{8,7},{9,10},{10,9},{11,... | collective-permute-start | bytes 86024 | tf_op jit(solution)/shard_map/ppermute | solution.py:41
  8.6 3.9 %collective-permute-start.1 = (f32[56,128]{1,0:T(8,128)S(1)}, f32[56,128]{1,0:T(8,128)S(1)}, u32[]{:S(2)}, u32[]{:S(2)}) collective-permute-start(f32[56,128]{1,0:T(8,128)S(1)} %get-tuple-element.104), channel_id=1, source_target_pairs={{0,1},{1,0},{2,3},{3,2},{4,5},{5,4},{6,7},{7,6},{8,9},{9,8},{10,11... | collective-permute-start | bytes 86024 | tf_op jit(solution)/shard_map/ppermute | solution.py:41
  14.2 11.1 %all-to-all-start = ((bf16[32,16,128]{2,1,0:T(8,128)(2,1)}), bf16[32,16,128]{2,1,0:T(8,128)(2,1)S(1)}, u32[]{:S(2)}, u32[]{:S(2)}) async-start(bf16[32,16,128]{2,1,0:T(8,128)(2,1)} %forward_remap.1), calls=%async_computation | async-start | bytes 262144 | tf_op jit(solution)/shard_map/all_to_all | solution.py:79
  26.8 8.3 %collective-permute-start.2 = (f32[136,128]{1,0:T(8,128)S(1)}, f32[136,128]{1,0:T(8,128)S(1)}, u32[]{:S(2)}, u32[]{:S(2)}) collective-permute-start(f32[136,128]{1,0:T(8,128)S(1)} %get-tuple-element.128), channel_id=1, source_target_pairs={{1,2},{2,1},{3,4},{4,3},{5,6},{6,5},{7,8},{8,7},{9,10},{10,9},{11,... | collective-permute-start | bytes 208904 | tf_op jit(solution)/shard_map/ppermute | solution.py:41
  28.5 6.6 %collective-permute-start.3 = (f32[136,128]{1,0:T(8,128)S(1)}, f32[136,128]{1,0:T(8,128)S(1)}, u32[]{:S(2)}, u32[]{:S(2)}) collective-permute-start(f32[136,128]{1,0:T(8,128)S(1)} %get-tuple-element.129), channel_id=1, source_target_pairs={{0,1},{1,0},{2,3},{3,2},{4,5},{5,4},{6,7},{7,6},{8,9},{9,8},{10,11... | collective-permute-start | bytes 208904 | tf_op jit(solution)/shard_map/ppermute | solution.py:41
  31.5 10.9 %all-to-all-start.1 = ((f32[32,2,128]{2,1,0:T(2,128)}), f32[32,2,128]{2,1,0:T(2,128)S(1)}, u32[]{:S(2)}, u32[]{:S(2)}) async-start(f32[32,2,128]{2,1,0:T(2,128)} %get-tuple-element.156), calls=%async_computation.1 | async-start | bytes 65536 | tf_op jit(solution)/shard_map/all_to_all | solution.py:79
  35.8 7.9 %collective-permute-start.4 = (f32[8,128]{1,0:T(8,128)S(1)}, f32[8,128]{1,0:T(8,128)S(1)}, u32[]{:S(2)}, u32[]{:S(2)}) collective-permute-start(f32[8,128]{1,0:T(8,128)S(1)} %get-tuple-element.162), channel_id=1, source_target_pairs={{1,2},{2,1},{3,4},{4,3},{5,6},{6,5},{7,8},{8,7},{9,10},{10,9},{11,... | collective-permute-start | bytes 12296 | tf_op jit(solution)/shard_map/ppermute | solution.py:41
  41.1 3.6 %collective-permute-start.5 = (f32[8,128]{1,0:T(8,128)S(1)}, f32[8,128]{1,0:T(8,128)S(1)}, u32[]{:S(2)}, u32[]{:S(2)}) collective-permute-start(f32[8,128]{1,0:T(8,128)S(1)} %get-tuple-element.163), channel_id=1, source_target_pairs={{0,1},{1,0},{2,3},{3,2},{4,5},{5,4},{6,7},{7,6},{8,9},{9,8},{10,11... | collective-permute-start | bytes 12296 | tf_op jit(solution)/shard_map/ppermute | solution.py:41
  45.4 6.7 %collective-permute-start.6 = (f32[8,128]{1,0:T(8,128)S(1)}, f32[8,128]{1,0:T(8,128)S(1)}, u32[]{:S(2)}, u32[]{:S(2)}) collective-permute-start(f32[8,128]{1,0:T(8,128)S(1)} %get-tuple-element.168), channel_id=1, source_target_pairs={{1,2},{2,1},{3,4},{4,3},{5,6},{6,5},{7,8},{8,7},{9,10},{10,9},{11,... | collective-permute-start | bytes 12296 | tf_op jit(solution)/shard_map/ppermute | solution.py:41
  48.5 3.6 %collective-permute-start.7 = (f32[8,128]{1,0:T(8,128)S(1)}, f32[8,128]{1,0:T(8,128)S(1)}, u32[]{:S(2)}, u32[]{:S(2)}) collective-permute-start(f32[8,128]{1,0:T(8,128)S(1)} %get-tuple-element.169), channel_id=1, source_target_pairs={{0,1},{1,0},{2,3},{3,2},{4,5},{5,4},{6,7},{7,6},{8,9},{9,8},{10,11... | collective-permute-start | bytes 12296 | tf_op jit(solution)/shard_map/ppermute | solution.py:41

commit v4 on v3

--- a/solution.py
+++ b/solution.py
@@ -30,6 +30,7 @@
 
 ROW_EDGE, ROW_BREADTH, ROW_ETA, ROW_U, ROW_V, ROW_SST = 0, 4, 8, 10, 12, 14
 ROW_PX, ROW_PY, ROW_IDX, ROW_W, ROWS_FIRST = 16, 18, 24, 40, 56
+MARK_COLUMN, MARK_OWN, MARK_HEAT, MARK_ANSWER, MARK_PLACE, MARK_READER = range(6)
 PER_DEST, ROW_HEAT, ROW_IDS = 16, 12, 14
 
 
@@ -246,8 +247,8 @@
 
 def plan_kernel(
     air_hbm, eastern_hbm, northern_hbm, breadth_hbm, pn_hbm, holder_hbm, across_hbm, down_hbm,
-    nb, span, flow, flux, slots, breadth, pn, across, own_rows, heat_rows, answer_rows, places,
-    idx, w, u, v, air, eastern, northern, holder, down, sems, *, devices, tiles
+    nb, span, flow, flux, slots, breadth, pn, marks, idx, w, u, v,
+    air, eastern, northern, holder, across, down, lists, sems, *, devices, tiles
 ):
     copies = load(
         (
@@ -265,6 +266,26 @@
     fill_tables(nb, span, flow, idx, w, u, v)
     for copy in copies:
         copy.wait()
+    rank = rank_among_equals(holder[...], CAP - 1)
+    place = across[...] * 2 + rank_among_equals(across[...], 1)
+    blocks = place.shape[1]
+    line = lax.broadcasted_iota(jnp.int32, (blocks, blocks), 0).astype(jnp.float32)
+    lane = lax.broadcasted_iota(jnp.int32, (blocks, blocks), 1).astype(jnp.float32)
+    here = as_column(place.astype(jnp.float32)) == lane
+    reader = jnp.sum(jnp.where(here, line, 0.0), axis=0, keepdims=True).astype(jnp.int32)
+    lists[...] = jnp.zeros_like(lists)
+    for mark, row in (
+        (MARK_COLUMN, across[...]),
+        (MARK_OWN, holder[...] * 8 + 2 * rank),
+        (MARK_HEAT, holder[...] * 8 + 4 + rank),
+        (MARK_ANSWER, holder[...] * CAP + rank),
+        (MARK_PLACE, place),
+        (MARK_READER, reader),
+    ):
+        lists[mark : mark + 1] = row
+    copy = pltpu.make_async_copy(lists, marks, sems.at[0])
+    copy.start()
+    slots[...] = slot_rows(holder[...], rank, down[...], devices, tiles)
     lines, count = air.shape[1], air.shape[2]
     ids, near = side_ids(pn)
     ids = [wide(line, lines) for line in ids]
@@ -277,17 +298,12 @@
     )
     for p in range(16):
         speed = jnp.sqrt(u[p] * u[p] + v[p] * v[p] + 1.0)
-        flux[p, 0:1] = result[p][0:1]
+        flux[p, 0:1] = (speed * result[p])[0:1]
         flux[p, 1:2] = (speed * u[p])[0:1]
         flux[p, 2:3] = (speed * v[p])[0:1]
         flux[p, 3:4] = speed[0:1]
         flux[p, 4:8] = jnp.zeros((4, count), jnp.float32)
-    rank = rank_among_equals(holder[...], CAP - 1)
-    slots[...] = slot_rows(holder[...], rank, down[...], devices, tiles)
-    own_rows[...] = holder[...] * 8 + 2 * rank
-    heat_rows[...] = holder[...] * 8 + 4 + rank
-    answer_rows[...] = holder[...] * CAP + rank
-    places[...] = across[...] * 2 + rank_among_equals(across[...], 1)
+    copy.wait()
 
 
 def local_step_kernel(
@@ -427,9 +443,21 @@
     lax.fori_loop(0, levels // lines, finish, 0)
 
 
+def home_sums_kernel(marks, flux, weights, own):
+    own[...] = jnp.zeros_like(own)
+    for b in range(weights.shape[0]):
+        sums = jnp.dot(
+            flux[marks[MARK_COLUMN, b]].astype(jnp.bfloat16), weights[b], preferred_element_type=jnp.float32
+        )
+        row = marks[MARK_OWN, b]
+        own[pl.ds(row, 1), :] = sums[1:2]
+        own[pl.ds(row + 1, 1), :] = sums[2:3]
+        own[pl.ds(marks[MARK_HEAT, b], 1), :] = sums[0:1]
+
+
 def forward_kernel(
-    across, own_rows, heat_rows, flux, slots, breadth, pn, first_far, first_near, odd, weights,
-    out, source, own, *, devices
+    marks, home, flux, slots, breadth, pn, first_far, first_near, odd, weights, out_hbm, out, extra,
+    sems, *, devices
 ):
     ids, near = side_ids(pn)
     jump = (JUMP_WEIGHT * STEP_SIZE) * breadth[...]
@@ -438,39 +466,42 @@
     from_west = lane_take(first.prev(slice(0, 8)), wide(ids[3], 8))
     from_east = jnp.where(near[1], 0.0, jump * from_east)
     from_west = jnp.where(near[3], 0.0, jump * from_west)
-    for p in range(16):
-        value = flux[p, 0:1]
-        if p % 4 == 3:
-            value = value + from_east[p // 4 : p // 4 + 1]
-        if p % 4 == 0:
-            value = value + from_west[p // 4 : p // 4 + 1]
-        source[p] = flux[p]
-        source[p, 0:1] = flux[p, 3:4] * value
-    own[...] = jnp.zeros_like(own)
-    for b in range(weights.shape[0]):
-        sums = jnp.dot(
-            source[across[0, b]].astype(jnp.bfloat16), weights[b], preferred_element_type=jnp.float32
-        )
-        row = own_rows[0, b]
-        own[pl.ds(row, 1), :] = sums[1:2]
-        own[pl.ds(row + 1, 1), :] = sums[2:3]
-        own[pl.ds(heat_rows[0, b], 1), :] = sums[0:1]
+    extra[...] = jnp.zeros_like(extra)
+    for n in range(4):
+        for p, change in ((3 + 4 * n, from_east), (4 * n, from_west)):
+            line = wide(flux[p, 3:4] * change[n : n + 1], 8).astype(jnp.bfloat16)
+            for reader in range(2):
+                b = marks[MARK_READER, 2 * p + reader]
+                sums = jnp.dot(line, weights[b], preferred_element_type=jnp.float32)
+                extra[pl.ds(marks[MARK_HEAT, b], 1), :] = sums[0:1]
     line = lax.broadcasted_iota(jnp.int32, (8, LANES), 0)
+    part, copies = devices // 4, []
     for d in range(devices):
         mine, prev, following = (
-            own[8 * (n % devices) : 8 * (n % devices) + 8] for n in (d, d - 1, d + 1)
+            home[8 * (n % devices) : 8 * (n % devices) + 8] for n in (d, d - 1, d + 1)
         )
         top = jnp.concatenate([mine[0:4], prev[0:4]], axis=0)
-        bottom = jnp.where(line < 4, following, mine)
+        bottom = jnp.where(line < 4, following, mine + extra[8 * d : 8 * d + 8])
         bottom = jnp.where(line == ROW_IDS - 8, wide(slots[d : d + 1], 8), bottom)
         out[d] = jnp.concatenate([top, bottom], axis=0).astype(jnp.bfloat16)
-
-
-def back_kernel(answer_rows, places, arrived, weights, surface, lines, share):
+        if (d + 1) % part == 0:
+            copies.append(
+                pltpu.make_async_copy(
+                    out.at[pl.ds(d + 1 - part, part)],
+                    out_hbm.at[pl.ds(d + 1 - part, part)],
+                    sems.at[d // part],
+                )
+            )
+            copies[-1].start()
+    for copy in copies:
+        copy.wait()
+
+
+def back_kernel(marks, arrived, weights, surface, lines, share):
     lines[...] = arrived[...].reshape(lines.shape)
     for b in range(weights.shape[0]):
-        line = lines[pl.ds(answer_rows[0, b], 1), :]
-        share[places[0, b]] = lax.dot_general(
+        line = lines[pl.ds(marks[MARK_ANSWER, b], 1), :]
+        share[marks[MARK_PLACE, b]] = lax.dot_general(
             wide(line, 8).astype(jnp.bfloat16),
             weights[b],
             (((1,), (1,)), ((), ())),
@@ -645,10 +676,18 @@
     idx, w, eta, eta_pack, eta_scale, u, v, fu, fv, eta_part, u_part, v_part,
     flow, flow_pack, flow_scale
 ):
+    current_kernel(idx, w, eta, eta_pack, eta_scale, u, v, fu, fv, u_part, v_part)
+    height_kernel(idx, w, eta, u_part, v_part, eta_part, flow, flow_pack, flow_scale)
+
+
+def current_kernel(idx, w, eta, eta_pack, eta_scale, u, v, fu, fv, u_part, v_part):
     own_gradient(idx, w, eta, eta_pack, eta_scale, u_part, v_part)
-    tiles = eta.shape[0]
     u_part[...] = DAMPING * u[...] - GRAVITY * u_part[...] + WIND_GAIN * fu[...]
     v_part[...] = DAMPING * v[...] - GRAVITY * v_part[...] + WIND_GAIN * fv[...]
+
+
+def height_kernel(idx, w, eta, u_part, v_part, eta_part, flow, flow_pack, flow_scale):
+    tiles = eta.shape[0]
     fill_flow(flow, u_part[...], v_part[...])
     for kk in range(3):
         fill_pack(flow[kk], flow_pack.at[kk], flow_scale.at[kk])
@@ -827,30 +866,39 @@
 
 def first_ocean_kernel(
     arrived, first_far, first_near, odd, gx, gy, eta, u, v, idx, w, rim_idx, rim_w,
-    east_pack, west_pack, eta_new, eta_pack, eta_scale, u_new, v_new, sides_new, far, near,
-    fu, fv, fside, side_idx, side_w, heat, ids,
-    flow, flow_pack, flow_scale, flow_outer, sides, up, dn
+    east_pack, west_pack, base, eta_new, eta_pack, eta_scale, u_new, v_new, sides_new, far, near,
+    fu, fv, fside, side_idx, side_w, heat, answers_hbm,
+    flow, flow_pack, flow_scale, flow_outer, sides, up, dn, parts, answers, sems
 ):
     tiles = eta.shape[0]
     devices = arrived.shape[0]
-    parts = arrived[...].astype(jnp.float32)
-    ids[...] = parts[:, ROW_IDS, :]
+    parts[...] = arrived[...].astype(jnp.float32).reshape(parts.shape)
+
+    def rows_of(r):
+        return parts[pl.ds(r, devices, stride=PER_DEST), :]
+
+    ids = rows_of(ROW_IDS)
     number = lax.broadcasted_iota(jnp.int32, (devices, LANES), 1).astype(jnp.float32)
     nothing = jnp.zeros((devices, LANES), jnp.float32)
     chosen, lines = [], []
     for j in range(3 * CAP):
-        chosen.append(jnp.where(ids[:, j : j + 1] == number, 1.0, 0.0))
-        first = parts[:, ROW_HEAT + j, :] if j < CAP else nothing
-        lines.append(
-            jnp.concatenate([first, parts[:, 2 * j, :], parts[:, 2 * j + 1, :]], axis=1)
-        )
+        chosen.append(jnp.where(ids[:, j : j + 1] == number, 1.0, 0.0).astype(jnp.bfloat16))
+        first = rows_of(ROW_HEAT + j) if j < CAP else nothing
+        lines.append(jnp.concatenate([first, rows_of(2 * j), rows_of(2 * j + 1)], axis=1))
     forcing = lax.dot_general(
-        jnp.concatenate(chosen, axis=0).astype(jnp.bfloat16),
+        jnp.concatenate(chosen, axis=0),
         jnp.concatenate(lines, axis=0).astype(jnp.bfloat16),
         (((0,), (0,)), ((), ())),
         preferred_element_type=jnp.float32,
     )
     heat[...] = forcing[0:tiles, 0:LANES]
+    half = (base[...] + WARMING_COEFF * forcing[0:tiles, 0:LANES]).astype(jnp.bfloat16)
+    for j in range(CAP):
+        answers[:, j, :] = jnp.dot(
+            chosen[j][:, 0:tiles], half, preferred_element_type=jnp.float32
+        )
+    copy = pltpu.make_async_copy(answers, answers_hbm, sems.at[0])
+    copy.start()
     fu[...] = forcing[0:tiles, LANES : 2 * LANES]
     fv[...] = forcing[0:tiles, 2 * LANES : 3 * LANES]
     fside[0 : 2 * HALO] = forcing[tiles : tiles + 2 * HALO, LANES : 2 * LANES]
@@ -871,17 +919,7 @@
     flag = jnp.broadcast_to(odd[0:1], east_pack.shape) > 0
     far[4 * HALO :] = jnp.where(flag, east_pack[...], west_pack[...])
     near[4 * HALO :] = jnp.where(flag, west_pack[...], east_pack[...])
-
-
-def sea_kernel(base, heat, ids, warm, answers):
-    tiles = base.shape[0]
-    devices = ids.shape[0]
-    warm[...] = base[...] + WARMING_COEFF * heat[...]
-    half = warm[...].astype(jnp.bfloat16)
-    number = lax.broadcasted_iota(jnp.int32, (devices, tiles), 1).astype(jnp.float32)
-    for j in range(CAP):
-        chosen = jnp.where(ids[:, j : j + 1] == number, 1.0, 0.0).astype(jnp.bfloat16)
-        answers[:, j, :] = jnp.dot(chosen, half, preferred_element_type=jnp.float32)
+    copy.wait()
 
 
 def ocean_kernel(
@@ -902,8 +940,9 @@
 
 def last_ocean_kernel(
     far, near, odd, eta, eta_part, u_part, v_part, sides, fside, idx, w, side_idx, side_w,
-    rim_idx, rim_w, eta_new, velocity, u_new, v_new, flow_outer
+    rim_idx, rim_w, base, heat, eta_new, velocity, warm, u_new, v_new, flow_outer
 ):
+    warm[...] = base[...] + WARMING_COEFF * heat[...]
     rows = (0, HALO, 2 * HALO)
     got = Received(far, near, odd)
     outer_subcycle(
@@ -989,23 +1028,21 @@
     )
     first_far, first_near = swap_both(far, near)
 
-    one_row = shape_of(1, blocks, dtype=jnp.int32)
     low_wind = pltpu.VMEM((points, 16, elements), jnp.bfloat16)
-    (
-        flux, slots, breadth, pn, across, own_rows, heat_rows, answer_rows, places, idx, w, u, v
-    ) = pl.pallas_call(
+    low_row = pltpu.VMEM((1, blocks), jnp.int32)
+    flux, slots, breadth, pn, marks, idx, w, u, v = pl.pallas_call(
         lambda *refs: plan_kernel(*refs, devices=devices, tiles=tiles),
         in_specs=hbm(8) + vmem(3),
-        out_specs=vmem(13),
+        out_specs=vmem(4) + smem(1) + vmem(4),
         out_shape=(
             shape_of(points, 8, elements), shape_of(devices, LANES), shape_of(1, elements),
-            shape_of(4, elements, dtype=jnp.int32), one_row, one_row, one_row, one_row, one_row,
+            shape_of(4, elements, dtype=jnp.int32), pltpu.SMEM((8, blocks), jnp.int32),
             shape_of(6 * tiles, LANES, dtype=jnp.int32), shape_of(6 * tiles, LANES),
             cell_rows, cell_rows
         ),
         scratch_shapes=[
             pltpu.VMEM((points, 8, elements), jnp.float32), low_wind, low_wind,
-            pltpu.VMEM((1, blocks), jnp.int32), pltpu.VMEM((1, blocks), jnp.int32), dma((8,))
+            low_row, low_row, low_row, pltpu.VMEM((8, blocks), jnp.int32), dma((8,))
         ],
         compiler_params=PARAMS,
         name="plan",
@@ -1025,20 +1062,28 @@
         flow,
     )
 
+    home = pl.pallas_call(
+        home_sums_kernel,
+        in_specs=smem(1) + vmem(2),
+        out_specs=pl.BlockSpec(memory_space=pltpu.VMEM),
+        out_shape=shape_of(devices * 8, LANES),
+        compiler_params=PARAMS,
+        name="home_sums",
+    )(marks, flux, transfer_coefficients)
     outgoing = pl.pallas_call(
         lambda *refs: forward_kernel(*refs, devices=devices),
-        in_specs=smem(3) + vmem(8),
-        out_specs=pl.BlockSpec(memory_space=pltpu.VMEM),
-        out_shape=shape_of(devices, PER_DEST, LANES, dtype=jnp.bfloat16),
+        in_specs=smem(1) + vmem(9),
+        out_specs=pl.BlockSpec(memory_space=pltpu.HBM),
+        out_shape=pltpu.HBM((devices, PER_DEST, LANES), jnp.bfloat16),
         scratch_shapes=[
-            pltpu.VMEM((points, 8, elements), jnp.float32),
+            pltpu.VMEM((devices, PER_DEST, LANES), jnp.bfloat16),
             pltpu.VMEM((devices * 8, LANES), jnp.float32),
+            dma((4,)),
         ],
         compiler_params=PARAMS,
         name="forward_remap",
     )(
-        across, own_rows, heat_rows, flux, slots, breadth, pn, first_far, first_near, odd,
-        transfer_coefficients
+        marks, home, flux, slots, breadth, pn, first_far, first_near, odd, transfer_coefficients
     )
     outgoing, pn, gradient_eta = lax.optimization_barrier((outgoing, pn, eta))
     arrived = exchange(outgoing)
@@ -1082,53 +1127,67 @@
     ]
     (
         eta, eta_pack, eta_scale, u, v, sides, far, near, fu, fv, fside, side_idx, side_w,
-        heat, ids
+        heat, answers
     ) = pl.pallas_call(
         first_ocean_kernel,
-        in_specs=vmem(15),
-        out_specs=vmem(15),
+        in_specs=vmem(16),
+        out_specs=vmem(14) + hbm(1),
         out_shape=(
             cell_rows, pack_rows, scale_rows, cell_rows, cell_rows, rim_rows, second_rows, second_rows,
             cell_rows, cell_rows, rim_rows,
             shape_of(2, 16, LANES, dtype=jnp.int32), shape_of(2, 16, LANES),
-            cell_rows, shape_of(devices, LANES),
+            cell_rows, pltpu.HBM((devices, CAP, LANES), jnp.float32),
         ),
-        scratch_shapes=flow_scratch + [rim_scratch] * 3,
+        scratch_shapes=flow_scratch + [rim_scratch] * 3 + [
+            pltpu.VMEM((devices * PER_DEST, LANES), jnp.float32),
+            pltpu.VMEM((devices, CAP, LANES), jnp.float32),
+            dma((1,)),
+        ],
         compiler_params=PARAMS,
         name="first_ocean",
     )(
         arrived, first_far, first_near, odd, gx, gy, eta, u, v, idx, w, rim_idx, rim_w,
-        east_pack, west_pack
+        east_pack, west_pack, base
     )
     far, near = swap_both(far, near)
     edges_far, edges_near = far, near
 
     for substep in range(1, NSUB):
-        eta_part, u_part, v_part = pl.pallas_call(
-            inner_kernel,
-            in_specs=vmem(9),
-            out_specs=vmem(3),
-            out_shape=(cell_rows,) * 3,
-            scratch_shapes=flow_scratch[:3],
-            compiler_params=PARAMS,
-            name="inner",
-        )(idx, w, eta, eta_pack, eta_scale, u, v, fu, fv)
         if substep == 1:
-            eta_part, heat = lax.optimization_barrier((eta_part, heat))
-            warm, answers = pl.pallas_call(
-                sea_kernel,
-                in_specs=vmem(3),
+            u_part, v_part = pl.pallas_call(
+                current_kernel,
+                in_specs=vmem(9),
                 out_specs=vmem(2),
-                out_shape=(cell_rows, shape_of(devices, CAP, LANES)),
+                out_shape=(cell_rows,) * 2,
                 compiler_params=PARAMS,
-                name="sea",
-            )(base, heat, ids)
+                name="current",
+            )(idx, w, eta, eta_pack, eta_scale, u, v, fu, fv)
+            answers, u_part = lax.optimization_barrier((answers, u_part))
             answered = exchange(answers)
+            eta_part = pl.pallas_call(
+                height_kernel,
+                in_specs=vmem(5),
+                out_specs=pl.BlockSpec(memory_space=pltpu.VMEM),
+                out_shape=cell_rows,
+                scratch_shapes=flow_scratch[:3],
+                compiler_params=PARAMS,
+                name="height",
+            )(idx, w, eta, u_part, v_part)
+        else:
+            eta_part, u_part, v_part = pl.pallas_call(
+                inner_kernel,
+                in_specs=vmem(9),
+                out_specs=vmem(3),
+                out_shape=(cell_rows,) * 3,
+                scratch_shapes=flow_scratch[:3],
+                compiler_params=PARAMS,
+                name="inner",
+            )(idx, w, eta, eta_pack, eta_scale, u, v, fu, fv)
         if substep == 2:
             eta_part, answered = lax.optimization_barrier((eta_part, answered))
             surface = pl.pallas_call(
                 back_kernel,
-                in_specs=smem(2) + vmem(2),
+                in_specs=smem(1) + vmem(2),
                 out_specs=pl.BlockSpec(memory_space=pltpu.VMEM),
                 out_shape=shape_of(points, LANES),
                 scratch_shapes=[
@@ -1137,7 +1196,7 @@
                 ],
                 compiler_params=PARAMS,
                 name="back_remap",
-            )(answer_rows, places, answered, transfer_coefficients)
+            )(marks, answered, transfer_coefficients)
             eta_part, surface = lax.optimization_barrier((eta_part, surface))
         operands = (
             far, near, odd, eta, eta_part, u_part, v_part, sides, fside, idx, w, side_idx, side_w, rim_idx, rim_w
@@ -1155,15 +1214,15 @@
             )(*operands)
             far, near = swap_both(far, near)
         else:
-            eta, velocity = pl.pallas_call(
+            eta, velocity, warm = pl.pallas_call(
                 last_ocean_kernel,
-                in_specs=vmem(15),
-                out_specs=vmem(2),
-                out_shape=(cell_rows, shape_of(2, cells)),
+                in_specs=vmem(17),
+                out_specs=vmem(3),
+                out_shape=(cell_rows, shape_of(2, cells), cell_rows),
                 scratch_shapes=[pltpu.VMEM((tiles, LANES), jnp.float32)] * 2 + outer_scratch,
                 compiler_params=PARAMS,
                 name="last_ocean",
-            )(*operands)
+            )(*operands, base, heat)
 
     closing = pl.pallas_call(
         second_step_kernel,

time: 53.5 us -> 52.4 us (0.979)
  Pallas kernels: 19.7 us -> 19 us
    pallas_call x3 -> x2, Pallas kernels: 4.09 us -> 2.74 us  [shards(): pl.pallas_call(inner_kernel, in_specs=vmem(9), out_specs=vmem(3), out_sha...]
    pallas_call x4 -> x6, Pallas kernels: 4.52 us -> 5.31 us  [the longest x1 1.78 us: shards(): pl.pallas_call(first_ocean_kernel, in_specs=vmem(16), out_specs=vmem(14)...]
    pallas_call x1, Pallas kernels: 1.69 us -> 1 us  [shards(): pl.pallas_call(lambda *refs: forward_kernel(*refs, devices=devices), in_s...]
    pallas_call x1, Pallas kernels: 1.22 us -> 1.81 us  [shards(): pl.pallas_call(lambda *refs: plan_kernel(*refs, devices=devices, tiles=ti...]
where the time goes in v4:
time: 52.4 us; the launch traced here: 52.1 us
  starting transfers between devices  24 us (46%)
  Pallas kernels  19 us (36%)
  waiting for transfers between devices  8.34 us (16%)
  between operations  0.77 us (1%)
    ppermute x8, starting transfers between devices, swapped(): return lax.ppermute(value, RING, pairs)  17.1 us
    all_to_all x2, starting transfers between devices, exchange(): return lax.all_to_all(value, RING, split_axis=0, concat_axis=0, tiled=True)  6.92 us
    all_to_all x2, waiting for transfers between devices, exchange(): return lax.all_to_all(value, RING, split_axis=0, concat_axis=0, tiled=True)  4.39 us
    ppermute x8, waiting for transfers between devices, swapped(): return lax.ppermute(value, RING, pairs)  3.94 us
    pallas_call x2, Pallas kernels, shards(): pl.pallas_call(inner_kernel, in_specs=vmem(9), out_specs=vmem(3), out_sha...  2.74 us
    pallas_call x1, Pallas kernels, shards(): pl.pallas_call(local_step_kernel, in_specs=hbm(3) + vmem(2), out_specs=vm...  2.02 us
    pallas_call x1, Pallas kernels, shards(): pl.pallas_call(lambda *refs: plan_kernel(*refs, devices=devices, tiles=ti...  1.81 us
    pallas_call x1, Pallas kernels, shards(): pl.pallas_call(second_step_kernel, in_specs=vmem(14), out_specs=pl.BlockS...  1.8 us
  transfers between devices with their start and end apart: 10, of which 5 were waited for; matrix products, arithmetic and copies ran while one was open for 0% of the time, Pallas kernels for 25%

profile of v4, /device:TPU:0, one launch (start us, length us, event | category | flops | bytes accessed | tf_op | source)
XLA Modules:
  0.0 52.1 jit_solution(14354787488278854565)
XLA Ops:
  0.6 0.0 copy-start
  0.6 1.5 %prepare.1 = (s32[6,4096]{1,0:T(8,128)S(1)}, f32[6,4096]{1,0:T(8,128)S(1)}, f32[2,4096]{1,0:T(2,128)S(1)}, s32[2,16,128]{2,1,0:T(8,128)S(1)}, f32[2,16,128]{2,1,...) custom-call(f32[16,64,128]{2,1,0:T(8,128)} %air_hbm.3, ...), custom_call_target="tpu_custom_call" | custom-call | tf_op jit(solution)/shard_map/prepare/pallas_call | solution.py:989
  2.2 6.4 %collective-permute-start = (f32[56,128]{1,0:T(8,128)S(1)}, f32[56,128]{1,0:T(8,128)S(1)}, u32[]{:S(2)}, u32[]{:S(2)}) collective-permute-start(f32[56,128]{1,0:T(8,128)S(1)} %get-tuple-element.95), channel_id=1, source_target_pairs={{1,2},{2,1},{3,4},{4,3},{5,6},{6,5},{7,8},{8,7},{9,10},{10,9},{11,... | collective-permute-start | bytes 86024 | tf_op jit(solution)/shard_map/ppermute | solution.py:42
  8.6 0.0 collective-permute-start.1
  8.6 1.8 %plan.1 = (f32[16,8,128]{2,1,0:T(8,128)S(1)}, f32[32,128]{1,0:T(8,128)S(1)}, f32[1,128]{1,0:T(1,128)S(1)}, s32[4,128]{1,0:T(4,128)S(1)}, s32[8,32]{1,0:T(8,128)S...) custom-call(f32[16,64,128]{2,1,0:T(8,128)} %air_hbm.3, ...), custom_call_target="tpu_custom_call" | custom-call | tf_op jit(solution)/shard_map/plan/pallas_call | solution.py:1033
  10.4 0.0 copy-done
  10.4 0.4 home_sums.1.refs_1_
  10.8 0.0 collective-permute-done.refs_6_.first_far
  10.8 1.7 %collective-permute-done.1.refs_7_.first_near = f32[56,128]{1,0:T(8,128)S(1)} collective-permute-done((f32[56,128]{1,0:T(8,128)S(1)}, f32[56,128]{1,0:T(8,128)S(1)}, u32[]{:S(2)}, u32[]{:S(2)}) %collective-permute-start.1) | collective-permute-done | bytes 28704 | tf_op jit(solution)/shard_map/ppermute | solution.py:42
  12.5 1.0 %forward_remap.1 = bf16[32,16,128]{2,1,0:T(8,128)(2,1)} custom-call(s32[8,32]{1,0:T(8,128)S(4)} %get-tuple-element.91.marks.refs_0_, f32[256,128]{1,0:T(8,128)S(1)} %home_sums.1.refs_1_, f32[16,8,128]{2,1,0:T(8,128)S(1)} %get-tuple-element.92.flux.refs_2_, f32[32,128]{1,0:T(8,128)S(1)} %get-tuple-element.93.refs_3_, ...), custom_call_target="tpu_custom_call" | custom-call | tf_op jit(solution)/shard_map/forward_remap/pallas_call | solution.py:1073
  13.5 3.4 %all-to-all-start = ((bf16[32,16,128]{2,1,0:T(8,128)(2,1)}), bf16[32,16,128]{2,1,0:T(8,128)(2,1)S(1)}, u32[]{:S(2)}, u32[]{:S(2)}) async-start(bf16[32,16,128]{2,1,0:T(8,128)(2,1)} %forward_remap.1), calls=%async_computation | async-start | bytes 262144 | tf_op jit(solution)/shard_map/all_to_all | solution.py:80
  16.9 2.0 %local_step.1 = (f32[16,64,128]{2,1,0:T(8,128)S(1)}, bf16[16,64,128]{2,1,0:T(8,128)(2,1)S(1)}, bf16[16,64,128]{2,1,0:T(8,128)(2,1)S(1)}, bf16[4,64,128]{2,1,0:T(...) custom-call(f32[16,64,128]{2,1,0:T(8,128)} %air_hbm.3, ...), custom_call_target="tpu_custom_call" | custom-call | tf_op jit(solution)/shard_map/local_step/pallas_call | solution.py:1108
  18.9 1.3 %first_gradient.1 = (f32[32,128]{1,0:T(8,128)S(1)}, f32[32,128]{1,0:T(8,128)S(1)}, f32[32,128]{1,0:T(8,128)S(1)}) custom-call(s32[192,128]{1,0:T(8,128)S(1)} %get-tuple-element.106.idx, f32[192,128]{1,0:T(8,128)S(1)} %get-tuple-element.107.w, f32[32,128]{1,0:T(8,128)S(1)} %get-tuple-element.108.eta, s32[16,128]{1,0:T(8,128)S(1)} %get-tuple-element.109.eta_pack, ...), custom_call_target="tpu_custom_call" | custom-call | tf_op jit(solution)/shard_map/first_gradient/pallas_call | solution.py:1090
  20.2 4.4 %all-to-all-done.arrived = bf16[32,16,128]{2,1,0:T(8,128)(2,1)S(1)} async-done(((bf16[32,16,128]{2,1,0:T(8,128)(2,1)}), bf16[32,16,128]{2,1,0:T(8,128)(2,1)S(1)}, u32[]{:S(2)}, u32[]{:S(2)}) %all-to-all-start) | async-done | bytes 131104 | tf_op jit(solution)/shard_map/all_to_all | solution.py:80
  24.6 1.8 %first_ocean.1 = (f32[32,128]{1,0:T(8,128)S(1)}, s32[16,128]{1,0:T(8,128)S(1)}, f32[8,128]{1,0:T(8,128)S(1)}, f32[32,128]{1,0:T(8,128)S(1)}, f32[32,128]{1,0:T(8...) custom-call(bf16[32,16,128]{2,1,0:T(8,128)(2,1)S(1)} %all-to-all-don, ...), custom_call_target="tpu_custom_call" | custom-call | tf_op jit(solution)/shard_map/first_ocean/pallas_call | solution.py:1131
  26.4 1.7 %collective-permute-start.2 = (f32[136,128]{1,0:T(8,128)S(1)}, f32[136,128]{1,0:T(8,128)S(1)}, u32[]{:S(2)}, u32[]{:S(2)}) collective-permute-start(f32[136,128]{1,0:T(8,128)S(1)} %get-tuple-element.121), channel_id=1, source_target_pairs={{1,2},{2,1},{3,4},{4,3},{5,6},{6,5},{7,8},{8,7},{9,10},{10,9},{11,... | collective-permute-start | bytes 208904 | tf_op jit(solution)/shard_map/ppermute | solution.py:42
  28.1 0.8 %collective-permute-start.3 = (f32[136,128]{1,0:T(8,128)S(1)}, f32[136,128]{1,0:T(8,128)S(1)}, u32[]{:S(2)}, u32[]{:S(2)}) collective-permute-start(f32[136,128]{1,0:T(8,128)S(1)} %get-tuple-element.122), channel_id=1, source_target_pairs={{0,1},{1,0},{2,3},{3,2},{4,5},{5,4},{6,7},{7,6},{8,9},{9,8},{10,11... | collective-permute-start | bytes 208904 | tf_op jit(solution)/shard_map/ppermute | solution.py:42
  29.0 0.6 %current.1 = (f32[32,128]{1,0:T(8,128)S(1)}, f32[32,128]{1,0:T(8,128)S(1)}) custom-call(s32[192,128]{1,0:T(8,128)S(1)} %get-tuple-element.106.idx, f32[192,128]{1,0:T(8,128)S(1)} %get-tuple-element.107.w, f32[32,128]{1,0:T(8,128)S(1)} %get-tuple-element.124.eta, s32[16,128]{1,0:T(8,128)S(1)} %get-tuple-element.126.eta_pack, ...), custom_call_target="tpu_custom_call" | custom-call | tf_op jit(solution)/shard_map/current/pallas_call | solution.py:1157
  29.6 3.5 %all-to-all-start.1 = ((f32[32,2,128]{2,1,0:T(2,128)}), f32[32,2,128]{2,1,0:T(2,128)S(1)}, u32[]{:S(2)}, u32[]{:S(2)}) async-start(f32[32,2,128]{2,1,0:T(2,128)} %get-tuple-element.145), calls=%async_computation.1 | async-start | bytes 65536 | tf_op jit(solution)/shard_map/all_to_all | solution.py:80
  33.2 0.8 %height.1.eta_part = f32[32,128]{1,0:T(8,128)S(1)} custom-call(s32[192,128]{1,0:T(8,128)S(1)} %get-tuple-element.106.idx, f32[192,128]{1,0:T(8,128)S(1)} %get-tuple-element.107.w, f32[32,128]{1,0:T(8,128)S(1)} %get-tuple-element.124.eta, f32[32,128]{1,0:T(8,128)S(1)} %get-tuple-element.133.u_part, f32[32,128]{1,0:T(8,128)S(1)} %get-tuple-element.134.v_part), custom_call_target="tpu_custom_call" | custom-call | tf_op jit(solution)/shard_map/height/pallas_call | solution.py:1167
  34.0 0.2 collective-permute-done.2.far
  34.2 0.0 collective-permute-done.3.near.near_swap
  34.2 0.7 %ocean.2 = (f32[32,128]{1,0:T(8,128)S(1)}, s32[16,128]{1,0:T(8,128)S(1)}, f32[8,128]{1,0:T(8,128)S(1)}, f32[32,128]{1,0:T(8,128)S(1)}, f32[32,128]{1,0:T(8,128)S...) custom-call(f32[136,128]{1,0:T(8,128)S(1)} %collective-permute-done.2.far, ...), custom_call_target="tpu_custom_call" | custom-call | tf_op jit(solution)/shard_map/ocean/pallas_call | solution.py:1206
  35.0 5.0 %collective-permute-start.4 = (f32[8,128]{1,0:T(8,128)S(1)}, f32[8,128]{1,0:T(8,128)S(1)}, u32[]{:S(2)}, u32[]{:S(2)}) collective-permute-start(f32[8,128]{1,0:T(8,128)S(1)} %get-tuple-element.149), channel_id=1, source_target_pairs={{1,2},{2,1},{3,4},{4,3},{5,6},{6,5},{7,8},{8,7},{9,10},{10,9},{11,... | collective-permute-start | bytes 12296 | tf_op jit(solution)/shard_map/ppermute | solution.py:42
  40.0 0.0 collective-permute-start.5
  40.0 1.4 %inner.2 = (f32[32,128]{1,0:T(8,128)S(1)}, f32[32,128]{1,0:T(8,128)S(1)}, f32[32,128]{1,0:T(8,128)S(1)}) custom-call(s32[192,128]{1,0:T(8,128)S(1)} %get-tuple-element.106.idx, f32[192,128]{1,0:T(8,128)S(1)} %get-tuple-element.107.w, f32[32,128]{1,0:T(8,128)S(1)} %get-tuple-element.139.eta, s32[16,128]{1,0:T(8,128)S(1)} %get-tuple-element.140.eta_pack, ...), custom_call_target="tpu_custom_call" | custom-call | tf_op jit(solution)/shard_map/inner/pallas_call | solution.py:1177
  41.4 0.0 all-to-all-done.1.arrived
  41.4 0.7 %back_remap.1.surface = f32[16,128]{1,0:T(8,128)S(1)} custom-call(s32[8,32]{1,0:T(8,128)S(4)} %get-tuple-element.91.marks.refs_0_, f32[32,2,128]{2,1,0:T(2,128)S(1)} %all-to-all-done.1.arrived, bf16[32,128,128]{2,1,0:T(8,128)(2,1)S(1)} %copy-done), custom_call_target="tpu_custom_call" | custom-call | tf_op jit(solution)/shard_map/back_remap/pallas_call | solution.py:1188
  42.1 0.0 collective-permute-done.4.far
  42.1 1.5 %collective-permute-done.5.near = f32[8,128]{1,0:T(8,128)S(1)} collective-permute-done((f32[8,128]{1,0:T(8,128)S(1)}, f32[8,128]{1,0:T(8,128)S(1)}, u32[]{:S(2)}, u32[]{:S(2)}) %collective-permute-start.5) | collective-permute-done | bytes 4128 | tf_op jit(solution)/shard_map/ppermute | solution.py:42
  43.6 0.7 %ocean.3 = (f32[32,128]{1,0:T(8,128)S(1)}, s32[16,128]{1,0:T(8,128)S(1)}, f32[8,128]{1,0:T(8,128)S(1)}, f32[32,128]{1,0:T(8,128)S(1)}, f32[32,128]{1,0:T(8,128)S...) custom-call(f32[8,128]{1,0:T(8,128)S(1)} %collective-permute-done.4.far, ...), custom_call_target="tpu_custom_call" | custom-call | tf_op jit(solution)/shard_map/ocean/pallas_call | solution.py:1206
  44.3 3.1 %collective-permute-start.6 = (f32[8,128]{1,0:T(8,128)S(1)}, f32[8,128]{1,0:T(8,128)S(1)}, u32[]{:S(2)}, u32[]{:S(2)}) collective-permute-start(f32[8,128]{1,0:T(8,128)S(1)} %get-tuple-element.155), channel_id=1, source_target_pairs={{1,2},{2,1},{3,4},{4,3},{5,6},{6,5},{7,8},{8,7},{9,10},{10,9},{11,... | collective-permute-start | bytes 12296 | tf_op jit(solution)/shard_map/ppermute | solution.py:42
  47.4 0.0 collective-permute-start.7
  47.4 1.8 %second_step.1 = f32[16,64,128]{2,1,0:T(8,128)} custom-call(f32[16,64,128]{2,1,0:T(8,128)S(1)} %get-tuple-element.100.loc, bf16[16,64,128]{2,1,0:T(8,128)(2,1)S(1)} %get-tuple-element.101.eastern, bf16[16,64,128]{2,1,0:T(8,128)(2,1)S(1)} %get-tuple-element.102.northern, f32[1,128]{1,0:T(1,128)S(1)} %get-tuple-element.90.refs_4_.breadth, ...), custom_call_target="tpu_custom_call" | custom-call | tf_op jit(solution)/shard_map/second_step/pallas_call | solution.py:1227
  49.2 1.4 %inner.3 = (f32[32,128]{1,0:T(8,128)S(1)}, f32[32,128]{1,0:T(8,128)S(1)}, f32[32,128]{1,0:T(8,128)S(1)}) custom-call(s32[192,128]{1,0:T(8,128)S(1)} %get-tuple-element.106.idx, f32[192,128]{1,0:T(8,128)S(1)} %get-tuple-element.107.w, f32[32,128]{1,0:T(8,128)S(1)} %get-tuple-element.157.eta, s32[16,128]{1,0:T(8,128)S(1)} %get-tuple-element.158.eta_pack, ...), custom_call_target="tpu_custom_call" | custom-call | tf_op jit(solution)/shard_map/inner/pallas_call | solution.py:1177
  50.6 0.4 collective-permute-done.6.far
  51.0 0.0 collective-permute-done.7.near
  51.1 1.0 %last_ocean.1 = (f32[32,128]{1,0:T(8,128)}, f32[2,4096]{1,0:T(2,128)}, f32[32,128]{1,0:T(8,128)}) custom-call(f32[8,128]{1,0:T(8,128)S(1)} %collective-permute-done.6.far, f32[8,128]{1,0:T(8,128)S(1)} %collective-permute-done.7.near, s32[8,128]{1,0:T(8,128)S(1)} %get-tuple-element.97.refs_8_.odd, f32[32,128]{1,0:T(8,128)S(1)} %get-tuple-element.157.eta, ...), custom_call_target="tpu_custom_call" | custom-call | tf_op jit(solution)/shard_map/last_ocean/pallas_call | solution.py:1217
Async XLA Ops:
  0.6 9.8 %copy-start = (bf16[32,128,128]{2,1,0:T(8,128)(2,1)S(1)}, bf16[32,128,128]{2,1,0:T(8,128)(2,1)}, u32[]{:S(2)}) copy-start(bf16[32,128,128]{2,1,0:T(8,128)(2,1)} %weights.3) | copy-start | bytes 3145732
  2.2 8.6 %collective-permute-start = (f32[56,128]{1,0:T(8,128)S(1)}, f32[56,128]{1,0:T(8,128)S(1)}, u32[]{:S(2)}, u32[]{:S(2)}) collective-permute-start(f32[56,128]{1,0:T(8,128)S(1)} %get-tuple-element.95), channel_id=1, source_target_pairs={{1,2},{2,1},{3,4},{4,3},{5,6},{6,5},{7,8},{8,7},{9,10},{10,9},{11,... | collective-permute-start | bytes 86024 | tf_op jit(solution)/shard_map/ppermute | solution.py:42
  8.6 3.9 %collective-permute-start.1 = (f32[56,128]{1,0:T(8,128)S(1)}, f32[56,128]{1,0:T(8,128)S(1)}, u32[]{:S(2)}, u32[]{:S(2)}) collective-permute-start(f32[56,128]{1,0:T(8,128)S(1)} %get-tuple-element.96), channel_id=1, source_target_pairs={{0,1},{1,0},{2,3},{3,2},{4,5},{5,4},{6,7},{7,6},{8,9},{9,8},{10,11... | collective-permute-start | bytes 86024 | tf_op jit(solution)/shard_map/ppermute | solution.py:42
  13.5 11.1 %all-to-all-start = ((bf16[32,16,128]{2,1,0:T(8,128)(2,1)}), bf16[32,16,128]{2,1,0:T(8,128)(2,1)S(1)}, u32[]{:S(2)}, u32[]{:S(2)}) async-start(bf16[32,16,128]{2,1,0:T(8,128)(2,1)} %forward_remap.1), calls=%async_computation | async-start | bytes 262144 | tf_op jit(solution)/shard_map/all_to_all | solution.py:80
  26.4 7.8 %collective-permute-start.2 = (f32[136,128]{1,0:T(8,128)S(1)}, f32[136,128]{1,0:T(8,128)S(1)}, u32[]{:S(2)}, u32[]{:S(2)}) collective-permute-start(f32[136,128]{1,0:T(8,128)S(1)} %get-tuple-element.121), channel_id=1, source_target_pairs={{1,2},{2,1},{3,4},{4,3},{5,6},{6,5},{7,8},{8,7},{9,10},{10,9},{11,... | collective-permute-start | bytes 208904 | tf_op jit(solution)/shard_map/ppermute | solution.py:42
  28.1 6.1 %collective-permute-start.3 = (f32[136,128]{1,0:T(8,128)S(1)}, f32[136,128]{1,0:T(8,128)S(1)}, u32[]{:S(2)}, u32[]{:S(2)}) collective-permute-start(f32[136,128]{1,0:T(8,128)S(1)} %get-tuple-element.122), channel_id=1, source_target_pairs={{0,1},{1,0},{2,3},{3,2},{4,5},{5,4},{6,7},{7,6},{8,9},{9,8},{10,11... | collective-permute-start | bytes 208904 | tf_op jit(solution)/shard_map/ppermute | solution.py:42
  29.6 11.8 %all-to-all-start.1 = ((f32[32,2,128]{2,1,0:T(2,128)}), f32[32,2,128]{2,1,0:T(2,128)S(1)}, u32[]{:S(2)}, u32[]{:S(2)}) async-start(f32[32,2,128]{2,1,0:T(2,128)} %get-tuple-element.145), calls=%async_computation.1 | async-start | bytes 65536 | tf_op jit(solution)/shard_map/all_to_all | solution.py:80
  35.0 7.1 %collective-permute-start.4 = (f32[8,128]{1,0:T(8,128)S(1)}, f32[8,128]{1,0:T(8,128)S(1)}, u32[]{:S(2)}, u32[]{:S(2)}) collective-permute-start(f32[8,128]{1,0:T(8,128)S(1)} %get-tuple-element.149), channel_id=1, source_target_pairs={{1,2},{2,1},{3,4},{4,3},{5,6},{6,5},{7,8},{8,7},{9,10},{10,9},{11,... | collective-permute-start | bytes 12296 | tf_op jit(solution)/shard_map/ppermute | solution.py:42
  40.0 3.6 %collective-permute-start.5 = (f32[8,128]{1,0:T(8,128)S(1)}, f32[8,128]{1,0:T(8,128)S(1)}, u32[]{:S(2)}, u32[]{:S(2)}) collective-permute-start(f32[8,128]{1,0:T(8,128)S(1)} %get-tuple-element.150), channel_id=1, source_target_pairs={{0,1},{1,0},{2,3},{3,2},{4,5},{5,4},{6,7},{7,6},{8,9},{9,8},{10,11... | collective-permute-start | bytes 12296 | tf_op jit(solution)/shard_map/ppermute | solution.py:42
  44.3 6.7 %collective-permute-start.6 = (f32[8,128]{1,0:T(8,128)S(1)}, f32[8,128]{1,0:T(8,128)S(1)}, u32[]{:S(2)}, u32[]{:S(2)}) collective-permute-start(f32[8,128]{1,0:T(8,128)S(1)} %get-tuple-element.155), channel_id=1, source_target_pairs={{1,2},{2,1},{3,4},{4,3},{5,6},{6,5},{7,8},{8,7},{9,10},{10,9},{11,... | collective-permute-start | bytes 12296 | tf_op jit(solution)/shard_map/ppermute | solution.py:42
  47.4 3.6 %collective-permute-start.7 = (f32[8,128]{1,0:T(8,128)S(1)}, f32[8,128]{1,0:T(8,128)S(1)}, u32[]{:S(2)}, u32[]{:S(2)}) collective-permute-start(f32[8,128]{1,0:T(8,128)S(1)} %get-tuple-element.156), channel_id=1, source_target_pairs={{0,1},{1,0},{2,3},{3,2},{4,5},{5,4},{6,7},{7,6},{8,9},{9,8},{10,11... | collective-permute-start | bytes 12296 | tf_op jit(solution)/shard_map/ppermute | solution.py:42

commit v5 on v4

--- a/solution.py
+++ b/solution.py
@@ -247,8 +247,8 @@
 
 def plan_kernel(
     air_hbm, eastern_hbm, northern_hbm, breadth_hbm, pn_hbm, holder_hbm, across_hbm, down_hbm,
-    nb, span, flow, flux, slots, breadth, pn, marks, idx, w, u, v,
-    air, eastern, northern, holder, across, down, lists, sems, *, devices, tiles
+    nb_hbm, span_hbm, flow_hbm, sst_hbm, flux, slots, breadth, pn, marks, idx, w, u, v, sst,
+    air, eastern, northern, holder, across, down, nb, span, flow, lists, sems, *, devices, tiles
 ):
     copies = load(
         (
@@ -260,10 +260,13 @@
             (holder_hbm, holder),
             (across_hbm, across),
             (down_hbm, down),
+            (nb_hbm, nb),
+            (span_hbm, span),
+            (flow_hbm, flow),
+            (sst_hbm, sst),
         ),
         sems,
     )
-    fill_tables(nb, span, flow, idx, w, u, v)
     for copy in copies:
         copy.wait()
     rank = rank_among_equals(holder[...], CAP - 1)
@@ -286,6 +289,7 @@
     copy = pltpu.make_async_copy(lists, marks, sems.at[0])
     copy.start()
     slots[...] = slot_rows(holder[...], rank, down[...], devices, tiles)
+    fill_tables(nb, span, flow, idx, w, u, v)
     lines, count = air.shape[1], air.shape[2]
     ids, near = side_ids(pn)
     ids = [wide(line, lines) for line in ids]
@@ -307,8 +311,8 @@
 
 
 def local_step_kernel(
-    air_hbm, eastern_hbm, northern_hbm, breadth, pn, loc, eastern, northern, east, west,
-    east_pack, west_pack, places, air, sems
+    air_hbm, eastern_hbm, northern_hbm, breadth, pn, odd, loc, eastern, northern, east, west,
+    far, near_swap, places, air, sems
 ):
     copies = load(((air_hbm, air), (eastern_hbm, eastern), (northern_hbm, northern)), sems)
     count = breadth.shape[1]
@@ -347,15 +351,17 @@
         )
         for p in range(16):
             loc[p, rows] = result[p]
-        beyond = pl.ds(pl.multiple_of(levels + at, lines), lines)
-        for own, pack, chosen, first in (
-            (east, east_pack, chosen_east, 3),
-            (west, west_pack, chosen_west, 0),
-        ):
-            for n in range(4):
-                own[n, rows] = state[first + 4 * n].astype(jnp.bfloat16)
-            pack[rows] = packed([state[first + 4 * n] for n in range(4)], chosen)
-            pack[beyond] = packed([result[first + 4 * n] for n in range(4)], chosen)
+        here = pl.ds(pl.multiple_of(4 * HALO + at, 8), lines)
+        beyond = pl.ds(pl.multiple_of(4 * HALO + levels + at, 8), lines)
+        for n in range(4):
+            east[n, rows] = state[3 + 4 * n].astype(jnp.bfloat16)
+            west[n, rows] = state[4 * n].astype(jnp.bfloat16)
+        flag = jnp.broadcast_to(odd[0:1], (lines, count)) > 0
+        for target, values in ((here, state), (beyond, result)):
+            to_next = packed([values[3 + 4 * n] for n in range(4)], chosen_east)
+            to_prev = packed([values[4 * n] for n in range(4)], chosen_west)
+            far[target] = jnp.where(flag, to_next, to_prev)
+            near_swap[target] = jnp.where(flag, to_prev, to_next)
         return carry
 
     lax.fori_loop(0, levels // lines, chunk, 0)
@@ -515,37 +521,52 @@
     return lax.shift_right_arithmetic(idx, 7), idx & (LANES - 1)
 
 
+def by_tiles(function, idx):
+    if idx.shape[0] <= 8:
+        return function(idx)
+    return jnp.concatenate(
+        [function(idx[at : at + 8]) for at in range(0, idx.shape[0], 8)], axis=0
+    )
+
+
 def pick(idx, sources):
-    high, low = split_index(idx)
-    result = jnp.zeros(idx.shape, jnp.float32)
-    for number, line in sources:
-        result = jnp.where(high == number, lane_take(wide(line, idx.shape[0]), low), result)
-    return result
+    def one(idx):
+        high, low = split_index(idx)
+        result = jnp.zeros(idx.shape, jnp.float32)
+        for number, line in sources:
+            result = jnp.where(high == number, lane_take(wide(line, idx.shape[0]), low), result)
+        return result
+
+    return by_tiles(one, idx)
 
 
 def fill_pack(values, packed, scales):
-    tiles = values.shape[0]
-    half = tiles // 2
-    largest = jnp.maximum(jnp.max(jnp.abs(values), axis=1, keepdims=True), 1e-30)
-    number = jnp.floor(values * (32767.0 / largest) + 0.5).astype(jnp.int32)
-    packed[...] = (number[half:] << 16) | (number[:half] & 0xFFFF)
-    lane = lax.broadcasted_iota(jnp.int32, (tiles, LANES), 1)
-    line = lax.broadcasted_iota(jnp.int32, (tiles, LANES), 0)
-    row = jnp.sum(jnp.where(lane == line, largest * (1.0 / 32767.0), 0.0), axis=0, keepdims=True)
-    scales[...] = wide(row, 8)
+    half = values.shape[0] // 2
+    numbers = []
+    for n, part in enumerate((values[:half], values[half:])):
+        largest = jnp.maximum(jnp.max(jnp.abs(part), axis=(0, 1), keepdims=True), 1e-30)
+        numbers.append(jnp.floor(part * (32767.0 / largest) + 0.5).astype(jnp.int32))
+        scales[n : n + 1] = jnp.broadcast_to(largest * (1.0 / 32767.0), (1, LANES))
+    packed[...] = (numbers[1] << 16) | (numbers[0] & 0xFFFF)
 
 
 def pick_own(idx, packed, scales):
-    lines = idx.shape[0]
     half = packed.shape[0]
-    high, low = split_index(idx)
-    own = high - HALO
-    row = jnp.where(own >= half, own - half, own)
-    words = jnp.zeros(idx.shape, jnp.int32)
-    for r in range(half):
-        words = jnp.where(row == r, lane_take(wide(packed[r : r + 1], lines), low), words)
-    number = jnp.where(own >= half, words >> 16, (words << 16) >> 16)
-    return number.astype(jnp.float32) * lane_take(wide(scales[0:1], lines), own & (LANES - 1))
+
+    def one(idx):
+        lines = idx.shape[0]
+        high, low = split_index(idx)
+        own = high - HALO
+        upper = own >= half
+        row = jnp.where(upper, own - half, own)
+        words = jnp.zeros(idx.shape, jnp.int32)
+        for r in range(half):
+            words = jnp.where(row == r, lane_take(wide(packed[r : r + 1], lines), low), words)
+        number = jnp.where(upper, words >> 16, (words << 16) >> 16)
+        scale = jnp.where(upper, wide(scales[1:2], lines), wide(scales[0:1], lines))
+        return number.astype(jnp.float32) * scale
+
+    return by_tiles(one, idx)
 
 
 def combine(terms, factors):
@@ -571,35 +592,34 @@
 
 def prepare_kernel(
     air_hbm, breadth_hbm, pn_hbm, eta_hbm, sst_hbm, flow_hbm, nb_hbm, span_hbm,
-    nb, span, flow, rim_idx, rim_w, eta, eta_pack, eta_scale, sst, far, near, odd,
-    up, dn, air, breadth, pn, sems
+    rim_idx, rim_w, eta, eta_pack, eta_scale, far, near, odd,
+    up, dn, air, breadth, pn, sst, flow, nb, span, sems
 ):
-    copies = load(
-        (
-            (nb_hbm, nb),
-            (span_hbm, span),
-            (flow_hbm, flow),
-            (eta_hbm, eta),
-            (sst_hbm, sst),
-            (breadth_hbm, breadth),
-            (pn_hbm, pn),
-            (air_hbm.at[:, pl.ds(0, 8), :], air),
-        ),
-        sems,
-    )
+    tiles, cells = eta.shape[0], nb_hbm.shape[1]
+    pairs = [(eta_hbm, eta)]
+    for side, at in ((0, 0), (1, cells - OY)):
+        cut = pl.ds(at, OY)
+        pairs.append((nb_hbm.at[:, cut], nb.at[side]))
+        pairs.append((span_hbm.at[:, cut], span.at[side]))
+        pairs.append((flow_hbm.at[:, cut], flow.at[side]))
+    for side, at in ((0, 0), (1, tiles - 8)):
+        pairs.append((sst_hbm.at[pl.ds(at, 8)], sst.at[side]))
+    pairs.append((breadth_hbm, breadth))
+    pairs.append((pn_hbm, pn))
+    pairs.append((air_hbm.at[:, pl.ds(0, 8), :], air))
+    copies = load(pairs, sems)
     for copy in copies:
         copy.wait()
     shard = lax.shift_right_logical(pn[0:1], pn.shape[1].bit_length() - 1)
     odd[...] = wide(shard & 1, 8)
-    tiles = eta.shape[0]
     fill_pack(eta[...], eta_pack, eta_scale)
     for side, first in ((0, 0), (1, tiles - HALO)):
         rim_idx[side, 12:16] = jnp.full((4, LANES), -1, jnp.int32)
         rim_w[side, 12:16] = jnp.zeros((4, LANES), jnp.float32)
         for j in range(HALO):
-            cut = slice((first + j) * LANES, (first + j + 1) * LANES)
-            links = nb[:, cut]
-            factors = slot_factors(links, span[:, cut])
+            cut = slice(j * LANES, (j + 1) * LANES)
+            links = nb[side, :, cut]
+            factors = slot_factors(links, span[side, :, cut])
             for k in range(6):
                 at = HALO * k + j
                 rim_idx[side, at : at + 1] = links[k : k + 1]
@@ -616,10 +636,11 @@
         cut = slice(first, first + HALO)
         target[ROW_ETA : ROW_ETA + HALO] = eta[cut]
         for j in range(HALO):
-            here = slice((first + j) * LANES, (first + j + 1) * LANES)
-            target[ROW_U + j : ROW_U + j + 1] = flow[0:1, here]
-            target[ROW_V + j : ROW_V + j + 1] = flow[1:2, here]
-        target[ROW_SST : ROW_SST + HALO] = sst[cut]
+            here = slice(j * LANES, (j + 1) * LANES)
+            target[ROW_U + j : ROW_U + j + 1] = flow[side, 0:1, here]
+            target[ROW_V + j : ROW_V + j + 1] = flow[side, 1:2, here]
+        start = first % 8
+        target[ROW_SST : ROW_SST + HALO] = sst[side, start : start + HALO]
         target[ROW_PX : ROW_PX + HALO] = part_x
         target[ROW_PY : ROW_PY + HALO] = part_y
         target[ROW_IDX : ROW_IDX + 16] = rim_idx[side].astype(jnp.float32)
@@ -773,7 +794,8 @@
 
 def first_subcycle(
     gx, gy, eta, u, v, sides, fu, fv, fside, before, after, idx, w, side_idx, side_w,
-    rim_idx, rim_w, flow, flow_pack, flow_scale, flow_outer, eta_new, u_new, v_new, sides_new
+    rim_idx, rim_w, flow, flow_pack, flow_scale, flow_outer, eta_new, u_new, v_new, sides_new,
+    midway
 ):
     tiles = eta.shape[0]
     u_new[...] = DAMPING * u[...] - GRAVITY * gx[...] + WIND_GAIN * fu[...]
@@ -795,6 +817,8 @@
         eta_new[pl.ds(at, 8)] = eta[pl.ds(at, 8)] - DEPTH_RATE * total
 
     for c in range(tiles // 8):
+        if c == tiles // 16:
+            midway()
         chunk(c * 8)
     for side, first, offset in ((0, 0, 0), (1, tiles - HALO, tiles + HALO)):
         total = jnp.zeros((HALO, LANES), jnp.float32)
@@ -866,7 +890,7 @@
 
 def first_ocean_kernel(
     arrived, first_far, first_near, odd, gx, gy, eta, u, v, idx, w, rim_idx, rim_w,
-    east_pack, west_pack, base, eta_new, eta_pack, eta_scale, u_new, v_new, sides_new, far, near,
+    far_old, near_old, base, eta_new, eta_pack, eta_scale, u_new, v_new, sides_new, far, near,
     fu, fv, fside, side_idx, side_w, heat, answers_hbm,
     flow, flow_pack, flow_scale, flow_outer, sides, up, dn, parts, answers, sems
 ):
@@ -897,12 +921,11 @@
         answers[:, j, :] = jnp.dot(
             chosen[j][:, 0:tiles], half, preferred_element_type=jnp.float32
         )
-    copy = pltpu.make_async_copy(answers, answers_hbm, sems.at[0])
-    copy.start()
     fu[...] = forcing[0:tiles, LANES : 2 * LANES]
     fv[...] = forcing[0:tiles, 2 * LANES : 3 * LANES]
     fside[0 : 2 * HALO] = forcing[tiles : tiles + 2 * HALO, LANES : 2 * LANES]
     fside[2 * HALO : 4 * HALO] = forcing[tiles : tiles + 2 * HALO, 2 * LANES : 3 * LANES]
+    copy = pltpu.make_async_copy(answers, answers_hbm, sems.at[0])
     first = Received(first_far, first_near, odd)
     for side, part in ((0, first.prev), (1, first.next)):
         side_idx[side] = part(slice(ROW_IDX, ROW_IDX + 16)).astype(jnp.int32)
@@ -913,12 +936,9 @@
     rows = (ROW_ETA, ROW_PX, ROW_PY)
     first_subcycle(
         gx, gy, eta, u, v, sides, fu, fv, fside, first.rims(0, rows), first.rims(1, rows), idx, w, side_idx, side_w, rim_idx, rim_w, flow, flow_pack, flow_scale, flow_outer,
-        eta_new, u_new, v_new, sides_new
+        eta_new, u_new, v_new, sides_new, copy.start
     )
     send_rims(eta_new, eta_pack, eta_scale, rim_idx, rim_w, odd, far, near, up, dn)
-    flag = jnp.broadcast_to(odd[0:1], east_pack.shape) > 0
-    far[4 * HALO :] = jnp.where(flag, east_pack[...], west_pack[...])
-    near[4 * HALO :] = jnp.where(flag, west_pack[...], east_pack[...])
     copy.wait()
 
 
@@ -986,20 +1006,22 @@
 
     pack_rows = shape_of(tiles // 2, LANES, dtype=jnp.int32)
     scale_rows = shape_of(8, LANES)
-    nb, span, flow, rim_idx, rim_w, eta, eta_pack, eta_scale, sst, far, near, odd = pl.pallas_call(
+    cell_tables = in_hbm(
+        marine_skin_warmth.reshape(tiles, LANES),
+        depth_mean_current,
+        patch_neighbours,
+        interface_span,
+    )
+    rim_idx, rim_w, eta, eta_pack, eta_scale, far, near, odd = pl.pallas_call(
         prepare_kernel,
         in_specs=hbm(8),
-        out_specs=vmem(12),
+        out_specs=vmem(8),
         out_shape=(
-            shape_of(6, cells, dtype=jnp.int32),
-            shape_of(6, cells),
-            shape_of(2, cells),
             shape_of(2, 16, LANES, dtype=jnp.int32),
             shape_of(2, 16, LANES),
             cell_rows,
             pack_rows,
             scale_rows,
-            cell_rows,
             shape_of(ROWS_FIRST, LANES),
             shape_of(ROWS_FIRST, LANES),
             shape_of(8, elements, dtype=jnp.int32),
@@ -1010,7 +1032,11 @@
             pltpu.VMEM((points, 8, elements), jnp.float32),
             pltpu.VMEM((1, elements), jnp.float32),
             pltpu.VMEM((4, elements), jnp.int32),
-            dma((8,)),
+            pltpu.VMEM((2, 8, LANES), jnp.float32),
+            pltpu.VMEM((2, 2, OY), jnp.float32),
+            pltpu.VMEM((2, 6, OY), jnp.int32),
+            pltpu.VMEM((2, 6, OY), jnp.float32),
+            dma((12,)),
         ],
         compiler_params=PARAMS,
         name="prepare",
@@ -1018,31 +1044,28 @@
         air,
         breadth_hbm,
         pn_hbm,
-        *in_hbm(
-            water_elevation.reshape(tiles, LANES),
-            marine_skin_warmth.reshape(tiles, LANES),
-            depth_mean_current,
-            patch_neighbours,
-            interface_span,
-        ),
+        *in_hbm(water_elevation.reshape(tiles, LANES)),
+        *cell_tables,
     )
     first_far, first_near = swap_both(far, near)
 
     low_wind = pltpu.VMEM((points, 16, elements), jnp.bfloat16)
     low_row = pltpu.VMEM((1, blocks), jnp.int32)
-    flux, slots, breadth, pn, marks, idx, w, u, v = pl.pallas_call(
+    flux, slots, breadth, pn, marks, idx, w, u, v, sst = pl.pallas_call(
         lambda *refs: plan_kernel(*refs, devices=devices, tiles=tiles),
-        in_specs=hbm(8) + vmem(3),
-        out_specs=vmem(4) + smem(1) + vmem(4),
+        in_specs=hbm(12),
+        out_specs=vmem(4) + smem(1) + vmem(5),
         out_shape=(
             shape_of(points, 8, elements), shape_of(devices, LANES), shape_of(1, elements),
             shape_of(4, elements, dtype=jnp.int32), pltpu.SMEM((8, blocks), jnp.int32),
             shape_of(6 * tiles, LANES, dtype=jnp.int32), shape_of(6 * tiles, LANES),
-            cell_rows, cell_rows
+            cell_rows, cell_rows, cell_rows
         ),
         scratch_shapes=[
             pltpu.VMEM((points, 8, elements), jnp.float32), low_wind, low_wind,
-            low_row, low_row, low_row, pltpu.VMEM((8, blocks), jnp.int32), dma((8,))
+            low_row, low_row, low_row, pltpu.VMEM((6, cells), jnp.int32),
+            pltpu.VMEM((6, cells), jnp.float32), pltpu.VMEM((2, cells), jnp.float32),
+            pltpu.VMEM((8, blocks), jnp.int32), dma((12,))
         ],
         compiler_params=PARAMS,
         name="plan",
@@ -1057,9 +1080,10 @@
             transfer_across_tile.reshape(1, blocks),
             transfer_down_tile.reshape(1, blocks),
         ),
-        nb,
-        span,
-        flow,
+        cell_tables[2],
+        cell_tables[3],
+        cell_tables[1],
+        cell_tables[0],
     )
 
     home = pl.pallas_call(
@@ -1103,22 +1127,22 @@
 
     field = shape_of(points, levels, elements)
     edge = shape_of(4, levels, elements, dtype=jnp.bfloat16)
-    pack = shape_of(2 * levels, elements)
+    swap_rows = shape_of(4 * HALO + 2 * levels, elements)
     wind = shape_of(points, levels, elements, dtype=jnp.bfloat16)
-    loc, eastern, northern, east, west, east_pack, west_pack, edge_places = pl.pallas_call(
+    loc, eastern, northern, east, west, far, near, edge_places = pl.pallas_call(
         local_step_kernel,
-        in_specs=hbm(3) + vmem(2),
+        in_specs=hbm(3) + vmem(3),
         out_specs=vmem(8),
         out_shape=(
-            field, wind, wind, edge, edge, pack, pack, shape_of(8, elements, dtype=jnp.int32)
+            field, wind, wind, edge, edge, swap_rows, swap_rows,
+            shape_of(8, elements, dtype=jnp.int32)
         ),
         scratch_shapes=[pltpu.VMEM((points, levels, elements), jnp.float32), dma((3,))],
         compiler_params=PARAMS,
         name="local_step",
-    )(air, eastern, northern, breadth, pn)
+    )(air, eastern, northern, breadth, pn, odd)
 
     rim_scratch = pltpu.VMEM((4 * HALO, LANES), jnp.float32)
-    second_rows = shape_of(4 * HALO + 2 * levels, elements)
     flow_scratch = [
         pltpu.VMEM((3, tiles, LANES), jnp.float32),
         pltpu.VMEM((3, tiles // 2, LANES), jnp.int32),
@@ -1133,7 +1157,7 @@
         in_specs=vmem(16),
         out_specs=vmem(14) + hbm(1),
         out_shape=(
-            cell_rows, pack_rows, scale_rows, cell_rows, cell_rows, rim_rows, second_rows, second_rows,
+            cell_rows, pack_rows, scale_rows, cell_rows, cell_rows, rim_rows, swap_rows, swap_rows,
             cell_rows, cell_rows, rim_rows,
             shape_of(2, 16, LANES, dtype=jnp.int32), shape_of(2, 16, LANES),
             cell_rows, pltpu.HBM((devices, CAP, LANES), jnp.float32),
@@ -1143,11 +1167,12 @@
             pltpu.VMEM((devices, CAP, LANES), jnp.float32),
             dma((1,)),
         ],
+        input_output_aliases={13: 6, 14: 7},
         compiler_params=PARAMS,
         name="first_ocean",
     )(
         arrived, first_far, first_near, odd, gx, gy, eta, u, v, idx, w, rim_idx, rim_w,
-        east_pack, west_pack, base
+        far, near, base
     )
     far, near = swap_both(far, near)
     edges_far, edges_near = far, near

time: 52.4 us -> 52.1 us (level)
  no operation moved by 1% of the time
where the time goes in v5:
time: 52.1 us; the launch traced here: 51.8 us
  starting transfers between devices  23.9 us (46%)
  Pallas kernels  18.8 us (36%)
  waiting for transfers between devices  8.33 us (16%)
  between operations  0.77 us (1%)
    ppermute x8, starting transfers between devices, swapped(): return lax.ppermute(value, RING, pairs)  17 us
    all_to_all x2, starting transfers between devices, exchange(): return lax.all_to_all(value, RING, split_axis=0, concat_axis=0, tiled=True)  6.91 us
    all_to_all x2, waiting for transfers between devices, exchange(): return lax.all_to_all(value, RING, split_axis=0, concat_axis=0, tiled=True)  4.46 us
    ppermute x8, waiting for transfers between devices, swapped(): return lax.ppermute(value, RING, pairs)  3.87 us
    pallas_call x2, Pallas kernels, shards(): pl.pallas_call(inner_kernel, in_specs=vmem(9), out_specs=vmem(3), out_sha...  2.57 us
    pallas_call x1, Pallas kernels, shards(): pl.pallas_call(lambda *refs: plan_kernel(*refs, devices=devices, tiles=ti...  2.18 us
    pallas_call x1, Pallas kernels, shards(): pl.pallas_call(local_step_kernel, in_specs=hbm(3) + vmem(3), out_specs=vm...  2.05 us
    pallas_call x1, Pallas kernels, shards(): pl.pallas_call(second_step_kernel, in_specs=vmem(14), out_specs=pl.BlockS...  1.8 us
  transfers between devices with their start and end apart: 10, of which 5 were waited for; matrix products, arithmetic and copies ran while one was open for 0% of the time, Pallas kernels for 25%

profile of v5, /device:TPU:0, one launch (start us, length us, event | category | flops | bytes accessed | tf_op | source)
XLA Modules:
  0.0 51.8 jit_solution(10991879919012037509)
XLA Ops:
  0.6 0.0 copy-start
  0.6 1.5 %prepare.1 = (s32[2,16,128]{2,1,0:T(8,128)S(1)}, f32[2,16,128]{2,1,0:T(8,128)S(1)}, f32[32,128]{1,0:T(8,128)S(1)}, s32[16,128]{1,0:T(8,128)S(1)}, f32[8,128]{1,0...) custom-call(f32[16,64,128]{2,1,0:T(8,128)} %air_hbm.3, f32[1,128]{1,0:T(1,128)} %bitcast.11, ...), custom_call_target="tpu_custom_call" | custom-call | tf_op jit(solution)/shard_map/prepare/pallas_call | solution.py:1015
  2.1 6.4 %collective-permute-start = (f32[56,128]{1,0:T(8,128)S(1)}, f32[56,128]{1,0:T(8,128)S(1)}, u32[]{:S(2)}, u32[]{:S(2)}) collective-permute-start(f32[56,128]{1,0:T(8,128)S(1)} %get-tuple-element.89), channel_id=1, source_target_pairs={{1,2},{2,1},{3,4},{4,3},{5,6},{6,5},{7,8},{8,7},{9,10},{10,9},{11,... | collective-permute-start | bytes 86024 | tf_op jit(solution)/shard_map/ppermute | solution.py:42
  8.6 0.0 collective-permute-start.1
  8.6 2.2 %plan.1 = (f32[16,8,128]{2,1,0:T(8,128)S(1)}, f32[32,128]{1,0:T(8,128)S(1)}, f32[1,128]{1,0:T(1,128)S(1)}, s32[4,128]{1,0:T(4,128)S(1)}, s32[8,32]{1,0:T(8,128)S...) custom-call(f32[16,64,128]{2,1,0:T(8,128)} %air_hbm.3, ...), custom_call_target="tpu_custom_call" | custom-call | tf_op jit(solution)/shard_map/plan/pallas_call | solution.py:1054
  10.8 0.0 copy-done
  10.8 0.4 home_sums.1.refs_1_
  11.1 0.0 collective-permute-done.refs_6_.first_far
  11.1 1.3 %collective-permute-done.1.refs_7_.first_near = f32[56,128]{1,0:T(8,128)S(1)} collective-permute-done((f32[56,128]{1,0:T(8,128)S(1)}, f32[56,128]{1,0:T(8,128)S(1)}, u32[]{:S(2)}, u32[]{:S(2)}) %collective-permute-start.1) | collective-permute-done | bytes 28704 | tf_op jit(solution)/shard_map/ppermute | solution.py:42
  12.4 1.0 %forward_remap.1 = bf16[32,16,128]{2,1,0:T(8,128)(2,1)} custom-call(s32[8,32]{1,0:T(8,128)S(4)} %get-tuple-element.85.marks.refs_0_, f32[256,128]{1,0:T(8,128)S(1)} %home_sums.1.refs_1_, f32[16,8,128]{2,1,0:T(8,128)S(1)} %get-tuple-element.86.flux.refs_2_, f32[32,128]{1,0:T(8,128)S(1)} %get-tuple-element.87.refs_3_, ...), custom_call_target="tpu_custom_call" | custom-call | tf_op jit(solution)/shard_map/forward_remap/pallas_call | solution.py:1097
  13.5 3.4 %all-to-all-start = ((bf16[32,16,128]{2,1,0:T(8,128)(2,1)}), bf16[32,16,128]{2,1,0:T(8,128)(2,1)S(1)}, u32[]{:S(2)}, u32[]{:S(2)}) async-start(bf16[32,16,128]{2,1,0:T(8,128)(2,1)} %forward_remap.1), calls=%async_computation | async-start | bytes 262144 | tf_op jit(solution)/shard_map/all_to_all | solution.py:80
  16.9 2.1 %local_step.1 = (f32[16,64,128]{2,1,0:T(8,128)S(1)}, bf16[16,64,128]{2,1,0:T(8,128)(2,1)S(1)}, bf16[16,64,128]{2,1,0:T(8,128)(2,1)S(1)}, bf16[4,64,128]{2,1,0:T(...) custom-call(f32[16,64,128]{2,1,0:T(8,128)} %air_hbm.3, ...), custom_call_target="tpu_custom_call" | custom-call | tf_op jit(solution)/shard_map/local_step/pallas_call | solution.py:1132
  18.9 1.2 %first_gradient.1 = (f32[32,128]{1,0:T(8,128)S(1)}, f32[32,128]{1,0:T(8,128)S(1)}, f32[32,128]{1,0:T(8,128)S(1)}) custom-call(s32[192,128]{1,0:T(8,128)S(1)} %get-tuple-element.100.idx, f32[192,128]{1,0:T(8,128)S(1)} %get-tuple-element.101.w, f32[32,128]{1,0:T(8,128)S(1)} %get-tuple-element.102.eta, s32[16,128]{1,0:T(8,128)S(1)} %get-tuple-element.103.eta_pack, ...), custom_call_target="tpu_custom_call" | custom-call | tf_op jit(solution)/shard_map/first_gradient/pallas_call | solution.py:1114
  20.1 4.5 %all-to-all-done.arrived = bf16[32,16,128]{2,1,0:T(8,128)(2,1)S(1)} async-done(((bf16[32,16,128]{2,1,0:T(8,128)(2,1)}), bf16[32,16,128]{2,1,0:T(8,128)(2,1)S(1)}, u32[]{:S(2)}, u32[]{:S(2)}) %all-to-all-start) | async-done | bytes 131104 | tf_op jit(solution)/shard_map/all_to_all | solution.py:80
  24.6 1.6 %first_ocean.1 = (f32[32,128]{1,0:T(8,128)S(1)}, s32[16,128]{1,0:T(8,128)S(1)}, f32[8,128]{1,0:T(8,128)S(1)}, f32[32,128]{1,0:T(8,128)S(1)}, f32[32,128]{1,0:T(8...) custom-call(bf16[32,16,128]{2,1,0:T(8,128)(2,1)S(1)} %all-to-all-don, ...), custom_call_target="tpu_custom_call", output_to_operand_aliasing={{6}: (13, {}), {7}: (14, {})} | custom-call | tf_op jit(solution)/shard_map/first_ocean/pallas_call | solution.py:1155
  26.2 1.7 %collective-permute-start.2 = (f32[136,128]{1,0:T(8,128)S(1)}, f32[136,128]{1,0:T(8,128)S(1)}, u32[]{:S(2)}, u32[]{:S(2)}) collective-permute-start(f32[136,128]{1,0:T(8,128)S(1)} %get-tuple-element.115), channel_id=1, source_target_pairs={{1,2},{2,1},{3,4},{4,3},{5,6},{6,5},{7,8},{8,7},{9,10},{10,9},{11,... | collective-permute-start | bytes 208904 | tf_op jit(solution)/shard_map/ppermute | solution.py:42
  27.9 0.8 %collective-permute-start.3 = (f32[136,128]{1,0:T(8,128)S(1)}, f32[136,128]{1,0:T(8,128)S(1)}, u32[]{:S(2)}, u32[]{:S(2)}) collective-permute-start(f32[136,128]{1,0:T(8,128)S(1)} %get-tuple-element.116), channel_id=1, source_target_pairs={{0,1},{1,0},{2,3},{3,2},{4,5},{5,4},{6,7},{7,6},{8,9},{9,8},{10,11... | collective-permute-start | bytes 208904 | tf_op jit(solution)/shard_map/ppermute | solution.py:42
  28.8 0.6 %current.1 = (f32[32,128]{1,0:T(8,128)S(1)}, f32[32,128]{1,0:T(8,128)S(1)}) custom-call(s32[192,128]{1,0:T(8,128)S(1)} %get-tuple-element.100.idx, f32[192,128]{1,0:T(8,128)S(1)} %get-tuple-element.101.w, f32[32,128]{1,0:T(8,128)S(1)} %get-tuple-element.118.eta, s32[16,128]{1,0:T(8,128)S(1)} %get-tuple-element.120.eta_pack, ...), custom_call_target="tpu_custom_call" | custom-call | tf_op jit(solution)/shard_map/current/pallas_call | solution.py:1182
  29.3 3.5 %all-to-all-start.1 = ((f32[32,2,128]{2,1,0:T(2,128)}), f32[32,2,128]{2,1,0:T(2,128)S(1)}, u32[]{:S(2)}, u32[]{:S(2)}) async-start(f32[32,2,128]{2,1,0:T(2,128)} %get-tuple-element.139), calls=%async_computation.1 | async-start | bytes 65536 | tf_op jit(solution)/shard_map/all_to_all | solution.py:80
  32.9 0.8 %height.1.eta_part = f32[32,128]{1,0:T(8,128)S(1)} custom-call(s32[192,128]{1,0:T(8,128)S(1)} %get-tuple-element.100.idx, f32[192,128]{1,0:T(8,128)S(1)} %get-tuple-element.101.w, f32[32,128]{1,0:T(8,128)S(1)} %get-tuple-element.118.eta, f32[32,128]{1,0:T(8,128)S(1)} %get-tuple-element.127.u_part, f32[32,128]{1,0:T(8,128)S(1)} %get-tuple-element.128.v_part), custom_call_target="tpu_custom_call" | custom-call | tf_op jit(solution)/shard_map/height/pallas_call | solution.py:1192
  33.6 0.4 collective-permute-done.2.far
  34.0 0.0 collective-permute-done.3.near.near_swap
  34.0 0.8 %ocean.2 = (f32[32,128]{1,0:T(8,128)S(1)}, s32[16,128]{1,0:T(8,128)S(1)}, f32[8,128]{1,0:T(8,128)S(1)}, f32[32,128]{1,0:T(8,128)S(1)}, f32[32,128]{1,0:T(8,128)S...) custom-call(f32[136,128]{1,0:T(8,128)S(1)} %collective-permute-done.2.far, ...), custom_call_target="tpu_custom_call" | custom-call | tf_op jit(solution)/shard_map/ocean/pallas_call | solution.py:1231
  34.8 4.9 %collective-permute-start.4 = (f32[8,128]{1,0:T(8,128)S(1)}, f32[8,128]{1,0:T(8,128)S(1)}, u32[]{:S(2)}, u32[]{:S(2)}) collective-permute-start(f32[8,128]{1,0:T(8,128)S(1)} %get-tuple-element.143), channel_id=1, source_target_pairs={{1,2},{2,1},{3,4},{4,3},{5,6},{6,5},{7,8},{8,7},{9,10},{10,9},{11,... | collective-permute-start | bytes 12296 | tf_op jit(solution)/shard_map/ppermute | solution.py:42
  39.7 0.0 collective-permute-start.5
  39.7 1.3 %inner.2 = (f32[32,128]{1,0:T(8,128)S(1)}, f32[32,128]{1,0:T(8,128)S(1)}, f32[32,128]{1,0:T(8,128)S(1)}) custom-call(s32[192,128]{1,0:T(8,128)S(1)} %get-tuple-element.100.idx, f32[192,128]{1,0:T(8,128)S(1)} %get-tuple-element.101.w, f32[32,128]{1,0:T(8,128)S(1)} %get-tuple-element.133.eta, s32[16,128]{1,0:T(8,128)S(1)} %get-tuple-element.134.eta_pack, ...), custom_call_target="tpu_custom_call" | custom-call | tf_op jit(solution)/shard_map/inner/pallas_call | solution.py:1202
  41.0 0.0 all-to-all-done.1.arrived
  41.0 0.7 %back_remap.1.surface = f32[16,128]{1,0:T(8,128)S(1)} custom-call(s32[8,32]{1,0:T(8,128)S(4)} %get-tuple-element.85.marks.refs_0_, f32[32,2,128]{2,1,0:T(2,128)S(1)} %all-to-all-done.1.arrived, bf16[32,128,128]{2,1,0:T(8,128)(2,1)S(1)} %copy-done), custom_call_target="tpu_custom_call" | custom-call | tf_op jit(solution)/shard_map/back_remap/pallas_call | solution.py:1213
  41.7 0.0 collective-permute-done.4.far
  41.7 1.6 %collective-permute-done.5.near = f32[8,128]{1,0:T(8,128)S(1)} collective-permute-done((f32[8,128]{1,0:T(8,128)S(1)}, f32[8,128]{1,0:T(8,128)S(1)}, u32[]{:S(2)}, u32[]{:S(2)}) %collective-permute-start.5) | collective-permute-done | bytes 4128 | tf_op jit(solution)/shard_map/ppermute | solution.py:42
  43.3 0.8 %ocean.3 = (f32[32,128]{1,0:T(8,128)S(1)}, s32[16,128]{1,0:T(8,128)S(1)}, f32[8,128]{1,0:T(8,128)S(1)}, f32[32,128]{1,0:T(8,128)S(1)}, f32[32,128]{1,0:T(8,128)S...) custom-call(f32[8,128]{1,0:T(8,128)S(1)} %collective-permute-done.4.far, ...), custom_call_target="tpu_custom_call" | custom-call | tf_op jit(solution)/shard_map/ocean/pallas_call | solution.py:1231
  44.0 3.1 %collective-permute-start.6 = (f32[8,128]{1,0:T(8,128)S(1)}, f32[8,128]{1,0:T(8,128)S(1)}, u32[]{:S(2)}, u32[]{:S(2)}) collective-permute-start(f32[8,128]{1,0:T(8,128)S(1)} %get-tuple-element.149), channel_id=1, source_target_pairs={{1,2},{2,1},{3,4},{4,3},{5,6},{6,5},{7,8},{8,7},{9,10},{10,9},{11,... | collective-permute-start | bytes 12296 | tf_op jit(solution)/shard_map/ppermute | solution.py:42
  47.1 0.0 collective-permute-start.7
  47.1 1.8 %second_step.1 = f32[16,64,128]{2,1,0:T(8,128)} custom-call(f32[16,64,128]{2,1,0:T(8,128)S(1)} %get-tuple-element.94.loc, bf16[16,64,128]{2,1,0:T(8,128)(2,1)S(1)} %get-tuple-element.95.eastern, bf16[16,64,128]{2,1,0:T(8,128)(2,1)S(1)} %get-tuple-element.96.northern, f32[1,128]{1,0:T(1,128)S(1)} %get-tuple-element.84.refs_4_.breadth, ...), custom_call_target="tpu_custom_call" | custom-call | tf_op jit(solution)/shard_map/second_step/pallas_call | solution.py:1252
  48.9 1.3 %inner.3 = (f32[32,128]{1,0:T(8,128)S(1)}, f32[32,128]{1,0:T(8,128)S(1)}, f32[32,128]{1,0:T(8,128)S(1)}) custom-call(s32[192,128]{1,0:T(8,128)S(1)} %get-tuple-element.100.idx, f32[192,128]{1,0:T(8,128)S(1)} %get-tuple-element.101.w, f32[32,128]{1,0:T(8,128)S(1)} %get-tuple-element.151.eta, s32[16,128]{1,0:T(8,128)S(1)} %get-tuple-element.152.eta_pack, ...), custom_call_target="tpu_custom_call" | custom-call | tf_op jit(solution)/shard_map/inner/pallas_call | solution.py:1202
  50.2 0.5 collective-permute-done.6.far
  50.7 0.0 collective-permute-done.7.near
  50.8 1.0 %last_ocean.1 = (f32[32,128]{1,0:T(8,128)}, f32[2,4096]{1,0:T(2,128)}, f32[32,128]{1,0:T(8,128)}) custom-call(f32[8,128]{1,0:T(8,128)S(1)} %collective-permute-done.6.far, f32[8,128]{1,0:T(8,128)S(1)} %collective-permute-done.7.near, s32[8,128]{1,0:T(8,128)S(1)} %get-tuple-element.91.refs_8_.odd, f32[32,128]{1,0:T(8,128)S(1)} %get-tuple-element.151.eta, ...), custom_call_target="tpu_custom_call" | custom-call | tf_op jit(solution)/shard_map/last_ocean/pallas_call | solution.py:1242
Async XLA Ops:
  0.6 10.1 %copy-start = (bf16[32,128,128]{2,1,0:T(8,128)(2,1)S(1)}, bf16[32,128,128]{2,1,0:T(8,128)(2,1)}, u32[]{:S(2)}) copy-start(bf16[32,128,128]{2,1,0:T(8,128)(2,1)} %weights.3) | copy-start | bytes 3145732
  2.1 9.0 %collective-permute-start = (f32[56,128]{1,0:T(8,128)S(1)}, f32[56,128]{1,0:T(8,128)S(1)}, u32[]{:S(2)}, u32[]{:S(2)}) collective-permute-start(f32[56,128]{1,0:T(8,128)S(1)} %get-tuple-element.89), channel_id=1, source_target_pairs={{1,2},{2,1},{3,4},{4,3},{5,6},{6,5},{7,8},{8,7},{9,10},{10,9},{11,... | collective-permute-start | bytes 86024 | tf_op jit(solution)/shard_map/ppermute | solution.py:42
  8.6 3.9 %collective-permute-start.1 = (f32[56,128]{1,0:T(8,128)S(1)}, f32[56,128]{1,0:T(8,128)S(1)}, u32[]{:S(2)}, u32[]{:S(2)}) collective-permute-start(f32[56,128]{1,0:T(8,128)S(1)} %get-tuple-element.90), channel_id=1, source_target_pairs={{0,1},{1,0},{2,3},{3,2},{4,5},{5,4},{6,7},{7,6},{8,9},{9,8},{10,11... | collective-permute-start | bytes 86024 | tf_op jit(solution)/shard_map/ppermute | solution.py:42
  13.5 11.1 %all-to-all-start = ((bf16[32,16,128]{2,1,0:T(8,128)(2,1)}), bf16[32,16,128]{2,1,0:T(8,128)(2,1)S(1)}, u32[]{:S(2)}, u32[]{:S(2)}) async-start(bf16[32,16,128]{2,1,0:T(8,128)(2,1)} %forward_remap.1), calls=%async_computation | async-start | bytes 262144 | tf_op jit(solution)/shard_map/all_to_all | solution.py:80
  26.2 7.8 %collective-permute-start.2 = (f32[136,128]{1,0:T(8,128)S(1)}, f32[136,128]{1,0:T(8,128)S(1)}, u32[]{:S(2)}, u32[]{:S(2)}) collective-permute-start(f32[136,128]{1,0:T(8,128)S(1)} %get-tuple-element.115), channel_id=1, source_target_pairs={{1,2},{2,1},{3,4},{4,3},{5,6},{6,5},{7,8},{8,7},{9,10},{10,9},{11,... | collective-permute-start | bytes 208904 | tf_op jit(solution)/shard_map/ppermute | solution.py:42
  27.9 6.1 %collective-permute-start.3 = (f32[136,128]{1,0:T(8,128)S(1)}, f32[136,128]{1,0:T(8,128)S(1)}, u32[]{:S(2)}, u32[]{:S(2)}) collective-permute-start(f32[136,128]{1,0:T(8,128)S(1)} %get-tuple-element.116), channel_id=1, source_target_pairs={{0,1},{1,0},{2,3},{3,2},{4,5},{5,4},{6,7},{7,6},{8,9},{9,8},{10,11... | collective-permute-start | bytes 208904 | tf_op jit(solution)/shard_map/ppermute | solution.py:42
  29.3 11.6 %all-to-all-start.1 = ((f32[32,2,128]{2,1,0:T(2,128)}), f32[32,2,128]{2,1,0:T(2,128)S(1)}, u32[]{:S(2)}, u32[]{:S(2)}) async-start(f32[32,2,128]{2,1,0:T(2,128)} %get-tuple-element.139), calls=%async_computation.1 | async-start | bytes 65536 | tf_op jit(solution)/shard_map/all_to_all | solution.py:80
  34.8 6.9 %collective-permute-start.4 = (f32[8,128]{1,0:T(8,128)S(1)}, f32[8,128]{1,0:T(8,128)S(1)}, u32[]{:S(2)}, u32[]{:S(2)}) collective-permute-start(f32[8,128]{1,0:T(8,128)S(1)} %get-tuple-element.143), channel_id=1, source_target_pairs={{1,2},{2,1},{3,4},{4,3},{5,6},{6,5},{7,8},{8,7},{9,10},{10,9},{11,... | collective-permute-start | bytes 12296 | tf_op jit(solution)/shard_map/ppermute | solution.py:42
  39.7 3.6 %collective-permute-start.5 = (f32[8,128]{1,0:T(8,128)S(1)}, f32[8,128]{1,0:T(8,128)S(1)}, u32[]{:S(2)}, u32[]{:S(2)}) collective-permute-start(f32[8,128]{1,0:T(8,128)S(1)} %get-tuple-element.144), channel_id=1, source_target_pairs={{0,1},{1,0},{2,3},{3,2},{4,5},{5,4},{6,7},{7,6},{8,9},{9,8},{10,11... | collective-permute-start | bytes 12296 | tf_op jit(solution)/shard_map/ppermute | solution.py:42
  44.0 6.7 %collective-permute-start.6 = (f32[8,128]{1,0:T(8,128)S(1)}, f32[8,128]{1,0:T(8,128)S(1)}, u32[]{:S(2)}, u32[]{:S(2)}) collective-permute-start(f32[8,128]{1,0:T(8,128)S(1)} %get-tuple-element.149), channel_id=1, source_target_pairs={{1,2},{2,1},{3,4},{4,3},{5,6},{6,5},{7,8},{8,7},{9,10},{10,9},{11,... | collective-permute-start | bytes 12296 | tf_op jit(solution)/shard_map/ppermute | solution.py:42
  47.1 3.6 %collective-permute-start.7 = (f32[8,128]{1,0:T(8,128)S(1)}, f32[8,128]{1,0:T(8,128)S(1)}, u32[]{:S(2)}, u32[]{:S(2)}) collective-permute-start(f32[8,128]{1,0:T(8,128)S(1)} %get-tuple-element.150), channel_id=1, source_target_pairs={{0,1},{1,0},{2,3},{3,2},{4,5},{5,4},{6,7},{7,6},{8,9},{9,8},{10,11... | collective-permute-start | bytes 12296 | tf_op jit(solution)/shard_map/ppermute | solution.py:42

commit v6 on v5

--- a/solution.py
+++ b/solution.py
@@ -596,7 +596,8 @@
     up, dn, air, breadth, pn, sst, flow, nb, span, sems
 ):
     tiles, cells = eta.shape[0], nb_hbm.shape[1]
-    pairs = [(eta_hbm, eta)]
+    pairs = [(air_hbm.at[:, 3 * side, pl.ds(0, 8), :], air.at[side]) for side in (0, 1)]
+    pairs.append((eta_hbm, eta))
     for side, at in ((0, 0), (1, cells - OY)):
         cut = pl.ds(at, OY)
         pairs.append((nb_hbm.at[:, cut], nb.at[side]))
@@ -606,7 +607,6 @@
         pairs.append((sst_hbm.at[pl.ds(at, 8)], sst.at[side]))
     pairs.append((breadth_hbm, breadth))
     pairs.append((pn_hbm, pn))
-    pairs.append((air_hbm.at[:, pl.ds(0, 8), :], air))
     copies = load(pairs, sems)
     for copy in copies:
         copy.wait()
@@ -627,8 +627,7 @@
     for side, first, target in ((0, 0, dn), (1, tiles - HALO, up)):
         target[...] = jnp.zeros_like(target)
         for n in range(4):
-            p = 4 * n if side == 0 else 3 + 4 * n
-            target[ROW_EDGE + n : ROW_EDGE + n + 1] = air[p, 0:1]
+            target[ROW_EDGE + n : ROW_EDGE + n + 1] = air[side, n, 0:1]
         target[ROW_BREADTH : ROW_BREADTH + 1] = breadth[...]
         part_x, part_y = rim_partial(
             rim_idx[side], rim_w[side], eta, eta_pack, eta_scale, first
@@ -918,7 +917,7 @@
     heat[...] = forcing[0:tiles, 0:LANES]
     half = (base[...] + WARMING_COEFF * forcing[0:tiles, 0:LANES]).astype(jnp.bfloat16)
     for j in range(CAP):
-        answers[:, j, :] = jnp.dot(
+        answers[pl.ds(j, devices, stride=CAP), :] = jnp.dot(
             chosen[j][:, 0:tiles], half, preferred_element_type=jnp.float32
         )
     fu[...] = forcing[0:tiles, LANES : 2 * LANES]
@@ -1029,19 +1028,19 @@
         scratch_shapes=[
             pltpu.VMEM((ROWS_FIRST, LANES), jnp.float32),
             pltpu.VMEM((ROWS_FIRST, LANES), jnp.float32),
-            pltpu.VMEM((points, 8, elements), jnp.float32),
+            pltpu.VMEM((2, 4, 8, elements), jnp.float32),
             pltpu.VMEM((1, elements), jnp.float32),
             pltpu.VMEM((4, elements), jnp.int32),
             pltpu.VMEM((2, 8, LANES), jnp.float32),
             pltpu.VMEM((2, 2, OY), jnp.float32),
             pltpu.VMEM((2, 6, OY), jnp.int32),
             pltpu.VMEM((2, 6, OY), jnp.float32),
-            dma((12,)),
+            dma((13,)),
         ],
         compiler_params=PARAMS,
         name="prepare",
     )(
-        air,
+        *in_hbm(air_warmth.reshape(4, 4, levels, elements)),
         breadth_hbm,
         pn_hbm,
         *in_hbm(water_elevation.reshape(tiles, LANES)),
@@ -1160,11 +1159,11 @@
             cell_rows, pack_rows, scale_rows, cell_rows, cell_rows, rim_rows, swap_rows, swap_rows,
             cell_rows, cell_rows, rim_rows,
             shape_of(2, 16, LANES, dtype=jnp.int32), shape_of(2, 16, LANES),
-            cell_rows, pltpu.HBM((devices, CAP, LANES), jnp.float32),
+            cell_rows, pltpu.HBM((devices * CAP, LANES), jnp.float32),
         ),
         scratch_shapes=flow_scratch + [rim_scratch] * 3 + [
             pltpu.VMEM((devices * PER_DEST, LANES), jnp.float32),
-            pltpu.VMEM((devices, CAP, LANES), jnp.float32),
+            pltpu.VMEM((devices * CAP, LANES), jnp.float32),
             dma((1,)),
         ],
         input_output_aliases={13: 6, 14: 7},
@@ -1188,7 +1187,7 @@
                 name="current",
             )(idx, w, eta, eta_pack, eta_scale, u, v, fu, fv)
             answers, u_part = lax.optimization_barrier((answers, u_part))
-            answered = exchange(answers)
+            answered = exchange(answers.reshape(devices, CAP, LANES))
             eta_part = pl.pallas_call(
                 height_kernel,
                 in_specs=vmem(5),

time: 52.1 us -> 51.9 us (level)
  no operation moved by 1% of the time
where the time goes in v6:
time: 51.9 us; the launch traced here: 51.7 us
  starting transfers between devices  23.9 us (46%)
  Pallas kernels  18.7 us (36%)
  waiting for transfers between devices  8.33 us (16%)
  between operations  0.77 us (1%)
    ppermute x8, starting transfers between devices, swapped(): return lax.ppermute(value, RING, pairs)  17 us
    all_to_all x2, starting transfers between devices, exchange(): return lax.all_to_all(value, RING, split_axis=0, concat_axis=0, tiled=True)  6.92 us
    all_to_all x2, waiting for transfers between devices, exchange(): return lax.all_to_all(value, RING, split_axis=0, concat_axis=0, tiled=True)  4.46 us
    ppermute x8, waiting for transfers between devices, swapped(): return lax.ppermute(value, RING, pairs)  3.87 us
    pallas_call x2, Pallas kernels, shards(): pl.pallas_call(inner_kernel, in_specs=vmem(9), out_specs=vmem(3), out_sha...  2.57 us
    pallas_call x1, Pallas kernels, shards(): pl.pallas_call(lambda *refs: plan_kernel(*refs, devices=devices, tiles=ti...  2.18 us
    pallas_call x1, Pallas kernels, shards(): pl.pallas_call(local_step_kernel, in_specs=hbm(3) + vmem(3), out_specs=vm...  2.05 us
    pallas_call x1, Pallas kernels, shards(): pl.pallas_call(second_step_kernel, in_specs=vmem(14), out_specs=pl.BlockS...  1.8 us
  transfers between devices with their start and end apart: 10, of which 5 were waited for; matrix products, arithmetic and copies ran while one was open for 0% of the time, Pallas kernels for 25%

profile of v6, /device:TPU:0, one launch (start us, length us, event | category | flops | bytes accessed | tf_op | source)
XLA Modules:
  0.0 51.7 jit_solution(821348576189272653)
XLA Ops:
  0.6 0.0 copy-start
  0.6 1.3 %prepare.1 = (s32[2,16,128]{2,1,0:T(8,128)S(1)}, f32[2,16,128]{2,1,0:T(8,128)S(1)}, f32[32,128]{1,0:T(8,128)S(1)}, s32[16,128]{1,0:T(8,128)S(1)}, f32[8,128]{1,0...) custom-call(f32[4,4,64,128]{3,2,1,0:T(8,128)} %bitcast.10, f32[1,128]{1,0:T(1,128)} %bitcast.14, ...), custom_call_target="tpu_custom_call" | custom-call | tf_op jit(solution)/shard_map/prepare/pallas_call | solution.py:1014
  2.0 6.4 %collective-permute-start = (f32[56,128]{1,0:T(8,128)S(1)}, f32[56,128]{1,0:T(8,128)S(1)}, u32[]{:S(2)}, u32[]{:S(2)}) collective-permute-start(f32[56,128]{1,0:T(8,128)S(1)} %get-tuple-element.89), channel_id=1, source_target_pairs={{1,2},{2,1},{3,4},{4,3},{5,6},{6,5},{7,8},{8,7},{9,10},{10,9},{11,... | collective-permute-start | bytes 86024 | tf_op jit(solution)/shard_map/ppermute | solution.py:42
  8.4 0.0 collective-permute-start.1
  8.4 2.2 %plan.1 = (f32[16,8,128]{2,1,0:T(8,128)S(1)}, f32[32,128]{1,0:T(8,128)S(1)}, f32[1,128]{1,0:T(1,128)S(1)}, s32[4,128]{1,0:T(4,128)S(1)}, s32[8,32]{1,0:T(8,128)S...) custom-call(f32[16,64,128]{2,1,0:T(8,128)} %air_hbm.1, ...), custom_call_target="tpu_custom_call" | custom-call | tf_op jit(solution)/shard_map/plan/pallas_call | solution.py:1053
  10.6 0.0 copy-done
  10.6 0.4 home_sums.1.refs_1_
  11.0 0.0 collective-permute-done.refs_6_.first_far
  11.0 1.3 %collective-permute-done.1.refs_7_.first_near = f32[56,128]{1,0:T(8,128)S(1)} collective-permute-done((f32[56,128]{1,0:T(8,128)S(1)}, f32[56,128]{1,0:T(8,128)S(1)}, u32[]{:S(2)}, u32[]{:S(2)}) %collective-permute-start.1) | collective-permute-done | bytes 28704 | tf_op jit(solution)/shard_map/ppermute | solution.py:42
  12.3 1.0 %forward_remap.1 = bf16[32,16,128]{2,1,0:T(8,128)(2,1)} custom-call(s32[8,32]{1,0:T(8,128)S(4)} %get-tuple-element.85.marks.refs_0_, f32[256,128]{1,0:T(8,128)S(1)} %home_sums.1.refs_1_, f32[16,8,128]{2,1,0:T(8,128)S(1)} %get-tuple-element.86.flux.refs_2_, f32[32,128]{1,0:T(8,128)S(1)} %get-tuple-element.87.refs_3_, ...), custom_call_target="tpu_custom_call" | custom-call | tf_op jit(solution)/shard_map/forward_remap/pallas_call | solution.py:1096
  13.3 3.4 %all-to-all-start = ((bf16[32,16,128]{2,1,0:T(8,128)(2,1)}), bf16[32,16,128]{2,1,0:T(8,128)(2,1)S(1)}, u32[]{:S(2)}, u32[]{:S(2)}) async-start(bf16[32,16,128]{2,1,0:T(8,128)(2,1)} %forward_remap.1), calls=%async_computation | async-start | bytes 262144 | tf_op jit(solution)/shard_map/all_to_all | solution.py:80
  16.7 2.0 %local_step.1 = (f32[16,64,128]{2,1,0:T(8,128)S(1)}, bf16[16,64,128]{2,1,0:T(8,128)(2,1)S(1)}, bf16[16,64,128]{2,1,0:T(8,128)(2,1)S(1)}, bf16[4,64,128]{2,1,0:T(...) custom-call(f32[16,64,128]{2,1,0:T(8,128)} %air_hbm.1, ...), custom_call_target="tpu_custom_call" | custom-call | tf_op jit(solution)/shard_map/local_step/pallas_call | solution.py:1131
  18.8 1.2 %first_gradient.1 = (f32[32,128]{1,0:T(8,128)S(1)}, f32[32,128]{1,0:T(8,128)S(1)}, f32[32,128]{1,0:T(8,128)S(1)}) custom-call(s32[192,128]{1,0:T(8,128)S(1)} %get-tuple-element.100.idx, f32[192,128]{1,0:T(8,128)S(1)} %get-tuple-element.101.w, f32[32,128]{1,0:T(8,128)S(1)} %get-tuple-element.102.eta, s32[16,128]{1,0:T(8,128)S(1)} %get-tuple-element.103.eta_pack, ...), custom_call_target="tpu_custom_call" | custom-call | tf_op jit(solution)/shard_map/first_gradient/pallas_call | solution.py:1113
  20.0 4.5 %all-to-all-done.arrived = bf16[32,16,128]{2,1,0:T(8,128)(2,1)S(1)} async-done(((bf16[32,16,128]{2,1,0:T(8,128)(2,1)}), bf16[32,16,128]{2,1,0:T(8,128)(2,1)S(1)}, u32[]{:S(2)}, u32[]{:S(2)}) %all-to-all-start) | async-done | bytes 131104 | tf_op jit(solution)/shard_map/all_to_all | solution.py:80
  24.5 1.6 %first_ocean.1 = (f32[32,128]{1,0:T(8,128)S(1)}, s32[16,128]{1,0:T(8,128)S(1)}, f32[8,128]{1,0:T(8,128)S(1)}, f32[32,128]{1,0:T(8,128)S(1)}, f32[32,128]{1,0:T(8...) custom-call(bf16[32,16,128]{2,1,0:T(8,128)(2,1)S(1)} %all-to-all-don, ...), custom_call_target="tpu_custom_call", output_to_operand_aliasing={{6}: (13, {}), {7}: (14, {})} | custom-call | tf_op jit(solution)/shard_map/first_ocean/pallas_call | solution.py:1154
  26.1 1.7 %collective-permute-start.2 = (f32[136,128]{1,0:T(8,128)S(1)}, f32[136,128]{1,0:T(8,128)S(1)}, u32[]{:S(2)}, u32[]{:S(2)}) collective-permute-start(f32[136,128]{1,0:T(8,128)S(1)} %get-tuple-element.115), channel_id=1, source_target_pairs={{1,2},{2,1},{3,4},{4,3},{5,6},{6,5},{7,8},{8,7},{9,10},{10,9},{11,... | collective-permute-start | bytes 208904 | tf_op jit(solution)/shard_map/ppermute | solution.py:42
  27.8 0.8 %collective-permute-start.3 = (f32[136,128]{1,0:T(8,128)S(1)}, f32[136,128]{1,0:T(8,128)S(1)}, u32[]{:S(2)}, u32[]{:S(2)}) collective-permute-start(f32[136,128]{1,0:T(8,128)S(1)} %get-tuple-element.116), channel_id=1, source_target_pairs={{0,1},{1,0},{2,3},{3,2},{4,5},{5,4},{6,7},{7,6},{8,9},{9,8},{10,11... | collective-permute-start | bytes 208904 | tf_op jit(solution)/shard_map/ppermute | solution.py:42
  28.6 0.6 %current.1 = (f32[32,128]{1,0:T(8,128)S(1)}, f32[32,128]{1,0:T(8,128)S(1)}) custom-call(s32[192,128]{1,0:T(8,128)S(1)} %get-tuple-element.100.idx, f32[192,128]{1,0:T(8,128)S(1)} %get-tuple-element.101.w, f32[32,128]{1,0:T(8,128)S(1)} %get-tuple-element.118.eta, s32[16,128]{1,0:T(8,128)S(1)} %get-tuple-element.120.eta_pack, ...), custom_call_target="tpu_custom_call" | custom-call | tf_op jit(solution)/shard_map/current/pallas_call | solution.py:1181
  29.2 3.5 %all-to-all-start.1 = ((f32[32,2,128]{2,1,0:T(2,128)}), f32[32,2,128]{2,1,0:T(2,128)S(1)}, u32[]{:S(2)}, u32[]{:S(2)}) async-start(f32[32,2,128]{2,1,0:T(2,128)} %bitcast.7), calls=%async_computation.1 | async-start | bytes 65536 | tf_op jit(solution)/shard_map/all_to_all | solution.py:80
  32.7 0.8 %height.1.eta_part = f32[32,128]{1,0:T(8,128)S(1)} custom-call(s32[192,128]{1,0:T(8,128)S(1)} %get-tuple-element.100.idx, f32[192,128]{1,0:T(8,128)S(1)} %get-tuple-element.101.w, f32[32,128]{1,0:T(8,128)S(1)} %get-tuple-element.118.eta, f32[32,128]{1,0:T(8,128)S(1)} %get-tuple-element.127.u_part, f32[32,128]{1,0:T(8,128)S(1)} %get-tuple-element.128.v_part), custom_call_target="tpu_custom_call" | custom-call | tf_op jit(solution)/shard_map/height/pallas_call | solution.py:1191
  33.5 0.4 collective-permute-done.2.far
  33.8 0.0 collective-permute-done.3.near.near_swap
  33.9 0.8 %ocean.2 = (f32[32,128]{1,0:T(8,128)S(1)}, s32[16,128]{1,0:T(8,128)S(1)}, f32[8,128]{1,0:T(8,128)S(1)}, f32[32,128]{1,0:T(8,128)S(1)}, f32[32,128]{1,0:T(8,128)S...) custom-call(f32[136,128]{1,0:T(8,128)S(1)} %collective-permute-done.2.far, ...), custom_call_target="tpu_custom_call" | custom-call | tf_op jit(solution)/shard_map/ocean/pallas_call | solution.py:1230
  34.6 4.9 %collective-permute-start.4 = (f32[8,128]{1,0:T(8,128)S(1)}, f32[8,128]{1,0:T(8,128)S(1)}, u32[]{:S(2)}, u32[]{:S(2)}) collective-permute-start(f32[8,128]{1,0:T(8,128)S(1)} %get-tuple-element.143), channel_id=1, source_target_pairs={{1,2},{2,1},{3,4},{4,3},{5,6},{6,5},{7,8},{8,7},{9,10},{10,9},{11,... | collective-permute-start | bytes 12296 | tf_op jit(solution)/shard_map/ppermute | solution.py:42
  39.5 0.0 collective-permute-start.5
  39.5 1.3 %inner.2 = (f32[32,128]{1,0:T(8,128)S(1)}, f32[32,128]{1,0:T(8,128)S(1)}, f32[32,128]{1,0:T(8,128)S(1)}) custom-call(s32[192,128]{1,0:T(8,128)S(1)} %get-tuple-element.100.idx, f32[192,128]{1,0:T(8,128)S(1)} %get-tuple-element.101.w, f32[32,128]{1,0:T(8,128)S(1)} %get-tuple-element.133.eta, s32[16,128]{1,0:T(8,128)S(1)} %get-tuple-element.134.eta_pack, ...), custom_call_target="tpu_custom_call" | custom-call | tf_op jit(solution)/shard_map/inner/pallas_call | solution.py:1201
  40.8 0.0 all-to-all-done.1.arrived
  40.8 0.7 %back_remap.1.surface = f32[16,128]{1,0:T(8,128)S(1)} custom-call(s32[8,32]{1,0:T(8,128)S(4)} %get-tuple-element.85.marks.refs_0_, f32[32,2,128]{2,1,0:T(2,128)S(1)} %all-to-all-done.1.arrived, bf16[32,128,128]{2,1,0:T(8,128)(2,1)S(1)} %copy-done), custom_call_target="tpu_custom_call" | custom-call | tf_op jit(solution)/shard_map/back_remap/pallas_call | solution.py:1212
  41.5 0.0 collective-permute-done.4.far
  41.5 1.6 %collective-permute-done.5.near = f32[8,128]{1,0:T(8,128)S(1)} collective-permute-done((f32[8,128]{1,0:T(8,128)S(1)}, f32[8,128]{1,0:T(8,128)S(1)}, u32[]{:S(2)}, u32[]{:S(2)}) %collective-permute-start.5) | collective-permute-done | bytes 4128 | tf_op jit(solution)/shard_map/ppermute | solution.py:42
  43.1 0.8 %ocean.3 = (f32[32,128]{1,0:T(8,128)S(1)}, s32[16,128]{1,0:T(8,128)S(1)}, f32[8,128]{1,0:T(8,128)S(1)}, f32[32,128]{1,0:T(8,128)S(1)}, f32[32,128]{1,0:T(8,128)S...) custom-call(f32[8,128]{1,0:T(8,128)S(1)} %collective-permute-done.4.far, ...), custom_call_target="tpu_custom_call" | custom-call | tf_op jit(solution)/shard_map/ocean/pallas_call | solution.py:1230
  43.9 3.1 %collective-permute-start.6 = (f32[8,128]{1,0:T(8,128)S(1)}, f32[8,128]{1,0:T(8,128)S(1)}, u32[]{:S(2)}, u32[]{:S(2)}) collective-permute-start(f32[8,128]{1,0:T(8,128)S(1)} %get-tuple-element.149), channel_id=1, source_target_pairs={{1,2},{2,1},{3,4},{4,3},{5,6},{6,5},{7,8},{8,7},{9,10},{10,9},{11,... | collective-permute-start | bytes 12296 | tf_op jit(solution)/shard_map/ppermute | solution.py:42
  47.0 0.0 collective-permute-start.7
  47.0 1.8 %second_step.1 = f32[16,64,128]{2,1,0:T(8,128)} custom-call(f32[16,64,128]{2,1,0:T(8,128)S(1)} %get-tuple-element.94.loc, bf16[16,64,128]{2,1,0:T(8,128)(2,1)S(1)} %get-tuple-element.95.eastern, bf16[16,64,128]{2,1,0:T(8,128)(2,1)S(1)} %get-tuple-element.96.northern, f32[1,128]{1,0:T(1,128)S(1)} %get-tuple-element.84.refs_4_.breadth, ...), custom_call_target="tpu_custom_call" | custom-call | tf_op jit(solution)/shard_map/second_step/pallas_call | solution.py:1251
  48.8 1.3 %inner.3 = (f32[32,128]{1,0:T(8,128)S(1)}, f32[32,128]{1,0:T(8,128)S(1)}, f32[32,128]{1,0:T(8,128)S(1)}) custom-call(s32[192,128]{1,0:T(8,128)S(1)} %get-tuple-element.100.idx, f32[192,128]{1,0:T(8,128)S(1)} %get-tuple-element.101.w, f32[32,128]{1,0:T(8,128)S(1)} %get-tuple-element.151.eta, s32[16,128]{1,0:T(8,128)S(1)} %get-tuple-element.152.eta_pack, ...), custom_call_target="tpu_custom_call" | custom-call | tf_op jit(solution)/shard_map/inner/pallas_call | solution.py:1201
  50.1 0.5 collective-permute-done.6.far
  50.6 0.0 collective-permute-done.7.near
  50.6 1.0 %last_ocean.1 = (f32[32,128]{1,0:T(8,128)}, f32[2,4096]{1,0:T(2,128)}, f32[32,128]{1,0:T(8,128)}) custom-call(f32[8,128]{1,0:T(8,128)S(1)} %collective-permute-done.6.far, f32[8,128]{1,0:T(8,128)S(1)} %collective-permute-done.7.near, s32[8,128]{1,0:T(8,128)S(1)} %get-tuple-element.91.refs_8_.odd, f32[32,128]{1,0:T(8,128)S(1)} %get-tuple-element.151.eta, ...), custom_call_target="tpu_custom_call" | custom-call | tf_op jit(solution)/shard_map/last_ocean/pallas_call | solution.py:1241
Async XLA Ops:
  0.6 10.0 %copy-start = (bf16[32,128,128]{2,1,0:T(8,128)(2,1)S(1)}, bf16[32,128,128]{2,1,0:T(8,128)(2,1)}, u32[]{:S(2)}) copy-start(bf16[32,128,128]{2,1,0:T(8,128)(2,1)} %weights.3) | copy-start | bytes 3145732
  2.0 9.0 %collective-permute-start = (f32[56,128]{1,0:T(8,128)S(1)}, f32[56,128]{1,0:T(8,128)S(1)}, u32[]{:S(2)}, u32[]{:S(2)}) collective-permute-start(f32[56,128]{1,0:T(8,128)S(1)} %get-tuple-element.89), channel_id=1, source_target_pairs={{1,2},{2,1},{3,4},{4,3},{5,6},{6,5},{7,8},{8,7},{9,10},{10,9},{11,... | collective-permute-start | bytes 86024 | tf_op jit(solution)/shard_map/ppermute | solution.py:42
  8.4 3.9 %collective-permute-start.1 = (f32[56,128]{1,0:T(8,128)S(1)}, f32[56,128]{1,0:T(8,128)S(1)}, u32[]{:S(2)}, u32[]{:S(2)}) collective-permute-start(f32[56,128]{1,0:T(8,128)S(1)} %get-tuple-element.90), channel_id=1, source_target_pairs={{0,1},{1,0},{2,3},{3,2},{4,5},{5,4},{6,7},{7,6},{8,9},{9,8},{10,11... | collective-permute-start | bytes 86024 | tf_op jit(solution)/shard_map/ppermute | solution.py:42
  13.3 11.1 %all-to-all-start = ((bf16[32,16,128]{2,1,0:T(8,128)(2,1)}), bf16[32,16,128]{2,1,0:T(8,128)(2,1)S(1)}, u32[]{:S(2)}, u32[]{:S(2)}) async-start(bf16[32,16,128]{2,1,0:T(8,128)(2,1)} %forward_remap.1), calls=%async_computation | async-start | bytes 262144 | tf_op jit(solution)/shard_map/all_to_all | solution.py:80
  26.1 7.8 %collective-permute-start.2 = (f32[136,128]{1,0:T(8,128)S(1)}, f32[136,128]{1,0:T(8,128)S(1)}, u32[]{:S(2)}, u32[]{:S(2)}) collective-permute-start(f32[136,128]{1,0:T(8,128)S(1)} %get-tuple-element.115), channel_id=1, source_target_pairs={{1,2},{2,1},{3,4},{4,3},{5,6},{6,5},{7,8},{8,7},{9,10},{10,9},{11,... | collective-permute-start | bytes 208904 | tf_op jit(solution)/shard_map/ppermute | solution.py:42
  27.8 6.1 %collective-permute-start.3 = (f32[136,128]{1,0:T(8,128)S(1)}, f32[136,128]{1,0:T(8,128)S(1)}, u32[]{:S(2)}, u32[]{:S(2)}) collective-permute-start(f32[136,128]{1,0:T(8,128)S(1)} %get-tuple-element.116), channel_id=1, source_target_pairs={{0,1},{1,0},{2,3},{3,2},{4,5},{5,4},{6,7},{7,6},{8,9},{9,8},{10,11... | collective-permute-start | bytes 208904 | tf_op jit(solution)/shard_map/ppermute | solution.py:42
  29.2 11.6 %all-to-all-start.1 = ((f32[32,2,128]{2,1,0:T(2,128)}), f32[32,2,128]{2,1,0:T(2,128)S(1)}, u32[]{:S(2)}, u32[]{:S(2)}) async-start(f32[32,2,128]{2,1,0:T(2,128)} %bitcast.7), calls=%async_computation.1 | async-start | bytes 65536 | tf_op jit(solution)/shard_map/all_to_all | solution.py:80
  34.6 6.9 %collective-permute-start.4 = (f32[8,128]{1,0:T(8,128)S(1)}, f32[8,128]{1,0:T(8,128)S(1)}, u32[]{:S(2)}, u32[]{:S(2)}) collective-permute-start(f32[8,128]{1,0:T(8,128)S(1)} %get-tuple-element.143), channel_id=1, source_target_pairs={{1,2},{2,1},{3,4},{4,3},{5,6},{6,5},{7,8},{8,7},{9,10},{10,9},{11,... | collective-permute-start | bytes 12296 | tf_op jit(solution)/shard_map/ppermute | solution.py:42
  39.5 3.6 %collective-permute-start.5 = (f32[8,128]{1,0:T(8,128)S(1)}, f32[8,128]{1,0:T(8,128)S(1)}, u32[]{:S(2)}, u32[]{:S(2)}) collective-permute-start(f32[8,128]{1,0:T(8,128)S(1)} %get-tuple-element.144), channel_id=1, source_target_pairs={{0,1},{1,0},{2,3},{3,2},{4,5},{5,4},{6,7},{7,6},{8,9},{9,8},{10,11... | collective-permute-start | bytes 12296 | tf_op jit(solution)/shard_map/ppermute | solution.py:42
  43.9 6.7 %collective-permute-start.6 = (f32[8,128]{1,0:T(8,128)S(1)}, f32[8,128]{1,0:T(8,128)S(1)}, u32[]{:S(2)}, u32[]{:S(2)}) collective-permute-start(f32[8,128]{1,0:T(8,128)S(1)} %get-tuple-element.149), channel_id=1, source_target_pairs={{1,2},{2,1},{3,4},{4,3},{5,6},{6,5},{7,8},{8,7},{9,10},{10,9},{11,... | collective-permute-start | bytes 12296 | tf_op jit(solution)/shard_map/ppermute | solution.py:42
  47.0 3.6 %collective-permute-start.7 = (f32[8,128]{1,0:T(8,128)S(1)}, f32[8,128]{1,0:T(8,128)S(1)}, u32[]{:S(2)}, u32[]{:S(2)}) collective-permute-start(f32[8,128]{1,0:T(8,128)S(1)} %get-tuple-element.150), channel_id=1, source_target_pairs={{0,1},{1,0},{2,3},{3,2},{4,5},{5,4},{6,7},{7,6},{8,9},{9,8},{10,11... | collective-permute-start | bytes 12296 | tf_op jit(solution)/shard_map/ppermute | solution.py:42

commit v7 on v6

--- a/solution.py
+++ b/solution.py
@@ -544,9 +544,13 @@
     half = values.shape[0] // 2
     numbers = []
     for n, part in enumerate((values[:half], values[half:])):
-        largest = jnp.maximum(jnp.max(jnp.abs(part), axis=(0, 1), keepdims=True), 1e-30)
-        numbers.append(jnp.floor(part * (32767.0 / largest) + 0.5).astype(jnp.int32))
-        scales[n : n + 1] = jnp.broadcast_to(largest * (1.0 / 32767.0), (1, LANES))
+        top = jnp.max(part, axis=(0, 1), keepdims=True)
+        bottom = jnp.min(part, axis=(0, 1), keepdims=True)
+        middle = 0.5 * (top + bottom)
+        reach = jnp.maximum(jnp.maximum(top - middle, middle - bottom), 1e-30)
+        numbers.append(jnp.floor((part - middle) * (32767.0 / reach) + 0.5).astype(jnp.int32))
+        scales[n : n + 1] = jnp.broadcast_to(reach * (1.0 / 32767.0), (1, LANES))
+        scales[2 + n : 3 + n] = jnp.broadcast_to(middle, (1, LANES))
     packed[...] = (numbers[1] << 16) | (numbers[0] & 0xFFFF)
 
 
@@ -564,7 +568,9 @@
             words = jnp.where(row == r, lane_take(wide(packed[r : r + 1], lines), low), words)
         number = jnp.where(upper, words >> 16, (words << 16) >> 16)
         scale = jnp.where(upper, wide(scales[1:2], lines), wide(scales[0:1], lines))
-        return number.astype(jnp.float32) * scale
+        middle = jnp.where(upper, wide(scales[3:4], lines), wide(scales[2:3], lines))
+        inside = (own >= 0) & (own < 2 * half)
+        return jnp.where(inside, number.astype(jnp.float32) * scale + middle, 0.0)
 
     return by_tiles(one, idx)
 

time: 51.9 us -> 51.8 us (level)
  no operation moved by 1% of the time
where the time goes in v7:
time: 51.8 us; the launch traced here: 51.5 us
  starting transfers between devices  23.9 us (46%)
  Pallas kernels  18.6 us (36%)
  waiting for transfers between devices  8.25 us (16%)
  between operations  0.76 us (1%)
    ppermute x8, starting transfers between devices, swapped(): return lax.ppermute(value, RING, pairs)  17 us
    all_to_all x2, starting transfers between devices, exchange(): return lax.all_to_all(value, RING, split_axis=0, concat_axis=0, tiled=True)  6.92 us
    all_to_all x2, waiting for transfers between devices, exchange(): return lax.all_to_all(value, RING, split_axis=0, concat_axis=0, tiled=True)  4.45 us
    ppermute x8, waiting for transfers between devices, swapped(): return lax.ppermute(value, RING, pairs)  3.8 us
    pallas_call x2, Pallas kernels, shards(): pl.pallas_call(inner_kernel, in_specs=vmem(9), out_specs=vmem(3), out_sha...  2.64 us
    pallas_call x1, Pallas kernels, shards(): pl.pallas_call(lambda *refs: plan_kernel(*refs, devices=devices, tiles=ti...  2.18 us
    pallas_call x1, Pallas kernels, shards(): pl.pallas_call(local_step_kernel, in_specs=hbm(3) + vmem(3), out_specs=vm...  2.05 us
    pallas_call x1, Pallas kernels, shards(): pl.pallas_call(second_step_kernel, in_specs=vmem(14), out_specs=pl.BlockS...  1.8 us
  transfers between devices with their start and end apart: 10, of which 5 were waited for; matrix products, arithmetic and copies ran while one was open for 0% of the time, Pallas kernels for 25%

profile of v7, /device:TPU:0, one launch (start us, length us, event | category | flops | bytes accessed | tf_op | source)
XLA Modules:
  0.0 51.5 jit_solution(18218074105370268552)
XLA Ops:
  0.6 0.0 copy-start
  0.6 1.4 %prepare.1 = (s32[2,16,128]{2,1,0:T(8,128)S(1)}, f32[2,16,128]{2,1,0:T(8,128)S(1)}, f32[32,128]{1,0:T(8,128)S(1)}, s32[16,128]{1,0:T(8,128)S(1)}, f32[8,128]{1,0...) custom-call(f32[4,4,64,128]{3,2,1,0:T(8,128)} %bitcast.10, f32[1,128]{1,0:T(1,128)} %bitcast.14, ...), custom_call_target="tpu_custom_call" | custom-call | tf_op jit(solution)/shard_map/prepare/pallas_call | solution.py:1020
  2.0 6.4 %collective-permute-start = (f32[56,128]{1,0:T(8,128)S(1)}, f32[56,128]{1,0:T(8,128)S(1)}, u32[]{:S(2)}, u32[]{:S(2)}) collective-permute-start(f32[56,128]{1,0:T(8,128)S(1)} %get-tuple-element.89), channel_id=1, source_target_pairs={{1,2},{2,1},{3,4},{4,3},{5,6},{6,5},{7,8},{8,7},{9,10},{10,9},{11,... | collective-permute-start | bytes 86024 | tf_op jit(solution)/shard_map/ppermute | solution.py:42
  8.4 0.0 collective-permute-start.1
  8.5 2.2 %plan.1 = (f32[16,8,128]{2,1,0:T(8,128)S(1)}, f32[32,128]{1,0:T(8,128)S(1)}, f32[1,128]{1,0:T(1,128)S(1)}, s32[4,128]{1,0:T(4,128)S(1)}, s32[8,32]{1,0:T(8,128)S...) custom-call(f32[16,64,128]{2,1,0:T(8,128)} %air_hbm.1, ...), custom_call_target="tpu_custom_call" | custom-call | tf_op jit(solution)/shard_map/plan/pallas_call | solution.py:1059
  10.6 0.0 copy-done
  10.6 0.4 home_sums.1.refs_1_
  11.0 0.0 collective-permute-done.refs_6_.first_far
  11.0 1.3 %collective-permute-done.1.refs_7_.first_near = f32[56,128]{1,0:T(8,128)S(1)} collective-permute-done((f32[56,128]{1,0:T(8,128)S(1)}, f32[56,128]{1,0:T(8,128)S(1)}, u32[]{:S(2)}, u32[]{:S(2)}) %collective-permute-start.1) | collective-permute-done | bytes 28704 | tf_op jit(solution)/shard_map/ppermute | solution.py:42
  12.3 1.0 %forward_remap.1 = bf16[32,16,128]{2,1,0:T(8,128)(2,1)} custom-call(s32[8,32]{1,0:T(8,128)S(4)} %get-tuple-element.85.marks.refs_0_, f32[256,128]{1,0:T(8,128)S(1)} %home_sums.1.refs_1_, f32[16,8,128]{2,1,0:T(8,128)S(1)} %get-tuple-element.86.flux.refs_2_, f32[32,128]{1,0:T(8,128)S(1)} %get-tuple-element.87.refs_3_, ...), custom_call_target="tpu_custom_call" | custom-call | tf_op jit(solution)/shard_map/forward_remap/pallas_call | solution.py:1102
  13.3 3.4 %all-to-all-start = ((bf16[32,16,128]{2,1,0:T(8,128)(2,1)}), bf16[32,16,128]{2,1,0:T(8,128)(2,1)S(1)}, u32[]{:S(2)}, u32[]{:S(2)}) async-start(bf16[32,16,128]{2,1,0:T(8,128)(2,1)} %forward_remap.1), calls=%async_computation | async-start | bytes 262144 | tf_op jit(solution)/shard_map/all_to_all | solution.py:80
  16.7 2.0 %local_step.1 = (f32[16,64,128]{2,1,0:T(8,128)S(1)}, bf16[16,64,128]{2,1,0:T(8,128)(2,1)S(1)}, bf16[16,64,128]{2,1,0:T(8,128)(2,1)S(1)}, bf16[4,64,128]{2,1,0:T(...) custom-call(f32[16,64,128]{2,1,0:T(8,128)} %air_hbm.1, ...), custom_call_target="tpu_custom_call" | custom-call | tf_op jit(solution)/shard_map/local_step/pallas_call | solution.py:1137
  18.8 1.2 %first_gradient.1 = (f32[32,128]{1,0:T(8,128)S(1)}, f32[32,128]{1,0:T(8,128)S(1)}, f32[32,128]{1,0:T(8,128)S(1)}) custom-call(s32[192,128]{1,0:T(8,128)S(1)} %get-tuple-element.100.idx, f32[192,128]{1,0:T(8,128)S(1)} %get-tuple-element.101.w, f32[32,128]{1,0:T(8,128)S(1)} %get-tuple-element.102.eta, s32[16,128]{1,0:T(8,128)S(1)} %get-tuple-element.103.eta_pack, ...), custom_call_target="tpu_custom_call" | custom-call | tf_op jit(solution)/shard_map/first_gradient/pallas_call | solution.py:1119
  20.0 4.4 %all-to-all-done.arrived = bf16[32,16,128]{2,1,0:T(8,128)(2,1)S(1)} async-done(((bf16[32,16,128]{2,1,0:T(8,128)(2,1)}), bf16[32,16,128]{2,1,0:T(8,128)(2,1)S(1)}, u32[]{:S(2)}, u32[]{:S(2)}) %all-to-all-start) | async-done | bytes 131104 | tf_op jit(solution)/shard_map/all_to_all | solution.py:80
  24.5 1.5 %first_ocean.1 = (f32[32,128]{1,0:T(8,128)S(1)}, s32[16,128]{1,0:T(8,128)S(1)}, f32[8,128]{1,0:T(8,128)S(1)}, f32[32,128]{1,0:T(8,128)S(1)}, f32[32,128]{1,0:T(8...) custom-call(bf16[32,16,128]{2,1,0:T(8,128)(2,1)S(1)} %all-to-all-don, ...), custom_call_target="tpu_custom_call", output_to_operand_aliasing={{6}: (13, {}), {7}: (14, {})} | custom-call | tf_op jit(solution)/shard_map/first_ocean/pallas_call | solution.py:1160
  25.9 1.7 %collective-permute-start.2 = (f32[136,128]{1,0:T(8,128)S(1)}, f32[136,128]{1,0:T(8,128)S(1)}, u32[]{:S(2)}, u32[]{:S(2)}) collective-permute-start(f32[136,128]{1,0:T(8,128)S(1)} %get-tuple-element.115), channel_id=1, source_target_pairs={{1,2},{2,1},{3,4},{4,3},{5,6},{6,5},{7,8},{8,7},{9,10},{10,9},{11,... | collective-permute-start | bytes 208904 | tf_op jit(solution)/shard_map/ppermute | solution.py:42
  27.7 0.8 %collective-permute-start.3 = (f32[136,128]{1,0:T(8,128)S(1)}, f32[136,128]{1,0:T(8,128)S(1)}, u32[]{:S(2)}, u32[]{:S(2)}) collective-permute-start(f32[136,128]{1,0:T(8,128)S(1)} %get-tuple-element.116), channel_id=1, source_target_pairs={{0,1},{1,0},{2,3},{3,2},{4,5},{5,4},{6,7},{7,6},{8,9},{9,8},{10,11... | collective-permute-start | bytes 208904 | tf_op jit(solution)/shard_map/ppermute | solution.py:42
  28.5 0.6 %current.1 = (f32[32,128]{1,0:T(8,128)S(1)}, f32[32,128]{1,0:T(8,128)S(1)}) custom-call(s32[192,128]{1,0:T(8,128)S(1)} %get-tuple-element.100.idx, f32[192,128]{1,0:T(8,128)S(1)} %get-tuple-element.101.w, f32[32,128]{1,0:T(8,128)S(1)} %get-tuple-element.118.eta, s32[16,128]{1,0:T(8,128)S(1)} %get-tuple-element.120.eta_pack, ...), custom_call_target="tpu_custom_call" | custom-call | tf_op jit(solution)/shard_map/current/pallas_call | solution.py:1187
  29.0 3.5 %all-to-all-start.1 = ((f32[32,2,128]{2,1,0:T(2,128)}), f32[32,2,128]{2,1,0:T(2,128)S(1)}, u32[]{:S(2)}, u32[]{:S(2)}) async-start(f32[32,2,128]{2,1,0:T(2,128)} %bitcast.7), calls=%async_computation.1 | async-start | bytes 65536 | tf_op jit(solution)/shard_map/all_to_all | solution.py:80
  32.6 0.8 %height.1.eta_part = f32[32,128]{1,0:T(8,128)S(1)} custom-call(s32[192,128]{1,0:T(8,128)S(1)} %get-tuple-element.100.idx, f32[192,128]{1,0:T(8,128)S(1)} %get-tuple-element.101.w, f32[32,128]{1,0:T(8,128)S(1)} %get-tuple-element.118.eta, f32[32,128]{1,0:T(8,128)S(1)} %get-tuple-element.127.u_part, f32[32,128]{1,0:T(8,128)S(1)} %get-tuple-element.128.v_part), custom_call_target="tpu_custom_call" | custom-call | tf_op jit(solution)/shard_map/height/pallas_call | solution.py:1197
  33.3 0.4 collective-permute-done.2.far
  33.7 0.0 collective-permute-done.3.near.near_swap
  33.7 0.7 %ocean.2 = (f32[32,128]{1,0:T(8,128)S(1)}, s32[16,128]{1,0:T(8,128)S(1)}, f32[8,128]{1,0:T(8,128)S(1)}, f32[32,128]{1,0:T(8,128)S(1)}, f32[32,128]{1,0:T(8,128)S...) custom-call(f32[136,128]{1,0:T(8,128)S(1)} %collective-permute-done.2.far, ...), custom_call_target="tpu_custom_call" | custom-call | tf_op jit(solution)/shard_map/ocean/pallas_call | solution.py:1236
  34.5 4.9 %collective-permute-start.4 = (f32[8,128]{1,0:T(8,128)S(1)}, f32[8,128]{1,0:T(8,128)S(1)}, u32[]{:S(2)}, u32[]{:S(2)}) collective-permute-start(f32[8,128]{1,0:T(8,128)S(1)} %get-tuple-element.143), channel_id=1, source_target_pairs={{1,2},{2,1},{3,4},{4,3},{5,6},{6,5},{7,8},{8,7},{9,10},{10,9},{11,... | collective-permute-start | bytes 12296 | tf_op jit(solution)/shard_map/ppermute | solution.py:42
  39.4 0.0 collective-permute-start.5
  39.4 1.3 %inner.2 = (f32[32,128]{1,0:T(8,128)S(1)}, f32[32,128]{1,0:T(8,128)S(1)}, f32[32,128]{1,0:T(8,128)S(1)}) custom-call(s32[192,128]{1,0:T(8,128)S(1)} %get-tuple-element.100.idx, f32[192,128]{1,0:T(8,128)S(1)} %get-tuple-element.101.w, f32[32,128]{1,0:T(8,128)S(1)} %get-tuple-element.133.eta, s32[16,128]{1,0:T(8,128)S(1)} %get-tuple-element.134.eta_pack, ...), custom_call_target="tpu_custom_call" | custom-call | tf_op jit(solution)/shard_map/inner/pallas_call | solution.py:1207
  40.7 0.0 all-to-all-done.1.arrived
  40.7 0.7 %back_remap.1.surface = f32[16,128]{1,0:T(8,128)S(1)} custom-call(s32[8,32]{1,0:T(8,128)S(4)} %get-tuple-element.85.marks.refs_0_, f32[32,2,128]{2,1,0:T(2,128)S(1)} %all-to-all-done.1.arrived, bf16[32,128,128]{2,1,0:T(8,128)(2,1)S(1)} %copy-done), custom_call_target="tpu_custom_call" | custom-call | tf_op jit(solution)/shard_map/back_remap/pallas_call | solution.py:1218
  41.4 0.0 collective-permute-done.4.far
  41.4 1.6 %collective-permute-done.5.near = f32[8,128]{1,0:T(8,128)S(1)} collective-permute-done((f32[8,128]{1,0:T(8,128)S(1)}, f32[8,128]{1,0:T(8,128)S(1)}, u32[]{:S(2)}, u32[]{:S(2)}) %collective-permute-start.5) | collective-permute-done | bytes 4128 | tf_op jit(solution)/shard_map/ppermute | solution.py:42
  43.0 0.7 %ocean.3 = (f32[32,128]{1,0:T(8,128)S(1)}, s32[16,128]{1,0:T(8,128)S(1)}, f32[8,128]{1,0:T(8,128)S(1)}, f32[32,128]{1,0:T(8,128)S(1)}, f32[32,128]{1,0:T(8,128)S...) custom-call(f32[8,128]{1,0:T(8,128)S(1)} %collective-permute-done.4.far, ...), custom_call_target="tpu_custom_call" | custom-call | tf_op jit(solution)/shard_map/ocean/pallas_call | solution.py:1236
  43.7 3.1 %collective-permute-start.6 = (f32[8,128]{1,0:T(8,128)S(1)}, f32[8,128]{1,0:T(8,128)S(1)}, u32[]{:S(2)}, u32[]{:S(2)}) collective-permute-start(f32[8,128]{1,0:T(8,128)S(1)} %get-tuple-element.149), channel_id=1, source_target_pairs={{1,2},{2,1},{3,4},{4,3},{5,6},{6,5},{7,8},{8,7},{9,10},{10,9},{11,... | collective-permute-start | bytes 12296 | tf_op jit(solution)/shard_map/ppermute | solution.py:42
  46.8 0.0 collective-permute-start.7
  46.8 1.8 %second_step.1 = f32[16,64,128]{2,1,0:T(8,128)} custom-call(f32[16,64,128]{2,1,0:T(8,128)S(1)} %get-tuple-element.94.loc, bf16[16,64,128]{2,1,0:T(8,128)(2,1)S(1)} %get-tuple-element.95.eastern, bf16[16,64,128]{2,1,0:T(8,128)(2,1)S(1)} %get-tuple-element.96.northern, f32[1,128]{1,0:T(1,128)S(1)} %get-tuple-element.84.refs_4_.breadth, ...), custom_call_target="tpu_custom_call" | custom-call | tf_op jit(solution)/shard_map/second_step/pallas_call | solution.py:1257
  48.6 1.3 %inner.3 = (f32[32,128]{1,0:T(8,128)S(1)}, f32[32,128]{1,0:T(8,128)S(1)}, f32[32,128]{1,0:T(8,128)S(1)}) custom-call(s32[192,128]{1,0:T(8,128)S(1)} %get-tuple-element.100.idx, f32[192,128]{1,0:T(8,128)S(1)} %get-tuple-element.101.w, f32[32,128]{1,0:T(8,128)S(1)} %get-tuple-element.151.eta, s32[16,128]{1,0:T(8,128)S(1)} %get-tuple-element.152.eta_pack, ...), custom_call_target="tpu_custom_call" | custom-call | tf_op jit(solution)/shard_map/inner/pallas_call | solution.py:1207
  50.0 0.5 collective-permute-done.6.far
  50.4 0.0 collective-permute-done.7.near
  50.5 1.0 %last_ocean.1 = (f32[32,128]{1,0:T(8,128)}, f32[2,4096]{1,0:T(2,128)}, f32[32,128]{1,0:T(8,128)}) custom-call(f32[8,128]{1,0:T(8,128)S(1)} %collective-permute-done.6.far, f32[8,128]{1,0:T(8,128)S(1)} %collective-permute-done.7.near, s32[8,128]{1,0:T(8,128)S(1)} %get-tuple-element.91.refs_8_.odd, f32[32,128]{1,0:T(8,128)S(1)} %get-tuple-element.151.eta, ...), custom_call_target="tpu_custom_call" | custom-call | tf_op jit(solution)/shard_map/last_ocean/pallas_call | solution.py:1247
Async XLA Ops:
  0.6 10.0 %copy-start = (bf16[32,128,128]{2,1,0:T(8,128)(2,1)S(1)}, bf16[32,128,128]{2,1,0:T(8,128)(2,1)}, u32[]{:S(2)}) copy-start(bf16[32,128,128]{2,1,0:T(8,128)(2,1)} %weights.3) | copy-start | bytes 3145732
  2.0 9.0 %collective-permute-start = (f32[56,128]{1,0:T(8,128)S(1)}, f32[56,128]{1,0:T(8,128)S(1)}, u32[]{:S(2)}, u32[]{:S(2)}) collective-permute-start(f32[56,128]{1,0:T(8,128)S(1)} %get-tuple-element.89), channel_id=1, source_target_pairs={{1,2},{2,1},{3,4},{4,3},{5,6},{6,5},{7,8},{8,7},{9,10},{10,9},{11,... | collective-permute-start | bytes 86024 | tf_op jit(solution)/shard_map/ppermute | solution.py:42
  8.4 3.9 %collective-permute-start.1 = (f32[56,128]{1,0:T(8,128)S(1)}, f32[56,128]{1,0:T(8,128)S(1)}, u32[]{:S(2)}, u32[]{:S(2)}) collective-permute-start(f32[56,128]{1,0:T(8,128)S(1)} %get-tuple-element.90), channel_id=1, source_target_pairs={{0,1},{1,0},{2,3},{3,2},{4,5},{5,4},{6,7},{7,6},{8,9},{9,8},{10,11... | collective-permute-start | bytes 86024 | tf_op jit(solution)/shard_map/ppermute | solution.py:42
  13.3 11.1 %all-to-all-start = ((bf16[32,16,128]{2,1,0:T(8,128)(2,1)}), bf16[32,16,128]{2,1,0:T(8,128)(2,1)S(1)}, u32[]{:S(2)}, u32[]{:S(2)}) async-start(bf16[32,16,128]{2,1,0:T(8,128)(2,1)} %forward_remap.1), calls=%async_computation | async-start | bytes 262144 | tf_op jit(solution)/shard_map/all_to_all | solution.py:80
  25.9 7.8 %collective-permute-start.2 = (f32[136,128]{1,0:T(8,128)S(1)}, f32[136,128]{1,0:T(8,128)S(1)}, u32[]{:S(2)}, u32[]{:S(2)}) collective-permute-start(f32[136,128]{1,0:T(8,128)S(1)} %get-tuple-element.115), channel_id=1, source_target_pairs={{1,2},{2,1},{3,4},{4,3},{5,6},{6,5},{7,8},{8,7},{9,10},{10,9},{11,... | collective-permute-start | bytes 208904 | tf_op jit(solution)/shard_map/ppermute | solution.py:42
  27.7 6.1 %collective-permute-start.3 = (f32[136,128]{1,0:T(8,128)S(1)}, f32[136,128]{1,0:T(8,128)S(1)}, u32[]{:S(2)}, u32[]{:S(2)}) collective-permute-start(f32[136,128]{1,0:T(8,128)S(1)} %get-tuple-element.116), channel_id=1, source_target_pairs={{0,1},{1,0},{2,3},{3,2},{4,5},{5,4},{6,7},{7,6},{8,9},{9,8},{10,11... | collective-permute-start | bytes 208904 | tf_op jit(solution)/shard_map/ppermute | solution.py:42
  29.0 11.7 %all-to-all-start.1 = ((f32[32,2,128]{2,1,0:T(2,128)}), f32[32,2,128]{2,1,0:T(2,128)S(1)}, u32[]{:S(2)}, u32[]{:S(2)}) async-start(f32[32,2,128]{2,1,0:T(2,128)} %bitcast.7), calls=%async_computation.1 | async-start | bytes 65536 | tf_op jit(solution)/shard_map/all_to_all | solution.py:80
  34.5 6.9 %collective-permute-start.4 = (f32[8,128]{1,0:T(8,128)S(1)}, f32[8,128]{1,0:T(8,128)S(1)}, u32[]{:S(2)}, u32[]{:S(2)}) collective-permute-start(f32[8,128]{1,0:T(8,128)S(1)} %get-tuple-element.143), channel_id=1, source_target_pairs={{1,2},{2,1},{3,4},{4,3},{5,6},{6,5},{7,8},{8,7},{9,10},{10,9},{11,... | collective-permute-start | bytes 12296 | tf_op jit(solution)/shard_map/ppermute | solution.py:42
  39.4 3.6 %collective-permute-start.5 = (f32[8,128]{1,0:T(8,128)S(1)}, f32[8,128]{1,0:T(8,128)S(1)}, u32[]{:S(2)}, u32[]{:S(2)}) collective-permute-start(f32[8,128]{1,0:T(8,128)S(1)} %get-tuple-element.144), channel_id=1, source_target_pairs={{0,1},{1,0},{2,3},{3,2},{4,5},{5,4},{6,7},{7,6},{8,9},{9,8},{10,11... | collective-permute-start | bytes 12296 | tf_op jit(solution)/shard_map/ppermute | solution.py:42
  43.7 6.7 %collective-permute-start.6 = (f32[8,128]{1,0:T(8,128)S(1)}, f32[8,128]{1,0:T(8,128)S(1)}, u32[]{:S(2)}, u32[]{:S(2)}) collective-permute-start(f32[8,128]{1,0:T(8,128)S(1)} %get-tuple-element.149), channel_id=1, source_target_pairs={{1,2},{2,1},{3,4},{4,3},{5,6},{6,5},{7,8},{8,7},{9,10},{10,9},{11,... | collective-permute-start | bytes 12296 | tf_op jit(solution)/shard_map/ppermute | solution.py:42
  46.8 3.6 %collective-permute-start.7 = (f32[8,128]{1,0:T(8,128)S(1)}, f32[8,128]{1,0:T(8,128)S(1)}, u32[]{:S(2)}, u32[]{:S(2)}) collective-permute-start(f32[8,128]{1,0:T(8,128)S(1)} %get-tuple-element.150), channel_id=1, source_target_pairs={{0,1},{1,0},{2,3},{3,2},{4,5},{5,4},{6,7},{7,6},{8,9},{9,8},{10,11... | collective-permute-start | bytes 12296 | tf_op jit(solution)/shard_map/ppermute | solution.py:42

commit v8 on v7

--- a/solution.py
+++ b/solution.py
@@ -481,7 +481,7 @@
                 sums = jnp.dot(line, weights[b], preferred_element_type=jnp.float32)
                 extra[pl.ds(marks[MARK_HEAT, b], 1), :] = sums[0:1]
     line = lax.broadcasted_iota(jnp.int32, (8, LANES), 0)
-    part, copies = devices // 4, []
+    part, copies = devices, []
     for d in range(devices):
         mine, prev, following = (
             home[8 * (n % devices) : 8 * (n % devices) + 8] for n in (d, d - 1, d + 1)
@@ -537,7 +537,7 @@
             result = jnp.where(high == number, lane_take(wide(line, idx.shape[0]), low), result)
         return result
 
-    return by_tiles(one, idx)
+    return one(idx)
 
 
 def fill_pack(values, packed, scales):

time: 51.8 us -> 51.8 us (level)
  no operation moved by 1% of the time
where the time goes in v8:
time: 51.8 us; the launch traced here: 51.5 us
  starting transfers between devices  23.9 us (46%)
  Pallas kernels  18.6 us (36%)
  waiting for transfers between devices  8.25 us (16%)
  between operations  0.76 us (1%)
    ppermute x8, starting transfers between devices, swapped(): return lax.ppermute(value, RING, pairs)  17 us
    all_to_all x2, starting transfers between devices, exchange(): return lax.all_to_all(value, RING, split_axis=0, concat_axis=0, tiled=True)  6.92 us
    all_to_all x2, waiting for transfers between devices, exchange(): return lax.all_to_all(value, RING, split_axis=0, concat_axis=0, tiled=True)  4.45 us
    ppermute x8, waiting for transfers between devices, swapped(): return lax.ppermute(value, RING, pairs)  3.8 us
    pallas_call x2, Pallas kernels, shards(): pl.pallas_call(inner_kernel, in_specs=vmem(9), out_specs=vmem(3), out_sha...  2.64 us
    pallas_call x1, Pallas kernels, shards(): pl.pallas_call(lambda *refs: plan_kernel(*refs, devices=devices, tiles=ti...  2.18 us
    pallas_call x1, Pallas kernels, shards(): pl.pallas_call(local_step_kernel, in_specs=hbm(3) + vmem(3), out_specs=vm...  2.05 us
    pallas_call x1, Pallas kernels, shards(): pl.pallas_call(second_step_kernel, in_specs=vmem(14), out_specs=pl.BlockS...  1.8 us
  transfers between devices with their start and end apart: 10, of which 5 were waited for; matrix products, arithmetic and copies ran while one was open for 0% of the time, Pallas kernels for 25%

profile of v8, /device:TPU:0, one launch (start us, length us, event | category | flops | bytes accessed | tf_op | source)
XLA Modules:
  0.0 51.5 jit_solution(9589547130962788970)
XLA Ops:
  0.6 0.0 copy-start
  0.6 1.4 %prepare.1 = (s32[2,16,128]{2,1,0:T(8,128)S(1)}, f32[2,16,128]{2,1,0:T(8,128)S(1)}, f32[32,128]{1,0:T(8,128)S(1)}, s32[16,128]{1,0:T(8,128)S(1)}, f32[8,128]{1,0...) custom-call(f32[4,4,64,128]{3,2,1,0:T(8,128)} %bitcast.10, f32[1,128]{1,0:T(1,128)} %bitcast.14, ...), custom_call_target="tpu_custom_call" | custom-call | tf_op jit(solution)/shard_map/prepare/pallas_call | solution.py:1020
  2.0 6.4 %collective-permute-start = (f32[56,128]{1,0:T(8,128)S(1)}, f32[56,128]{1,0:T(8,128)S(1)}, u32[]{:S(2)}, u32[]{:S(2)}) collective-permute-start(f32[56,128]{1,0:T(8,128)S(1)} %get-tuple-element.89), channel_id=1, source_target_pairs={{1,2},{2,1},{3,4},{4,3},{5,6},{6,5},{7,8},{8,7},{9,10},{10,9},{11,... | collective-permute-start | bytes 86024 | tf_op jit(solution)/shard_map/ppermute | solution.py:42
  8.4 0.0 collective-permute-start.1
  8.5 2.2 %plan.1 = (f32[16,8,128]{2,1,0:T(8,128)S(1)}, f32[32,128]{1,0:T(8,128)S(1)}, f32[1,128]{1,0:T(1,128)S(1)}, s32[4,128]{1,0:T(4,128)S(1)}, s32[8,32]{1,0:T(8,128)S...) custom-call(f32[16,64,128]{2,1,0:T(8,128)} %air_hbm.1, ...), custom_call_target="tpu_custom_call" | custom-call | tf_op jit(solution)/shard_map/plan/pallas_call | solution.py:1059
  10.6 0.0 copy-done
  10.6 0.4 home_sums.1.refs_1_
  11.0 0.0 collective-permute-done.refs_6_.first_far
  11.0 1.3 %collective-permute-done.1.refs_7_.first_near = f32[56,128]{1,0:T(8,128)S(1)} collective-permute-done((f32[56,128]{1,0:T(8,128)S(1)}, f32[56,128]{1,0:T(8,128)S(1)}, u32[]{:S(2)}, u32[]{:S(2)}) %collective-permute-start.1) | collective-permute-done | bytes 28704 | tf_op jit(solution)/shard_map/ppermute | solution.py:42
  12.3 1.0 %forward_remap.1 = bf16[32,16,128]{2,1,0:T(8,128)(2,1)} custom-call(s32[8,32]{1,0:T(8,128)S(4)} %get-tuple-element.85.marks.refs_0_, f32[256,128]{1,0:T(8,128)S(1)} %home_sums.1.refs_1_, f32[16,8,128]{2,1,0:T(8,128)S(1)} %get-tuple-element.86.flux.refs_2_, f32[32,128]{1,0:T(8,128)S(1)} %get-tuple-element.87.refs_3_, ...), custom_call_target="tpu_custom_call" | custom-call | tf_op jit(solution)/shard_map/forward_remap/pallas_call | solution.py:1102
  13.4 3.4 %all-to-all-start = ((bf16[32,16,128]{2,1,0:T(8,128)(2,1)}), bf16[32,16,128]{2,1,0:T(8,128)(2,1)S(1)}, u32[]{:S(2)}, u32[]{:S(2)}) async-start(bf16[32,16,128]{2,1,0:T(8,128)(2,1)} %forward_remap.1), calls=%async_computation | async-start | bytes 262144 | tf_op jit(solution)/shard_map/all_to_all | solution.py:80
  16.8 2.0 %local_step.1 = (f32[16,64,128]{2,1,0:T(8,128)S(1)}, bf16[16,64,128]{2,1,0:T(8,128)(2,1)S(1)}, bf16[16,64,128]{2,1,0:T(8,128)(2,1)S(1)}, bf16[4,64,128]{2,1,0:T(...) custom-call(f32[16,64,128]{2,1,0:T(8,128)} %air_hbm.1, ...), custom_call_target="tpu_custom_call" | custom-call | tf_op jit(solution)/shard_map/local_step/pallas_call | solution.py:1137
  18.8 1.2 %first_gradient.1 = (f32[32,128]{1,0:T(8,128)S(1)}, f32[32,128]{1,0:T(8,128)S(1)}, f32[32,128]{1,0:T(8,128)S(1)}) custom-call(s32[192,128]{1,0:T(8,128)S(1)} %get-tuple-element.100.idx, f32[192,128]{1,0:T(8,128)S(1)} %get-tuple-element.101.w, f32[32,128]{1,0:T(8,128)S(1)} %get-tuple-element.102.eta, s32[16,128]{1,0:T(8,128)S(1)} %get-tuple-element.103.eta_pack, ...), custom_call_target="tpu_custom_call" | custom-call | tf_op jit(solution)/shard_map/first_gradient/pallas_call | solution.py:1119
  20.1 4.4 %all-to-all-done.arrived = bf16[32,16,128]{2,1,0:T(8,128)(2,1)S(1)} async-done(((bf16[32,16,128]{2,1,0:T(8,128)(2,1)}), bf16[32,16,128]{2,1,0:T(8,128)(2,1)S(1)}, u32[]{:S(2)}, u32[]{:S(2)}) %all-to-all-start) | async-done | bytes 131104 | tf_op jit(solution)/shard_map/all_to_all | solution.py:80
  24.5 1.4 %first_ocean.1 = (f32[32,128]{1,0:T(8,128)S(1)}, s32[16,128]{1,0:T(8,128)S(1)}, f32[8,128]{1,0:T(8,128)S(1)}, f32[32,128]{1,0:T(8,128)S(1)}, f32[32,128]{1,0:T(8...) custom-call(bf16[32,16,128]{2,1,0:T(8,128)(2,1)S(1)} %all-to-all-don, ...), custom_call_target="tpu_custom_call", output_to_operand_aliasing={{6}: (13, {}), {7}: (14, {})} | custom-call | tf_op jit(solution)/shard_map/first_ocean/pallas_call | solution.py:1160
  26.0 1.7 %collective-permute-start.2 = (f32[136,128]{1,0:T(8,128)S(1)}, f32[136,128]{1,0:T(8,128)S(1)}, u32[]{:S(2)}, u32[]{:S(2)}) collective-permute-start(f32[136,128]{1,0:T(8,128)S(1)} %get-tuple-element.115), channel_id=1, source_target_pairs={{1,2},{2,1},{3,4},{4,3},{5,6},{6,5},{7,8},{8,7},{9,10},{10,9},{11,... | collective-permute-start | bytes 208904 | tf_op jit(solution)/shard_map/ppermute | solution.py:42
  27.7 0.8 %collective-permute-start.3 = (f32[136,128]{1,0:T(8,128)S(1)}, f32[136,128]{1,0:T(8,128)S(1)}, u32[]{:S(2)}, u32[]{:S(2)}) collective-permute-start(f32[136,128]{1,0:T(8,128)S(1)} %get-tuple-element.116), channel_id=1, source_target_pairs={{0,1},{1,0},{2,3},{3,2},{4,5},{5,4},{6,7},{7,6},{8,9},{9,8},{10,11... | collective-permute-start | bytes 208904 | tf_op jit(solution)/shard_map/ppermute | solution.py:42
  28.5 0.6 %current.1 = (f32[32,128]{1,0:T(8,128)S(1)}, f32[32,128]{1,0:T(8,128)S(1)}) custom-call(s32[192,128]{1,0:T(8,128)S(1)} %get-tuple-element.100.idx, f32[192,128]{1,0:T(8,128)S(1)} %get-tuple-element.101.w, f32[32,128]{1,0:T(8,128)S(1)} %get-tuple-element.118.eta, s32[16,128]{1,0:T(8,128)S(1)} %get-tuple-element.120.eta_pack, ...), custom_call_target="tpu_custom_call" | custom-call | tf_op jit(solution)/shard_map/current/pallas_call | solution.py:1187
  29.1 3.5 %all-to-all-start.1 = ((f32[32,2,128]{2,1,0:T(2,128)}), f32[32,2,128]{2,1,0:T(2,128)S(1)}, u32[]{:S(2)}, u32[]{:S(2)}) async-start(f32[32,2,128]{2,1,0:T(2,128)} %bitcast.7), calls=%async_computation.1 | async-start | bytes 65536 | tf_op jit(solution)/shard_map/all_to_all | solution.py:80
  32.6 0.8 %height.1.eta_part = f32[32,128]{1,0:T(8,128)S(1)} custom-call(s32[192,128]{1,0:T(8,128)S(1)} %get-tuple-element.100.idx, f32[192,128]{1,0:T(8,128)S(1)} %get-tuple-element.101.w, f32[32,128]{1,0:T(8,128)S(1)} %get-tuple-element.118.eta, f32[32,128]{1,0:T(8,128)S(1)} %get-tuple-element.127.u_part, f32[32,128]{1,0:T(8,128)S(1)} %get-tuple-element.128.v_part), custom_call_target="tpu_custom_call" | custom-call | tf_op jit(solution)/shard_map/height/pallas_call | solution.py:1197
  33.4 0.4 collective-permute-done.2.far
  33.7 0.0 collective-permute-done.3.near.near_swap
  33.8 0.8 %ocean.2 = (f32[32,128]{1,0:T(8,128)S(1)}, s32[16,128]{1,0:T(8,128)S(1)}, f32[8,128]{1,0:T(8,128)S(1)}, f32[32,128]{1,0:T(8,128)S(1)}, f32[32,128]{1,0:T(8,128)S...) custom-call(f32[136,128]{1,0:T(8,128)S(1)} %collective-permute-done.2.far, ...), custom_call_target="tpu_custom_call" | custom-call | tf_op jit(solution)/shard_map/ocean/pallas_call | solution.py:1236
  34.5 4.9 %collective-permute-start.4 = (f32[8,128]{1,0:T(8,128)S(1)}, f32[8,128]{1,0:T(8,128)S(1)}, u32[]{:S(2)}, u32[]{:S(2)}) collective-permute-start(f32[8,128]{1,0:T(8,128)S(1)} %get-tuple-element.143), channel_id=1, source_target_pairs={{1,2},{2,1},{3,4},{4,3},{5,6},{6,5},{7,8},{8,7},{9,10},{10,9},{11,... | collective-permute-start | bytes 12296 | tf_op jit(solution)/shard_map/ppermute | solution.py:42
  39.4 0.0 collective-permute-start.5
  39.4 1.3 %inner.2 = (f32[32,128]{1,0:T(8,128)S(1)}, f32[32,128]{1,0:T(8,128)S(1)}, f32[32,128]{1,0:T(8,128)S(1)}) custom-call(s32[192,128]{1,0:T(8,128)S(1)} %get-tuple-element.100.idx, f32[192,128]{1,0:T(8,128)S(1)} %get-tuple-element.101.w, f32[32,128]{1,0:T(8,128)S(1)} %get-tuple-element.133.eta, s32[16,128]{1,0:T(8,128)S(1)} %get-tuple-element.134.eta_pack, ...), custom_call_target="tpu_custom_call" | custom-call | tf_op jit(solution)/shard_map/inner/pallas_call | solution.py:1207
  40.7 0.0 all-to-all-done.1.arrived
  40.8 0.7 %back_remap.1.surface = f32[16,128]{1,0:T(8,128)S(1)} custom-call(s32[8,32]{1,0:T(8,128)S(4)} %get-tuple-element.85.marks.refs_0_, f32[32,2,128]{2,1,0:T(2,128)S(1)} %all-to-all-done.1.arrived, bf16[32,128,128]{2,1,0:T(8,128)(2,1)S(1)} %copy-done), custom_call_target="tpu_custom_call" | custom-call | tf_op jit(solution)/shard_map/back_remap/pallas_call | solution.py:1218
  41.4 0.0 collective-permute-done.4.far
  41.4 1.6 %collective-permute-done.5.near = f32[8,128]{1,0:T(8,128)S(1)} collective-permute-done((f32[8,128]{1,0:T(8,128)S(1)}, f32[8,128]{1,0:T(8,128)S(1)}, u32[]{:S(2)}, u32[]{:S(2)}) %collective-permute-start.5) | collective-permute-done | bytes 4128 | tf_op jit(solution)/shard_map/ppermute | solution.py:42
  43.0 0.8 %ocean.3 = (f32[32,128]{1,0:T(8,128)S(1)}, s32[16,128]{1,0:T(8,128)S(1)}, f32[8,128]{1,0:T(8,128)S(1)}, f32[32,128]{1,0:T(8,128)S(1)}, f32[32,128]{1,0:T(8,128)S...) custom-call(f32[8,128]{1,0:T(8,128)S(1)} %collective-permute-done.4.far, ...), custom_call_target="tpu_custom_call" | custom-call | tf_op jit(solution)/shard_map/ocean/pallas_call | solution.py:1236
  43.8 3.1 %collective-permute-start.6 = (f32[8,128]{1,0:T(8,128)S(1)}, f32[8,128]{1,0:T(8,128)S(1)}, u32[]{:S(2)}, u32[]{:S(2)}) collective-permute-start(f32[8,128]{1,0:T(8,128)S(1)} %get-tuple-element.149), channel_id=1, source_target_pairs={{1,2},{2,1},{3,4},{4,3},{5,6},{6,5},{7,8},{8,7},{9,10},{10,9},{11,... | collective-permute-start | bytes 12296 | tf_op jit(solution)/shard_map/ppermute | solution.py:42
  46.9 0.0 collective-permute-start.7
  46.9 1.8 %second_step.1 = f32[16,64,128]{2,1,0:T(8,128)} custom-call(f32[16,64,128]{2,1,0:T(8,128)S(1)} %get-tuple-element.94.loc, bf16[16,64,128]{2,1,0:T(8,128)(2,1)S(1)} %get-tuple-element.95.eastern, bf16[16,64,128]{2,1,0:T(8,128)(2,1)S(1)} %get-tuple-element.96.northern, f32[1,128]{1,0:T(1,128)S(1)} %get-tuple-element.84.refs_4_.breadth, ...), custom_call_target="tpu_custom_call" | custom-call | tf_op jit(solution)/shard_map/second_step/pallas_call | solution.py:1257
  48.7 1.3 %inner.3 = (f32[32,128]{1,0:T(8,128)S(1)}, f32[32,128]{1,0:T(8,128)S(1)}, f32[32,128]{1,0:T(8,128)S(1)}) custom-call(s32[192,128]{1,0:T(8,128)S(1)} %get-tuple-element.100.idx, f32[192,128]{1,0:T(8,128)S(1)} %get-tuple-element.101.w, f32[32,128]{1,0:T(8,128)S(1)} %get-tuple-element.151.eta, s32[16,128]{1,0:T(8,128)S(1)} %get-tuple-element.152.eta_pack, ...), custom_call_target="tpu_custom_call" | custom-call | tf_op jit(solution)/shard_map/inner/pallas_call | solution.py:1207
  50.0 0.5 collective-permute-done.6.far
  50.5 0.0 collective-permute-done.7.near
  50.5 1.0 %last_ocean.1 = (f32[32,128]{1,0:T(8,128)}, f32[2,4096]{1,0:T(2,128)}, f32[32,128]{1,0:T(8,128)}) custom-call(f32[8,128]{1,0:T(8,128)S(1)} %collective-permute-done.6.far, f32[8,128]{1,0:T(8,128)S(1)} %collective-permute-done.7.near, s32[8,128]{1,0:T(8,128)S(1)} %get-tuple-element.91.refs_8_.odd, f32[32,128]{1,0:T(8,128)S(1)} %get-tuple-element.151.eta, ...), custom_call_target="tpu_custom_call" | custom-call | tf_op jit(solution)/shard_map/last_ocean/pallas_call | solution.py:1247
Async XLA Ops:
  0.6 10.0 %copy-start = (bf16[32,128,128]{2,1,0:T(8,128)(2,1)S(1)}, bf16[32,128,128]{2,1,0:T(8,128)(2,1)}, u32[]{:S(2)}) copy-start(bf16[32,128,128]{2,1,0:T(8,128)(2,1)} %weights.3) | copy-start | bytes 3145732
  2.0 9.0 %collective-permute-start = (f32[56,128]{1,0:T(8,128)S(1)}, f32[56,128]{1,0:T(8,128)S(1)}, u32[]{:S(2)}, u32[]{:S(2)}) collective-permute-start(f32[56,128]{1,0:T(8,128)S(1)} %get-tuple-element.89), channel_id=1, source_target_pairs={{1,2},{2,1},{3,4},{4,3},{5,6},{6,5},{7,8},{8,7},{9,10},{10,9},{11,... | collective-permute-start | bytes 86024 | tf_op jit(solution)/shard_map/ppermute | solution.py:42
  8.4 3.9 %collective-permute-start.1 = (f32[56,128]{1,0:T(8,128)S(1)}, f32[56,128]{1,0:T(8,128)S(1)}, u32[]{:S(2)}, u32[]{:S(2)}) collective-permute-start(f32[56,128]{1,0:T(8,128)S(1)} %get-tuple-element.90), channel_id=1, source_target_pairs={{0,1},{1,0},{2,3},{3,2},{4,5},{5,4},{6,7},{7,6},{8,9},{9,8},{10,11... | collective-permute-start | bytes 86024 | tf_op jit(solution)/shard_map/ppermute | solution.py:42
  13.4 11.1 %all-to-all-start = ((bf16[32,16,128]{2,1,0:T(8,128)(2,1)}), bf16[32,16,128]{2,1,0:T(8,128)(2,1)S(1)}, u32[]{:S(2)}, u32[]{:S(2)}) async-start(bf16[32,16,128]{2,1,0:T(8,128)(2,1)} %forward_remap.1), calls=%async_computation | async-start | bytes 262144 | tf_op jit(solution)/shard_map/all_to_all | solution.py:80
  26.0 7.8 %collective-permute-start.2 = (f32[136,128]{1,0:T(8,128)S(1)}, f32[136,128]{1,0:T(8,128)S(1)}, u32[]{:S(2)}, u32[]{:S(2)}) collective-permute-start(f32[136,128]{1,0:T(8,128)S(1)} %get-tuple-element.115), channel_id=1, source_target_pairs={{1,2},{2,1},{3,4},{4,3},{5,6},{6,5},{7,8},{8,7},{9,10},{10,9},{11,... | collective-permute-start | bytes 208904 | tf_op jit(solution)/shard_map/ppermute | solution.py:42
  27.7 6.1 %collective-permute-start.3 = (f32[136,128]{1,0:T(8,128)S(1)}, f32[136,128]{1,0:T(8,128)S(1)}, u32[]{:S(2)}, u32[]{:S(2)}) collective-permute-start(f32[136,128]{1,0:T(8,128)S(1)} %get-tuple-element.116), channel_id=1, source_target_pairs={{0,1},{1,0},{2,3},{3,2},{4,5},{5,4},{6,7},{7,6},{8,9},{9,8},{10,11... | collective-permute-start | bytes 208904 | tf_op jit(solution)/shard_map/ppermute | solution.py:42
  29.1 11.7 %all-to-all-start.1 = ((f32[32,2,128]{2,1,0:T(2,128)}), f32[32,2,128]{2,1,0:T(2,128)S(1)}, u32[]{:S(2)}, u32[]{:S(2)}) async-start(f32[32,2,128]{2,1,0:T(2,128)} %bitcast.7), calls=%async_computation.1 | async-start | bytes 65536 | tf_op jit(solution)/shard_map/all_to_all | solution.py:80
  34.5 6.9 %collective-permute-start.4 = (f32[8,128]{1,0:T(8,128)S(1)}, f32[8,128]{1,0:T(8,128)S(1)}, u32[]{:S(2)}, u32[]{:S(2)}) collective-permute-start(f32[8,128]{1,0:T(8,128)S(1)} %get-tuple-element.143), channel_id=1, source_target_pairs={{1,2},{2,1},{3,4},{4,3},{5,6},{6,5},{7,8},{8,7},{9,10},{10,9},{11,... | collective-permute-start | bytes 12296 | tf_op jit(solution)/shard_map/ppermute | solution.py:42
  39.4 3.6 %collective-permute-start.5 = (f32[8,128]{1,0:T(8,128)S(1)}, f32[8,128]{1,0:T(8,128)S(1)}, u32[]{:S(2)}, u32[]{:S(2)}) collective-permute-start(f32[8,128]{1,0:T(8,128)S(1)} %get-tuple-element.144), channel_id=1, source_target_pairs={{0,1},{1,0},{2,3},{3,2},{4,5},{5,4},{6,7},{7,6},{8,9},{9,8},{10,11... | collective-permute-start | bytes 12296 | tf_op jit(solution)/shard_map/ppermute | solution.py:42
  43.8 6.7 %collective-permute-start.6 = (f32[8,128]{1,0:T(8,128)S(1)}, f32[8,128]{1,0:T(8,128)S(1)}, u32[]{:S(2)}, u32[]{:S(2)}) collective-permute-start(f32[8,128]{1,0:T(8,128)S(1)} %get-tuple-element.149), channel_id=1, source_target_pairs={{1,2},{2,1},{3,4},{4,3},{5,6},{6,5},{7,8},{8,7},{9,10},{10,9},{11,... | collective-permute-start | bytes 12296 | tf_op jit(solution)/shard_map/ppermute | solution.py:42
  46.9 3.6 %collective-permute-start.7 = (f32[8,128]{1,0:T(8,128)S(1)}, f32[8,128]{1,0:T(8,128)S(1)}, u32[]{:S(2)}, u32[]{:S(2)}) collective-permute-start(f32[8,128]{1,0:T(8,128)S(1)} %get-tuple-element.150), channel_id=1, source_target_pairs={{0,1},{1,0},{2,3},{3,2},{4,5},{5,4},{6,7},{7,6},{8,9},{9,8},{10,11... | collective-permute-start | bytes 12296 | tf_op jit(solution)/shard_map/ppermute | solution.py:42
